TPU v7x, 32 devices: a whole 2x2x4 slice. The times are simulated.
32 devices in a mesh: row: 4 (over x, core), col: 8 (over z, y).
Axes of the slice: x: 2, y: 2, z: 4, core: 2. Of those that a mesh axis runs over, the one named last changes fastest.
Arguments:
- currents: bfloat16 [12288, 256], P(('row', 'col')), may hold values from -6 to 6
- incidence: int32 [2, 12288], P(None, ('row', 'col')), may hold values from 0 to 8191, as said below
- centroids: int32 [3, 8192], P(None, ('row', 'col')), may hold values from 0 to 255, as said below
- sweep_weights: float32 [2], replicated, may hold values from 0.2 to 0.6
Outputs:
- updated: bfloat16 [12288, 256], P(('row', 'col'))
- potentials: bfloat16 [8192, 256], P(('row', 'col'))
Inputs may be any that keep to these rules, and one draw needn't show every extreme that they name: `incidence`: triangles o * 256 to (o + 1) * 256 - 1 form owner block o. Counting both rows, the edges of one device name at most 64 triangles of any one owner block, and exactly 64 of some block on every device. `centroids`: first two rows from 0 to 255, third row from 0 to 3.
All inputs are finite; a program needn't handle non-finite values.
Results may differ from a plain program's by a relative error of at most 0.006.
Values may be sent and summed in bfloat16 or wider, within the bound.
No kernel may reach another device: no remote copies, remote signals or barrier semaphores. Data moves between devices by JAX's collectives and lax.ppermute only.
A program may use at most 128 MiB of HBM per device.

v0:
```python
import math

import jax
import jax.numpy as jnp
from jax import lax
from jax.sharding import PartitionSpec as P

WAVE = 0.19634954084936207
SOFT = 1.0
SPACING = 0.2


def tile_pair(row_pts, col_pts):
    dx = (row_pts[0][:, None] - col_pts[0][None, :]).astype(jnp.float32)
    dy = (row_pts[1][:, None] - col_pts[1][None, :]).astype(jnp.float32)
    dz = (row_pts[2][:, None] - col_pts[2][None, :]).astype(jnp.float32)
    radius = jnp.sqrt(dx * dx + dy * dy + dz * dz + SOFT * SOFT)
    scaled = SPACING / radius
    return (
        (scaled * jnp.cos(WAVE * radius)).astype(jnp.bfloat16),
        (-scaled * jnp.sin(WAVE * radius)).astype(jnp.bfloat16),
    )


def blend(real_part, imag_part):
    half = real_part.shape[1] // 2
    return jnp.concatenate(
        [real_part[:, :half] - imag_part[:, half:], real_part[:, half:] + imag_part[:, :half]], 1
    )


def row_block(row_count, col_count):
    target = max(1, 2**20 // max(1, col_count))
    power = 1 << target.bit_length() - 1
    return max(min(512, row_count), math.gcd(row_count, power))


def per_device(currents, incidence, centroids, sweep_weights):
    n_row = lax.axis_size("row")
    n_col = lax.axis_size("col")
    devices = n_row * n_col
    tri_dev = centroids.shape[1]
    edge_dev = currents.shape[0]
    width = currents.shape[1]
    slots = 8 * tri_dev // devices
    cells = devices * slots
    row_points = lax.all_gather(centroids, "col", axis=1, tiled=True)
    col_points = lax.all_gather(centroids, "row", axis=1, tiled=True)
    row_count = row_points.shape[1]
    triangle = incidence.reshape(-1)
    owner = triangle // tri_dev
    local = triangle % tri_dev
    owner_hits = (owner[:, None] == jnp.arange(devices, dtype=jnp.int32)[None, :]).astype(jnp.int32)
    position = jnp.cumsum(owner_hits, axis=0)
    rank = jnp.sum(owner_hits * position, axis=1) - 1
    slot = owner * slots + rank
    labels = jnp.zeros((cells,), jnp.int32).at[slot].set(local + 1)
    keep_block = row_block(row_count, col_points.shape[1])

    def make_block(index):
        points = lax.dynamic_slice_in_dim(row_points, index * keep_block, keep_block, 1)
        return tile_pair(points, col_points)

    kept_real, kept_imag = lax.map(make_block, jnp.arange(row_count // keep_block, dtype=jnp.int32))
    kept_real = kept_real.reshape(row_count, col_points.shape[1])
    kept_imag = kept_imag.reshape(row_count, col_points.shape[1])
    current = currents
    potential = None
    for sweep in range(sweep_weights.shape[0]):
        signed = jnp.concatenate([current, -current], 0)
        outgoing = jnp.zeros((cells, width), jnp.bfloat16).at[slot].set(signed)
        route_flat_vals = outgoing.reshape(devices, slots, width)
        flat_marks = labels.reshape(devices, slots)
        got_vals = lax.all_to_all(
            route_flat_vals, ("row", "col"), split_axis=0, concat_axis=0, tiled=True
        )
        got_marks = lax.all_to_all(
            flat_marks, ("row", "col"), split_axis=0, concat_axis=0, tiled=True
        )
        arrived = got_vals.reshape(cells, width)
        arrived_marks = got_marks.reshape(cells)
        slot_map = (
            arrived_marks[:, None] == jnp.arange(1, tri_dev + 1, dtype=jnp.int32)[None, :]
        ).astype(jnp.bfloat16)
        charges = lax.dot_general(
            slot_map, arrived, (((0,), (0,)), ((), ())), preferred_element_type=jnp.float32
        ).astype(jnp.bfloat16)
        piece = lax.all_gather(charges, "row", axis=0, tiled=True)
        partial_value = blend(
            jnp.dot(kept_real, piece, preferred_element_type=jnp.float32),
            jnp.dot(kept_imag, piece, preferred_element_type=jnp.float32),
        )
        owned = lax.psum_scatter(partial_value, "col", scatter_dimension=0, tiled=True)
        potential = owned.astype(jnp.bfloat16)
        answers = jnp.dot(slot_map, potential, preferred_element_type=jnp.float32).astype(
            jnp.bfloat16
        )
        flat_vals = answers.reshape(devices, slots, width)
        got = lax.all_to_all(flat_vals, ("row", "col"), split_axis=0, concat_axis=0, tiled=True)
        returned = got.reshape(cells, width)
        picked = returned[slot]
        slope = picked[:edge_dev].astype(jnp.float32) - picked[edge_dev:].astype(jnp.float32)
        current = (current.astype(jnp.float32) - sweep_weights[sweep] * slope).astype(jnp.bfloat16)
    return (current, potential)


def solution(mesh):
    in_specs = (P(("row", "col"), None), P(None, ("row", "col")), P(None, ("row", "col")), P())
    out_specs = (P(("row", "col"), None), P(("row", "col"), None))
    return jax.shard_map(
        per_device, mesh=mesh, in_specs=in_specs, out_specs=out_specs, check_vma=False
    )
```

profile of v0, /device:TPU:0, one launch (start us, length us, event | category | flops | bytes accessed | tf_op | source)
XLA Modules:
  0.0 401.1 jit_solution(16908688588934819719)
XLA Ops:
  7.2 0.7 reshape.535
  7.9 0.7 reshape.536
  8.6 1.7 reduce-window.6
  10.3 0.3 slice_reduce_fusion
  10.8 0.7 copy.10
  11.5 3.4 scatter_custom_fusion
  14.9 0.7 all_to_all.19
  15.6 7.3 %all-to-all-start = ((s32[32,1,64]{2,1,0:T(1,128)}), s32[32,1,64]{2,1,0:T(1,128)S(1)}, u32[]{:S(2)}, u32[]{:S(2)}) async-start(s32[32,1,64]{2,1,0:T(1,128)} %all_to_all.19), calls=%async_computation | async-start | bytes 32768 | tf_op jit(solution)/shard_map/all_to_all | solution.py:77
  22.9 1.0 neg.16
  23.9 7.7 %scatter_custom_fusion.1 = bf16[2048,256]{1,0:T(8,128)(2,1)} fusion(s32[768]{0:T(1024)S(1)} %fusion.51, bf16[]{:T(256)} %constant.64.clone.1, bf16[384,256]{1,0:T(8,128)(2,1)S(1)} %neg.16, bf16[]{:T(256)} %constant.70, bf16[384,256]{1,0:T(8,128)(2,1)} %param.6), kind=kCustom, calls=%fused_computation.40 | custom fusion | flops 786432 | bytes 1441796 | tf_op jit(solution)/shard_map/scatter | solution.py:71
  31.6 5.3 %all_gather.13 = s32[3,1024]{1,0:T(4,128)S(1)} all-gather(s32[3,256]{1,0:T(4,128)} %param.8), channel_id=1, replica_groups=mesh['row'=4,'col'=8] {'row'}, dimensions={1}, use_global_device_ids=true | all-gather | bytes 15360 | tf_op jit(solution)/shard_map/all_gather | solution.py:48
  36.9 30.9 %all_gather.12 = s32[3,2048]{1,0:T(4,128)S(1)} all-gather(s32[3,256]{1,0:T(4,128)} %param.8), channel_id=1, replica_groups=mesh['row'=4,'col'=8] {'col'}, dimensions={1}, use_global_device_ids=true | all-gather | bytes 27648 | tf_op jit(solution)/shard_map/all_gather | solution.py:47
  67.8 5.5 %all-to-all-start.1 = ((bf16[32,64,256]{2,1,0:T(8,128)(2,1)}), bf16[32,64,256]{2,1,0:T(8,128)(2,1)S(1)}, u32[]{:S(2)}, u32[]{:S(2)}) async-start(bf16[32,64,256]{2,1,0:T(8,128)(2,1)} %bitcast.10), calls=%async_computation.1 | async-start | bytes 2097152 | tf_op jit(solution)/shard_map/all_to_all | solution.py:74
  73.3 44.3 %while.12 = (s32[]{:T(128)}, bf16[2,1024,1024]{2,1,0:T(8,128)(2,1)}, bf16[2,1024,1024]{2,1,0:T(8,128)(2,1)}, s32[2]{0:T(128)S(1)}, s32[3,2048]{1,0:T(4,128)S(1)}...) while((s32[]{:T(128)}, ...), condition=%wide.region_5.6_spmd, body=%wide.region_4.5_spmd.sunk | while | flops 19922952 | bytes 4268255 | solution.py:64
  73.3 0.6 dynamic_slice.8
  74.7 20.8 %fusion.72 = (bf16[2,1024,1024]{2,1,0:T(8,128)(2,1)}, bf16[2,1024,1024]{2,1,0:T(8,128)(2,1)}) fusion(bf16[2,1024,1024]{2,1,0:T(8,128)(2,1)} %get-tuple-element.141, s32[]{:T(128)S(6)} %copy.17, s32[1024]{0:T(1024)S(1)} %bitcast.73, s32[1024]{0:T(1024)S(1)} %bitcast.71, s32[1024]{0:T(1024)S(1)} %bitcast.72, s32[1024]{0:T(1024)S(1)} %bitcast.70, ...), kind=kLoop, calls=%fused_computation.10.clone.1 | loop fusion | flops 19922944 | bytes 4218884 | tf_op jit(solution)/shard_map/while/body/jit(dynamic_update_index_in_dim)/dynamic_update_slice | solution.py:64
  95.5 0.6 dynamic_slice.8
  96.8 20.8 %fusion.72 = (bf16[2,1024,1024]{2,1,0:T(8,128)(2,1)}, bf16[2,1024,1024]{2,1,0:T(8,128)(2,1)}) fusion(bf16[2,1024,1024]{2,1,0:T(8,128)(2,1)} %get-tuple-element.141, s32[]{:T(128)S(6)} %copy.17, s32[1024]{0:T(1024)S(1)} %bitcast.73, s32[1024]{0:T(1024)S(1)} %bitcast.71, s32[1024]{0:T(1024)S(1)} %bitcast.72, s32[1024]{0:T(1024)S(1)} %bitcast.70, ...), kind=kLoop, calls=%fused_computation.10.clone.1 | loop fusion | flops 19922944 | bytes 4218884 | tf_op jit(solution)/shard_map/while/body/jit(dynamic_update_index_in_dim)/dynamic_update_slice | solution.py:64
  117.6 0.5 broadcast.457
  118.1 0.7 reduce.7
  118.9 1.1 fusion.17
  119.9 7.6 %all_gather.14 = bf16[1024,256]{1,0:T(8,128)(2,1)S(1)} all-gather(bf16[256,256]{1,0:T(8,128)(2,1)S(1)} %fusion.17), channel_id=1, replica_groups=mesh['row'=4,'col'=8] {'row'}, dimensions={0}, use_global_device_ids=true | all-gather | bytes 655360 | tf_op jit(solution)/shard_map/all_gather | solution.py:88
  127.6 3.6 fusion.57
  131.2 1.3 fusion.56
  132.8 1.5 pad_maximum_fusion
  134.3 69.1 %reduce-scatter.3.cloned.1.call-done = f32[256,256]{0,1:T(8,128)} async-done(((f32[2048,256]{0,1:T(8,128)}), f32[256,256]{0,1:T(8,128)}) %reduce-scatter.3.cloned.1.call-update) | async-done | bytes 262160 | tf_op jit(solution)/shard_map/reduce_scatter | solution.py:93
  203.5 2.5 fusion.11
  206.0 3.7 all-to-all-start.2
  209.8 0.6 fusion.55
  210.4 26.9 %all-to-all-done.2 = bf16[32,64,256]{2,1,0:T(8,128)(2,1)S(1)} async-done(((bf16[32,64,256]{2,1,0:T(8,128)(2,1)}), bf16[32,64,256]{2,1,0:T(8,128)(2,1)S(1)}, u32[]{:S(2)}, u32[]{:S(2)}) %all-to-all-start.2) | async-done | bytes 1048608 | tf_op jit(solution)/shard_map/all_to_all | solution.py:99
  237.3 2.6 gather_fusion
  240.0 0.8 fusion.53
  240.7 6.5 %scatter_custom_fusion.2 = bf16[2048,256]{1,0:T(8,128)(2,1)S(1)} fusion(s32[768]{0:T(1024)S(1)} %fusion.51, bf16[]{:T(256)} %constant.64.clone.1, bf16[384,256]{1,0:T(8,128)(2,1)S(1)} %get-tuple-element.53, bf16[]{:T(256)} %constant.70, bf16[384,256]{1,0:T(8,128)(2,1)S(1)} %get-tuple-element.54), kind=kCustom, calls=%fused_computation.38 | custom fusion | flops 786432 | bytes 1441796 | tf_op jit(solution)/shard_map/scatter | solution.py:71
  247.3 29.7 %all_to_all.30 = bf16[32,64,256]{2,1,0:T(8,128)(2,1)S(1)} all-to-all(bf16[32,64,256]{2,1,0:T(8,128)(2,1)S(1)} %bitcast.66), channel_id=1, replica_groups=mesh['row'=4,'col'=8] {'row','col'}, dimensions={0} | all-to-all | bytes 2097152 | tf_op jit(solution)/shard_map/all_to_all | solution.py:74
  277.0 1.0 fusion.20
  278.0 6.8 %all_gather.15 = bf16[1024,256]{1,0:T(8,128)(2,1)S(1)} all-gather(bf16[256,256]{1,0:T(8,128)(2,1)S(1)} %fusion.20), channel_id=1, replica_groups=mesh['row'=4,'col'=8] {'row'}, dimensions={0}, use_global_device_ids=true | all-gather | bytes 655360 | tf_op jit(solution)/shard_map/all_gather | solution.py:88
  284.9 1.3 fusion.59
  286.2 0.9 copy-done.3
  287.0 1.3 fusion.58
  288.6 1.5 pad_maximum_fusion.1
  290.1 66.4 %reduce-scatter.5.cloned.1.call-done = f32[256,256]{0,1:T(8,128)} async-done(((f32[2048,256]{0,1:T(8,128)}), f32[256,256]{0,1:T(8,128)}) %reduce-scatter.5.cloned.1.call-update) | async-done | bytes 262160 | tf_op jit(solution)/shard_map/reduce_scatter | solution.py:93
  356.5 1.0 convert_element_type.121
  357.4 1.6 fusion.14
  359.0 3.6 all-to-all-start.4
  362.6 0.8 copy.8
  363.4 26.8 %all-to-all-done.4 = bf16[32,64,256]{2,1,0:T(8,128)(2,1)S(1)} async-done(((bf16[32,64,256]{2,1,0:T(8,128)(2,1)}), bf16[32,64,256]{2,1,0:T(8,128)(2,1)S(1)}, u32[]{:S(2)}, u32[]{:S(2)}) %all-to-all-start.4) | async-done | bytes 1048608 | tf_op jit(solution)/shard_map/all_to_all | solution.py:99
  390.2 2.6 gather_fusion.1
  392.9 1.4 subtract_convert_fusion
  (32 shorter events, 1.1 us)
Async XLA Ops:
  15.6 52.2 %all-to-all-start = ((s32[32,1,64]{2,1,0:T(1,128)}), s32[32,1,64]{2,1,0:T(1,128)S(1)}, u32[]{:S(2)}, u32[]{:S(2)}) async-start(s32[32,1,64]{2,1,0:T(1,128)} %all_to_all.19), calls=%async_computation | async-start | bytes 32768 | tf_op jit(solution)/shard_map/all_to_all | solution.py:77
  67.8 51.1 %all-to-all-start.1 = ((bf16[32,64,256]{2,1,0:T(8,128)(2,1)}), bf16[32,64,256]{2,1,0:T(8,128)(2,1)S(1)}, u32[]{:S(2)}, u32[]{:S(2)}) async-start(bf16[32,64,256]{2,1,0:T(8,128)(2,1)} %bitcast.10), calls=%async_computation.1 | async-start | bytes 2097152 | tf_op jit(solution)/shard_map/all_to_all | solution.py:74
  73.3 130.2 %reduce-scatter.3.cloned.1.call-start = ((), (), s32[]{:S(2)}) async-start(), calls=%async_computation.7 | async-start | bytes 2359296 | tf_op jit(solution)/shard_map/reduce_scatter | solution.py:93
  127.6 3.6 copy-start.2
  132.8 77.0 %copy-start.1 = (f32[2]{0:T(128)S(1)}, f32[2]{0:T(128)}, u32[]{:S(2)}) copy-start(f32[2]{0:T(128)} %param.9) | copy-start | bytes 28
  134.3 105.6 %copy-start = (bf16[384,256]{1,0:T(8,128)(2,1)S(1)}, bf16[384,256]{1,0:T(8,128)(2,1)}, u32[]{:S(2)}) copy-start(bf16[384,256]{1,0:T(8,128)(2,1)} %param.6) | copy-start | bytes 589828
  206.0 31.3 %all-to-all-start.2 = ((bf16[32,64,256]{2,1,0:T(8,128)(2,1)}), bf16[32,64,256]{2,1,0:T(8,128)(2,1)S(1)}, u32[]{:S(2)}, u32[]{:S(2)}) async-start(bf16[32,64,256]{2,1,0:T(8,128)(2,1)} %bitcast.13), calls=%async_computation.3 | async-start | bytes 2097152 | tf_op jit(solution)/shard_map/all_to_all | solution.py:99
  209.7 146.8 %reduce-scatter.5.cloned.1.call-start = ((), (), s32[]{:S(2)}) async-start(), calls=%async_computation.8 | async-start | bytes 2359296 | tf_op jit(solution)/shard_map/reduce_scatter | solution.py:93
  247.3 37.6 %copy-start.4 = (bf16[2,1024,1024]{2,1,0:T(8,128)(2,1)S(1)}, bf16[2,1024,1024]{2,1,0:T(8,128)(2,1)}, u32[]{:S(2)}) copy-start(bf16[2,1024,1024]{2,1,0:T(8,128)(2,1)} %get-tuple-element.36) | copy-start | bytes 12582916
  284.9 2.2 copy-start.3
  359.0 31.2 %all-to-all-start.4 = ((bf16[32,64,256]{2,1,0:T(8,128)(2,1)}), bf16[32,64,256]{2,1,0:T(8,128)(2,1)S(1)}, u32[]{:S(2)}, u32[]{:S(2)}) async-start(bf16[32,64,256]{2,1,0:T(8,128)(2,1)} %bitcast.18), calls=%async_computation.6 | async-start | bytes 2097152 | tf_op jit(solution)/shard_map/all_to_all | solution.py:99
Sparse Core Ops, SparseCore 0:
  134.5 68.9 reduce-scatter.2
  290.2 66.1 reduce-scatter.4
where the time goes:
time: 402 us; the launch traced here: 401 us
  waiting for transfers between devices  189 us (47%)
  blocking collectives  80.3 us (20%)
  other arithmetic  66.1 us (16%)
  starting transfers between devices  20.2 us (5%)
  local copies, waits for them, and re-layouts  16 us (4%)
  between operations  14.3 us (4%)
  matrix products  13.7 us (3%)
    reduce_scatter x2, waiting for transfers between devices, per_device(): lax.psum_scatter(partial_value, 'col', scatter_dimension=0, tiled=True)  135 us
    all_to_all x2, waiting for transfers between devices, per_device(): lax.all_to_all(flat_vals, ('row', 'col'), split_axis=0, concat_axis=0, ti...  53.7 us
    dynamic_update_slice x2, other arithmetic, per_device(): lax.map(make_block, jnp.arange(row_count // keep_block, dtype=jnp.int32))  41.6 us
    all_gather x1, blocking collectives, per_device(): row_points = lax.all_gather(centroids, 'col', axis=1, tiled=True)  30.9 us
    all_to_all x1, blocking collectives, per_device(): lax.all_to_all(route_flat_vals, ('row', 'col'), split_axis=0, concat_axis...  29.7 us
    all_gather x2, blocking collectives, per_device(): piece = lax.all_gather(charges, 'row', axis=0, tiled=True)  14.5 us
    scatter x2, other arithmetic, per_device(): outgoing = jnp.zeros((cells, width), jnp.bfloat16).at[slot].set(signed)  14.3 us
  transfers between devices with their start and end apart: 6, of which 4 were waited for; matrix products, arithmetic and copies ran while one was open for 14% of the time, Pallas kernels for 0%

commit v1 on v0

v1 whole, which is shorter than its diff:
```python
import functools

import jax
import jax.numpy as jnp
from jax import lax
from jax.experimental import pallas as pl
from jax.experimental.pallas import tpu as pltpu
from jax.sharding import PartitionSpec as P

SPACING = 0.2
TURNS = 32.0
AXES = ("row", "col")
ROUND = 12582912.0
COS = (
    0.9999992107823218,
    -19.738980355763992,
    64.92865742103312,
    -85.27162153429882,
    58.79049212013072,
    -21.07110562764302,
)
SIN = (
    6.283184916495431,
    -41.34158923268858,
    81.59994332978287,
    -76.61447253124996,
    41.342882354568324,
    -12.471243535026977,
)
VMEM_LIMIT = 48 * 2**20


def poly(coefs, scale, u):
    value = jnp.full_like(u, coefs[-1] * scale)
    for coef in coefs[-2::-1]:
        value = value * u + coef * scale
    return value


def tile_kernel(row_ref, col_ref, real_ref, imag_ref):
    square = jnp.dot(row_ref[...], col_ref[...], preferred_element_type=jnp.float32)
    inverse = lax.rsqrt(square)
    turns = square * inverse
    frac = turns - ((turns + ROUND) - ROUND)
    u = frac * frac
    real_ref[...] = (poly(COS, SPACING / TURNS, u) * inverse).astype(jnp.bfloat16)
    imag_ref[...] = (poly(SIN, -SPACING / TURNS, u) * (frac * inverse)).astype(jnp.bfloat16)


def build_tiles(row_points, col_points, block=512):
    rows, cols = row_points.shape[1], col_points.shape[1]
    block = min(block, cols)

    def norms(points):
        total = jnp.sum(points * points, axis=0)
        return total & 255, total & 0xFF00, total & 0xFF0000

    one_row = jnp.ones((rows,), jnp.int32)
    one_col = jnp.ones((cols,), jnp.int32)
    r0, r1, r2 = norms(row_points)
    c0, c1, c2 = norms(col_points)
    row_features = jnp.stack(
        [-2 * row_points[0], -2 * row_points[1], -2 * row_points[2], r0, r1, r2]
        + [one_row] * 4
        + [0 * one_row] * 6,
        axis=1,
    )
    col_features = jnp.stack(
        [col_points[0], col_points[1], col_points[2], one_col, one_col, one_col]
        + [c0, c1, c2, one_col]
        + [0 * one_col] * 6,
        axis=0,
    )
    row_features = (row_features.astype(jnp.float32) / (TURNS * TURNS)).astype(jnp.bfloat16)
    col_features = col_features.astype(jnp.bfloat16)
    depth = row_features.shape[1]
    return pl.pallas_call(
        tile_kernel,
        grid=(cols // block,),
        in_specs=[
            pl.BlockSpec((rows, depth), lambda j: (0, 0)),
            pl.BlockSpec((depth, block), lambda j: (0, j)),
        ],
        out_specs=[pl.BlockSpec((rows, block), lambda j: (0, j))] * 2,
        out_shape=[jax.ShapeDtypeStruct((rows, cols), jnp.bfloat16)] * 2,
        compiler_params=pltpu.CompilerParams(vmem_limit_bytes=VMEM_LIMIT),
        cost_estimate=pl.CostEstimate(
            flops=rows * cols * 60, bytes_accessed=rows * cols * 4, transcendentals=rows * cols
        ),
    )(row_features, col_features)


def adjacency_kernel(chunk, mark_ref, other_ref, out_ref):
    rows, block = out_ref.shape
    ends = other_ref.shape[0]
    base = pl.program_id(0) * block
    lane = lax.broadcasted_iota(jnp.int32, (chunk, block), 1) + base
    wanted = lax.broadcasted_iota(jnp.int32, (rows, chunk), 0) + 1

    def step(k, total):
        marks = mark_ref[:, pl.ds(pl.multiple_of(k * chunk, chunk), chunk)]
        others = other_ref[pl.ds(pl.multiple_of(k * chunk, chunk), chunk), :]
        pick = (marks == wanted).astype(jnp.float32).astype(jnp.bfloat16)
        spread = (others == lane).astype(jnp.float32).astype(jnp.bfloat16)
        return total + jnp.dot(pick, spread, preferred_element_type=jnp.float32)

    total = lax.fori_loop(0, ends // chunk, step, jnp.zeros((rows, block), jnp.float32))
    out_ref[...] = total.astype(jnp.bfloat16)


def build_adjacency(marks, others, rows, cols, block=512, chunk=256):
    ends = marks.shape[0]
    block = min(block, cols)
    return pl.pallas_call(
        functools.partial(adjacency_kernel, chunk),
        grid=(cols // block,),
        in_specs=[
            pl.BlockSpec((1, ends), lambda j: (0, 0)),
            pl.BlockSpec((ends, 1), lambda j: (0, 0)),
        ],
        out_specs=pl.BlockSpec((rows, block), lambda j: (0, j)),
        out_shape=jax.ShapeDtypeStruct((rows, cols), jnp.bfloat16),
        compiler_params=pltpu.CompilerParams(vmem_limit_bytes=VMEM_LIMIT),
        cost_estimate=pl.CostEstimate(
            flops=2 * rows * cols * ends, bytes_accessed=rows * cols * 2, transcendentals=0
        ),
    )(marks.reshape(1, ends), others.reshape(ends, 1))


def blend(real_part, imag_part):
    half = real_part.shape[1] // 2
    return jnp.concatenate(
        [real_part[:, :half] - imag_part[:, half:], real_part[:, half:] + imag_part[:, :half]], 1
    )


def per_device(currents, incidence, centroids, sweep_weights):
    devices = lax.axis_size("row") * lax.axis_size("col")
    me = lax.axis_index(AXES)
    tri_dev = centroids.shape[1]
    edge_dev, width = currents.shape
    slots = 8 * tri_dev // devices
    cells = devices * slots
    sweeps = sweep_weights.shape[0]
    triangles = devices * tri_dev

    numbers = jnp.concatenate([incidence.reshape(-1), centroids.reshape(-1)])
    numbers = lax.all_gather(numbers, AXES, axis=0, tiled=False)
    ends = numbers[:, : 2 * edge_dev].reshape(devices, 2, edge_dev)
    plus, minus = ends[:, 0].reshape(1, -1), ends[:, 1].reshape(1, -1)
    points = numbers[:, 2 * edge_dev :].reshape(devices, 3, tri_dev)
    points = points.transpose(1, 0, 2).reshape(3, triangles)
    all_currents = lax.all_gather(currents, AXES, axis=0, tiled=True)

    triangle = incidence.reshape(-1)
    other = incidence[::-1].reshape(-1)
    owner = triangle // tri_dev
    local = triangle % tri_dev
    hits = (owner[:, None] == jnp.arange(devices, dtype=jnp.int32)[None, :]).astype(jnp.int32)
    rank = jnp.sum(hits * jnp.cumsum(hits, axis=0), axis=1) - 1
    slot = owner * slots + rank
    packed = other * (2 * tri_dev) + local + 1
    outgoing = jnp.zeros((cells,), jnp.int32).at[slot].set(packed)
    arrived = lax.all_to_all(
        outgoing.reshape(devices, slots), AXES, split_axis=0, concat_axis=0, tiled=True
    ).reshape(cells)
    marks = arrived % (2 * tri_dev)
    others = arrived // (2 * tri_dev)

    real_tile, imag_tile = build_tiles(centroids, points)
    mine = (me * tri_dev + jnp.arange(tri_dev, dtype=jnp.int32))[:, None]
    signs = (plus == mine).astype(jnp.bfloat16) - (minus == mine).astype(jnp.bfloat16)
    charge = jnp.dot(signs, all_currents, preferred_element_type=jnp.float32)
    neighbours = build_adjacency(marks, others, tri_dev, triangles)
    degree = jnp.sum((marks[None, :] == jnp.arange(1, tri_dev + 1)[:, None]).astype(jnp.float32), 1)

    current = currents
    potential = None
    for sweep in range(sweeps):
        piece = lax.all_gather(charge.astype(jnp.bfloat16), AXES, axis=0, tiled=True)
        potential = blend(
            jnp.dot(real_tile, piece, preferred_element_type=jnp.float32),
            jnp.dot(imag_tile, piece, preferred_element_type=jnp.float32),
        ).astype(jnp.bfloat16)
        everywhere = lax.all_gather(potential, AXES, axis=0, tiled=True)
        if sweep + 1 < sweeps:
            around = jnp.dot(neighbours, everywhere, preferred_element_type=jnp.float32)
            change = degree[:, None] * potential.astype(jnp.float32) - around
            charge = charge - sweep_weights[sweep] * change
        picked = everywhere[triangle]
        slope = picked[:edge_dev].astype(jnp.float32) - picked[edge_dev:].astype(jnp.float32)
        current = (current.astype(jnp.float32) - sweep_weights[sweep] * slope).astype(jnp.bfloat16)
    return current, potential


def solution(mesh):
    in_specs = (P(AXES, None), P(None, AXES), P(None, AXES), P())
    out_specs = (P(AXES, None), P(AXES, None))
    return jax.shard_map(
        per_device, mesh=mesh, in_specs=in_specs, out_specs=out_specs, check_vma=False
    )
```

time: 402 us -> 385 us (0.958)
  other arithmetic: 66.1 us -> 7.18 us
  Pallas kernels: 0 us -> 57.1 us
  starting transfers between devices: 20.2 us -> 3.53 us
  local copies, waits for them, and re-layouts: 16 us -> 32.5 us
  waiting for transfers between devices: 189 us -> 173 us
  matrix products: 13.7 us -> 25.1 us
  blocking collectives: 80.3 us -> 71.8 us
    all_gather x0 -> x5, waiting for transfers between devices: none -> 165 us  [the longest x2 104 us: per_device(): lax.all_gather(charge.astype(jnp.bfloat16), AXES, axis=0, tiled=True)]
    reduce_scatter x2 -> x0, waiting for transfers between devices: 135 us -> none  [per_device(): lax.psum_scatter(partial_value, 'col', scatter_dimension=0, tiled=True)]
    pallas_call x0 -> x2, Pallas kernels: none -> 57.1 us  [the longest x1 45.3 us: build_adjacency(): pl.pallas_call(functools.partial(adjacency_kernel, chunk), grid=(cols //...]
    all_to_all x4 -> x1, waiting for transfers between devices: 53.7 us -> 6.45 us  [per_device(): lax.all_to_all(outgoing.reshape(devices, slots), AXES, split_axis=0, conc...]
    dynamic_update_slice x2 -> x0, other arithmetic: 41.6 us -> none  [per_device(): lax.map(make_block, jnp.arange(row_count // keep_block, dtype=jnp.int32))]
    all_to_all x1 -> x0, blocking collectives: 29.7 us -> none  [per_device(): lax.all_to_all(route_flat_vals, ('row', 'col'), split_axis=0, concat_axis...]
    all_gather x4 -> x1, blocking collectives: 50.7 us -> 71.8 us  [per_device(): numbers = lax.all_gather(numbers, AXES, axis=0, tiled=False)]
    all_to_all x4 -> x1, starting transfers between devices: 20.1 us -> 3.15 us  [per_device(): lax.all_to_all(outgoing.reshape(devices, slots), AXES, split_axis=0, conc...]
  transfers between devices with their start and end apart: 6 -> 6, of which waited for: 4 -> 5; matrix products, arithmetic and copies ran while one was open for 14% -> 5% of each run, Pallas kernels for 0% -> 15%
where the time goes in v1:
time: 385 us; the launch traced here: 384 us
  waiting for transfers between devices  173 us (45%)
  blocking collectives  71.8 us (19%)
  Pallas kernels  57.1 us (15%)
  local copies, waits for them, and re-layouts  32.5 us (8%)
  matrix products  25.1 us (7%)
  between operations  14.2 us (4%)
  other arithmetic  7.18 us (2%)
    all_gather x2, waiting for transfers between devices, per_device(): lax.all_gather(charge.astype(jnp.bfloat16), AXES, axis=0, tiled=True)  104 us
    all_gather x1, blocking collectives, per_device(): numbers = lax.all_gather(numbers, AXES, axis=0, tiled=False)  71.8 us
    all_gather x2, waiting for transfers between devices, per_device(): everywhere = lax.all_gather(potential, AXES, axis=0, tiled=True)  58.7 us
    pallas_call x1, Pallas kernels, build_adjacency(): pl.pallas_call(functools.partial(adjacency_kernel, chunk), grid=(cols //...  45.3 us
    pallas_call x1, Pallas kernels, build_tiles(): pl.pallas_call(tile_kernel, grid=(cols // block,), in_specs=[pl.BlockSpec...  11.8 us
    gather x2, local copies, waits for them, and re-layouts, per_device(): picked = everywhere[triangle]  9.65 us
  transfers between devices with their start and end apart: 6, of which 5 were waited for; matrix products, arithmetic and copies ran while one was open for 5% of the time, Pallas kernels for 15%

profile of v1, /device:TPU:0, one launch (start us, length us, event | category | flops | bytes accessed | tf_op | source)
XLA Modules:
  0.0 384.1 jit_solution(12954622043107299932)
XLA Ops:
  7.2 0.7 all-gather.8.cloned.1.call-update
  7.9 0.7 reshape.433
  8.6 0.7 reshape.434
  9.4 71.8 %all-gather.1 = s32[32,1,1536]{2,1,0:T(1,128)S(1)} all-gather(s32[1,1,1536]{2,1,0:T(1,128)S(1)} %reshape.470), channel_id=2, replica_groups=mesh['row'=4,'col'=8] {'row','col'}, dimensions={0}, use_global_device_ids=true | all-gather | bytes 202752 | tf_op jit(solution)/shard_map/all_gather | solution.py:148
  81.3 0.1 fusion.34
  81.4 2.4 all-gather.8.cloned.1.call-done
  83.8 5.9 %fusion.37 = (bf16[256,256]{1,0:T(8,128)(2,1)}, f32[256,256]{1,0:T(8,128)S(1)}) fusion(bf16[12288,256]{1,0:T(8,128)(2,1)} %all-gather.8.cloned.1.call-done, s32[12288]{0:T(1024)S(1)} %bitcast.77, s32[12288]{0:T(1024)S(1)} %bitcast.76, s32[256]{0:T(256)S(1)} %iota_add_fusion.1), kind=kOutput, calls=%fused_computation.104 | convolution fusion | flops 1626406912 | bytes 6784000 | tf_op jit(solution)/shard_map/dot_general | solution.py:173
  89.9 0.1 stack.37
  90.0 0.1 copy.55.row_ref
  90.2 0.1 reduce_sum.37
  90.6 0.5 stack.41.col_ref
  91.2 11.8 %shard_map.59 = (bf16[256,8192]{1,0:T(8,128)(2,1)S(1)}, bf16[256,8192]{1,0:T(8,128)(2,1)}) custom-call(bf16[256,16]{1,0:T(8,128)(2,1)S(1)} %copy.55.row_ref, bf16[16,8192]{1,0:T(8,128)(2,1)S(1)} %stack.41.col_ref), custom_call_target="tpu_custom_call" | custom-call | flops 125829120 | bytes 8388608 | tf_op jit(solution)/shard_map/pallas_call | solution.py:77
  102.9 2.0 copy-done
  104.9 45.9 %all-gather.10.cloned.1.call-done = bf16[8192,256]{1,0:T(8,128)(2,1)} async-done(((bf16[256,256]{1,0:T(8,128)(2,1)}), bf16[8192,256]{1,0:T(8,128)(2,1)}) %all-gather.10.cloned.1.call-update) | async-done | bytes 4194320 | tf_op jit(solution)/shard_map/all_gather | solution.py:180
  150.8 4.8 %fusion.38 = f32[256,256]{1,0:T(8,128)S(1)} fusion(bf16[256,8192]{1,0:T(8,128)(2,1)} %copy-done, bf16[8192,256]{1,0:T(8,128)(2,1)} %all-gather.10.cloned.1.call-done), kind=kOutput, calls=%fused_computation.105 | convolution fusion | flops 1073741824 | bytes 8650752 | tf_op jit(solution)/shard_map/dot_general | solution.py:182
  155.6 1.1 copy-done.9
  156.7 1.2 fusion.39
  158.0 0.7 pad_maximum_fusion
  158.7 0.1 rev.3
  158.9 1.7 reduce-window.6
  160.6 0.3 slice_reduce_fusion
  160.9 0.1 fusion.16
  161.1 3.4 scatter_custom_fusion
  164.5 0.7 all_to_all.6
  165.2 3.1 all-to-all-start
  168.4 0.6 fusion.36
  169.0 6.4 %all-to-all-done = s32[32,1,64]{2,1,0:T(1,128)S(1)} async-done(((s32[32,1,64]{2,1,0:T(1,128)}), s32[32,1,64]{2,1,0:T(1,128)S(1)}, u32[]{:S(2)}, u32[]{:S(2)}) %all-to-all-start) | async-done | bytes 8224 | tf_op jit(solution)/shard_map/all_to_all | solution.py:164
  175.4 0.1 reshape.441
  175.5 1.0 reshape.473
  176.5 0.5 broadcast.402
  177.0 0.7 reduce.15
  177.8 0.4 convert_reduce_fusion
  178.2 0.6 add_select_fusion.other_ref
  178.8 45.3 %shard_map.60 = bf16[256,8192]{1,0:T(8,128)(2,1)S(1)} custom-call(s32[1,2048]{1,0:T(1,128)S(1)} %and_select_fusion.mark_ref, s32[2048,1]{1,0:T(8,128)S(1)} %add_select_fusion.other_ref), custom_call_target="tpu_custom_call" | custom-call | flops 8589934592 | bytes 4194304 | tf_op jit(solution)/shard_map/pallas_call | solution.py:114
  224.1 1.9 copy-done.2
  226.0 6.0 %fusion.8 = bf16[256,256]{1,0:T(8,128)(2,1)} fusion(f32[256,256]{1,0:T(8,128)S(1)} %get-tuple-element.44, bf16[256,8192]{1,0:T(8,128)(2,1)} %copy-done.2, bf16[8192,256]{1,0:T(8,128)(2,1)} %all-gather.12.cloned.1.call-done, f32[256]{0:T(256)S(1)} %convert_reduce_fusion, f32[]{:T(128)} %bitcast, bf16[256,128]{1,0:T(8,128)(2,1)S(1)} %get-tuple-element.21, ...), kind=kOutput, calls=%fused_computation.18 | convolution fusion | flops 1074331648 | bytes 8913924 | tf_op jit(solution)/shard_map/dot_general | solution.py:187
  232.0 0.2 all-gather.16.cloned.1.call-start
  232.3 58.4 %all-gather.14.cloned.1.call-done = bf16[8192,256]{1,0:T(8,128)(2,1)} async-done(((bf16[256,256]{1,0:T(8,128)(2,1)}), bf16[8192,256]{1,0:T(8,128)(2,1)}) %all-gather.14.cloned.1.call-update) | async-done | bytes 4194320 | tf_op jit(solution)/shard_map/all_gather | solution.py:180
  290.7 5.3 %fusion.41 = f32[256,256]{0,1:T(8,128)S(1)} fusion(bf16[256,8192]{1,0:T(8,128)(2,1)} %get-tuple-element.5, bf16[8192,256]{1,0:T(8,128)(2,1)} %all-gather.14.cloned.1.call-done), kind=kOutput, calls=%fused_computation.108 | convolution fusion | flops 1073741824 | bytes 8650752 | tf_op jit(solution)/shard_map/dot_general | solution.py:183
  296.1 0.6 copy-done.3
  296.6 1.8 fusion.40
  298.5 0.7 pad_maximum_fusion.1
  299.2 4.8 %gather_fusion = bf16[768,256]{1,0:T(8,128)(2,1)S(1)} fusion(bf16[8192,256]{1,0:T(8,128)(2,1)} %all-gather.12.cloned.1.call-done, s32[1024]{0:T(1024)S(1)} %pad_clamp_fusion), kind=kCustom, calls=%fused_computation | custom fusion | bytes 789504 | tf_op jit(solution)/shard_map/gather | solution.py:190
  304.0 1.7 copy.66
  305.7 58.7 %all-gather.16.cloned.1.call-done = bf16[8192,256]{0,1:T(8,128)(2,1)} async-done(((bf16[256,256]{0,1:T(8,128)(2,1)}), bf16[8192,256]{0,1:T(8,128)(2,1)}) %all-gather.16.cloned.1.call-update) | async-done | bytes 4194320 | tf_op jit(solution)/shard_map/all_gather | solution.py:185
  364.4 6.4 %copy.65 = bf16[8192,256]{1,0:T(8,128)(2,1)} copy(bf16[8192,256]{0,1:T(8,128)(2,1)} %all-gather.16.cloned.1.call-done) | data formatting | bytes 8388608 | tf_op jit(solution)/shard_map/all_gather | solution.py:185
  370.8 4.8 %gather_fusion.1 = bf16[768,256]{1,0:T(8,128)(2,1)S(1)} fusion(bf16[8192,256]{1,0:T(8,128)(2,1)} %copy.65, s32[1024]{0:T(1024)S(1)} %pad_clamp_fusion), kind=kCustom, calls=%fused_computation.1 | custom fusion | bytes 789504 | tf_op jit(solution)/shard_map/gather | solution.py:190
  375.6 2.0 subtract_convert_fusion
  (66 shorter events, 1.1 us)
Async XLA Ops:
  7.2 76.7 %all-gather.8.cloned.1.call-start = ((), (), s32[]{:S(2)}) async-start(), calls=%async_computation.1 | async-start | bytes 6488064 | tf_op jit(solution)/shard_map/all_gather | solution.py:153
  7.9 142.9 %all-gather.10.cloned.1.call-start = ((), (), s32[]{:S(2)}) async-start(), calls=%async_computation.2 | async-start | bytes 4325376 | tf_op jit(solution)/shard_map/all_gather | solution.py:180
  83.8 6.0 %copy-start.7 = (s32[3,256]{1,0:T(4,128)S(1)}, s32[3,256]{1,0:T(4,128)}, u32[]{:S(2)}) copy-start(s32[3,256]{1,0:T(4,128)} %param.6) | copy-start | bytes 9220
  89.7 136.3 %all-gather.12.cloned.1.call-start = ((), (), s32[]{:S(2)}) async-start(), calls=%async_computation.3 | async-start | bytes 4325376 | tf_op jit(solution)/shard_map/all_gather | solution.py:185
  102.9 2.0 copy-start
  150.8 4.9 %copy-start.4 = (bf16[256,8192]{1,0:T(8,128)(2,1)S(1)}, bf16[256,8192]{1,0:T(8,128)(2,1)}, u32[]{:S(2)}) copy-start(bf16[256,8192]{1,0:T(8,128)(2,1)} %get-tuple-element.5) | copy-start | bytes 12582916
  150.8 5.9 %copy-start.9 = (bf16[8192,256]{1,0:T(8,128)(2,1)S(1)}, bf16[8192,256]{1,0:T(8,128)(2,1)}, u32[]{:S(2)}) copy-start(bf16[8192,256]{1,0:T(8,128)(2,1)} %all-gather.10.cloned.1.call-done) | copy-start | bytes 12582916
  156.7 2.0 copy-start.6
  156.7 11.7 %copy-start.8 = (f32[2]{0:T(128)S(1)}, f32[2]{0:T(128)}, u32[]{:S(2)}) copy-start(f32[2]{0:T(128)} %param.7) | copy-start | bytes 28
  165.2 10.2 %all-to-all-start = ((s32[32,1,64]{2,1,0:T(1,128)}), s32[32,1,64]{2,1,0:T(1,128)S(1)}, u32[]{:S(2)}, u32[]{:S(2)}) async-start(s32[32,1,64]{2,1,0:T(1,128)} %all_to_all.6), calls=%async_computation | async-start | bytes 32768 | tf_op jit(solution)/shard_map/all_to_all | solution.py:164
  168.3 122.4 %all-gather.14.cloned.1.call-start = ((), (), s32[]{:S(2)}) async-start(), calls=%async_computation.4 | async-start | bytes 4325376 | tf_op jit(solution)/shard_map/all_gather | solution.py:180
  224.1 1.9 copy-start.2
  232.0 132.4 %all-gather.16.cloned.1.call-start = ((), (), s32[]{:S(2)}) async-start(), calls=%async_computation.5 | async-start | bytes 4325376 | tf_op jit(solution)/shard_map/all_gather | solution.py:185
  290.7 5.3 %copy-start.1 = (bf16[256,8192]{1,0:T(8,128)(2,1)S(1)}, bf16[256,8192]{1,0:T(8,128)(2,1)}, u32[]{:S(2)}) copy-start(bf16[256,8192]{1,0:T(8,128)(2,1)} %copy-done) | copy-start | bytes 12582916
  290.7 5.9 %copy-start.3 = (bf16[8192,256]{1,0:T(8,128)(2,1)S(1)}, bf16[8192,256]{1,0:T(8,128)(2,1)}, u32[]{:S(2)}) copy-start(bf16[8192,256]{1,0:T(8,128)(2,1)} %all-gather.14.cloned.1.call-done) | copy-start | bytes 12582916
  305.7 69.9 %copy-start.5 = (bf16[384,256]{1,0:T(8,128)(2,1)S(1)}, bf16[384,256]{1,0:T(8,128)(2,1)}, u32[]{:S(2)}) copy-start(bf16[384,256]{1,0:T(8,128)(2,1)} %param.4) | copy-start | bytes 589828
Sparse Core Ops, SparseCore 0:
  10.9 72.8 all-gather.7
  89.9 60.8 all-gather.9
  158.8 60.6 all-gather.11
  232.2 58.5 all-gather.13
  299.3 65.0 all-gather.15

commit v2 on v1

v2 whole, which is shorter than its diff:
```python
import functools
import math

import jax
import jax.numpy as jnp
from jax import lax
from jax.experimental import pallas as pl
from jax.experimental.pallas import tpu as pltpu
from jax.sharding import PartitionSpec as P

SPACING = 0.2
TURNS = 32.0
AXES = ("row", "col")
ROUND = 12582912.0
COS = (
    0.9999992107823218,
    -19.738980355763992,
    64.92865742103312,
    -85.27162153429882,
    58.79049212013072,
    -21.07110562764302,
)
SIN = (
    6.283184916495431,
    -41.34158923268858,
    81.59994332978287,
    -76.61447253124996,
    41.342882354568324,
    -12.471243535026977,
)
PARAMS = pltpu.CompilerParams(vmem_limit_bytes=48 * 2**20)
F32, BF16, I32 = jnp.float32, jnp.bfloat16, jnp.int32


def whole():
    return pl.BlockSpec(memory_space=pltpu.VMEM)


def iota(shape, dim):
    return lax.broadcasted_iota(I32, shape, dim)


def ones_where(mask):
    return jnp.where(mask, jnp.ones((), F32), jnp.zeros((), F32)).astype(BF16)


def matmul(a, b):
    return jnp.dot(a, b, preferred_element_type=F32)


def matmul_nt(a, b):
    return lax.dot_general(a, b, (((1,), (1,)), ((), ())), preferred_element_type=F32)


class Layout:
    def __init__(self, n_row, n_col):
        self.core = 2 if n_row % 2 == 0 else 1
        self.x = n_row // self.core
        self.y = math.gcd(n_col, self.x)
        self.z = n_col // self.y
        self.devices = n_row * n_col
        self.plane = [(dx, dy) for dx in range(self.x) for dy in range(self.y)]

    def digits(self, index):
        y = index % self.y
        z = index // self.y % self.z
        core = index // (self.y * self.z) % self.core
        return index // (self.y * self.z * self.core), core, z, y

    def shift(self, value, dx=0, dc=0, dz=0, dy=0):
        pairs = []
        for i in range(self.devices):
            x, c, z, y = self.digits(i)
            x, c = (x + dx) % self.x, (c + dc) % self.core
            z, y = (z + dz) % self.z, (y + dy) % self.y
            pairs.append((i, ((x * self.core + c) * self.z + z) * self.y + y))
        return lax.ppermute(value, AXES, pairs)

    def line(self, value):
        along = [value] + [self.shift(value, dz=-dz) for dz in range(1, self.z)]
        pieces = []
        for piece in along:
            pieces.append(piece)
            pieces += [self.shift(piece, dc=-dc) for dc in range(1, self.core)]
        return pieces

    def across(self, value):
        return [value] + [self.shift(value, dx=-dx, dy=-dy) for dx, dy in self.plane[1:]]

    def give(self, blocks):
        return [
            self.shift(block, dx=dx, dy=dy)
            for block, (dx, dy) in zip(blocks, self.plane[1:])
        ]

    def place(self, triangle, tri_dev, me):
        x, core, z, y = self.digits(triangle // tri_dev)
        mx, mcore, mz, my = self.digits(me)
        block = (z - mz) % self.z * self.core + (core - mcore) % self.core
        inside = (x == mx) & (y == my)
        return jnp.where(inside, block * tri_dev + triangle % tri_dev, -1)


def route_kernel(tri_dev, slots, tri_ref, other_ref, cur_ref, out_ref, label_ref):
    ends, edges = tri_ref.shape[1], cur_ref.shape[0]
    cells = out_ref.shape[0]
    devices = cells // slots
    chunk = min(256, cells)
    tri, other = tri_ref[...], other_ref[...]
    owner = tri // tri_dev
    hits = iota((devices, ends), 0) == owner
    upper = ones_where(iota((ends, ends), 0) <= iota((ends, ends), 1))
    count = matmul(ones_where(hits), upper)
    rank = jnp.sum(jnp.where(hits, count, 0.0), axis=0, keepdims=True)
    slot = owner * slots + rank.astype(I32) - 1
    digits = jnp.concatenate(
        [tri % tri_dev + 1, other & 255, other >> 8, jnp.zeros((5, ends), I32)], axis=0
    )
    digits = digits.astype(F32).astype(BF16)
    for base in range(0, cells, chunk):
        mask = jnp.where(iota((chunk, ends), 0) + base == slot, 1.0, 0.0).astype(F32)
        signed = (mask[:, :edges] - mask[:, edges:]).astype(BF16)
        out_ref[base : base + chunk, :] = matmul(signed, cur_ref[...]).astype(BF16)
        label = matmul_nt(digits, mask.astype(BF16)).astype(I32)
        label_ref[:, base : base + chunk] = (label[2:3] * 256 + label[1:2]) * (
            2 * tri_dev
        ) + label[0:1]


def route(incidence, currents, tri_dev, slots, cells):
    edges, width = currents.shape
    return pl.pallas_call(
        functools.partial(route_kernel, tri_dev, slots),
        in_specs=[whole()] * 3,
        out_specs=[whole()] * 2,
        out_shape=[
            jax.ShapeDtypeStruct((cells, width), BF16),
            jax.ShapeDtypeStruct((1, cells), I32),
        ],
        compiler_params=PARAMS,
    )(incidence.reshape(1, -1), incidence[::-1].reshape(1, -1), currents)


def features(points, scale, first):
    rows, count = points.shape
    square = jnp.sum(points * points, axis=0, keepdims=True)
    norms = [square & 255, square & 0xFF00, square & 0xFF0000]
    ones = [jnp.ones_like(square)] * 3
    zeros = [jnp.zeros((16 - rows - 7, count), I32)]
    if first:
        parts = [-2 * points] + norms + ones + [ones[0]] + zeros
    else:
        parts = [points] + ones + norms + [ones[0]] + zeros
    return (jnp.concatenate(parts, axis=0).astype(F32) * scale).astype(BF16)


def poly(coefs, scale, u):
    value = jnp.full_like(u, coefs[-1] * scale)
    for coef in coefs[-2::-1]:
        value = value * u + coef * scale
    return value


def tile_kernel(row_ref, col_ref, real_ref, imag_ref):
    row = features(row_ref[...], 1.0 / (TURNS * TURNS), True)
    col = features(col_ref[...], 1.0, False)
    square = lax.dot_general(row, col, (((0,), (0,)), ((), ())), preferred_element_type=F32)
    inverse = lax.rsqrt(square)
    turns = square * inverse
    frac = turns - ((turns + ROUND) - ROUND)
    u = frac * frac
    real_ref[...] = (poly(COS, SPACING / TURNS, u) * inverse).astype(BF16)
    imag_ref[...] = (poly(SIN, -SPACING / TURNS, u) * (frac * inverse)).astype(BF16)


def build_tiles(row_points, col_points, tri_dev):
    rows, cols = row_points.shape[1], col_points.shape[1]
    block = min(512, cols)
    return pl.pallas_call(
        tile_kernel,
        grid=(rows // tri_dev, cols // block),
        in_specs=[
            pl.BlockSpec((3, tri_dev), lambda i, j: (0, i)),
            pl.BlockSpec((3, block), lambda i, j: (0, j)),
        ],
        out_specs=[pl.BlockSpec((tri_dev, block), lambda i, j: (i, j))] * 2,
        out_shape=[jax.ShapeDtypeStruct((rows, cols), BF16)] * 2,
        compiler_params=PARAMS,
        cost_estimate=pl.CostEstimate(
            flops=rows * cols * 60, bytes_accessed=rows * cols * 4, transcendentals=rows * cols
        ),
    )(row_points, col_points)


def pick(row, base, count):
    low = jnp.where((row >= base) & (row < base + count), row - base, -1)
    wanted = iota((count, row.shape[1]), 0).astype(F32).astype(BF16)
    same = wanted == low.astype(F32).astype(BF16)
    return jnp.where(same, jnp.ones((), BF16), jnp.zeros((), BF16))


def adjacency_kernel(mark_ref, place_ref, out_ref):
    rows, cols = out_ref.shape
    mark, place = mark_ref[0], place_ref[0]
    low = pick(jnp.where(place >= 0, place % rows, -1), 0, rows)
    for base in range(0, cols, rows):
        inside = (place >= base) & (place < base + rows)
        here = pick(jnp.where(inside, mark - 1, -1), 0, rows)
        out_ref[:, base : base + rows] = matmul_nt(here, low).astype(BF16)


def build_adjacency(marks, places, rows, cols):
    count, _, ends = marks.shape
    return pl.pallas_call(
        adjacency_kernel,
        grid=(count,),
        in_specs=[pl.BlockSpec((1, 1, ends), lambda j: (j, 0, 0))] * 2,
        out_specs=pl.BlockSpec((rows, cols), lambda j: (j, 0)),
        out_shape=jax.ShapeDtypeStruct((count * rows, cols), BF16),
        compiler_params=PARAMS,
        cost_estimate=pl.CostEstimate(
            flops=2 * count * rows * cols * ends, bytes_accessed=0, transcendentals=0
        ),
    )(marks, places)


def incidence_kernel(tri_dev, place_ref, out_ref):
    edges, cols = out_ref.shape
    plus, minus = place_ref[0, :, :edges], place_ref[0, :, edges:]
    eye = ones_where(iota((edges, edges), 0) == iota((edges, edges), 1))
    for base in range(0, cols, tri_dev):
        signed = pick(plus, base, tri_dev) - pick(minus, base, tri_dev)
        out_ref[:, base : base + tri_dev] = matmul_nt(eye, signed).astype(BF16)


def build_incidence(places, tri_dev, cols):
    count, _, ends = places.shape
    edges = ends // 2
    return pl.pallas_call(
        functools.partial(incidence_kernel, tri_dev),
        grid=(count,),
        in_specs=[pl.BlockSpec((1, 1, ends), lambda j: (j, 0, 0))],
        out_specs=pl.BlockSpec((edges, cols), lambda j: (j, 0)),
        out_shape=jax.ShapeDtypeStruct((count * edges, cols), BF16),
        compiler_params=PARAMS,
        cost_estimate=pl.CostEstimate(
            flops=2 * count * edges * cols * edges, bytes_accessed=0, transcendentals=0
        ),
    )(places)


def collect_kernel(mark_ref, value_ref, charge_ref, degree_ref):
    here = pick(mark_ref[...] - 1, 0, charge_ref.shape[0])
    charge_ref[...] = matmul(here, value_ref[...])
    degree_ref[...] = matmul(here, jnp.ones((here.shape[1], degree_ref.shape[1]), BF16))


def collect(marks, values, tri_dev):
    return pl.pallas_call(
        collect_kernel,
        in_specs=[whole()] * 2,
        out_specs=[whole()] * 2,
        out_shape=[
            jax.ShapeDtypeStruct((tri_dev, values.shape[1]), F32),
            jax.ShapeDtypeStruct((tri_dev, 128), F32),
        ],
        compiler_params=PARAMS,
    )(marks, values)


def apply_kernel(mats, count, *refs):
    matrices, pieces, outs = refs[:mats], refs[mats:-count], refs[-count:]
    block = pieces[0].shape[0]
    half = pieces[0].shape[1] // 2
    sums = []
    for matrix in matrices:
        total = None
        for k, piece in enumerate(pieces):
            term = matmul(matrix[:, k * block : (k + 1) * block], piece[...])
            total = term if total is None else total + term
        sums.append(total)
    value = sums[0]
    if mats == 2:
        real, imag = sums
        value = jnp.concatenate(
            [real[:, :half] - imag[:, half:], real[:, half:] + imag[:, :half]], axis=1
        )
    for k, out in enumerate(outs):

        @pl.when(pl.program_id(0) == k)
        def _(out=out):
            out[...] = value.astype(out.dtype)


def apply(matrices, pieces, count):
    rows, cols = matrices[0].shape
    block = rows // count
    size, width = pieces[0].shape
    return pl.pallas_call(
        functools.partial(apply_kernel, len(matrices), count),
        grid=(count,),
        in_specs=[pl.BlockSpec((block, cols), lambda j: (j, 0))] * len(matrices)
        + [pl.BlockSpec((size, width), lambda j: (0, 0))] * len(pieces),
        out_specs=[pl.BlockSpec((block, width), lambda j: (0, 0))] * count,
        out_shape=[
            jax.ShapeDtypeStruct((block, width), F32 if k == 0 else BF16) for k in range(count)
        ],
        compiler_params=PARAMS,
        cost_estimate=pl.CostEstimate(
            flops=2 * len(matrices) * rows * cols * width,
            bytes_accessed=2 * len(matrices) * rows * cols,
            transcendentals=0,
        ),
    )(*matrices, *pieces)


def total_of(layout, blocks):
    total = blocks[0]
    for part in layout.give(blocks[1:]):
        total = total + part.astype(F32)
    return total


def per_device(currents, incidence, centroids, sweep_weights):
    layout = Layout(lax.axis_size("row"), lax.axis_size("col"))
    devices = layout.devices
    me = lax.axis_index(AXES)
    tri_dev = centroids.shape[1]
    edge_dev, width = currents.shape
    slots = 8 * tri_dev // devices
    cells = devices * slots
    sweeps = sweep_weights.shape[0]
    count = len(layout.plane)
    cols = layout.z * layout.core * tri_dev

    outgoing, labels = route(incidence, currents, tri_dev, slots, cells)
    labels = lax.all_to_all(
        labels.reshape(devices, slots), AXES, split_axis=0, concat_axis=0, tiled=True
    ).reshape(1, cells)
    arrived = lax.all_to_all(
        outgoing.reshape(devices, slots, width), AXES, split_axis=0, concat_axis=0, tiled=True
    ).reshape(cells, width)

    line_points = jnp.concatenate(layout.line(centroids), axis=1)
    numbers = jnp.concatenate([incidence.reshape(-1), centroids.reshape(-1)])
    numbers = jnp.stack(layout.across(numbers))
    ends = numbers[:, : 2 * edge_dev].reshape(count, 1, 2 * edge_dev)
    plane_points = numbers[:, 2 * edge_dev :].reshape(count, 3, tri_dev)
    plane_points = plane_points.transpose(1, 0, 2).reshape(3, count * tri_dev)
    tiles = build_tiles(plane_points, line_points, tri_dev)
    slopes_of = build_incidence(layout.place(ends, tri_dev, me), tri_dev, cols)
    all_labels = jnp.stack(layout.across(labels))
    marks, others = all_labels % (2 * tri_dev), all_labels // (2 * tri_dev)
    places = jnp.where(marks > 0, layout.place(others, tri_dev, me), -1)
    neighbours = build_adjacency(marks, places, tri_dev, cols)

    charge, degree = collect(labels % (2 * tri_dev), arrived, tri_dev)
    current = currents
    potential = None
    for sweep in range(sweeps):
        pieces = layout.line(charge.astype(BF16))
        potential = total_of(layout, apply(tiles, pieces, count)).astype(BF16)
        pieces = layout.line(potential)
        if sweep + 1 < sweeps:
            around = total_of(layout, apply([neighbours], pieces, count))
            change = degree[:, :1] * potential.astype(F32) - around
            charge = charge - sweep_weights[sweep] * change
        slope = total_of(layout, apply([slopes_of], pieces, count))
        current = (current.astype(F32) - sweep_weights[sweep] * slope).astype(BF16)
    return current, potential


def solution(mesh):
    in_specs = (P(AXES, None), P(None, AXES), P(None, AXES), P())
    out_specs = (P(AXES, None), P(AXES, None))
    return jax.shard_map(
        per_device, mesh=mesh, in_specs=in_specs, out_specs=out_specs, check_vma=False
    )
```

time: 385 us -> 202 us (0.52)
  waiting for transfers between devices: 173 us -> 64 us
  blocking collectives: 71.8 us -> 14.2 us
  starting transfers between devices: 3.53 us -> 56.7 us
  local copies, waits for them, and re-layouts: 32.5 us -> 6.72 us
  matrix products: 25.1 us -> 0 us
  between operations: 14.2 us -> 0.98 us
  Pallas kernels: 57.1 us -> 53 us
    all_gather x5 -> x0, waiting for transfers between devices: 165 us -> none  [the longest x2 104 us: per_device(): lax.all_gather(charge.astype(jnp.bfloat16), AXES, axis=0, tiled=True)]
    all_gather x1 -> x0, blocking collectives: 71.8 us -> none  [per_device(): numbers = lax.all_gather(numbers, AXES, axis=0, tiled=False)]
    ppermute x0 -> x56, waiting for transfers between devices: none -> 64 us  [shift(): return lax.ppermute(value, AXES, pairs)]
    ppermute x0 -> x56, starting transfers between devices: none -> 54 us  [shift(): return lax.ppermute(value, AXES, pairs)]
    dot_general x6 -> x0, matrix products: 25.1 us -> none  [the longest x2 6.67 us: per_device(): jnp.dot(real_tile, piece, preferred_element_type=jnp.float32)]
    all_to_all x0 -> x1, blocking collectives: none -> 14.2 us  [per_device(): lax.all_to_all(labels.reshape(devices, slots), AXES, split_axis=0, concat...]
    gather x2 -> x0, local copies, waits for them, and re-layouts: 9.65 us -> none  [per_device(): picked = everywhere[triangle]]
    all_to_all x1, waiting for transfers between devices: 6.45 us -> 0.01 us  [per_device(): lax.all_to_all(outgoing.reshape(devices, slots, width), AXES, split_axis=...]
  transfers between devices with their start and end apart: 6 -> 57, of which waited for: 5 -> 22; matrix products, arithmetic and copies ran while one was open for 5% -> 3% of each run, Pallas kernels for 15% -> 19%
where the time goes in v2:
time: 202 us
  waiting for transfers between devices  64 us (32%)
  starting transfers between devices  56.7 us (28%)
  Pallas kernels  53 us (26%)
  blocking collectives  14.2 us (7%)
  local copies, waits for them, and re-layouts  6.72 us (3%)
  other arithmetic  5.94 us (3%)
    ppermute x56, waiting for transfers between devices, shift(): return lax.ppermute(value, AXES, pairs)  64 us
    ppermute x56, starting transfers between devices, shift(): return lax.ppermute(value, AXES, pairs)  54 us
    pallas_call x5, Pallas kernels, apply(): pl.pallas_call(functools.partial(apply_kernel, len(matrices), count), gri...  22 us
    all_to_all x1, blocking collectives, per_device(): lax.all_to_all(labels.reshape(devices, slots), AXES, split_axis=0, concat...  14.2 us
    pallas_call x1, Pallas kernels, build_tiles(): pl.pallas_call(tile_kernel, grid=(rows // tri_dev, cols // block), in_spe...  12.4 us
    pallas_call x1, Pallas kernels, build_adjacency(): pl.pallas_call(adjacency_kernel, grid=(count,), in_specs=[pl.BlockSpec((1...  9.54 us
    pallas_call x1, Pallas kernels, build_incidence(): pl.pallas_call(functools.partial(incidence_kernel, tri_dev), grid=(count,...  5.48 us
  transfers between devices with their start and end apart: 57, of which 22 were waited for; matrix products, arithmetic and copies ran while one was open for 3% of the time, Pallas kernels for 19%

profile of v2, /device:TPU:0, one launch (start us, length us, event | category | flops | bytes accessed | tf_op | source)
XLA Modules:
  0.0 201.6 jit_solution(7124417974167628306)
XLA Ops:
  0.6 1.4 rev.3
  3.7 2.9 %shard_map.61 = (bf16[2048,256]{1,0:T(8,128)(2,1)}, s32[1,2048]{1,0:T(1,128)S(1)}) custom-call(s32[1,768]{1,0:T(1,128)S(1)} %bitcast.22, s32[1,768]{1,0:T(1,128)S(1)} %bitcast.23, bf16[384,256]{1,0:T(8,128)(2,1)S(1)} %copy-done.2), custom_call_target="tpu_custom_call" | custom-call | tf_op jit(solution)/shard_map/pallas_call | solution.py:132
  7.8 14.2 %all_to_all.14 = s32[32,1,64]{2,1,0:T(1,128)S(1)} all-to-all(s32[32,1,64]{2,1,0:T(1,128)S(1)} %bitcast.25), channel_id=1, replica_groups=mesh['row'=4,'col'=8] {'row','col'}, dimensions={0} | all-to-all | bytes 16384 | tf_op jit(solution)/shard_map/all_to_all | solution.py:337
  22.0 2.6 %all-to-all-start.1 = ((bf16[32,64,256]{2,1,0:T(8,128)(2,1)}), bf16[32,64,256]{2,1,0:T(8,128)(2,1)S(1)}, u32[]{:S(2)}, u32[]{:S(2)}) async-start(bf16[32,64,256]{2,1,0:T(8,128)(2,1)} %bitcast.4), calls=%async_computation.1 | async-start | bytes 2097152 | tf_op jit(solution)/shard_map/all_to_all | solution.py:340
  24.6 2.7 %collective-permute-start.6 = (s32[3,256]{1,0:T(4,128)}, s32[3,256]{1,0:T(4,128)S(1)}, u32[]{:S(2)}, u32[]{:S(2)}) collective-permute-start(s32[3,256]{1,0:T(4,128)} %param.6), channel_id=1, source_target_pairs={{0,4},{1,5},{2,6},{3,7},{4,0},{5,1},{6,2},{7,3},{8,12},{9,13},{10,... | collective-permute-start | bytes 9224 | tf_op jit(solution)/shard_map/ppermute | solution.py:77
  27.4 1.4 collective-permute-start.4
  30.8 2.5 %collective-permute-start.2 = (s32[1536]{0:T(1024)S(1)}, s32[1536]{0:T(1024)S(1)}, u32[]{:S(2)}, u32[]{:S(2)}) collective-permute-start(s32[1536]{0:T(1024)S(1)} %constant_dynamic-update-slice_fusion.9), channel_id=1, source_target_pairs={{0,17},{1,16},{2,19},{3,18},{4,21},{5,20},{6,23},{7,22},{8,25},{9,... | collective-permute-start | bytes 18440 | tf_op jit(solution)/shard_map/ppermute | solution.py:77
  34.6 16.6 %collective-permute-done.6 = s32[3,256]{1,0:T(4,128)S(1)} collective-permute-done((s32[3,256]{1,0:T(4,128)}, s32[3,256]{1,0:T(4,128)S(1)}, u32[]{:S(2)}, u32[]{:S(2)}) %collective-permute-start.6) | collective-permute-done | bytes 3104 | tf_op jit(solution)/shard_map/ppermute | solution.py:77
  51.2 1.5 collective-permute-start
  53.3 1.5 collective-permute-done
  56.6 1.7 collective-permute-start.13
  58.3 2.1 %collective-permute-start.11 = (bf16[256,256]{1,0:T(8,128)(2,1)S(1)}, bf16[256,256]{1,0:T(8,128)(2,1)S(1)}, u32[]{:S(2)}, u32[]{:S(2)}) collective-permute-start(bf16[256,256]{1,0:T(8,128)(2,1)S(1)} %convert_element_type.73.refs_2_), channel_id=1, source_target_pairs={{0,6},{1,7},{2,0},{3,1},{4,2},{5,3},{6,4},{7,5},{8,14},{9,15},{10,... | collective-permute-start | bytes 393224 | tf_op jit(solution)/shard_map/ppermute | solution.py:77
  60.5 4.4 %collective-permute-done.15.refs_8_ = bf16[256,256]{1,0:T(8,128)(2,1)S(1)} collective-permute-done((bf16[256,256]{1,0:T(8,128)(2,1)S(1)}, bf16[256,256]{1,0:T(8,128)(2,1)S(1)}, u32[]{:S(2)}, u32[]{:S(2)}) %collective-permute-start.15) | collective-permute-done | bytes 131104 | tf_op jit(solution)/shard_map/ppermute | solution.py:77
  64.9 3.8 %collective-permute-done.13.refs_6_ = bf16[256,256]{1,0:T(8,128)(2,1)S(1)} collective-permute-done((bf16[256,256]{1,0:T(8,128)(2,1)S(1)}, bf16[256,256]{1,0:T(8,128)(2,1)S(1)}, u32[]{:S(2)}, u32[]{:S(2)}) %collective-permute-start.13) | collective-permute-done | bytes 131104 | tf_op jit(solution)/shard_map/ppermute | solution.py:77
  69.3 12.4 %shard_map.60 = (bf16[1024,2048]{1,0:T(8,128)(2,1)S(1)}, bf16[1024,2048]{1,0:T(8,128)(2,1)}) custom-call(s32[3,1024]{1,0:T(4,128)S(1)} %bitcast.21, s32[3,2048]{1,0:T(4,128)S(1)} %constant_dynamic-update-slice_fusion.1.col_ref), custom_call_target="tpu_custom_call" | custom-call | flops 125829120 | bytes 8388608 | tf_op jit(solution)/shard_map/pallas_call | solution.py:179
  81.7 5.8 %shard_map.63 = (f32[256,256]{1,0:T(8,128)S(1)}, bf16[256,256]{1,0:T(8,128)(2,1)S(1)}, bf16[256,256]{1,0:T(8,128)(2,1)S(1)}, bf16[256,256]{1,0:T(8,128)(2,1)S(1)}) custom-call(bf16[1024,2048]{1,0:T(8,128)(2,1)S(1)} %get-tuple-element.28.refs_0_, bf16[1024,2048]{1,0:T(8,128)(2,1)} %get-tuple-element.29.refs_1_, ...), custom_call_target="tpu_custom_call" | custom-call | flops 2147483648 | bytes 8388608 | tf_op jit(solution)/shard_map/pallas_call | solution.py:299
  88.3 1.6 collective-permute-start.18
  91.8 1.6 collective-permute-start.31
  93.5 1.5 collective-permute-start.32
  95.1 2.2 %collective-permute-done.19 = bf16[256,256]{1,0:T(8,128)(2,1)S(1)} collective-permute-done((bf16[256,256]{1,0:T(8,128)(2,1)S(1)}, bf16[256,256]{1,0:T(8,128)(2,1)S(1)}, u32[]{:S(2)}, u32[]{:S(2)}) %collective-permute-start.19) | collective-permute-done | bytes 131104 | tf_op jit(solution)/shard_map/ppermute | solution.py:77
  97.3 2.4 %collective-permute-start.25 = (bf16[256,256]{1,0:T(8,128)(2,1)S(1)}, bf16[256,256]{1,0:T(8,128)(2,1)S(1)}, u32[]{:S(2)}, u32[]{:S(2)}) collective-permute-start(bf16[256,256]{1,0:T(8,128)(2,1)S(1)} %add_convert_fusion.1.refs_1_), channel_id=1, source_target_pairs={{0,2},{1,3},{2,4},{3,5},{4,6},{5,7},{6,0},{7,1},{8,10},{9,11},{10,... | collective-permute-start | bytes 393224 | tf_op jit(solution)/shard_map/ppermute | solution.py:77
  99.8 2.3 %collective-permute-start.21 = (bf16[256,256]{1,0:T(8,128)(2,1)S(1)}, bf16[256,256]{1,0:T(8,128)(2,1)S(1)}, u32[]{:S(2)}, u32[]{:S(2)}) collective-permute-start(bf16[256,256]{1,0:T(8,128)(2,1)S(1)} %add_convert_fusion.1.refs_1_), channel_id=1, source_target_pairs={{0,6},{1,7},{2,0},{3,1},{4,2},{5,3},{6,4},{7,5},{8,14},{9,15},{10,... | collective-permute-start | bytes 393224 | tf_op jit(solution)/shard_map/ppermute | solution.py:77
  103.6 2.0 collective-permute-done.25.refs_7_
  105.6 3.5 %collective-permute-done.23.refs_5_ = bf16[256,256]{1,0:T(8,128)(2,1)S(1)} collective-permute-done((bf16[256,256]{1,0:T(8,128)(2,1)S(1)}, bf16[256,256]{1,0:T(8,128)(2,1)S(1)}, u32[]{:S(2)}, u32[]{:S(2)}) %collective-permute-start.23) | collective-permute-done | bytes 131104 | tf_op jit(solution)/shard_map/ppermute | solution.py:77
  109.6 9.5 %shard_map.65.refs_0_ = bf16[1024,2048]{1,0:T(8,128)(2,1)S(1)} custom-call(s32[4,1,2048]{2,1,0:T(1,128)S(1)} %get-tuple-element.55.mark_ref, s32[4,1,2048]{2,1,0:T(1,128)S(1)} %get-tuple-element.54.place_ref), custom_call_target="tpu_custom_call" | custom-call | flops 8589934592 | tf_op jit(solution)/shard_map/pallas_call | solution.py:214
  119.2 1.9 shard_map.66
  126.7 1.6 collective-permute-done.34
  128.3 2.2 %collective-permute-done.35 = bf16[256,256]{1,0:T(8,128)(2,1)S(1)} collective-permute-done((bf16[256,256]{1,0:T(8,128)(2,1)S(1)}, bf16[256,256]{1,0:T(8,128)(2,1)S(1)}, u32[]{:S(2)}, u32[]{:S(2)}) %collective-permute-start.35) | collective-permute-done | bytes 131104 | tf_op jit(solution)/shard_map/ppermute | solution.py:77
  131.3 3.3 %collective-permute-start.41 = (bf16[256,256]{1,0:T(8,128)(2,1)S(1)}, bf16[256,256]{1,0:T(8,128)(2,1)S(1)}, u32[]{:S(2)}, u32[]{:S(2)}) collective-permute-start(bf16[256,256]{1,0:T(8,128)(2,1)S(1)} %subtract_convert_fusion.2.refs_2_), channel_id=1, source_target_pairs={{0,2},{1,3},{2,4},{3,5},{4,6},{5,7},{6,0},{7,1},{8,10},{9,11},{10,... | collective-permute-start | bytes 393224 | tf_op jit(solution)/shard_map/ppermute | solution.py:77
  134.6 1.6 collective-permute-start.39
  137.1 3.0 %collective-permute-done.41.refs_8_ = bf16[256,256]{1,0:T(8,128)(2,1)S(1)} collective-permute-done((bf16[256,256]{1,0:T(8,128)(2,1)S(1)}, bf16[256,256]{1,0:T(8,128)(2,1)S(1)}, u32[]{:S(2)}, u32[]{:S(2)}) %collective-permute-start.41) | collective-permute-done | bytes 131104 | tf_op jit(solution)/shard_map/ppermute | solution.py:77
  140.1 4.0 %collective-permute-done.39.refs_6_ = bf16[256,256]{1,0:T(8,128)(2,1)S(1)} collective-permute-done((bf16[256,256]{1,0:T(8,128)(2,1)S(1)}, bf16[256,256]{1,0:T(8,128)(2,1)S(1)}, u32[]{:S(2)}, u32[]{:S(2)}) %collective-permute-start.39) | collective-permute-done | bytes 131104 | tf_op jit(solution)/shard_map/ppermute | solution.py:77
  145.7 4.8 %shard_map.67 = (f32[256,256]{1,0:T(8,128)S(1)}, bf16[256,256]{1,0:T(8,128)(2,1)S(1)}, bf16[256,256]{1,0:T(8,128)(2,1)S(1)}, bf16[256,256]{1,0:T(8,128)(2,1)S(1)}) custom-call(bf16[1024,2048]{1,0:T(8,128)(2,1)S(1)} %copy-done.1, bf16[1024,2048]{1,0:T(8,128)(2,1)} %get-tuple-element.29.refs_1_, bf16[256,256]{1,0:T(8,128)(2,1)S(1)} %subtract_convert_fusion.2.refs_2_, ...), custom_call_target="tpu_custom_call" | custom-call | flops 2147483648 | bytes 8388608 | tf_op jit(solution)/shard_map/pallas_call | solution.py:299
  151.4 1.4 collective-permute-start.44
  154.0 2.2 %collective-permute-done.43 = bf16[256,256]{1,0:T(8,128)(2,1)S(1)} collective-permute-done((bf16[256,256]{1,0:T(8,128)(2,1)S(1)}, bf16[256,256]{1,0:T(8,128)(2,1)S(1)}, u32[]{:S(2)}, u32[]{:S(2)}) %collective-permute-start.43) | collective-permute-done | bytes 131104 | tf_op jit(solution)/shard_map/ppermute | solution.py:77
  156.2 1.5 collective-permute-done.44
  157.7 2.5 %collective-permute-done.45 = bf16[256,256]{1,0:T(8,128)(2,1)S(1)} collective-permute-done((bf16[256,256]{1,0:T(8,128)(2,1)S(1)}, bf16[256,256]{1,0:T(8,128)(2,1)S(1)}, u32[]{:S(2)}, u32[]{:S(2)}) %collective-permute-start.45) | collective-permute-done | bytes 131104 | tf_op jit(solution)/shard_map/ppermute | solution.py:77
  160.3 3.0 %collective-permute-start.51 = (bf16[256,256]{1,0:T(8,128)(2,1)S(1)}, bf16[256,256]{1,0:T(8,128)(2,1)S(1)}, u32[]{:S(2)}, u32[]{:S(2)}) collective-permute-start(bf16[256,256]{1,0:T(8,128)(2,1)S(1)} %add_convert_fusion.refs_1_), channel_id=1, source_target_pairs={{0,2},{1,3},{2,4},{3,5},{4,6},{5,7},{6,0},{7,1},{8,10},{9,11},{10,... | collective-permute-start | bytes 393224 | tf_op jit(solution)/shard_map/ppermute | solution.py:77
  163.3 2.0 collective-permute-start.49
  165.7 5.5 %shard_map.59.refs_0_ = bf16[1536,2048]{1,0:T(8,128)(2,1)} custom-call(s32[4,1,768]{2,1,0:T(1,128)S(1)} %select_n.263.place_ref), custom_call_target="tpu_custom_call" | custom-call | flops 2415919104 | tf_op jit(solution)/shard_map/pallas_call | solution.py:239
  171.7 1.6 collective-permute-done.49.refs_5_
  173.8 4.8 %shard_map.64 = (f32[384,256]{1,0:T(8,128)S(1)}, bf16[384,256]{1,0:T(8,128)(2,1)S(1)}, bf16[384,256]{1,0:T(8,128)(2,1)S(1)}, bf16[384,256]{1,0:T(8,128)(2,1)S(1)}) custom-call(bf16[1536,2048]{1,0:T(8,128)(2,1)} %shard_map.59.refs_0_, bf16[256,256]{1,0:T(8,128)(2,1)S(1)} %add_convert_fusion.1.refs_1_, bf16[256,256]{1,0:T(8,128)(2,1)S(1)} %collective-permute-done.20.refs_2_, ...), custom_call_target="tpu_custom_call" | custom-call | flops 1610612736 | bytes 6291456 | tf_op jit(solution)/shard_map/pallas_call | solution.py:299
  179.6 1.4 collective-permute-start.28
  182.1 4.8 %shard_map.68 = (f32[384,256]{1,0:T(8,128)S(1)}, bf16[384,256]{1,0:T(8,128)(2,1)S(1)}, bf16[384,256]{1,0:T(8,128)(2,1)S(1)}, bf16[384,256]{1,0:T(8,128)(2,1)S(1)}) custom-call(bf16[1536,2048]{1,0:T(8,128)(2,1)} %shard_map.59.refs_0_, bf16[256,256]{1,0:T(8,128)(2,1)S(1)} %add_convert_fusion.refs_1_, bf16[256,256]{1,0:T(8,128)(2,1)S(1)} %collective-permute-done.46.refs_2_, ...), custom_call_target="tpu_custom_call" | custom-call | flops 1610612736 | bytes 6291456 | tf_op jit(solution)/shard_map/pallas_call | solution.py:299
  187.9 1.4 collective-permute-start.54
  191.8 4.5 %collective-permute-done.53 = bf16[384,256]{1,0:T(8,128)(2,1)S(1)} collective-permute-done((bf16[384,256]{1,0:T(8,128)(2,1)S(1)}, bf16[384,256]{1,0:T(8,128)(2,1)S(1)}, u32[]{:S(2)}, u32[]{:S(2)}) %collective-permute-start.53) | collective-permute-done | bytes 196640 | tf_op jit(solution)/shard_map/ppermute | solution.py:77
  196.3 3.1 %collective-permute-done.55 = bf16[384,256]{1,0:T(8,128)(2,1)S(1)} collective-permute-done((bf16[384,256]{1,0:T(8,128)(2,1)S(1)}, bf16[384,256]{1,0:T(8,128)(2,1)S(1)}, u32[]{:S(2)}, u32[]{:S(2)}) %collective-permute-start.55) | collective-permute-done | bytes 196640 | tf_op jit(solution)/shard_map/ppermute | solution.py:77
  199.4 2.2 %subtract_convert_fusion = bf16[384,256]{1,0:T(8,128)(2,1)} fusion(bf16[384,256]{1,0:T(8,128)(2,1)S(1)} %collective-permute-done.55, bf16[384,256]{1,0:T(8,128)(2,1)S(1)} %collective-permute-done.54, f32[384,256]{1,0:T(8,128)S(1)} %get-tuple-element.50, bf16[384,256]{1,0:T(8,128)(2,1)S(1)} %collective-permute-done.53, ...), kind=kLoop, calls=%fused_computation | loop fusion | flops 1966080 | bytes 2359304 | tf_op jit(solution)/shard_map/convert_element_type | solution.py:369
  (128 shorter events, 32.0 us)
Async XLA Ops:
  22.0 33.8 %all-to-all-start.1 = ((bf16[32,64,256]{2,1,0:T(8,128)(2,1)}), bf16[32,64,256]{2,1,0:T(8,128)(2,1)S(1)}, u32[]{:S(2)}, u32[]{:S(2)}) async-start(bf16[32,64,256]{2,1,0:T(8,128)(2,1)} %bitcast.4), calls=%async_computation.1 | async-start | bytes 2097152 | tf_op jit(solution)/shard_map/all_to_all | solution.py:340
  24.6 26.5 %collective-permute-start.6 = (s32[3,256]{1,0:T(4,128)}, s32[3,256]{1,0:T(4,128)S(1)}, u32[]{:S(2)}, u32[]{:S(2)}) collective-permute-start(s32[3,256]{1,0:T(4,128)} %param.6), channel_id=1, source_target_pairs={{0,4},{1,5},{2,6},{3,7},{4,0},{5,1},{6,2},{7,3},{8,12},{9,13},{10,... | collective-permute-start | bytes 9224 | tf_op jit(solution)/shard_map/ppermute | solution.py:77
  27.4 25.3 %collective-permute-start.4 = (s32[3,256]{1,0:T(4,128)}, s32[3,256]{1,0:T(4,128)S(1)}, u32[]{:S(2)}, u32[]{:S(2)}) collective-permute-start(s32[3,256]{1,0:T(4,128)} %param.6), channel_id=1, source_target_pairs={{0,6},{1,7},{2,0},{3,1},{4,2},{5,3},{6,4},{7,5},{8,14},{9,15},{10,... | collective-permute-start | bytes 9224 | tf_op jit(solution)/shard_map/ppermute | solution.py:77
  28.7 23.9 %collective-permute-start.8 = (s32[3,256]{1,0:T(4,128)}, s32[3,256]{1,0:T(4,128)S(1)}, u32[]{:S(2)}, u32[]{:S(2)}) collective-permute-start(s32[3,256]{1,0:T(4,128)} %param.6), channel_id=1, source_target_pairs={{0,2},{1,3},{2,4},{3,5},{4,6},{5,7},{6,0},{7,1},{8,10},{9,11},{10,... | collective-permute-start | bytes 9224 | tf_op jit(solution)/shard_map/ppermute | solution.py:77
  30.8 22.4 %collective-permute-start.2 = (s32[1536]{0:T(1024)S(1)}, s32[1536]{0:T(1024)S(1)}, u32[]{:S(2)}, u32[]{:S(2)}) collective-permute-start(s32[1536]{0:T(1024)S(1)} %constant_dynamic-update-slice_fusion.9), channel_id=1, source_target_pairs={{0,17},{1,16},{2,19},{3,18},{4,21},{5,20},{6,23},{7,22},{8,25},{9,... | collective-permute-start | bytes 18440 | tf_op jit(solution)/shard_map/ppermute | solution.py:77
  34.0 19.3 %collective-permute-start.1 = (s32[1536]{0:T(1024)S(1)}, s32[1536]{0:T(1024)S(1)}, u32[]{:S(2)}, u32[]{:S(2)}) collective-permute-start(s32[1536]{0:T(1024)S(1)} %constant_dynamic-update-slice_fusion.9), channel_id=1, source_target_pairs={{0,16},{1,17},{2,18},{3,19},{4,20},{5,21},{6,22},{7,23},{8,24},{9,... | collective-permute-start | bytes 18440 | tf_op jit(solution)/shard_map/ppermute | solution.py:77
  52.7 7.8 %collective-permute-start.7 = (s32[3,256]{1,0:T(4,128)S(1)}, s32[3,256]{1,0:T(4,128)S(1)}, u32[]{:S(2)}, u32[]{:S(2)}) collective-permute-start(s32[3,256]{1,0:T(4,128)S(1)} %collective-permute-done.6), channel_id=1, source_target_pairs={{0,8},{1,9},{2,10},{3,11},{4,12},{5,13},{6,14},{7,15},{8,0},{9,1},... | collective-permute-start | bytes 9224 | tf_op jit(solution)/shard_map/ppermute | solution.py:77
  53.2 16.1 %collective-permute-start.9 = (s32[3,256]{1,0:T(4,128)S(1)}, s32[3,256]{1,0:T(4,128)S(1)}, u32[]{:S(2)}, u32[]{:S(2)}) collective-permute-start(s32[3,256]{1,0:T(4,128)S(1)} %collective-permute-done.8), channel_id=1, source_target_pairs={{0,8},{1,9},{2,10},{3,11},{4,12},{5,13},{6,14},{7,15},{8,0},{9,1},... | collective-permute-start | bytes 9224 | tf_op jit(solution)/shard_map/ppermute | solution.py:77
  56.5 8.3 %collective-permute-start.15 = (bf16[256,256]{1,0:T(8,128)(2,1)S(1)}, bf16[256,256]{1,0:T(8,128)(2,1)S(1)}, u32[]{:S(2)}, u32[]{:S(2)}) collective-permute-start(bf16[256,256]{1,0:T(8,128)(2,1)S(1)} %convert_element_type.73.refs_2_), channel_id=1, source_target_pairs={{0,2},{1,3},{2,4},{3,5},{4,6},{5,7},{6,0},{7,1},{8,10},{9,11},{10,... | collective-permute-start | bytes 393224 | tf_op jit(solution)/shard_map/ppermute | solution.py:77
  56.6 12.1 %collective-permute-start.13 = (bf16[256,256]{1,0:T(8,128)(2,1)S(1)}, bf16[256,256]{1,0:T(8,128)(2,1)S(1)}, u32[]{:S(2)}, u32[]{:S(2)}) collective-permute-start(bf16[256,256]{1,0:T(8,128)(2,1)S(1)} %convert_element_type.73.refs_2_), channel_id=1, source_target_pairs={{0,4},{1,5},{2,6},{3,7},{4,0},{5,1},{6,2},{7,3},{8,12},{9,13},{10,... | collective-permute-start | bytes 393224 | tf_op jit(solution)/shard_map/ppermute | solution.py:77
  58.3 10.4 %collective-permute-start.11 = (bf16[256,256]{1,0:T(8,128)(2,1)S(1)}, bf16[256,256]{1,0:T(8,128)(2,1)S(1)}, u32[]{:S(2)}, u32[]{:S(2)}) collective-permute-start(bf16[256,256]{1,0:T(8,128)(2,1)S(1)} %convert_element_type.73.refs_2_), channel_id=1, source_target_pairs={{0,6},{1,7},{2,0},{3,1},{4,2},{5,3},{6,4},{7,5},{8,14},{9,15},{10,... | collective-permute-start | bytes 393224 | tf_op jit(solution)/shard_map/ppermute | solution.py:77
  60.4 21.3 %collective-permute-start.10 = (bf16[256,256]{1,0:T(8,128)(2,1)S(1)}, bf16[256,256]{1,0:T(8,128)(2,1)S(1)}, u32[]{:S(2)}, u32[]{:S(2)}) collective-permute-start(bf16[256,256]{1,0:T(8,128)(2,1)S(1)} %convert_element_type.73.refs_2_), channel_id=1, source_target_pairs={{0,8},{1,9},{2,10},{3,11},{4,12},{5,13},{6,14},{7,15},{8,0},{9,1},... | collective-permute-start | bytes 393224 | tf_op jit(solution)/shard_map/ppermute | solution.py:77
  64.9 16.8 %collective-permute-start.16 = (bf16[256,256]{1,0:T(8,128)(2,1)S(1)}, bf16[256,256]{1,0:T(8,128)(2,1)S(1)}, u32[]{:S(2)}, u32[]{:S(2)}) collective-permute-start(bf16[256,256]{1,0:T(8,128)(2,1)S(1)} %collective-permute-done.15.refs_8_), channel_id=1, source_target_pairs={{0,8},{1,9},{2,10},{3,11},{4,12},{5,13},{6,14},{7,15},{8,0},{9,1},... | collective-permute-start | bytes 393224 | tf_op jit(solution)/shard_map/ppermute | solution.py:77
  68.7 13.0 %collective-permute-start.14 = (bf16[256,256]{1,0:T(8,128)(2,1)S(1)}, bf16[256,256]{1,0:T(8,128)(2,1)S(1)}, u32[]{:S(2)}, u32[]{:S(2)}) collective-permute-start(bf16[256,256]{1,0:T(8,128)(2,1)S(1)} %collective-permute-done.13.refs_6_), channel_id=1, source_target_pairs={{0,8},{1,9},{2,10},{3,11},{4,12},{5,13},{6,14},{7,15},{8,0},{9,1},... | collective-permute-start | bytes 393224 | tf_op jit(solution)/shard_map/ppermute | solution.py:77
  68.7 13.0 %collective-permute-start.12 = (bf16[256,256]{1,0:T(8,128)(2,1)S(1)}, bf16[256,256]{1,0:T(8,128)(2,1)S(1)}, u32[]{:S(2)}, u32[]{:S(2)}) collective-permute-start(bf16[256,256]{1,0:T(8,128)(2,1)S(1)} %collective-permute-done.11.refs_4_), channel_id=1, source_target_pairs={{0,8},{1,9},{2,10},{3,11},{4,12},{5,13},{6,14},{7,15},{8,0},{9,1},... | collective-permute-start | bytes 393224 | tf_op jit(solution)/shard_map/ppermute | solution.py:77
  88.3 6.7 %collective-permute-start.18 = (bf16[256,256]{1,0:T(8,128)(2,1)S(1)}, bf16[256,256]{1,0:T(8,128)(2,1)S(1)}, u32[]{:S(2)}, u32[]{:S(2)}) collective-permute-start(bf16[256,256]{1,0:T(8,128)(2,1)S(1)} %get-tuple-element.35), channel_id=1, source_target_pairs={{0,16},{1,17},{2,18},{3,19},{4,20},{5,21},{6,22},{7,23},{8,24},{9,... | collective-permute-start | bytes 393224 | tf_op jit(solution)/shard_map/ppermute | solution.py:77
  90.0 7.3 %collective-permute-start.19 = (bf16[256,256]{1,0:T(8,128)(2,1)S(1)}, bf16[256,256]{1,0:T(8,128)(2,1)S(1)}, u32[]{:S(2)}, u32[]{:S(2)}) collective-permute-start(bf16[256,256]{1,0:T(8,128)(2,1)S(1)} %get-tuple-element.36), channel_id=1, source_target_pairs={{0,17},{1,16},{2,19},{3,18},{4,21},{5,20},{6,23},{7,22},{8,25},{9,... | collective-permute-start | bytes 393224 | tf_op jit(solution)/shard_map/ppermute | solution.py:77
  91.1 8.7 %collective-permute-start.30 = (s32[1,2048]{1,0:T(1,128)S(1)}, s32[1,2048]{1,0:T(1,128)S(1)}, u32[]{:S(2)}, u32[]{:S(2)}) collective-permute-start(s32[1,2048]{1,0:T(1,128)S(1)} %reshape.1200), channel_id=1, source_target_pairs={{0,1},{1,0},{2,3},{3,2},{4,5},{5,4},{6,7},{7,6},{8,9},{9,8},{10,11... | collective-permute-start | bytes 24584 | tf_op jit(solution)/shard_map/ppermute | solution.py:77
  91.8 10.3 %collective-permute-start.31 = (s32[1,2048]{1,0:T(1,128)S(1)}, s32[1,2048]{1,0:T(1,128)S(1)}, u32[]{:S(2)}, u32[]{:S(2)}) collective-permute-start(s32[1,2048]{1,0:T(1,128)S(1)} %reshape.1200), channel_id=1, source_target_pairs={{0,16},{1,17},{2,18},{3,19},{4,20},{5,21},{6,22},{7,23},{8,24},{9,... | collective-permute-start | bytes 24584 | tf_op jit(solution)/shard_map/ppermute | solution.py:77
  93.5 8.6 %collective-permute-start.32 = (s32[1,2048]{1,0:T(1,128)S(1)}, s32[1,2048]{1,0:T(1,128)S(1)}, u32[]{:S(2)}, u32[]{:S(2)}) collective-permute-start(s32[1,2048]{1,0:T(1,128)S(1)} %reshape.1200), channel_id=1, source_target_pairs={{0,17},{1,16},{2,19},{3,18},{4,21},{5,20},{6,23},{7,22},{8,25},{9,... | collective-permute-start | bytes 24584 | tf_op jit(solution)/shard_map/ppermute | solution.py:77
  97.3 8.3 %collective-permute-start.25 = (bf16[256,256]{1,0:T(8,128)(2,1)S(1)}, bf16[256,256]{1,0:T(8,128)(2,1)S(1)}, u32[]{:S(2)}, u32[]{:S(2)}) collective-permute-start(bf16[256,256]{1,0:T(8,128)(2,1)S(1)} %add_convert_fusion.1.refs_1_), channel_id=1, source_target_pairs={{0,2},{1,3},{2,4},{3,5},{4,6},{5,7},{6,0},{7,1},{8,10},{9,11},{10,... | collective-permute-start | bytes 393224 | tf_op jit(solution)/shard_map/ppermute | solution.py:77
  99.7 9.4 %collective-permute-start.23 = (bf16[256,256]{1,0:T(8,128)(2,1)S(1)}, bf16[256,256]{1,0:T(8,128)(2,1)S(1)}, u32[]{:S(2)}, u32[]{:S(2)}) collective-permute-start(bf16[256,256]{1,0:T(8,128)(2,1)S(1)} %add_convert_fusion.1.refs_1_), channel_id=1, source_target_pairs={{0,4},{1,5},{2,6},{3,7},{4,0},{5,1},{6,2},{7,3},{8,12},{9,13},{10,... | collective-permute-start | bytes 393224 | tf_op jit(solution)/shard_map/ppermute | solution.py:77
  99.8 9.3 %collective-permute-start.21 = (bf16[256,256]{1,0:T(8,128)(2,1)S(1)}, bf16[256,256]{1,0:T(8,128)(2,1)S(1)}, u32[]{:S(2)}, u32[]{:S(2)}) collective-permute-start(bf16[256,256]{1,0:T(8,128)(2,1)S(1)} %add_convert_fusion.1.refs_1_), channel_id=1, source_target_pairs={{0,6},{1,7},{2,0},{3,1},{4,2},{5,3},{6,4},{7,5},{8,14},{9,15},{10,... | collective-permute-start | bytes 393224 | tf_op jit(solution)/shard_map/ppermute | solution.py:77
  103.5 15.6 %collective-permute-start.20 = (bf16[256,256]{1,0:T(8,128)(2,1)S(1)}, bf16[256,256]{1,0:T(8,128)(2,1)S(1)}, u32[]{:S(2)}, u32[]{:S(2)}) collective-permute-start(bf16[256,256]{1,0:T(8,128)(2,1)S(1)} %add_convert_fusion.1.refs_1_), channel_id=1, source_target_pairs={{0,8},{1,9},{2,10},{3,11},{4,12},{5,13},{6,14},{7,15},{8,0},{9,1},... | collective-permute-start | bytes 393224 | tf_op jit(solution)/shard_map/ppermute | solution.py:77
  105.6 13.6 %collective-permute-start.26 = (bf16[256,256]{1,0:T(8,128)(2,1)S(1)}, bf16[256,256]{1,0:T(8,128)(2,1)S(1)}, u32[]{:S(2)}, u32[]{:S(2)}) collective-permute-start(bf16[256,256]{1,0:T(8,128)(2,1)S(1)} %collective-permute-done.25.refs_7_), channel_id=1, source_target_pairs={{0,8},{1,9},{2,10},{3,11},{4,12},{5,13},{6,14},{7,15},{8,0},{9,1},... | collective-permute-start | bytes 393224 | tf_op jit(solution)/shard_map/ppermute | solution.py:77
  109.1 10.1 %collective-permute-start.24 = (bf16[256,256]{1,0:T(8,128)(2,1)S(1)}, bf16[256,256]{1,0:T(8,128)(2,1)S(1)}, u32[]{:S(2)}, u32[]{:S(2)}) collective-permute-start(bf16[256,256]{1,0:T(8,128)(2,1)S(1)} %collective-permute-done.23.refs_5_), channel_id=1, source_target_pairs={{0,8},{1,9},{2,10},{3,11},{4,12},{5,13},{6,14},{7,15},{8,0},{9,1},... | collective-permute-start | bytes 393224 | tf_op jit(solution)/shard_map/ppermute | solution.py:77
  109.1 10.1 %collective-permute-start.22 = (bf16[256,256]{1,0:T(8,128)(2,1)S(1)}, bf16[256,256]{1,0:T(8,128)(2,1)S(1)}, u32[]{:S(2)}, u32[]{:S(2)}) collective-permute-start(bf16[256,256]{1,0:T(8,128)(2,1)S(1)} %collective-permute-done.21.refs_3_), channel_id=1, source_target_pairs={{0,8},{1,9},{2,10},{3,11},{4,12},{5,13},{6,14},{7,15},{8,0},{9,1},... | collective-permute-start | bytes 393224 | tf_op jit(solution)/shard_map/ppermute | solution.py:77
  122.1 6.2 %collective-permute-start.34 = (bf16[256,256]{1,0:T(8,128)(2,1)S(1)}, bf16[256,256]{1,0:T(8,128)(2,1)S(1)}, u32[]{:S(2)}, u32[]{:S(2)}) collective-permute-start(bf16[256,256]{1,0:T(8,128)(2,1)S(1)} %get-tuple-element.44), channel_id=1, source_target_pairs={{0,16},{1,17},{2,18},{3,19},{4,20},{5,21},{6,22},{7,23},{8,24},{9,... | collective-permute-start | bytes 393224 | tf_op jit(solution)/shard_map/ppermute | solution.py:77
  123.5 7.1 %collective-permute-start.35 = (bf16[256,256]{1,0:T(8,128)(2,1)S(1)}, bf16[256,256]{1,0:T(8,128)(2,1)S(1)}, u32[]{:S(2)}, u32[]{:S(2)}) collective-permute-start(bf16[256,256]{1,0:T(8,128)(2,1)S(1)} %get-tuple-element.45), channel_id=1, source_target_pairs={{0,17},{1,16},{2,19},{3,18},{4,21},{5,20},{6,23},{7,22},{8,25},{9,... | collective-permute-start | bytes 393224 | tf_op jit(solution)/shard_map/ppermute | solution.py:77
  131.3 8.8 %collective-permute-start.41 = (bf16[256,256]{1,0:T(8,128)(2,1)S(1)}, bf16[256,256]{1,0:T(8,128)(2,1)S(1)}, u32[]{:S(2)}, u32[]{:S(2)}) collective-permute-start(bf16[256,256]{1,0:T(8,128)(2,1)S(1)} %subtract_convert_fusion.2.refs_2_), channel_id=1, source_target_pairs={{0,2},{1,3},{2,4},{3,5},{4,6},{5,7},{6,0},{7,1},{8,10},{9,11},{10,... | collective-permute-start | bytes 393224 | tf_op jit(solution)/shard_map/ppermute | solution.py:77
  134.6 9.5 %collective-permute-start.39 = (bf16[256,256]{1,0:T(8,128)(2,1)S(1)}, bf16[256,256]{1,0:T(8,128)(2,1)S(1)}, u32[]{:S(2)}, u32[]{:S(2)}) collective-permute-start(bf16[256,256]{1,0:T(8,128)(2,1)S(1)} %subtract_convert_fusion.2.refs_2_), channel_id=1, source_target_pairs={{0,4},{1,5},{2,6},{3,7},{4,0},{5,1},{6,2},{7,3},{8,12},{9,13},{10,... | collective-permute-start | bytes 393224 | tf_op jit(solution)/shard_map/ppermute | solution.py:77
  136.2 7.9 %collective-permute-start.37 = (bf16[256,256]{1,0:T(8,128)(2,1)S(1)}, bf16[256,256]{1,0:T(8,128)(2,1)S(1)}, u32[]{:S(2)}, u32[]{:S(2)}) collective-permute-start(bf16[256,256]{1,0:T(8,128)(2,1)S(1)} %subtract_convert_fusion.2.refs_2_), channel_id=1, source_target_pairs={{0,6},{1,7},{2,0},{3,1},{4,2},{5,3},{6,4},{7,5},{8,14},{9,15},{10,... | collective-permute-start | bytes 393224 | tf_op jit(solution)/shard_map/ppermute | solution.py:77
  137.1 7.6 %collective-permute-start.36 = (bf16[256,256]{1,0:T(8,128)(2,1)S(1)}, bf16[256,256]{1,0:T(8,128)(2,1)S(1)}, u32[]{:S(2)}, u32[]{:S(2)}) collective-permute-start(bf16[256,256]{1,0:T(8,128)(2,1)S(1)} %subtract_convert_fusion.2.refs_2_), channel_id=1, source_target_pairs={{0,8},{1,9},{2,10},{3,11},{4,12},{5,13},{6,14},{7,15},{8,0},{9,1},... | collective-permute-start | bytes 393224 | tf_op jit(solution)/shard_map/ppermute | solution.py:77
  151.4 6.4 %collective-permute-start.44 = (bf16[256,256]{1,0:T(8,128)(2,1)S(1)}, bf16[256,256]{1,0:T(8,128)(2,1)S(1)}, u32[]{:S(2)}, u32[]{:S(2)}) collective-permute-start(bf16[256,256]{1,0:T(8,128)(2,1)S(1)} %get-tuple-element.48), channel_id=1, source_target_pairs={{0,16},{1,17},{2,18},{3,19},{4,20},{5,21},{6,22},{7,23},{8,24},{9,... | collective-permute-start | bytes 393224 | tf_op jit(solution)/shard_map/ppermute | solution.py:77
  152.8 7.4 %collective-permute-start.45 = (bf16[256,256]{1,0:T(8,128)(2,1)S(1)}, bf16[256,256]{1,0:T(8,128)(2,1)S(1)}, u32[]{:S(2)}, u32[]{:S(2)}) collective-permute-start(bf16[256,256]{1,0:T(8,128)(2,1)S(1)} %get-tuple-element.49), channel_id=1, source_target_pairs={{0,17},{1,16},{2,19},{3,18},{4,21},{5,20},{6,23},{7,22},{8,25},{9,... | collective-permute-start | bytes 393224 | tf_op jit(solution)/shard_map/ppermute | solution.py:77
  160.3 10.9 %collective-permute-start.51 = (bf16[256,256]{1,0:T(8,128)(2,1)S(1)}, bf16[256,256]{1,0:T(8,128)(2,1)S(1)}, u32[]{:S(2)}, u32[]{:S(2)}) collective-permute-start(bf16[256,256]{1,0:T(8,128)(2,1)S(1)} %add_convert_fusion.refs_1_), channel_id=1, source_target_pairs={{0,2},{1,3},{2,4},{3,5},{4,6},{5,7},{6,0},{7,1},{8,10},{9,11},{10,... | collective-permute-start | bytes 393224 | tf_op jit(solution)/shard_map/ppermute | solution.py:77
  163.3 10.0 %collective-permute-start.49 = (bf16[256,256]{1,0:T(8,128)(2,1)S(1)}, bf16[256,256]{1,0:T(8,128)(2,1)S(1)}, u32[]{:S(2)}, u32[]{:S(2)}) collective-permute-start(bf16[256,256]{1,0:T(8,128)(2,1)S(1)} %add_convert_fusion.refs_1_), channel_id=1, source_target_pairs={{0,4},{1,5},{2,6},{3,7},{4,0},{5,1},{6,2},{7,3},{8,12},{9,13},{10,... | collective-permute-start | bytes 393224 | tf_op jit(solution)/shard_map/ppermute | solution.py:77
  165.2 8.1 %collective-permute-start.47 = (bf16[256,256]{1,0:T(8,128)(2,1)S(1)}, bf16[256,256]{1,0:T(8,128)(2,1)S(1)}, u32[]{:S(2)}, u32[]{:S(2)}) collective-permute-start(bf16[256,256]{1,0:T(8,128)(2,1)S(1)} %add_convert_fusion.refs_1_), channel_id=1, source_target_pairs={{0,6},{1,7},{2,0},{3,1},{4,2},{5,3},{6,4},{7,5},{8,14},{9,15},{10,... | collective-permute-start | bytes 393224 | tf_op jit(solution)/shard_map/ppermute | solution.py:77
  171.2 8.4 %collective-permute-start.46 = (bf16[256,256]{1,0:T(8,128)(2,1)S(1)}, bf16[256,256]{1,0:T(8,128)(2,1)S(1)}, u32[]{:S(2)}, u32[]{:S(2)}) collective-permute-start(bf16[256,256]{1,0:T(8,128)(2,1)S(1)} %add_convert_fusion.refs_1_), channel_id=1, source_target_pairs={{0,8},{1,9},{2,10},{3,11},{4,12},{5,13},{6,14},{7,15},{8,0},{9,1},... | collective-permute-start | bytes 393224 | tf_op jit(solution)/shard_map/ppermute | solution.py:77
  171.2 9.8 %collective-permute-start.52 = (bf16[256,256]{1,0:T(8,128)(2,1)S(1)}, bf16[256,256]{1,0:T(8,128)(2,1)S(1)}, u32[]{:S(2)}, u32[]{:S(2)}) collective-permute-start(bf16[256,256]{1,0:T(8,128)(2,1)S(1)} %collective-permute-done.51.refs_7_), channel_id=1, source_target_pairs={{0,8},{1,9},{2,10},{3,11},{4,12},{5,13},{6,14},{7,15},{8,0},{9,1},... | collective-permute-start | bytes 393224 | tf_op jit(solution)/shard_map/ppermute | solution.py:77
  173.3 8.9 %collective-permute-start.50 = (bf16[256,256]{1,0:T(8,128)(2,1)S(1)}, bf16[256,256]{1,0:T(8,128)(2,1)S(1)}, u32[]{:S(2)}, u32[]{:S(2)}) collective-permute-start(bf16[256,256]{1,0:T(8,128)(2,1)S(1)} %collective-permute-done.49.refs_5_), channel_id=1, source_target_pairs={{0,8},{1,9},{2,10},{3,11},{4,12},{5,13},{6,14},{7,15},{8,0},{9,1},... | collective-permute-start | bytes 393224 | tf_op jit(solution)/shard_map/ppermute | solution.py:77
  173.4 8.8 %collective-permute-start.48 = (bf16[256,256]{1,0:T(8,128)(2,1)S(1)}, bf16[256,256]{1,0:T(8,128)(2,1)S(1)}, u32[]{:S(2)}, u32[]{:S(2)}) collective-permute-start(bf16[256,256]{1,0:T(8,128)(2,1)S(1)} %collective-permute-done.47.refs_3_), channel_id=1, source_target_pairs={{0,8},{1,9},{2,10},{3,11},{4,12},{5,13},{6,14},{7,15},{8,0},{9,1},... | collective-permute-start | bytes 393224 | tf_op jit(solution)/shard_map/ppermute | solution.py:77
  178.6 10.8 %collective-permute-start.27 = (bf16[384,256]{1,0:T(8,128)(2,1)S(1)}, bf16[384,256]{1,0:T(8,128)(2,1)S(1)}, u32[]{:S(2)}, u32[]{:S(2)}) collective-permute-start(bf16[384,256]{1,0:T(8,128)(2,1)S(1)} %get-tuple-element.38), channel_id=1, source_target_pairs={{0,1},{1,0},{2,3},{3,2},{4,5},{5,4},{6,7},{7,6},{8,9},{9,8},{10,11... | collective-permute-start | bytes 589832 | tf_op jit(solution)/shard_map/ppermute | solution.py:77
  179.6 10.9 %collective-permute-start.28 = (bf16[384,256]{1,0:T(8,128)(2,1)S(1)}, bf16[384,256]{1,0:T(8,128)(2,1)S(1)}, u32[]{:S(2)}, u32[]{:S(2)}) collective-permute-start(bf16[384,256]{1,0:T(8,128)(2,1)S(1)} %get-tuple-element.39), channel_id=1, source_target_pairs={{0,16},{1,17},{2,18},{3,19},{4,20},{5,21},{6,22},{7,23},{8,24},{9,... | collective-permute-start | bytes 589832 | tf_op jit(solution)/shard_map/ppermute | solution.py:77
  180.9 10.8 %collective-permute-start.29 = (bf16[384,256]{1,0:T(8,128)(2,1)S(1)}, bf16[384,256]{1,0:T(8,128)(2,1)S(1)}, u32[]{:S(2)}, u32[]{:S(2)}) collective-permute-start(bf16[384,256]{1,0:T(8,128)(2,1)S(1)} %get-tuple-element.40), channel_id=1, source_target_pairs={{0,17},{1,16},{2,19},{3,18},{4,21},{5,20},{6,23},{7,22},{8,25},{9,... | collective-permute-start | bytes 589832 | tf_op jit(solution)/shard_map/ppermute | solution.py:77
  186.9 9.4 %collective-permute-start.53 = (bf16[384,256]{1,0:T(8,128)(2,1)S(1)}, bf16[384,256]{1,0:T(8,128)(2,1)S(1)}, u32[]{:S(2)}, u32[]{:S(2)}) collective-permute-start(bf16[384,256]{1,0:T(8,128)(2,1)S(1)} %get-tuple-element.51), channel_id=1, source_target_pairs={{0,1},{1,0},{2,3},{3,2},{4,5},{5,4},{6,7},{7,6},{8,9},{9,8},{10,11... | collective-permute-start | bytes 589832 | tf_op jit(solution)/shard_map/ppermute | solution.py:77
  187.9 8.4 %collective-permute-start.54 = (bf16[384,256]{1,0:T(8,128)(2,1)S(1)}, bf16[384,256]{1,0:T(8,128)(2,1)S(1)}, u32[]{:S(2)}, u32[]{:S(2)}) collective-permute-start(bf16[384,256]{1,0:T(8,128)(2,1)S(1)} %get-tuple-element.52), channel_id=1, source_target_pairs={{0,16},{1,17},{2,18},{3,19},{4,20},{5,21},{6,22},{7,23},{8,24},{9,... | collective-permute-start | bytes 589832 | tf_op jit(solution)/shard_map/ppermute | solution.py:77
  189.3 10.0 %collective-permute-start.55 = (bf16[384,256]{1,0:T(8,128)(2,1)S(1)}, bf16[384,256]{1,0:T(8,128)(2,1)S(1)}, u32[]{:S(2)}, u32[]{:S(2)}) collective-permute-start(bf16[384,256]{1,0:T(8,128)(2,1)S(1)} %get-tuple-element.53), channel_id=1, source_target_pairs={{0,17},{1,16},{2,19},{3,18},{4,21},{5,20},{6,23},{7,22},{8,25},{9,... | collective-permute-start | bytes 589832 | tf_op jit(solution)/shard_map/ppermute | solution.py:77
  (15 other events, 117.2 us)

commit v3 on v2

v3 whole, which is shorter than its diff:
```python
import functools
import math

import jax
import jax.numpy as jnp
from jax import lax
from jax.experimental import pallas as pl
from jax.experimental.pallas import tpu as pltpu
from jax.sharding import PartitionSpec as P

SPACING = 0.2
TURNS = 32.0
AXES = ("row", "col")
ROUND = 12582912.0
COS = (
    0.9999992107823218,
    -19.738980355763992,
    64.92865742103312,
    -85.27162153429882,
    58.79049212013072,
    -21.07110562764302,
)
SIN = (
    6.283184916495431,
    -41.34158923268858,
    81.59994332978287,
    -76.61447253124996,
    41.342882354568324,
    -12.471243535026977,
)
PARAMS = pltpu.CompilerParams(vmem_limit_bytes=24 * 2**20)
PEAK = 1.15e15
F32, BF16, I32 = jnp.float32, jnp.bfloat16, jnp.int32


def whole():
    return pl.BlockSpec(memory_space=pltpu.VMEM)


def anywhere():
    return pl.BlockSpec(memory_space=pl.ANY)


def cost(microseconds):
    return pl.CostEstimate(
        flops=int(microseconds * 1e-6 * PEAK), bytes_accessed=0, transcendentals=0
    )


def iota(shape, dim):
    return lax.broadcasted_iota(I32, shape, dim)


def ones_where(mask):
    return jnp.where(mask, jnp.ones((), F32), jnp.zeros((), F32)).astype(BF16)


def matmul(a, b):
    return jnp.dot(a, b, preferred_element_type=F32)


def matmul_nt(a, b):
    return lax.dot_general(a, b, (((1,), (1,)), ((), ())), preferred_element_type=F32)


class Layout:
    def __init__(self, n_row, n_col):
        self.core = 2 if n_row % 2 == 0 else 1
        self.x = n_row // self.core
        self.y = math.gcd(n_col, self.x)
        self.z = n_col // self.y
        self.devices = n_row * n_col
        self.plane = [(dx, dy) for dx in range(self.x) for dy in range(self.y)]

    def digits(self, index):
        y = index % self.y
        z = index // self.y % self.z
        core = index // (self.y * self.z) % self.core
        return index // (self.y * self.z * self.core), core, z, y

    def shift(self, value, dx=0, dc=0, dz=0, dy=0):
        pairs = []
        for i in range(self.devices):
            x, c, z, y = self.digits(i)
            x, c = (x + dx) % self.x, (c + dc) % self.core
            z, y = (z + dz) % self.z, (y + dy) % self.y
            pairs.append((i, ((x * self.core + c) * self.z + z) * self.y + y))
        return lax.ppermute(value, AXES, pairs)

    def line(self, value):
        along = [value] + [self.shift(value, dz=-dz) for dz in range(1, self.z)]
        pieces = []
        for piece in along:
            pieces.append(piece)
            pieces += [self.shift(piece, dc=-dc) for dc in range(1, self.core)]
        return pieces

    def across(self, value):
        return [value] + [self.shift(value, dx=-dx, dy=-dy) for dx, dy in self.plane[1:]]

    def give(self, blocks):
        return [
            self.shift(block, dx=dx, dy=dy)
            for block, (dx, dy) in zip(blocks, self.plane[1:])
        ]

    def place(self, triangle, tri_dev, me):
        x, core, z, y = self.digits(triangle // tri_dev)
        mx, mcore, mz, my = self.digits(me)
        block = (z - mz) % self.z * self.core + (core - mcore) % self.core
        inside = (x == mx) & (y == my)
        return jnp.where(inside, block * tri_dev + triangle % tri_dev, -1)


def tie_kernel(*refs):
    del refs


def tie(value, *others):
    return pl.pallas_call(
        tie_kernel,
        in_specs=[anywhere()] * (1 + len(others)),
        out_specs=anywhere(),
        out_shape=jax.ShapeDtypeStruct(value.shape, value.dtype),
        input_output_aliases={0: 0},
    )(value, *others)


def route_kernel(slots, inc_ref, points_ref, cur_ref, out_ref, label_ref, number_ref):
    edges, tri_dev = inc_ref.shape[1], points_ref.shape[1]
    ends, cells = 2 * edges, out_ref.shape[0]
    devices = cells // slots
    chunk = min(256, cells)
    number_ref[...] = jnp.zeros(number_ref.shape, I32)
    number_ref[0:2, :edges] = inc_ref[...]
    number_ref[2:5, :tri_dev] = points_ref[...]
    plus, minus = inc_ref[0:1, :], inc_ref[1:2, :]
    tri = jnp.concatenate([plus, minus], axis=1)
    other = jnp.concatenate([minus, plus], axis=1)
    owner = tri // tri_dev
    hits = iota((devices, ends), 0) == owner
    upper = ones_where(iota((ends, ends), 0) <= iota((ends, ends), 1))
    count = matmul(ones_where(hits), upper)
    rank = jnp.sum(jnp.where(hits, count, 0.0), axis=0, keepdims=True).astype(I32) - 1
    slot = owner * slots + rank
    order = ones_where(iota((slots, ends), 0) == rank)
    label = jnp.zeros((devices, slots), I32)
    for digit, weight in ((tri % tri_dev + 1, 1), (other & 255, 2 * tri_dev), (other >> 8, 512 * tri_dev)):
        spread = jnp.where(hits, digit.astype(F32), 0.0).astype(BF16)
        label = label + matmul_nt(spread, order).astype(I32) * weight
    label_ref[...] = label
    for base in range(0, cells, chunk):
        mask = jnp.where(iota((chunk, ends), 0) + base == slot, 1.0, 0.0).astype(F32)
        signed = (mask[:, :edges] - mask[:, edges:]).astype(BF16)
        out_ref[base : base + chunk, :] = matmul(signed, cur_ref[...]).astype(BF16)


def route(incidence, centroids, currents, slots, devices):
    edges, width = currents.shape
    lanes = max(edges, centroids.shape[1])
    return pl.pallas_call(
        functools.partial(route_kernel, slots),
        in_specs=[whole()] * 3,
        out_specs=[whole()] * 3,
        out_shape=[
            jax.ShapeDtypeStruct((devices * slots, width), BF16),
            jax.ShapeDtypeStruct((devices, slots), I32),
            jax.ShapeDtypeStruct((8, lanes), I32),
        ],
        compiler_params=PARAMS,
        cost_estimate=cost(3),
    )(incidence, centroids, currents)


def features(points, scale, first):
    rows, count = points.shape
    square = jnp.sum(points * points, axis=0, keepdims=True)
    norms = [square & 255, square & 0xFF00, square & 0xFF0000]
    ones = [jnp.ones_like(square)] * 3
    zeros = [jnp.zeros((16 - rows - 7, count), I32)]
    if first:
        parts = [-2 * points] + norms + ones + [ones[0]] + zeros
    else:
        parts = [points] + ones + norms + [ones[0]] + zeros
    return (jnp.concatenate(parts, axis=0).astype(F32) * scale).astype(BF16)


def poly(coefs, scale, u):
    value = jnp.full_like(u, coefs[-1] * scale)
    for coef in coefs[-2::-1]:
        value = value * u + coef * scale
    return value


def tile_kernel(count, block, tri_dev, *refs):
    plane, line = refs[:count], refs[count:-4]
    real_ref, imag_ref, row_ref, col_ref = refs[-4:]

    @pl.when(pl.program_id(0) == 0)
    def _():
        for k, ref in enumerate(plane):
            row_ref[k] = features(ref[2:5, :tri_dev], 1.0 / (TURNS * TURNS), True)
        for k, ref in enumerate(line):
            col_ref[:, k * tri_dev : (k + 1) * tri_dev] = features(ref[2:5, :tri_dev], 1.0, False)

    row = row_ref[pl.program_id(0)]
    for base in range(0, col_ref.shape[1], block):
        cols = slice(base, base + block)
        square = lax.dot_general(
            row, col_ref[:, cols], (((0,), (0,)), ((), ())), preferred_element_type=F32
        )
        inverse = lax.rsqrt(square)
        turns = square * inverse
        frac = turns - ((turns + ROUND) - ROUND)
        u = frac * frac
        real_ref[:, cols] = (poly(COS, SPACING / TURNS, u) * inverse).astype(BF16)
        imag_ref[:, cols] = (poly(SIN, -SPACING / TURNS, u) * (frac * inverse)).astype(BF16)


def build_tiles(plane, line, tri_dev):
    count, cols = len(plane), len(line) * tri_dev
    shape = plane[0].shape
    return pl.pallas_call(
        functools.partial(tile_kernel, count, min(512, cols), tri_dev),
        grid=(count,),
        in_specs=[pl.BlockSpec(shape, lambda i: (0, 0))] * (count + len(line)),
        out_specs=[pl.BlockSpec((tri_dev, cols), lambda i: (i, 0))] * 2,
        out_shape=[jax.ShapeDtypeStruct((count * tri_dev, cols), BF16)] * 2,
        scratch_shapes=[pltpu.VMEM((count, 16, tri_dev), BF16), pltpu.VMEM((16, cols), BF16)],
        compiler_params=PARAMS,
        cost_estimate=cost(12),
    )(*plane, *line)


def pick(row, base, count):
    low = jnp.where((row >= base) & (row < base + count), row - base, -1)
    wanted = iota((count, row.shape[1]), 0).astype(F32).astype(BF16)
    same = wanted == low.astype(F32).astype(BF16)
    return jnp.where(same, jnp.ones((), BF16), jnp.zeros((), BF16))


def adjacency_kernel(layout, tri_dev, me_ref, *refs):
    labels, out_ref = refs[:-1], refs[-1]
    rows, cols = out_ref.shape
    for k, label_ref in enumerate(labels):

        @pl.when(pl.program_id(0) == k)
        def _(label_ref=label_ref):
            label = label_ref[...]
            mark = label % (2 * tri_dev) - 1
            place = layout.place(label // (2 * tri_dev), tri_dev, me_ref[0])
            place = jnp.where(mark >= 0, place, -1)
            low = pick(jnp.where(place >= 0, place % rows, -1), 0, rows)
            for base in range(0, cols, rows):
                inside = (place >= base) & (place < base + rows)
                here = pick(jnp.where(inside, mark, -1), 0, rows)
                out_ref[:, base : base + rows] = matmul_nt(here, low).astype(BF16)


def build_adjacency(layout, me, labels, rows, cols):
    count, shape = len(labels), labels[0].shape
    return pl.pallas_call(
        functools.partial(adjacency_kernel, layout, rows),
        grid=(count,),
        in_specs=[pl.BlockSpec(memory_space=pltpu.SMEM)]
        + [pl.BlockSpec(shape, lambda j: (0, 0))] * count,
        out_specs=pl.BlockSpec((rows, cols), lambda j: (j, 0)),
        out_shape=jax.ShapeDtypeStruct((count * rows, cols), BF16),
        compiler_params=PARAMS,
        cost_estimate=cost(10),
    )(me, *labels)


def incidence_kernel(layout, tri_dev, me_ref, *refs):
    numbers, out_ref = refs[:-1], refs[-1]
    edges, cols = out_ref.shape
    for k, number_ref in enumerate(numbers):

        @pl.when(pl.program_id(0) == k)
        def _(number_ref=number_ref):
            places = layout.place(number_ref[0:2, :edges], tri_dev, me_ref[0])
            plus, minus = places[0:1], places[1:2]
            eye = ones_where(iota((edges, edges), 0) == iota((edges, edges), 1))
            for base in range(0, cols, tri_dev):
                signed = pick(plus, base, tri_dev) - pick(minus, base, tri_dev)
                out_ref[:, base : base + tri_dev] = matmul_nt(eye, signed).astype(BF16)


def build_incidence(layout, me, numbers, edges, tri_dev, cols):
    count, shape = len(numbers), numbers[0].shape
    return pl.pallas_call(
        functools.partial(incidence_kernel, layout, tri_dev),
        grid=(count,),
        in_specs=[pl.BlockSpec(memory_space=pltpu.SMEM)]
        + [pl.BlockSpec(shape, lambda j: (0, 0))] * count,
        out_specs=pl.BlockSpec((edges, cols), lambda j: (j, 0)),
        out_shape=jax.ShapeDtypeStruct((count * edges, cols), BF16),
        compiler_params=PARAMS,
        cost_estimate=cost(6),
    )(me, *numbers)


def collect_kernel(tri_dev, label_ref, value_ref, *refs):
    charge_ref, rounded_ref, degree_ref = refs[-3:]
    here = pick(label_ref[...] % (2 * tri_dev) - 1, 0, tri_dev)
    charge = matmul(here, value_ref[...])
    charge_ref[...] = charge
    rounded_ref[...] = charge.astype(BF16)
    degree_ref[...] = matmul(here, jnp.ones((here.shape[1], degree_ref.shape[1]), BF16))


def collect(labels, values, tri_dev, after):
    width = values.shape[1]
    return pl.pallas_call(
        functools.partial(collect_kernel, tri_dev),
        in_specs=[whole()] * 2 + [anywhere()] * len(after),
        out_specs=[whole()] * 3,
        out_shape=[
            jax.ShapeDtypeStruct((tri_dev, width), F32),
            jax.ShapeDtypeStruct((tri_dev, width), BF16),
            jax.ShapeDtypeStruct((tri_dev, 128), F32),
        ],
        compiler_params=PARAMS,
        cost_estimate=cost(1),
    )(labels, values, *after)


def apply_kernel(mats, fed, count, *refs):
    matrices, pieces, outs = refs[:mats], refs[mats : mats + fed], refs[-count:]
    block = pieces[0].shape[0]
    half = pieces[0].shape[1] // 2
    sums = []
    for matrix in matrices:
        total = None
        for k, piece in enumerate(pieces):
            term = matmul(matrix[:, k * block : (k + 1) * block], piece[...])
            total = term if total is None else total + term
        sums.append(total)
    value = sums[0]
    if mats == 2:
        real, imag = sums
        value = jnp.concatenate(
            [real[:, :half] - imag[:, half:], real[:, half:] + imag[:, :half]], axis=1
        )
    for k, out in enumerate(outs):

        @pl.when(pl.program_id(0) == k)
        def _(out=out):
            out[...] = value.astype(out.dtype)


def apply(matrices, pieces, count, after=()):
    rows, cols = matrices[0].shape
    block = rows // count
    size, width = pieces[0].shape
    return pl.pallas_call(
        functools.partial(apply_kernel, len(matrices), len(pieces), count),
        grid=(count,),
        in_specs=[pl.BlockSpec((block, cols), lambda j: (j, 0))] * len(matrices)
        + [pl.BlockSpec((size, width), lambda j: (0, 0))] * len(pieces)
        + [anywhere()] * len(after),
        out_specs=[pl.BlockSpec((block, width), lambda j: (0, 0))] * count,
        out_shape=[
            jax.ShapeDtypeStruct((block, width), F32 if k == 0 else BF16) for k in range(count)
        ],
        compiler_params=PARAMS,
        cost_estimate=cost(2 * len(matrices)),
    )(*matrices, *pieces, *after)


def total_of(layout, blocks):
    total = blocks[0]
    for part in layout.give(blocks[1:]):
        total = total + part.astype(F32)
    return total


def per_device(currents, incidence, centroids, sweep_weights):
    layout = Layout(lax.axis_size("row"), lax.axis_size("col"))
    devices = layout.devices
    me = lax.axis_index(AXES)
    tri_dev = centroids.shape[1]
    edge_dev, width = currents.shape
    slots = 8 * tri_dev // devices
    cells = devices * slots
    sweeps = sweep_weights.shape[0]
    count = len(layout.plane)
    cols = layout.z * layout.core * tri_dev

    outgoing, labels, numbers = route(incidence, centroids, currents, slots, devices)
    plane = layout.across(numbers)
    line = layout.line(numbers)
    labels = lax.all_to_all(labels, AXES, split_axis=0, concat_axis=0, tiled=True)
    labels = labels.reshape(1, cells)
    outgoing = tie(outgoing, labels, *plane[1:], *line[1:])
    arrived = lax.all_to_all(
        outgoing.reshape(devices, slots, width), AXES, split_axis=0, concat_axis=0, tiled=True
    ).reshape(cells, width)
    where = me.astype(I32).reshape(1)
    tiles = build_tiles(plane, line, tri_dev)
    slopes_of = build_incidence(layout, where, plane, edge_dev, tri_dev, cols)
    neighbours = build_adjacency(layout, where, layout.across(labels), tri_dev, cols)

    charge, rounded, degree = collect(
        labels, arrived, tri_dev, (*tiles, slopes_of, neighbours)
    )
    current = currents
    potential = None
    slopes = ()
    for sweep in range(sweeps):
        pieces = layout.line(rounded)
        blocks = apply(tiles, pieces, count, slopes)
        if sweep > 0:
            change = sweep_weights[sweep - 1] * total_of(layout, slopes)
            current = (current.astype(F32) - change).astype(BF16)
        potential = total_of(layout, blocks).astype(BF16)
        pieces = layout.line(potential)
        if sweep + 1 < sweeps:
            around = total_of(layout, apply([neighbours], pieces, count))
            change = degree[:, :1] * potential.astype(F32) - around
            charge = charge - sweep_weights[sweep] * change
            rounded = charge.astype(BF16)
        slopes = apply([slopes_of], pieces, count)
    change = sweep_weights[sweeps - 1] * total_of(layout, slopes)
    return (current.astype(F32) - change).astype(BF16), potential


def solution(mesh):
    in_specs = (P(AXES, None), P(None, AXES), P(None, AXES), P())
    out_specs = (P(AXES, None), P(AXES, None))
    return jax.shard_map(
        per_device, mesh=mesh, in_specs=in_specs, out_specs=out_specs, check_vma=False
    )
```

time: 202 us -> 195 us (0.965)
  local copies, waits for them, and re-layouts: 6.72 us -> 23.7 us
  blocking collectives: 14.2 us -> 0 us
  Pallas kernels: 53 us -> 39.3 us
  starting transfers between devices: 56.7 us -> 60.2 us
  other arithmetic: 5.94 us -> 3.71 us
    unnamed x23 -> x80, local copies, waits for them, and re-layouts: 2.38 us -> 21.8 us
    all_to_all x1 -> x0, blocking collectives: 14.2 us -> none  [per_device(): lax.all_to_all(labels.reshape(devices, slots), AXES, split_axis=0, concat...]
    pallas_call x10 -> x11, Pallas kernels: 53 us -> 39.3 us  [the longest x5 12.7 us: apply(): pl.pallas_call(functools.partial(apply_kernel, len(matrices), len(pieces)...]
    all_to_all x0 -> x1, waiting for transfers between devices: none -> 3.2 us  [per_device(): lax.all_to_all(labels, AXES, split_axis=0, concat_axis=0, tiled=True)]
    all_to_all x0 -> x1, starting transfers between devices: none -> 2.92 us  [per_device(): lax.all_to_all(labels, AXES, split_axis=0, concat_axis=0, tiled=True)]
    ppermute x56, waiting for transfers between devices: 64 us -> 61.1 us  [shift(): return lax.ppermute(value, AXES, pairs)]
  transfers between devices with their start and end apart: 57 -> 58, of which waited for: 22 -> 28; matrix products, arithmetic and copies ran while one was open for 3% -> 1% of each run, Pallas kernels for 19% -> 15%
where the time goes in v3:
time: 195 us; the launch traced here: 194 us
  waiting for transfers between devices  66 us (34%)
  starting transfers between devices  60.2 us (31%)
  Pallas kernels  39.3 us (20%)
  local copies, waits for them, and re-layouts  23.7 us (12%)
  other arithmetic  3.71 us (2%)
    ppermute x56, waiting for transfers between devices, shift(): return lax.ppermute(value, AXES, pairs)  61.1 us
    ppermute x56, starting transfers between devices, shift(): return lax.ppermute(value, AXES, pairs)  54.4 us
    unnamed x80, local copies, waits for them, and re-layouts  21.8 us
    pallas_call x5, Pallas kernels, apply(): pl.pallas_call(functools.partial(apply_kernel, len(matrices), len(pieces)...  12.7 us
    pallas_call x1, Pallas kernels, build_adjacency(): pl.pallas_call(functools.partial(adjacency_kernel, layout, rows), grid=(c...  10.5 us
    pallas_call x1, Pallas kernels, build_tiles(): pl.pallas_call(functools.partial(tile_kernel, count, min(512, cols), tri_...  9.09 us
    pallas_call x1, Pallas kernels, build_incidence(): pl.pallas_call(functools.partial(incidence_kernel, layout, tri_dev), grid...  4.37 us
  transfers between devices with their start and end apart: 58, of which 28 were waited for; matrix products, arithmetic and copies ran while one was open for 1% of the time, Pallas kernels for 15%

profile of v3, /device:TPU:0, one launch (start us, length us, event | category | flops | bytes accessed | tf_op | source)
XLA Modules:
  0.0 194.2 jit_solution(6253268460417818731)
XLA Ops:
  5.1 3.0 %collective-permute-start.8 = (s32[8,384]{1,0:T(8,128)S(1)}, s32[8,384]{1,0:T(8,128)S(1)}, u32[]{:S(2)}, u32[]{:S(2)}) collective-permute-start(s32[8,384]{1,0:T(8,128)S(1)} %get-tuple-element.30.refs_0_.refs_4_), channel_id=1, source_target_pairs={{0,2},{1,3},{2,4},{3,5},{4,6},{5,7},{6,0},{7,1},{8,10},{9,11},{10,... | collective-permute-start | bytes 36872 | tf_op jit(solution)/shard_map/ppermute | solution.py:88
  8.2 2.6 %collective-permute-start.6 = (s32[8,384]{1,0:T(8,128)S(1)}, s32[8,384]{1,0:T(8,128)S(1)}, u32[]{:S(2)}, u32[]{:S(2)}) collective-permute-start(s32[8,384]{1,0:T(8,128)S(1)} %get-tuple-element.30.refs_0_.refs_4_), channel_id=1, source_target_pairs={{0,4},{1,5},{2,6},{3,7},{4,0},{5,1},{6,2},{7,3},{8,12},{9,13},{10,... | collective-permute-start | bytes 36872 | tf_op jit(solution)/shard_map/ppermute | solution.py:88
  12.1 2.9 %all-to-all-start = ((s32[32,1,64]{2,1,0:T(1,128)}), s32[32,1,64]{2,1,0:T(1,128)S(1)}, u32[]{:S(2)}, u32[]{:S(2)}) async-start(s32[32,1,64]{2,1,0:T(1,128)} %bitcast.3), calls=%async_computation | async-start | bytes 32768 | tf_op jit(solution)/shard_map/all_to_all | solution.py:393
  15.4 2.6 %collective-permute-start.2 = (s32[8,384]{1,0:T(8,128)S(1)}, s32[8,384]{1,0:T(8,128)S(1)}, u32[]{:S(2)}, u32[]{:S(2)}) collective-permute-start(s32[8,384]{1,0:T(8,128)S(1)} %get-tuple-element.30.refs_0_.refs_4_), channel_id=1, source_target_pairs={{0,17},{1,16},{2,19},{3,18},{4,21},{5,20},{6,23},{7,22},{8,25},{9,... | collective-permute-start | bytes 36872 | tf_op jit(solution)/shard_map/ppermute | solution.py:88
  18.9 3.2 %all-to-all-done = s32[32,1,64]{2,1,0:T(1,128)S(1)} async-done(((s32[32,1,64]{2,1,0:T(1,128)}), s32[32,1,64]{2,1,0:T(1,128)S(1)}, u32[]{:S(2)}, u32[]{:S(2)}) %all-to-all-start) | async-done | bytes 8224 | tf_op jit(solution)/shard_map/all_to_all | solution.py:393
  28.0 4.4 %shard_map.60.refs_2_.refs_0_ = bf16[1536,2048]{1,0:T(8,128)(2,1)S(1)} custom-call(s32[1]{0:T(128)} %bitcast.1.me_ref, s32[8,384]{1,0:T(8,128)S(1)} %get-tuple-element.30.refs_0_.refs_4_, s32[8,384]{1,0:T(8,128)S(1)} %collective-permute-done.refs_1_.refs_2_, s32[8,384]{1,0:T(8,128)S(1)} %collective-permute-done.1.refs_2_.refs_3_, ...), custom_call_target="tpu_custom_call" | custom-call | flops 6899999744 | tf_op jit(solution)/shard_map/pallas_call | solution.py:291
  32.4 2.6 %copy-done = bf16[1536,2048]{1,0:T(8,128)(2,1)} copy-done((bf16[1536,2048]{1,0:T(8,128)(2,1)}, bf16[1536,2048]{1,0:T(8,128)(2,1)S(1)}, u32[]{:S(2)}) %copy-start) | copy-done | bytes 6291480
  35.6 2.8 %all-to-all-start.1 = ((bf16[32,64,256]{2,1,0:T(8,128)(2,1)}), bf16[32,64,256]{2,1,0:T(8,128)(2,1)S(1)}, u32[]{:S(2)}, u32[]{:S(2)}) async-start(bf16[32,64,256]{2,1,0:T(8,128)(2,1)} %bitcast.11), calls=%async_computation.1 | async-start | bytes 2097152 | tf_op jit(solution)/shard_map/all_to_all | solution.py:396
  38.6 10.5 %shard_map.63.refs_3_.refs_0_ = bf16[1024,2048]{1,0:T(8,128)(2,1)S(1)} custom-call(s32[1]{0:T(128)} %bitcast.1.me_ref, s32[1,2048]{1,0:T(1,128)} %reshape.20.refs_1_.refs_0_.label_ref, s32[1,2048]{1,0:T(1,128)S(1)} %collective-permute-done.10.refs_1_, s32[1,2048]{1,0:T(1,128)S(1)} %collective-permute-done.11.refs_2_, ...), custom_call_target="tpu_custom_call" | custom-call | flops 11500000256 | tf_op jit(solution)/shard_map/pallas_call | solution.py:262
  49.1 2.0 %copy-done.9 = bf16[1024,2048]{1,0:T(8,128)(2,1)} copy-done((bf16[1024,2048]{1,0:T(8,128)(2,1)}, bf16[1024,2048]{1,0:T(8,128)(2,1)S(1)}, u32[]{:S(2)}) %copy-start.9) | copy-done | bytes 4194328
  51.2 9.1 %shard_map.61 = (bf16[1024,2048]{1,0:T(8,128)(2,1)S(1)}, bf16[1024,2048]{1,0:T(8,128)(2,1)S(1)}) custom-call(s32[8,384]{1,0:T(8,128)S(1)} %get-tuple-element.30.refs_0_.refs_4_, s32[8,384]{1,0:T(8,128)S(1)} %copy-done.28, s32[8,384]{1,0:T(8,128)S(1)} %copy-done.26, s32[8,384]{1,0:T(8,128)S(1)} %copy-done.24, s32[8,384]{1,0:T(8,128)S(1)} %get-tuple-element.30.refs_0_.refs_4_, ...), custom_call_target="tpu_custom_call" | custom-call | flops 13799999488 | tf_op jit(solution)/shard_map/pallas_call | solution.py:223
  60.3 1.9 %copy-done.3 = bf16[1024,2048]{1,0:T(8,128)(2,1)} copy-done((bf16[1024,2048]{1,0:T(8,128)(2,1)}, bf16[1024,2048]{1,0:T(8,128)(2,1)S(1)}, u32[]{:S(2)}) %copy-start.3) | copy-done | bytes 4194328
  62.2 1.9 %copy-done.6 = bf16[1024,2048]{1,0:T(8,128)(2,1)} copy-done((bf16[1024,2048]{1,0:T(8,128)(2,1)}, bf16[1024,2048]{1,0:T(8,128)(2,1)S(1)}, u32[]{:S(2)}) %copy-start.6) | copy-done | bytes 4194328
  64.2 1.7 all-to-all-done.1
  65.9 2.8 %copy-done.1 = bf16[1536,2048]{1,0:T(8,128)(2,1)S(1)} copy-done((bf16[1536,2048]{1,0:T(8,128)(2,1)S(1)}, bf16[1536,2048]{1,0:T(8,128)(2,1)}, u32[]{:S(2)}) %copy-start.1) | copy-done | bytes 6291480
  68.7 2.2 %copy-done.4 = bf16[1024,2048]{1,0:T(8,128)(2,1)S(1)} copy-done((bf16[1024,2048]{1,0:T(8,128)(2,1)S(1)}, bf16[1024,2048]{1,0:T(8,128)(2,1)}, u32[]{:S(2)}) %copy-start.4) | copy-done | bytes 4194328
  70.8 2.2 %copy-done.7 = bf16[1024,2048]{1,0:T(8,128)(2,1)S(1)} copy-done((bf16[1024,2048]{1,0:T(8,128)(2,1)S(1)}, bf16[1024,2048]{1,0:T(8,128)(2,1)}, u32[]{:S(2)}) %copy-start.7) | copy-done | bytes 4194328
  73.0 2.2 %copy-done.10 = bf16[1024,2048]{1,0:T(8,128)(2,1)S(1)} copy-done((bf16[1024,2048]{1,0:T(8,128)(2,1)S(1)}, bf16[1024,2048]{1,0:T(8,128)(2,1)}, u32[]{:S(2)}) %copy-start.10) | copy-done | bytes 4194328
  77.0 2.2 %collective-permute-start.16 = (bf16[256,256]{1,0:T(8,128)(2,1)S(1)}, bf16[256,256]{1,0:T(8,128)(2,1)S(1)}, u32[]{:S(2)}, u32[]{:S(2)}) collective-permute-start(bf16[256,256]{1,0:T(8,128)(2,1)S(1)} %get-tuple-element.35.refs_2_), channel_id=1, source_target_pairs={{0,4},{1,5},{2,6},{3,7},{4,0},{5,1},{6,2},{7,3},{8,12},{9,13},{10,... | collective-permute-start | bytes 393224 | tf_op jit(solution)/shard_map/ppermute | solution.py:88
  80.7 4.4 %collective-permute-done.18.refs_8_ = bf16[256,256]{1,0:T(8,128)(2,1)S(1)} collective-permute-done((bf16[256,256]{1,0:T(8,128)(2,1)S(1)}, bf16[256,256]{1,0:T(8,128)(2,1)S(1)}, u32[]{:S(2)}, u32[]{:S(2)}) %collective-permute-start.18) | collective-permute-done | bytes 131104 | tf_op jit(solution)/shard_map/ppermute | solution.py:88
  85.1 4.3 %collective-permute-done.16.refs_6_ = bf16[256,256]{1,0:T(8,128)(2,1)S(1)} collective-permute-done((bf16[256,256]{1,0:T(8,128)(2,1)S(1)}, bf16[256,256]{1,0:T(8,128)(2,1)S(1)}, u32[]{:S(2)}, u32[]{:S(2)}) %collective-permute-start.16) | collective-permute-done | bytes 131104 | tf_op jit(solution)/shard_map/ppermute | solution.py:88
  91.0 3.0 %shard_map.65 = (f32[256,256]{1,0:T(8,128)S(1)}, bf16[256,256]{1,0:T(8,128)(2,1)S(1)}, bf16[256,256]{1,0:T(8,128)(2,1)S(1)}, bf16[256,256]{1,0:T(8,128)(2,1)S(1)}) custom-call(bf16[1024,2048]{1,0:T(8,128)(2,1)S(1)} %copy-done.5, bf16[1024,2048]{1,0:T(8,128)(2,1)S(1)} %copy-done.7, bf16[256,256]{1,0:T(8,128)(2,1)S(1)} %get-tuple-element.35.refs_2_, ...), custom_call_target="tpu_custom_call" | custom-call | flops 4600000000 | tf_op jit(solution)/shard_map/pallas_call | solution.py:356
  95.8 1.7 collective-permute-start.22
  97.5 2.2 %collective-permute-done.20 = bf16[256,256]{1,0:T(8,128)(2,1)S(1)} collective-permute-done((bf16[256,256]{1,0:T(8,128)(2,1)S(1)}, bf16[256,256]{1,0:T(8,128)(2,1)S(1)}, u32[]{:S(2)}, u32[]{:S(2)}) %collective-permute-start.20) | collective-permute-done | bytes 131104 | tf_op jit(solution)/shard_map/ppermute | solution.py:88
  99.7 1.8 collective-permute-done.21
  101.5 2.2 %collective-permute-done.22 = bf16[256,256]{1,0:T(8,128)(2,1)S(1)} collective-permute-done((bf16[256,256]{1,0:T(8,128)(2,1)S(1)}, bf16[256,256]{1,0:T(8,128)(2,1)S(1)}, u32[]{:S(2)}, u32[]{:S(2)}) %collective-permute-start.22) | collective-permute-done | bytes 131104 | tf_op jit(solution)/shard_map/ppermute | solution.py:88
  103.8 2.7 %collective-permute-start.28 = (bf16[256,256]{1,0:T(8,128)(2,1)S(1)}, bf16[256,256]{1,0:T(8,128)(2,1)S(1)}, u32[]{:S(2)}, u32[]{:S(2)}) collective-permute-start(bf16[256,256]{1,0:T(8,128)(2,1)S(1)} %add_convert_fusion.1.refs_1_), channel_id=1, source_target_pairs={{0,2},{1,3},{2,4},{3,5},{4,6},{5,7},{6,0},{7,1},{8,10},{9,11},{10,... | collective-permute-start | bytes 393224 | tf_op jit(solution)/shard_map/ppermute | solution.py:88
  108.9 3.3 %collective-permute-done.28.refs_7_ = bf16[256,256]{1,0:T(8,128)(2,1)S(1)} collective-permute-done((bf16[256,256]{1,0:T(8,128)(2,1)S(1)}, bf16[256,256]{1,0:T(8,128)(2,1)S(1)}, u32[]{:S(2)}, u32[]{:S(2)}) %collective-permute-start.28) | collective-permute-done | bytes 131104 | tf_op jit(solution)/shard_map/ppermute | solution.py:88
  112.2 3.8 %collective-permute-done.26.refs_5_ = bf16[256,256]{1,0:T(8,128)(2,1)S(1)} collective-permute-done((bf16[256,256]{1,0:T(8,128)(2,1)S(1)}, bf16[256,256]{1,0:T(8,128)(2,1)S(1)}, u32[]{:S(2)}, u32[]{:S(2)}) %collective-permute-start.26) | collective-permute-done | bytes 131104 | tf_op jit(solution)/shard_map/ppermute | solution.py:88
  117.5 1.9 shard_map.67
  125.1 1.8 collective-permute-done.34
  127.0 2.2 %collective-permute-done.35 = bf16[256,256]{1,0:T(8,128)(2,1)S(1)} collective-permute-done((bf16[256,256]{1,0:T(8,128)(2,1)S(1)}, bf16[256,256]{1,0:T(8,128)(2,1)S(1)}, u32[]{:S(2)}, u32[]{:S(2)}) %collective-permute-start.35) | collective-permute-done | bytes 131104 | tf_op jit(solution)/shard_map/ppermute | solution.py:88
  129.9 3.0 %collective-permute-start.41 = (bf16[256,256]{1,0:T(8,128)(2,1)S(1)}, bf16[256,256]{1,0:T(8,128)(2,1)S(1)}, u32[]{:S(2)}, u32[]{:S(2)}) collective-permute-start(bf16[256,256]{1,0:T(8,128)(2,1)S(1)} %subtract_convert_fusion.2.refs_2_), channel_id=1, source_target_pairs={{0,2},{1,3},{2,4},{3,5},{4,6},{5,7},{6,0},{7,1},{8,10},{9,11},{10,... | collective-permute-start | bytes 393224 | tf_op jit(solution)/shard_map/ppermute | solution.py:88
  135.3 3.1 %collective-permute-done.41.refs_8_ = bf16[256,256]{1,0:T(8,128)(2,1)S(1)} collective-permute-done((bf16[256,256]{1,0:T(8,128)(2,1)S(1)}, bf16[256,256]{1,0:T(8,128)(2,1)S(1)}, u32[]{:S(2)}, u32[]{:S(2)}) %collective-permute-start.41) | collective-permute-done | bytes 131104 | tf_op jit(solution)/shard_map/ppermute | solution.py:88
  138.4 4.1 %collective-permute-done.39.refs_6_ = bf16[256,256]{1,0:T(8,128)(2,1)S(1)} collective-permute-done((bf16[256,256]{1,0:T(8,128)(2,1)S(1)}, bf16[256,256]{1,0:T(8,128)(2,1)S(1)}, u32[]{:S(2)}, u32[]{:S(2)}) %collective-permute-start.39) | collective-permute-done | bytes 131104 | tf_op jit(solution)/shard_map/ppermute | solution.py:88
  143.0 2.4 %shard_map.66 = (f32[384,256]{1,0:T(8,128)S(1)}, bf16[384,256]{1,0:T(8,128)(2,1)S(1)}, bf16[384,256]{1,0:T(8,128)(2,1)S(1)}, bf16[384,256]{1,0:T(8,128)(2,1)S(1)}) custom-call(bf16[1536,2048]{1,0:T(8,128)(2,1)S(1)} %bitcast.9, bf16[256,256]{1,0:T(8,128)(2,1)S(1)} %add_convert_fusion.1.refs_1_, bf16[256,256]{1,0:T(8,128)(2,1)S(1)} %collective-permute-done.23.refs_2_, ...), custom_call_target="tpu_custom_call" | custom-call | flops 2300000000 | tf_op jit(solution)/shard_map/pallas_call | solution.py:356
  145.5 3.0 %shard_map.68 = (f32[256,256]{1,0:T(8,128)S(1)}, bf16[256,256]{1,0:T(8,128)(2,1)S(1)}, bf16[256,256]{1,0:T(8,128)(2,1)S(1)}, bf16[256,256]{1,0:T(8,128)(2,1)S(1)}) custom-call(bf16[1024,2048]{1,0:T(8,128)(2,1)S(1)} %copy-done.5, bf16[1024,2048]{1,0:T(8,128)(2,1)S(1)} %copy-done.8, bf16[256,256]{1,0:T(8,128)(2,1)S(1)} %subtract_convert_fusion.2.refs_2_, ...), custom_call_target="tpu_custom_call" | custom-call | flops 4600000000 | tf_op jit(solution)/shard_map/pallas_call | solution.py:356
  152.0 2.0 %collective-permute-done.43 = bf16[256,256]{1,0:T(8,128)(2,1)S(1)} collective-permute-done((bf16[256,256]{1,0:T(8,128)(2,1)S(1)}, bf16[256,256]{1,0:T(8,128)(2,1)S(1)}, u32[]{:S(2)}, u32[]{:S(2)}) %collective-permute-start.43) | collective-permute-done | bytes 131104 | tf_op jit(solution)/shard_map/ppermute | solution.py:88
  154.1 2.1 %collective-permute-done.44 = bf16[256,256]{1,0:T(8,128)(2,1)S(1)} collective-permute-done((bf16[256,256]{1,0:T(8,128)(2,1)S(1)}, bf16[256,256]{1,0:T(8,128)(2,1)S(1)}, u32[]{:S(2)}, u32[]{:S(2)}) %collective-permute-start.44) | collective-permute-done | bytes 131104 | tf_op jit(solution)/shard_map/ppermute | solution.py:88
  156.1 1.9 collective-permute-done.45
  158.1 3.2 %collective-permute-start.51 = (bf16[256,256]{1,0:T(8,128)(2,1)S(1)}, bf16[256,256]{1,0:T(8,128)(2,1)S(1)}, u32[]{:S(2)}, u32[]{:S(2)}) collective-permute-start(bf16[256,256]{1,0:T(8,128)(2,1)S(1)} %add_convert_fusion.refs_1_), channel_id=1, source_target_pairs={{0,2},{1,3},{2,4},{3,5},{4,6},{5,7},{6,0},{7,1},{8,10},{9,11},{10,... | collective-permute-start | bytes 393224 | tf_op jit(solution)/shard_map/ppermute | solution.py:88
  163.8 2.7 %collective-permute-done.51.refs_7_ = bf16[256,256]{1,0:T(8,128)(2,1)S(1)} collective-permute-done((bf16[256,256]{1,0:T(8,128)(2,1)S(1)}, bf16[256,256]{1,0:T(8,128)(2,1)S(1)}, u32[]{:S(2)}, u32[]{:S(2)}) %collective-permute-start.51) | collective-permute-done | bytes 131104 | tf_op jit(solution)/shard_map/ppermute | solution.py:88
  166.5 4.3 %collective-permute-done.49.refs_5_ = bf16[256,256]{1,0:T(8,128)(2,1)S(1)} collective-permute-done((bf16[256,256]{1,0:T(8,128)(2,1)S(1)}, bf16[256,256]{1,0:T(8,128)(2,1)S(1)}, u32[]{:S(2)}, u32[]{:S(2)}) %collective-permute-start.49) | collective-permute-done | bytes 131104 | tf_op jit(solution)/shard_map/ppermute | solution.py:88
  174.8 2.4 %shard_map.69 = (f32[384,256]{1,0:T(8,128)S(1)}, bf16[384,256]{1,0:T(8,128)(2,1)S(1)}, bf16[384,256]{1,0:T(8,128)(2,1)S(1)}, bf16[384,256]{1,0:T(8,128)(2,1)S(1)}) custom-call(bf16[1536,2048]{1,0:T(8,128)(2,1)S(1)} %bitcast.9, bf16[256,256]{1,0:T(8,128)(2,1)S(1)} %add_convert_fusion.refs_1_, bf16[256,256]{1,0:T(8,128)(2,1)S(1)} %collective-permute-done.46.refs_2_, ...), custom_call_target="tpu_custom_call" | custom-call | flops 2300000000 | tf_op jit(solution)/shard_map/pallas_call | solution.py:356
  180.8 4.0 %collective-permute-done.32 = bf16[384,256]{1,0:T(8,128)(2,1)S(1)} collective-permute-done((bf16[384,256]{1,0:T(8,128)(2,1)S(1)}, bf16[384,256]{1,0:T(8,128)(2,1)S(1)}, u32[]{:S(2)}, u32[]{:S(2)}) %collective-permute-start.32) | collective-permute-done | bytes 196640 | tf_op jit(solution)/shard_map/ppermute | solution.py:88
  184.8 2.6 %collective-permute-done.53 = bf16[384,256]{1,0:T(8,128)(2,1)S(1)} collective-permute-done((bf16[384,256]{1,0:T(8,128)(2,1)S(1)}, bf16[384,256]{1,0:T(8,128)(2,1)S(1)}, u32[]{:S(2)}, u32[]{:S(2)}) %collective-permute-start.53) | collective-permute-done | bytes 196640 | tf_op jit(solution)/shard_map/ppermute | solution.py:88
  188.8 3.2 %collective-permute-done.55 = bf16[384,256]{1,0:T(8,128)(2,1)S(1)} collective-permute-done((bf16[384,256]{1,0:T(8,128)(2,1)S(1)}, bf16[384,256]{1,0:T(8,128)(2,1)S(1)}, u32[]{:S(2)}, u32[]{:S(2)}) %collective-permute-start.55) | collective-permute-done | bytes 196640 | tf_op jit(solution)/shard_map/ppermute | solution.py:88
  192.0 2.2 %subtract_convert_fusion = bf16[384,256]{1,0:T(8,128)(2,1)} fusion(bf16[384,256]{1,0:T(8,128)(2,1)S(1)} %collective-permute-done.55, bf16[384,256]{1,0:T(8,128)(2,1)S(1)} %collective-permute-done.54, f32[384,256]{1,0:T(8,128)S(1)} %get-tuple-element.54, bf16[384,256]{1,0:T(8,128)(2,1)S(1)} %collective-permute-done.53, ...), kind=kLoop, calls=%fused_computation | loop fusion | flops 1966080 | bytes 2359304 | tf_op jit(solution)/shard_map/convert_element_type | solution.py:425
  (169 shorter events, 48.8 us)
Async XLA Ops:
  5.1 12.8 %collective-permute-start.8 = (s32[8,384]{1,0:T(8,128)S(1)}, s32[8,384]{1,0:T(8,128)S(1)}, u32[]{:S(2)}, u32[]{:S(2)}) collective-permute-start(s32[8,384]{1,0:T(8,128)S(1)} %get-tuple-element.30.refs_0_.refs_4_), channel_id=1, source_target_pairs={{0,2},{1,3},{2,4},{3,5},{4,6},{5,7},{6,0},{7,1},{8,10},{9,11},{10,... | collective-permute-start | bytes 36872 | tf_op jit(solution)/shard_map/ppermute | solution.py:88
  8.2 10.3 %collective-permute-start.6 = (s32[8,384]{1,0:T(8,128)S(1)}, s32[8,384]{1,0:T(8,128)S(1)}, u32[]{:S(2)}, u32[]{:S(2)}) collective-permute-start(s32[8,384]{1,0:T(8,128)S(1)} %get-tuple-element.30.refs_0_.refs_4_), channel_id=1, source_target_pairs={{0,4},{1,5},{2,6},{3,7},{4,0},{5,1},{6,2},{7,3},{8,12},{9,13},{10,... | collective-permute-start | bytes 36872 | tf_op jit(solution)/shard_map/ppermute | solution.py:88
  10.8 8.1 %collective-permute-start.4 = (s32[8,384]{1,0:T(8,128)S(1)}, s32[8,384]{1,0:T(8,128)S(1)}, u32[]{:S(2)}, u32[]{:S(2)}) collective-permute-start(s32[8,384]{1,0:T(8,128)S(1)} %get-tuple-element.30.refs_0_.refs_4_), channel_id=1, source_target_pairs={{0,6},{1,7},{2,0},{3,1},{4,2},{5,3},{6,4},{7,5},{8,14},{9,15},{10,... | collective-permute-start | bytes 36872 | tf_op jit(solution)/shard_map/ppermute | solution.py:88
  12.1 10.0 %all-to-all-start = ((s32[32,1,64]{2,1,0:T(1,128)}), s32[32,1,64]{2,1,0:T(1,128)S(1)}, u32[]{:S(2)}, u32[]{:S(2)}) async-start(s32[32,1,64]{2,1,0:T(1,128)} %bitcast.3), calls=%async_computation | async-start | bytes 32768 | tf_op jit(solution)/shard_map/all_to_all | solution.py:393
  15.0 8.9 %collective-permute-start.3 = (s32[8,384]{1,0:T(8,128)S(1)}, s32[8,384]{1,0:T(8,128)S(1)}, u32[]{:S(2)}, u32[]{:S(2)}) collective-permute-start(s32[8,384]{1,0:T(8,128)S(1)} %get-tuple-element.30.refs_0_.refs_4_), channel_id=1, source_target_pairs={{0,8},{1,9},{2,10},{3,11},{4,12},{5,13},{6,14},{7,15},{8,0},{9,1},... | collective-permute-start | bytes 36872 | tf_op jit(solution)/shard_map/ppermute | solution.py:88
  15.4 8.6 %collective-permute-start.2 = (s32[8,384]{1,0:T(8,128)S(1)}, s32[8,384]{1,0:T(8,128)S(1)}, u32[]{:S(2)}, u32[]{:S(2)}) collective-permute-start(s32[8,384]{1,0:T(8,128)S(1)} %get-tuple-element.30.refs_0_.refs_4_), channel_id=1, source_target_pairs={{0,17},{1,16},{2,19},{3,18},{4,21},{5,20},{6,23},{7,22},{8,25},{9,... | collective-permute-start | bytes 36872 | tf_op jit(solution)/shard_map/ppermute | solution.py:88
  17.9 6.5 %collective-permute-start.1 = (s32[8,384]{1,0:T(8,128)S(1)}, s32[8,384]{1,0:T(8,128)S(1)}, u32[]{:S(2)}, u32[]{:S(2)}) collective-permute-start(s32[8,384]{1,0:T(8,128)S(1)} %get-tuple-element.30.refs_0_.refs_4_), channel_id=1, source_target_pairs={{0,16},{1,17},{2,18},{3,19},{4,20},{5,21},{6,22},{7,23},{8,24},{9,... | collective-permute-start | bytes 36872 | tf_op jit(solution)/shard_map/ppermute | solution.py:88
  18.5 6.6 %collective-permute-start = (s32[8,384]{1,0:T(8,128)S(1)}, s32[8,384]{1,0:T(8,128)S(1)}, u32[]{:S(2)}, u32[]{:S(2)}) collective-permute-start(s32[8,384]{1,0:T(8,128)S(1)} %get-tuple-element.30.refs_0_.refs_4_), channel_id=1, source_target_pairs={{0,1},{1,0},{2,3},{3,2},{4,5},{5,4},{6,7},{7,6},{8,9},{9,8},{10,11... | collective-permute-start | bytes 36872 | tf_op jit(solution)/shard_map/ppermute | solution.py:88
  18.9 7.7 %collective-permute-start.9 = (s32[8,384]{1,0:T(8,128)S(1)}, s32[8,384]{1,0:T(8,128)S(1)}, u32[]{:S(2)}, u32[]{:S(2)}) collective-permute-start(s32[8,384]{1,0:T(8,128)S(1)} %collective-permute-done.8.refs_10_), channel_id=1, source_target_pairs={{0,8},{1,9},{2,10},{3,11},{4,12},{5,13},{6,14},{7,15},{8,0},{9,1},... | collective-permute-start | bytes 36872 | tf_op jit(solution)/shard_map/ppermute | solution.py:88
  24.0 11.1 %collective-permute-start.7 = (s32[8,384]{1,0:T(8,128)S(1)}, s32[8,384]{1,0:T(8,128)S(1)}, u32[]{:S(2)}, u32[]{:S(2)}) collective-permute-start(s32[8,384]{1,0:T(8,128)S(1)} %collective-permute-done.6.refs_8_), channel_id=1, source_target_pairs={{0,8},{1,9},{2,10},{3,11},{4,12},{5,13},{6,14},{7,15},{8,0},{9,1},... | collective-permute-start | bytes 36872 | tf_op jit(solution)/shard_map/ppermute | solution.py:88
  24.0 11.0 %collective-permute-start.5 = (s32[8,384]{1,0:T(8,128)S(1)}, s32[8,384]{1,0:T(8,128)S(1)}, u32[]{:S(2)}, u32[]{:S(2)}) collective-permute-start(s32[8,384]{1,0:T(8,128)S(1)} %collective-permute-done.4.refs_6_), channel_id=1, source_target_pairs={{0,8},{1,9},{2,10},{3,11},{4,12},{5,13},{6,14},{7,15},{8,0},{9,1},... | collective-permute-start | bytes 36872 | tf_op jit(solution)/shard_map/ppermute | solution.py:88
  24.5 14.1 %collective-permute-start.12 = (s32[1,2048]{1,0:T(1,128)}, s32[1,2048]{1,0:T(1,128)S(1)}, u32[]{:S(2)}, u32[]{:S(2)}) collective-permute-start(s32[1,2048]{1,0:T(1,128)} %reshape.20.refs_1_.refs_0_.label_ref), channel_id=1, source_target_pairs={{0,17},{1,16},{2,19},{3,18},{4,21},{5,20},{6,23},{7,22},{8,25},{9,... | collective-permute-start | bytes 24584 | tf_op jit(solution)/shard_map/ppermute | solution.py:88
  25.1 13.5 %collective-permute-start.11 = (s32[1,2048]{1,0:T(1,128)}, s32[1,2048]{1,0:T(1,128)S(1)}, u32[]{:S(2)}, u32[]{:S(2)}) collective-permute-start(s32[1,2048]{1,0:T(1,128)} %reshape.20.refs_1_.refs_0_.label_ref), channel_id=1, source_target_pairs={{0,16},{1,17},{2,18},{3,19},{4,20},{5,21},{6,22},{7,23},{8,24},{9,... | collective-permute-start | bytes 24584 | tf_op jit(solution)/shard_map/ppermute | solution.py:88
  26.6 12.0 %collective-permute-start.10 = (s32[1,2048]{1,0:T(1,128)}, s32[1,2048]{1,0:T(1,128)S(1)}, u32[]{:S(2)}, u32[]{:S(2)}) collective-permute-start(s32[1,2048]{1,0:T(1,128)} %reshape.20.refs_1_.refs_0_.label_ref), channel_id=1, source_target_pairs={{0,1},{1,0},{2,3},{3,2},{4,5},{5,4},{6,7},{7,6},{8,9},{9,8},{10,11... | collective-permute-start | bytes 24584 | tf_op jit(solution)/shard_map/ppermute | solution.py:88
  35.6 30.2 %all-to-all-start.1 = ((bf16[32,64,256]{2,1,0:T(8,128)(2,1)}), bf16[32,64,256]{2,1,0:T(8,128)(2,1)S(1)}, u32[]{:S(2)}, u32[]{:S(2)}) async-start(bf16[32,64,256]{2,1,0:T(8,128)(2,1)} %bitcast.11), calls=%async_computation.1 | async-start | bytes 2097152 | tf_op jit(solution)/shard_map/all_to_all | solution.py:396
  76.8 8.3 %collective-permute-start.18 = (bf16[256,256]{1,0:T(8,128)(2,1)S(1)}, bf16[256,256]{1,0:T(8,128)(2,1)S(1)}, u32[]{:S(2)}, u32[]{:S(2)}) collective-permute-start(bf16[256,256]{1,0:T(8,128)(2,1)S(1)} %get-tuple-element.35.refs_2_), channel_id=1, source_target_pairs={{0,2},{1,3},{2,4},{3,5},{4,6},{5,7},{6,0},{7,1},{8,10},{9,11},{10,... | collective-permute-start | bytes 393224 | tf_op jit(solution)/shard_map/ppermute | solution.py:88
  77.0 12.5 %collective-permute-start.16 = (bf16[256,256]{1,0:T(8,128)(2,1)S(1)}, bf16[256,256]{1,0:T(8,128)(2,1)S(1)}, u32[]{:S(2)}, u32[]{:S(2)}) collective-permute-start(bf16[256,256]{1,0:T(8,128)(2,1)S(1)} %get-tuple-element.35.refs_2_), channel_id=1, source_target_pairs={{0,4},{1,5},{2,6},{3,7},{4,0},{5,1},{6,2},{7,3},{8,12},{9,13},{10,... | collective-permute-start | bytes 393224 | tf_op jit(solution)/shard_map/ppermute | solution.py:88
  79.2 10.3 %collective-permute-start.14 = (bf16[256,256]{1,0:T(8,128)(2,1)S(1)}, bf16[256,256]{1,0:T(8,128)(2,1)S(1)}, u32[]{:S(2)}, u32[]{:S(2)}) collective-permute-start(bf16[256,256]{1,0:T(8,128)(2,1)S(1)} %get-tuple-element.35.refs_2_), channel_id=1, source_target_pairs={{0,6},{1,7},{2,0},{3,1},{4,2},{5,3},{6,4},{7,5},{8,14},{9,15},{10,... | collective-permute-start | bytes 393224 | tf_op jit(solution)/shard_map/ppermute | solution.py:88
  80.7 9.3 %collective-permute-start.13 = (bf16[256,256]{1,0:T(8,128)(2,1)S(1)}, bf16[256,256]{1,0:T(8,128)(2,1)S(1)}, u32[]{:S(2)}, u32[]{:S(2)}) collective-permute-start(bf16[256,256]{1,0:T(8,128)(2,1)S(1)} %get-tuple-element.35.refs_2_), channel_id=1, source_target_pairs={{0,8},{1,9},{2,10},{3,11},{4,12},{5,13},{6,14},{7,15},{8,0},{9,1},... | collective-permute-start | bytes 393224 | tf_op jit(solution)/shard_map/ppermute | solution.py:88
  93.9 5.8 %collective-permute-start.20 = (bf16[256,256]{1,0:T(8,128)(2,1)S(1)}, bf16[256,256]{1,0:T(8,128)(2,1)S(1)}, u32[]{:S(2)}, u32[]{:S(2)}) collective-permute-start(bf16[256,256]{1,0:T(8,128)(2,1)S(1)} %get-tuple-element.37), channel_id=1, source_target_pairs={{0,1},{1,0},{2,3},{3,2},{4,5},{5,4},{6,7},{7,6},{8,9},{9,8},{10,11... | collective-permute-start | bytes 393224 | tf_op jit(solution)/shard_map/ppermute | solution.py:88
  95.2 6.4 %collective-permute-start.21 = (bf16[256,256]{1,0:T(8,128)(2,1)S(1)}, bf16[256,256]{1,0:T(8,128)(2,1)S(1)}, u32[]{:S(2)}, u32[]{:S(2)}) collective-permute-start(bf16[256,256]{1,0:T(8,128)(2,1)S(1)} %get-tuple-element.38), channel_id=1, source_target_pairs={{0,16},{1,17},{2,18},{3,19},{4,20},{5,21},{6,22},{7,23},{8,24},{9,... | collective-permute-start | bytes 393224 | tf_op jit(solution)/shard_map/ppermute | solution.py:88
  95.8 7.9 %collective-permute-start.22 = (bf16[256,256]{1,0:T(8,128)(2,1)S(1)}, bf16[256,256]{1,0:T(8,128)(2,1)S(1)}, u32[]{:S(2)}, u32[]{:S(2)}) collective-permute-start(bf16[256,256]{1,0:T(8,128)(2,1)S(1)} %get-tuple-element.39), channel_id=1, source_target_pairs={{0,17},{1,16},{2,19},{3,18},{4,21},{5,20},{6,23},{7,22},{8,25},{9,... | collective-permute-start | bytes 393224 | tf_op jit(solution)/shard_map/ppermute | solution.py:88
  103.8 8.4 %collective-permute-start.28 = (bf16[256,256]{1,0:T(8,128)(2,1)S(1)}, bf16[256,256]{1,0:T(8,128)(2,1)S(1)}, u32[]{:S(2)}, u32[]{:S(2)}) collective-permute-start(bf16[256,256]{1,0:T(8,128)(2,1)S(1)} %add_convert_fusion.1.refs_1_), channel_id=1, source_target_pairs={{0,2},{1,3},{2,4},{3,5},{4,6},{5,7},{6,0},{7,1},{8,10},{9,11},{10,... | collective-permute-start | bytes 393224 | tf_op jit(solution)/shard_map/ppermute | solution.py:88
  106.4 9.5 %collective-permute-start.26 = (bf16[256,256]{1,0:T(8,128)(2,1)S(1)}, bf16[256,256]{1,0:T(8,128)(2,1)S(1)}, u32[]{:S(2)}, u32[]{:S(2)}) collective-permute-start(bf16[256,256]{1,0:T(8,128)(2,1)S(1)} %add_convert_fusion.1.refs_1_), channel_id=1, source_target_pairs={{0,4},{1,5},{2,6},{3,7},{4,0},{5,1},{6,2},{7,3},{8,12},{9,13},{10,... | collective-permute-start | bytes 393224 | tf_op jit(solution)/shard_map/ppermute | solution.py:88
  107.5 8.5 %collective-permute-start.24 = (bf16[256,256]{1,0:T(8,128)(2,1)S(1)}, bf16[256,256]{1,0:T(8,128)(2,1)S(1)}, u32[]{:S(2)}, u32[]{:S(2)}) collective-permute-start(bf16[256,256]{1,0:T(8,128)(2,1)S(1)} %add_convert_fusion.1.refs_1_), channel_id=1, source_target_pairs={{0,6},{1,7},{2,0},{3,1},{4,2},{5,3},{6,4},{7,5},{8,14},{9,15},{10,... | collective-permute-start | bytes 393224 | tf_op jit(solution)/shard_map/ppermute | solution.py:88
  108.9 7.6 %collective-permute-start.23 = (bf16[256,256]{1,0:T(8,128)(2,1)S(1)}, bf16[256,256]{1,0:T(8,128)(2,1)S(1)}, u32[]{:S(2)}, u32[]{:S(2)}) collective-permute-start(bf16[256,256]{1,0:T(8,128)(2,1)S(1)} %add_convert_fusion.1.refs_1_), channel_id=1, source_target_pairs={{0,8},{1,9},{2,10},{3,11},{4,12},{5,13},{6,14},{7,15},{8,0},{9,1},... | collective-permute-start | bytes 393224 | tf_op jit(solution)/shard_map/ppermute | solution.py:88
  119.3 5.8 %collective-permute-start.33 = (bf16[256,256]{1,0:T(8,128)(2,1)S(1)}, bf16[256,256]{1,0:T(8,128)(2,1)S(1)}, u32[]{:S(2)}, u32[]{:S(2)}) collective-permute-start(bf16[256,256]{1,0:T(8,128)(2,1)S(1)} %get-tuple-element.47), channel_id=1, source_target_pairs={{0,1},{1,0},{2,3},{3,2},{4,5},{5,4},{6,7},{7,6},{8,9},{9,8},{10,11... | collective-permute-start | bytes 393224 | tf_op jit(solution)/shard_map/ppermute | solution.py:88
  120.6 6.4 %collective-permute-start.34 = (bf16[256,256]{1,0:T(8,128)(2,1)S(1)}, bf16[256,256]{1,0:T(8,128)(2,1)S(1)}, u32[]{:S(2)}, u32[]{:S(2)}) collective-permute-start(bf16[256,256]{1,0:T(8,128)(2,1)S(1)} %get-tuple-element.48), channel_id=1, source_target_pairs={{0,16},{1,17},{2,18},{3,19},{4,20},{5,21},{6,22},{7,23},{8,24},{9,... | collective-permute-start | bytes 393224 | tf_op jit(solution)/shard_map/ppermute | solution.py:88
  121.9 7.2 %collective-permute-start.35 = (bf16[256,256]{1,0:T(8,128)(2,1)S(1)}, bf16[256,256]{1,0:T(8,128)(2,1)S(1)}, u32[]{:S(2)}, u32[]{:S(2)}) collective-permute-start(bf16[256,256]{1,0:T(8,128)(2,1)S(1)} %get-tuple-element.49), channel_id=1, source_target_pairs={{0,17},{1,16},{2,19},{3,18},{4,21},{5,20},{6,23},{7,22},{8,25},{9,... | collective-permute-start | bytes 393224 | tf_op jit(solution)/shard_map/ppermute | solution.py:88
  129.9 8.5 %collective-permute-start.41 = (bf16[256,256]{1,0:T(8,128)(2,1)S(1)}, bf16[256,256]{1,0:T(8,128)(2,1)S(1)}, u32[]{:S(2)}, u32[]{:S(2)}) collective-permute-start(bf16[256,256]{1,0:T(8,128)(2,1)S(1)} %subtract_convert_fusion.2.refs_2_), channel_id=1, source_target_pairs={{0,2},{1,3},{2,4},{3,5},{4,6},{5,7},{6,0},{7,1},{8,10},{9,11},{10,... | collective-permute-start | bytes 393224 | tf_op jit(solution)/shard_map/ppermute | solution.py:88
  132.8 9.6 %collective-permute-start.39 = (bf16[256,256]{1,0:T(8,128)(2,1)S(1)}, bf16[256,256]{1,0:T(8,128)(2,1)S(1)}, u32[]{:S(2)}, u32[]{:S(2)}) collective-permute-start(bf16[256,256]{1,0:T(8,128)(2,1)S(1)} %subtract_convert_fusion.2.refs_2_), channel_id=1, source_target_pairs={{0,4},{1,5},{2,6},{3,7},{4,0},{5,1},{6,2},{7,3},{8,12},{9,13},{10,... | collective-permute-start | bytes 393224 | tf_op jit(solution)/shard_map/ppermute | solution.py:88
  134.5 8.1 %collective-permute-start.37 = (bf16[256,256]{1,0:T(8,128)(2,1)S(1)}, bf16[256,256]{1,0:T(8,128)(2,1)S(1)}, u32[]{:S(2)}, u32[]{:S(2)}) collective-permute-start(bf16[256,256]{1,0:T(8,128)(2,1)S(1)} %subtract_convert_fusion.2.refs_2_), channel_id=1, source_target_pairs={{0,6},{1,7},{2,0},{3,1},{4,2},{5,3},{6,4},{7,5},{8,14},{9,15},{10,... | collective-permute-start | bytes 393224 | tf_op jit(solution)/shard_map/ppermute | solution.py:88
  135.3 10.2 %collective-permute-start.36 = (bf16[256,256]{1,0:T(8,128)(2,1)S(1)}, bf16[256,256]{1,0:T(8,128)(2,1)S(1)}, u32[]{:S(2)}, u32[]{:S(2)}) collective-permute-start(bf16[256,256]{1,0:T(8,128)(2,1)S(1)} %subtract_convert_fusion.2.refs_2_), channel_id=1, source_target_pairs={{0,8},{1,9},{2,10},{3,11},{4,12},{5,13},{6,14},{7,15},{8,0},{9,1},... | collective-permute-start | bytes 393224 | tf_op jit(solution)/shard_map/ppermute | solution.py:88
  138.4 7.1 %collective-permute-start.42 = (bf16[256,256]{1,0:T(8,128)(2,1)S(1)}, bf16[256,256]{1,0:T(8,128)(2,1)S(1)}, u32[]{:S(2)}, u32[]{:S(2)}) collective-permute-start(bf16[256,256]{1,0:T(8,128)(2,1)S(1)} %collective-permute-done.41.refs_8_), channel_id=1, source_target_pairs={{0,8},{1,9},{2,10},{3,11},{4,12},{5,13},{6,14},{7,15},{8,0},{9,1},... | collective-permute-start | bytes 393224 | tf_op jit(solution)/shard_map/ppermute | solution.py:88
  148.5 5.6 %collective-permute-start.43 = (bf16[256,256]{1,0:T(8,128)(2,1)S(1)}, bf16[256,256]{1,0:T(8,128)(2,1)S(1)}, u32[]{:S(2)}, u32[]{:S(2)}) collective-permute-start(bf16[256,256]{1,0:T(8,128)(2,1)S(1)} %get-tuple-element.51), channel_id=1, source_target_pairs={{0,1},{1,0},{2,3},{3,2},{4,5},{5,4},{6,7},{7,6},{8,9},{9,8},{10,11... | collective-permute-start | bytes 393224 | tf_op jit(solution)/shard_map/ppermute | solution.py:88
  149.7 6.4 %collective-permute-start.44 = (bf16[256,256]{1,0:T(8,128)(2,1)S(1)}, bf16[256,256]{1,0:T(8,128)(2,1)S(1)}, u32[]{:S(2)}, u32[]{:S(2)}) collective-permute-start(bf16[256,256]{1,0:T(8,128)(2,1)S(1)} %get-tuple-element.52), channel_id=1, source_target_pairs={{0,16},{1,17},{2,18},{3,19},{4,20},{5,21},{6,22},{7,23},{8,24},{9,... | collective-permute-start | bytes 393224 | tf_op jit(solution)/shard_map/ppermute | solution.py:88
  151.0 7.1 %collective-permute-start.45 = (bf16[256,256]{1,0:T(8,128)(2,1)S(1)}, bf16[256,256]{1,0:T(8,128)(2,1)S(1)}, u32[]{:S(2)}, u32[]{:S(2)}) collective-permute-start(bf16[256,256]{1,0:T(8,128)(2,1)S(1)} %get-tuple-element.53), channel_id=1, source_target_pairs={{0,17},{1,16},{2,19},{3,18},{4,21},{5,20},{6,23},{7,22},{8,25},{9,... | collective-permute-start | bytes 393224 | tf_op jit(solution)/shard_map/ppermute | solution.py:88
  158.1 8.4 %collective-permute-start.51 = (bf16[256,256]{1,0:T(8,128)(2,1)S(1)}, bf16[256,256]{1,0:T(8,128)(2,1)S(1)}, u32[]{:S(2)}, u32[]{:S(2)}) collective-permute-start(bf16[256,256]{1,0:T(8,128)(2,1)S(1)} %add_convert_fusion.refs_1_), channel_id=1, source_target_pairs={{0,2},{1,3},{2,4},{3,5},{4,6},{5,7},{6,0},{7,1},{8,10},{9,11},{10,... | collective-permute-start | bytes 393224 | tf_op jit(solution)/shard_map/ppermute | solution.py:88
  161.3 9.4 %collective-permute-start.49 = (bf16[256,256]{1,0:T(8,128)(2,1)S(1)}, bf16[256,256]{1,0:T(8,128)(2,1)S(1)}, u32[]{:S(2)}, u32[]{:S(2)}) collective-permute-start(bf16[256,256]{1,0:T(8,128)(2,1)S(1)} %add_convert_fusion.refs_1_), channel_id=1, source_target_pairs={{0,4},{1,5},{2,6},{3,7},{4,0},{5,1},{6,2},{7,3},{8,12},{9,13},{10,... | collective-permute-start | bytes 393224 | tf_op jit(solution)/shard_map/ppermute | solution.py:88
  162.7 8.1 %collective-permute-start.47 = (bf16[256,256]{1,0:T(8,128)(2,1)S(1)}, bf16[256,256]{1,0:T(8,128)(2,1)S(1)}, u32[]{:S(2)}, u32[]{:S(2)}) collective-permute-start(bf16[256,256]{1,0:T(8,128)(2,1)S(1)} %add_convert_fusion.refs_1_), channel_id=1, source_target_pairs={{0,6},{1,7},{2,0},{3,1},{4,2},{5,3},{6,4},{7,5},{8,14},{9,15},{10,... | collective-permute-start | bytes 393224 | tf_op jit(solution)/shard_map/ppermute | solution.py:88
  163.8 8.7 %collective-permute-start.46 = (bf16[256,256]{1,0:T(8,128)(2,1)S(1)}, bf16[256,256]{1,0:T(8,128)(2,1)S(1)}, u32[]{:S(2)}, u32[]{:S(2)}) collective-permute-start(bf16[256,256]{1,0:T(8,128)(2,1)S(1)} %add_convert_fusion.refs_1_), channel_id=1, source_target_pairs={{0,8},{1,9},{2,10},{3,11},{4,12},{5,13},{6,14},{7,15},{8,0},{9,1},... | collective-permute-start | bytes 393224 | tf_op jit(solution)/shard_map/ppermute | solution.py:88
  166.5 7.2 %collective-permute-start.52 = (bf16[256,256]{1,0:T(8,128)(2,1)S(1)}, bf16[256,256]{1,0:T(8,128)(2,1)S(1)}, u32[]{:S(2)}, u32[]{:S(2)}) collective-permute-start(bf16[256,256]{1,0:T(8,128)(2,1)S(1)} %collective-permute-done.51.refs_7_), channel_id=1, source_target_pairs={{0,8},{1,9},{2,10},{3,11},{4,12},{5,13},{6,14},{7,15},{8,0},{9,1},... | collective-permute-start | bytes 393224 | tf_op jit(solution)/shard_map/ppermute | solution.py:88
  171.3 8.5 %collective-permute-start.30 = (bf16[384,256]{1,0:T(8,128)(2,1)S(1)}, bf16[384,256]{1,0:T(8,128)(2,1)S(1)}, u32[]{:S(2)}, u32[]{:S(2)}) collective-permute-start(bf16[384,256]{1,0:T(8,128)(2,1)S(1)} %get-tuple-element.41.refs_11_), channel_id=1, source_target_pairs={{0,1},{1,0},{2,3},{3,2},{4,5},{5,4},{6,7},{7,6},{8,9},{9,8},{10,11... | collective-permute-start | bytes 589832 | tf_op jit(solution)/shard_map/ppermute | solution.py:88
  172.5 8.3 %collective-permute-start.31 = (bf16[384,256]{1,0:T(8,128)(2,1)S(1)}, bf16[384,256]{1,0:T(8,128)(2,1)S(1)}, u32[]{:S(2)}, u32[]{:S(2)}) collective-permute-start(bf16[384,256]{1,0:T(8,128)(2,1)S(1)} %get-tuple-element.42.refs_12_), channel_id=1, source_target_pairs={{0,16},{1,17},{2,18},{3,19},{4,20},{5,21},{6,22},{7,23},{8,24},{9,... | collective-permute-start | bytes 589832 | tf_op jit(solution)/shard_map/ppermute | solution.py:88
  173.7 11.1 %collective-permute-start.32 = (bf16[384,256]{1,0:T(8,128)(2,1)S(1)}, bf16[384,256]{1,0:T(8,128)(2,1)S(1)}, u32[]{:S(2)}, u32[]{:S(2)}) collective-permute-start(bf16[384,256]{1,0:T(8,128)(2,1)S(1)} %get-tuple-element.43.refs_13_), channel_id=1, source_target_pairs={{0,17},{1,16},{2,19},{3,18},{4,21},{5,20},{6,23},{7,22},{8,25},{9,... | collective-permute-start | bytes 589832 | tf_op jit(solution)/shard_map/ppermute | solution.py:88
  177.3 10.2 %collective-permute-start.53 = (bf16[384,256]{1,0:T(8,128)(2,1)S(1)}, bf16[384,256]{1,0:T(8,128)(2,1)S(1)}, u32[]{:S(2)}, u32[]{:S(2)}) collective-permute-start(bf16[384,256]{1,0:T(8,128)(2,1)S(1)} %get-tuple-element.55), channel_id=1, source_target_pairs={{0,1},{1,0},{2,3},{3,2},{4,5},{5,4},{6,7},{7,6},{8,9},{9,8},{10,11... | collective-permute-start | bytes 589832 | tf_op jit(solution)/shard_map/ppermute | solution.py:88
  178.5 10.2 %collective-permute-start.54 = (bf16[384,256]{1,0:T(8,128)(2,1)S(1)}, bf16[384,256]{1,0:T(8,128)(2,1)S(1)}, u32[]{:S(2)}, u32[]{:S(2)}) collective-permute-start(bf16[384,256]{1,0:T(8,128)(2,1)S(1)} %get-tuple-element.56), channel_id=1, source_target_pairs={{0,16},{1,17},{2,18},{3,19},{4,20},{5,21},{6,22},{7,23},{8,24},{9,... | collective-permute-start | bytes 589832 | tf_op jit(solution)/shard_map/ppermute | solution.py:88
  179.8 12.2 %collective-permute-start.55 = (bf16[384,256]{1,0:T(8,128)(2,1)S(1)}, bf16[384,256]{1,0:T(8,128)(2,1)S(1)}, u32[]{:S(2)}, u32[]{:S(2)}) collective-permute-start(bf16[384,256]{1,0:T(8,128)(2,1)S(1)} %get-tuple-element.57), channel_id=1, source_target_pairs={{0,17},{1,16},{2,19},{3,18},{4,21},{5,20},{6,23},{7,22},{8,25},{9,... | collective-permute-start | bytes 589832 | tf_op jit(solution)/shard_map/ppermute | solution.py:88
  (50 other events, 535.1 us)

commit v4 on v3

--- a/solution.py
+++ b/solution.py
@@ -37,14 +37,17 @@
     return pl.BlockSpec(memory_space=pltpu.VMEM)
 
 
-def anywhere():
-    return pl.BlockSpec(memory_space=pl.ANY)
-
-
 def cost(microseconds):
     return pl.CostEstimate(
         flops=int(microseconds * 1e-6 * PEAK), bytes_accessed=0, transcendentals=0
     )
+
+
+TOKEN = jax.ShapeDtypeStruct((8, 128), F32)
+
+
+def token_spec():
+    return pl.BlockSpec((8, 128), lambda *_: (0, 0))
 
 
 def iota(shape, dim):
@@ -87,21 +90,23 @@
             pairs.append((i, ((x * self.core + c) * self.z + z) * self.y + y))
         return lax.ppermute(value, AXES, pairs)
 
-    def line(self, value):
-        along = [value] + [self.shift(value, dz=-dz) for dz in range(1, self.z)]
+    def along(self, value):
+        return [value] + [self.shift(value, dz=-dz) for dz in range(1, self.z)]
+
+    def swapped(self, values):
         pieces = []
-        for piece in along:
-            pieces.append(piece)
-            pieces += [self.shift(piece, dc=-dc) for dc in range(1, self.core)]
+        for value in values:
+            pieces.append(value)
+            pieces += [self.shift(value, dc=-dc) for dc in range(1, self.core)]
         return pieces
 
     def across(self, value):
         return [value] + [self.shift(value, dx=-dx, dy=-dy) for dx, dy in self.plane[1:]]
 
-    def give(self, blocks):
-        return [
+    def given(self, blocks):
+        return [blocks[0]] + [
             self.shift(block, dx=dx, dy=dy)
-            for block, (dx, dy) in zip(blocks, self.plane[1:])
+            for block, (dx, dy) in zip(blocks[1:], self.plane[1:])
         ]
 
     def place(self, triangle, tri_dev, me):
@@ -112,25 +117,9 @@
         return jnp.where(inside, block * tri_dev + triangle % tri_dev, -1)
 
 
-def tie_kernel(*refs):
-    del refs
-
-
-def tie(value, *others):
-    return pl.pallas_call(
-        tie_kernel,
-        in_specs=[anywhere()] * (1 + len(others)),
-        out_specs=anywhere(),
-        out_shape=jax.ShapeDtypeStruct(value.shape, value.dtype),
-        input_output_aliases={0: 0},
-    )(value, *others)
-
-
-def route_kernel(slots, inc_ref, points_ref, cur_ref, out_ref, label_ref, number_ref):
+def number_kernel(slots, inc_ref, points_ref, label_ref, slot_ref, number_ref):
     edges, tri_dev = inc_ref.shape[1], points_ref.shape[1]
-    ends, cells = 2 * edges, out_ref.shape[0]
-    devices = cells // slots
-    chunk = min(256, cells)
+    ends, devices = 2 * edges, label_ref.shape[0]
     number_ref[...] = jnp.zeros(number_ref.shape, I32)
     number_ref[0:2, :edges] = inc_ref[...]
     number_ref[2:5, :tri_dev] = points_ref[...]
@@ -142,34 +131,58 @@
     upper = ones_where(iota((ends, ends), 0) <= iota((ends, ends), 1))
     count = matmul(ones_where(hits), upper)
     rank = jnp.sum(jnp.where(hits, count, 0.0), axis=0, keepdims=True).astype(I32) - 1
-    slot = owner * slots + rank
+    slot_ref[...] = owner * slots + rank
     order = ones_where(iota((slots, ends), 0) == rank)
     label = jnp.zeros((devices, slots), I32)
-    for digit, weight in ((tri % tri_dev + 1, 1), (other & 255, 2 * tri_dev), (other >> 8, 512 * tri_dev)):
+    digits = (
+        (tri % tri_dev + 1, 1),
+        (other & 255, 2 * tri_dev),
+        (other >> 8, 512 * tri_dev),
+    )
+    for digit, weight in digits:
         spread = jnp.where(hits, digit.astype(F32), 0.0).astype(BF16)
         label = label + matmul_nt(spread, order).astype(I32) * weight
     label_ref[...] = label
+
+
+def number(incidence, centroids, slots, devices):
+    edges = incidence.shape[1]
+    lanes = max(edges, centroids.shape[1])
+    return pl.pallas_call(
+        functools.partial(number_kernel, slots),
+        in_specs=[whole()] * 2,
+        out_specs=[whole()] * 3,
+        out_shape=[
+            jax.ShapeDtypeStruct((devices, slots), I32),
+            jax.ShapeDtypeStruct((1, 2 * edges), I32),
+            jax.ShapeDtypeStruct((8, lanes), I32),
+        ],
+        compiler_params=PARAMS,
+        cost_estimate=cost(1),
+    )(incidence, centroids)
+
+
+def route_kernel(slot_ref, cur_ref, *refs):
+    out_ref, token_ref = refs[-2:]
+    token_ref[...] = jnp.zeros_like(token_ref)
+    edges, cells = cur_ref.shape[0], out_ref.shape[0]
+    chunk = min(256, cells)
+    slot = slot_ref[...]
     for base in range(0, cells, chunk):
-        mask = jnp.where(iota((chunk, ends), 0) + base == slot, 1.0, 0.0).astype(F32)
+        mask = jnp.where(iota((chunk, 2 * edges), 0) + base == slot, 1.0, 0.0).astype(F32)
         signed = (mask[:, :edges] - mask[:, edges:]).astype(BF16)
         out_ref[base : base + chunk, :] = matmul(signed, cur_ref[...]).astype(BF16)
 
 
-def route(incidence, centroids, currents, slots, devices):
-    edges, width = currents.shape
-    lanes = max(edges, centroids.shape[1])
-    return pl.pallas_call(
-        functools.partial(route_kernel, slots),
-        in_specs=[whole()] * 3,
-        out_specs=[whole()] * 3,
-        out_shape=[
-            jax.ShapeDtypeStruct((devices * slots, width), BF16),
-            jax.ShapeDtypeStruct((devices, slots), I32),
-            jax.ShapeDtypeStruct((8, lanes), I32),
-        ],
-        compiler_params=PARAMS,
-        cost_estimate=cost(3),
-    )(incidence, centroids, currents)
+def route(slot, currents, cells, after):
+    return pl.pallas_call(
+        route_kernel,
+        in_specs=[whole()] * (2 + len(after)),
+        out_specs=[whole()] * 2,
+        out_shape=[jax.ShapeDtypeStruct((cells, currents.shape[1]), BF16), TOKEN],
+        compiler_params=PARAMS,
+        cost_estimate=cost(1),
+    )(slot, currents, *after)
 
 
 def features(points, scale, first):
@@ -193,8 +206,9 @@
 
 
 def tile_kernel(count, block, tri_dev, *refs):
-    plane, line = refs[:count], refs[count:-4]
-    real_ref, imag_ref, row_ref, col_ref = refs[-4:]
+    plane, line = refs[:count], refs[count:-6]
+    real_ref, imag_ref, token_ref, row_ref, col_ref = refs[-5:]
+    token_ref[...] = jnp.zeros_like(token_ref)
 
     @pl.when(pl.program_id(0) == 0)
     def _():
@@ -217,19 +231,19 @@
         imag_ref[:, cols] = (poly(SIN, -SPACING / TURNS, u) * (frac * inverse)).astype(BF16)
 
 
-def build_tiles(plane, line, tri_dev):
+def build_tiles(plane, line, tri_dev, after):
     count, cols = len(plane), len(line) * tri_dev
     shape = plane[0].shape
     return pl.pallas_call(
         functools.partial(tile_kernel, count, min(512, cols), tri_dev),
         grid=(count,),
-        in_specs=[pl.BlockSpec(shape, lambda i: (0, 0))] * (count + len(line)),
-        out_specs=[pl.BlockSpec((tri_dev, cols), lambda i: (i, 0))] * 2,
-        out_shape=[jax.ShapeDtypeStruct((count * tri_dev, cols), BF16)] * 2,
+        in_specs=[pl.BlockSpec(shape, lambda i: (0, 0))] * (count + len(line)) + [token_spec()],
+        out_specs=[pl.BlockSpec((tri_dev, cols), lambda i: (i, 0))] * 2 + [token_spec()],
+        out_shape=[jax.ShapeDtypeStruct((count * tri_dev, cols), BF16)] * 2 + [TOKEN],
         scratch_shapes=[pltpu.VMEM((count, 16, tri_dev), BF16), pltpu.VMEM((16, cols), BF16)],
         compiler_params=PARAMS,
         cost_estimate=cost(12),
-    )(*plane, *line)
+    )(*plane, *line, after)
 
 
 def pick(row, base, count):
@@ -240,7 +254,8 @@
 
 
 def adjacency_kernel(layout, tri_dev, me_ref, *refs):
-    labels, out_ref = refs[:-1], refs[-1]
+    labels, (out_ref, token_ref) = refs[:-3], refs[-2:]
+    token_ref[...] = jnp.zeros_like(token_ref)
     rows, cols = out_ref.shape
     for k, label_ref in enumerate(labels):
 
@@ -257,22 +272,24 @@
                 out_ref[:, base : base + rows] = matmul_nt(here, low).astype(BF16)
 
 
-def build_adjacency(layout, me, labels, rows, cols):
+def build_adjacency(layout, me, labels, rows, cols, after):
     count, shape = len(labels), labels[0].shape
     return pl.pallas_call(
         functools.partial(adjacency_kernel, layout, rows),
         grid=(count,),
         in_specs=[pl.BlockSpec(memory_space=pltpu.SMEM)]
-        + [pl.BlockSpec(shape, lambda j: (0, 0))] * count,
-        out_specs=pl.BlockSpec((rows, cols), lambda j: (j, 0)),
-        out_shape=jax.ShapeDtypeStruct((count * rows, cols), BF16),
+        + [pl.BlockSpec(shape, lambda j: (0, 0))] * count
+        + [token_spec()],
+        out_specs=[pl.BlockSpec((rows, cols), lambda j: (j, 0)), token_spec()],
+        out_shape=[jax.ShapeDtypeStruct((count * rows, cols), BF16), TOKEN],
         compiler_params=PARAMS,
         cost_estimate=cost(10),
-    )(me, *labels)
+    )(me, *labels, after)
 
 
 def incidence_kernel(layout, tri_dev, me_ref, *refs):
-    numbers, out_ref = refs[:-1], refs[-1]
+    numbers, (out_ref, token_ref) = refs[:-3], refs[-2:]
+    token_ref[...] = jnp.zeros_like(token_ref)
     edges, cols = out_ref.shape
     for k, number_ref in enumerate(numbers):
 
@@ -286,18 +303,19 @@
                 out_ref[:, base : base + tri_dev] = matmul_nt(eye, signed).astype(BF16)
 
 
-def build_incidence(layout, me, numbers, edges, tri_dev, cols):
+def build_incidence(layout, me, numbers, edges, tri_dev, cols, after):
     count, shape = len(numbers), numbers[0].shape
     return pl.pallas_call(
         functools.partial(incidence_kernel, layout, tri_dev),
         grid=(count,),
         in_specs=[pl.BlockSpec(memory_space=pltpu.SMEM)]
-        + [pl.BlockSpec(shape, lambda j: (0, 0))] * count,
-        out_specs=pl.BlockSpec((edges, cols), lambda j: (j, 0)),
-        out_shape=jax.ShapeDtypeStruct((count * edges, cols), BF16),
+        + [pl.BlockSpec(shape, lambda j: (0, 0))] * count
+        + [token_spec()],
+        out_specs=[pl.BlockSpec((edges, cols), lambda j: (j, 0)), token_spec()],
+        out_shape=[jax.ShapeDtypeStruct((count * edges, cols), BF16), TOKEN],
         compiler_params=PARAMS,
         cost_estimate=cost(6),
-    )(me, *numbers)
+    )(me, *numbers, after)
 
 
 def collect_kernel(tri_dev, label_ref, value_ref, *refs):
@@ -313,7 +331,7 @@
     width = values.shape[1]
     return pl.pallas_call(
         functools.partial(collect_kernel, tri_dev),
-        in_specs=[whole()] * 2 + [anywhere()] * len(after),
+        in_specs=[whole()] * (2 + len(after)),
         out_specs=[whole()] * 3,
         out_shape=[
             jax.ShapeDtypeStruct((tri_dev, width), F32),
@@ -326,7 +344,8 @@
 
 
 def apply_kernel(mats, fed, count, *refs):
-    matrices, pieces, outs = refs[:mats], refs[mats : mats + fed], refs[-count:]
+    matrices, pieces, outs = refs[:mats], refs[mats : mats + fed], refs[-count - 1 : -1]
+    refs[-1][...] = jnp.zeros_like(refs[-1])
     block = pieces[0].shape[0]
     half = pieces[0].shape[1] // 2
     sums = []
@@ -358,21 +377,79 @@
         grid=(count,),
         in_specs=[pl.BlockSpec((block, cols), lambda j: (j, 0))] * len(matrices)
         + [pl.BlockSpec((size, width), lambda j: (0, 0))] * len(pieces)
-        + [anywhere()] * len(after),
-        out_specs=[pl.BlockSpec((block, width), lambda j: (0, 0))] * count,
+        + [token_spec()] * len(after),
+        out_specs=[pl.BlockSpec((block, width), lambda j: (0, 0))] * count + [token_spec()],
         out_shape=[
             jax.ShapeDtypeStruct((block, width), F32 if k == 0 else BF16) for k in range(count)
-        ],
+        ]
+        + [TOKEN],
         compiler_params=PARAMS,
         cost_estimate=cost(2 * len(matrices)),
     )(*matrices, *pieces, *after)
 
 
-def total_of(layout, blocks):
-    total = blocks[0]
-    for part in layout.give(blocks[1:]):
-        total = total + part.astype(F32)
-    return total
+def potential_kernel(count, own_ref, *refs):
+    total = own_ref[...]
+    for ref in refs[:count]:
+        total = total + ref[...].astype(F32)
+    refs[-1][...] = total.astype(BF16)
+
+
+def potential_of(blocks, after):
+    got = blocks[1:]
+    return pl.pallas_call(
+        functools.partial(potential_kernel, len(got)),
+        in_specs=[whole()] * (len(blocks) + len(after)),
+        out_specs=whole(),
+        out_shape=jax.ShapeDtypeStruct(blocks[0].shape, BF16),
+        compiler_params=PARAMS,
+        cost_estimate=cost(1),
+    )(*blocks, *after)
+
+
+def charge_kernel(count, weight_ref, charge_ref, degree_ref, potential_ref, own_ref, *refs):
+    around = own_ref[...]
+    for ref in refs[:count]:
+        around = around + ref[...].astype(F32)
+    out_ref, rounded_ref = refs[-2:]
+    change = degree_ref[:, 0:1] * potential_ref[...].astype(F32) - around
+    value = charge_ref[...] - weight_ref[0] * change
+    out_ref[...] = value
+    rounded_ref[...] = value.astype(BF16)
+
+
+def charge_of(weight, charge, degree, potential, blocks):
+    return pl.pallas_call(
+        functools.partial(charge_kernel, len(blocks) - 1),
+        in_specs=[pl.BlockSpec(memory_space=pltpu.SMEM)] + [whole()] * (3 + len(blocks)),
+        out_specs=[whole()] * 2,
+        out_shape=[
+            jax.ShapeDtypeStruct(charge.shape, F32),
+            jax.ShapeDtypeStruct(charge.shape, BF16),
+        ],
+        compiler_params=PARAMS,
+        cost_estimate=cost(1),
+    )(weight, charge, degree, potential, *blocks)
+
+
+def current_kernel(count, weight_ref, current_ref, own_ref, *refs):
+    slope = own_ref[...]
+    for ref in refs[:count]:
+        slope = slope + ref[...].astype(F32)
+    out_ref, token_ref = refs[-2:]
+    out_ref[...] = (current_ref[...].astype(F32) - weight_ref[0] * slope).astype(BF16)
+    token_ref[...] = jnp.zeros_like(token_ref)
+
+
+def current_of(weight, current, blocks):
+    return pl.pallas_call(
+        functools.partial(current_kernel, len(blocks) - 1),
+        in_specs=[pl.BlockSpec(memory_space=pltpu.SMEM)] + [whole()] * (1 + len(blocks)),
+        out_specs=[whole()] * 2,
+        out_shape=[jax.ShapeDtypeStruct(current.shape, BF16), TOKEN],
+        compiler_params=PARAMS,
+        cost_estimate=cost(1),
+    )(weight, current, *blocks)
 
 
 def per_device(currents, incidence, centroids, sweep_weights):
@@ -387,42 +464,45 @@
     count = len(layout.plane)
     cols = layout.z * layout.core * tri_dev
 
-    outgoing, labels, numbers = route(incidence, centroids, currents, slots, devices)
+    labels, slot, numbers = number(incidence, centroids, slots, devices)
+    along = layout.along(numbers)
     plane = layout.across(numbers)
-    line = layout.line(numbers)
-    labels = lax.all_to_all(labels, AXES, split_axis=0, concat_axis=0, tiled=True)
-    labels = labels.reshape(1, cells)
-    outgoing = tie(outgoing, labels, *plane[1:], *line[1:])
+    outgoing, token = route(slot, currents, cells, (*along[1:], *plane[1:]))
     arrived = lax.all_to_all(
         outgoing.reshape(devices, slots, width), AXES, split_axis=0, concat_axis=0, tiled=True
     ).reshape(cells, width)
+    labels = lax.all_to_all(labels, AXES, split_axis=0, concat_axis=0, tiled=True)
+    labels = labels.reshape(1, cells)
     where = me.astype(I32).reshape(1)
-    tiles = build_tiles(plane, line, tri_dev)
-    slopes_of = build_incidence(layout, where, plane, edge_dev, tri_dev, cols)
-    neighbours = build_adjacency(layout, where, layout.across(labels), tri_dev, cols)
-
-    charge, rounded, degree = collect(
-        labels, arrived, tri_dev, (*tiles, slopes_of, neighbours)
+    slopes_of, token_1 = build_incidence(layout, where, plane, edge_dev, tri_dev, cols, token)
+    *tiles, token_2 = build_tiles(plane, layout.swapped(along), tri_dev, token)
+    neighbours, token_3 = build_adjacency(
+        layout, where, layout.across(labels), tri_dev, cols, token
     )
+
+    charge, rounded, degree = collect(labels, arrived, tri_dev, (token_1, token_2, token_3))
     current = currents
     potential = None
-    slopes = ()
+    slopes, after = None, ()
     for sweep in range(sweeps):
-        pieces = layout.line(rounded)
-        blocks = apply(tiles, pieces, count, slopes)
-        if sweep > 0:
-            change = sweep_weights[sweep - 1] * total_of(layout, slopes)
-            current = (current.astype(F32) - change).astype(BF16)
-        potential = total_of(layout, blocks).astype(BF16)
-        pieces = layout.line(potential)
+        weight = sweep_weights[sweep].reshape(1)
+        pieces = layout.swapped(layout.along(rounded))
+        *blocks, _ = apply(tiles, pieces, count, after)
+        after = ()
+        if slopes is not None:
+            current, token = current_of(last_weight, current, layout.given(slopes))
+            after = (token,)
+        potential = potential_of(layout.given(blocks), after)
+        pieces = layout.swapped(layout.along(potential))
         if sweep + 1 < sweeps:
-            around = total_of(layout, apply([neighbours], pieces, count))
-            change = degree[:, :1] * potential.astype(F32) - around
-            charge = charge - sweep_weights[sweep] * change
-            rounded = charge.astype(BF16)
-        slopes = apply([slopes_of], pieces, count)
-    change = sweep_weights[sweeps - 1] * total_of(layout, slopes)
-    return (current.astype(F32) - change).astype(BF16), potential
+            *blocks, _ = apply([neighbours], pieces, count)
+            charge, rounded = charge_of(
+                weight, charge, degree, potential, layout.given(blocks)
+            )
+        *slopes, token = apply([slopes_of], pieces, count)
+        after, last_weight = (token,), weight
+    current, _ = current_of(last_weight, current, layout.given(slopes))
+    return current, potential
 
 
 def solution(mesh):

time: 195 us -> 190 us (0.974)
  local copies, waits for them, and re-layouts: 23.7 us -> 14.3 us
  Pallas kernels: 39.3 us -> 46.4 us
  other arithmetic: 3.71 us -> 0.69 us
    unnamed x80 -> x30, local copies, waits for them, and re-layouts: 21.8 us -> 13.1 us
    pallas_call x2 -> x7, Pallas kernels: 1.2 us -> 7.32 us  [the longest x2 2.2 us: current_of(): pl.pallas_call(functools.partial(current_kernel, len(blocks) - 1), in_spe...]
    convert_element_type x4 -> x0, other arithmetic: 3.02 us -> none  [the longest x1 2.16 us: per_device(): return ((current.astype(F32) - change).astype(BF16), potential)]
    pallas_call x5, Pallas kernels: 12.7 us -> 14.9 us  [apply(): pl.pallas_call(functools.partial(apply_kernel, len(matrices), len(pieces)...]
  transfers between devices with their start and end apart: 58 -> 58, of which waited for: 28 -> 29; matrix products, arithmetic and copies ran while one was open for 1% -> 1% of each run, Pallas kernels for 15% -> 17%
where the time goes in v4:
time: 190 us; the launch traced here: 189 us
  waiting for transfers between devices  65.1 us (34%)
  starting transfers between devices  61.8 us (33%)
  Pallas kernels  46.4 us (24%)
  local copies, waits for them, and re-layouts  14.3 us (8%)
    ppermute x56, waiting for transfers between devices, shift(): return lax.ppermute(value, AXES, pairs)  60.5 us
    ppermute x56, starting transfers between devices, shift(): return lax.ppermute(value, AXES, pairs)  56.2 us
    pallas_call x5, Pallas kernels, apply(): pl.pallas_call(functools.partial(apply_kernel, len(matrices), len(pieces)...  14.9 us
    unnamed x30, local copies, waits for them, and re-layouts  13.1 us
    pallas_call x1, Pallas kernels, build_adjacency(): pl.pallas_call(functools.partial(adjacency_kernel, layout, rows), grid=(c...  9.77 us
    pallas_call x1, Pallas kernels, build_tiles(): pl.pallas_call(functools.partial(tile_kernel, count, min(512, cols), tri_...  9.28 us
    all_to_all x1, waiting for transfers between devices, per_device(): lax.all_to_all(labels, AXES, split_axis=0, concat_axis=0, tiled=True)  4.63 us
    pallas_call x1, Pallas kernels, build_incidence(): pl.pallas_call(functools.partial(incidence_kernel, layout, tri_dev), grid...  4.36 us
  transfers between devices with their start and end apart: 58, of which 29 were waited for; matrix products, arithmetic and copies ran while one was open for 1% of the time, Pallas kernels for 17%

profile of v4, /device:TPU:0, one launch (start us, length us, event | category | flops | bytes accessed | tf_op | source)
XLA Modules:
  0.0 189.2 jit_solution(13535502329820656677)
XLA Ops:
  3.1 3.0 %collective-permute-start.5 = (s32[8,384]{1,0:T(8,128)S(1)}, s32[8,384]{1,0:T(8,128)S(1)}, u32[]{:S(2)}, u32[]{:S(2)}) collective-permute-start(s32[8,384]{1,0:T(8,128)S(1)} %get-tuple-element.42.refs_0_.refs_4_), channel_id=1, source_target_pairs={{0,2},{1,3},{2,4},{3,5},{4,6},{5,7},{6,0},{7,1},{8,10},{9,11},{10,... | collective-permute-start | bytes 36872 | tf_op jit(solution)/shard_map/ppermute | solution.py:91
  6.2 2.6 %collective-permute-start.4 = (s32[8,384]{1,0:T(8,128)S(1)}, s32[8,384]{1,0:T(8,128)S(1)}, u32[]{:S(2)}, u32[]{:S(2)}) collective-permute-start(s32[8,384]{1,0:T(8,128)S(1)} %get-tuple-element.42.refs_0_.refs_4_), channel_id=1, source_target_pairs={{0,4},{1,5},{2,6},{3,7},{4,0},{5,1},{6,2},{7,3},{8,12},{9,13},{10,... | collective-permute-start | bytes 36872 | tf_op jit(solution)/shard_map/ppermute | solution.py:91
  10.1 2.4 %collective-permute-start.2 = (s32[8,384]{1,0:T(8,128)S(1)}, s32[8,384]{1,0:T(8,128)S(1)}, u32[]{:S(2)}, u32[]{:S(2)}) collective-permute-start(s32[8,384]{1,0:T(8,128)S(1)} %get-tuple-element.42.refs_0_.refs_4_), channel_id=1, source_target_pairs={{0,17},{1,16},{2,19},{3,18},{4,21},{5,20},{6,23},{7,22},{8,25},{9,... | collective-permute-start | bytes 36872 | tf_op jit(solution)/shard_map/ppermute | solution.py:91
  13.6 2.9 %all-to-all-start = ((s32[32,1,64]{2,1,0:T(1,128)}), s32[32,1,64]{2,1,0:T(1,128)S(1)}, u32[]{:S(2)}, u32[]{:S(2)}) async-start(s32[32,1,64]{2,1,0:T(1,128)} %bitcast.2), calls=%async_computation | async-start | bytes 32768 | tf_op jit(solution)/shard_map/all_to_all | solution.py:474
  17.2 1.8 shard_map.60
  18.9 4.6 %all-to-all-done = s32[32,1,64]{2,1,0:T(1,128)S(1)} async-done(((s32[32,1,64]{2,1,0:T(1,128)}), s32[32,1,64]{2,1,0:T(1,128)S(1)}, u32[]{:S(2)}, u32[]{:S(2)}) %all-to-all-start) | async-done | bytes 8224 | tf_op jit(solution)/shard_map/all_to_all | solution.py:474
  23.6 2.6 %all-to-all-start.1 = ((bf16[32,64,256]{2,1,0:T(8,128)(2,1)}), bf16[32,64,256]{2,1,0:T(8,128)(2,1)S(1)}, u32[]{:S(2)}, u32[]{:S(2)}) async-start(bf16[32,64,256]{2,1,0:T(8,128)(2,1)} %bitcast.3), calls=%async_computation.1 | async-start | bytes 2097152 | tf_op jit(solution)/shard_map/all_to_all | solution.py:471
  27.5 2.6 %collective-permute-start.12 = (s32[1,2048]{1,0:T(1,128)S(1)}, s32[1,2048]{1,0:T(1,128)S(1)}, u32[]{:S(2)}, u32[]{:S(2)}) collective-permute-start(s32[1,2048]{1,0:T(1,128)S(1)} %reshape.20.refs_0_.label_ref), channel_id=1, source_target_pairs={{0,17},{1,16},{2,19},{3,18},{4,21},{5,20},{6,23},{7,22},{8,25},{9,... | collective-permute-start | bytes 24584 | tf_op jit(solution)/shard_map/ppermute | solution.py:91
  31.0 4.4 %shard_map.61 = (bf16[1536,2048]{1,0:T(8,128)(2,1)S(1)}, f32[8,128]{1,0:T(8,128)S(1)}) custom-call(s32[1]{0:T(128)} %bitcast.me_ref, s32[8,384]{1,0:T(8,128)S(1)} %get-tuple-element.42.refs_0_.refs_4_, s32[8,384]{1,0:T(8,128)S(1)} %collective-permute-done.refs_3_.refs_1_, s32[8,384]{1,0:T(8,128)S(1)} %collective-permute-done.1.refs_4_.refs_2_, ...), custom_call_target="tpu_custom_call" | custom-call | flops 6899999744 | tf_op jit(solution)/shard_map/pallas_call | solution.py:308
  35.4 2.6 %copy-done.4 = bf16[1536,2048]{1,0:T(8,128)(2,1)} copy-done((bf16[1536,2048]{1,0:T(8,128)(2,1)}, bf16[1536,2048]{1,0:T(8,128)(2,1)S(1)}, u32[]{:S(2)}) %copy-start.4) | copy-done | bytes 6291480
  38.5 9.8 %shard_map.63 = (bf16[1024,2048]{1,0:T(8,128)(2,1)S(1)}, f32[8,128]{1,0:T(8,128)S(1)}) custom-call(s32[1]{0:T(128)} %bitcast.me_ref, s32[1,2048]{1,0:T(1,128)S(1)} %reshape.20.refs_0_.label_ref, s32[1,2048]{1,0:T(1,128)S(1)} %collective-permute-done.10.refs_1_, s32[1,2048]{1,0:T(1,128)S(1)} %collective-permute-done.11.refs_2_, ...), custom_call_target="tpu_custom_call" | custom-call | flops 11500000256 | tf_op jit(solution)/shard_map/pallas_call | solution.py:277
  48.3 2.0 %copy-done.5 = bf16[1024,2048]{1,0:T(8,128)(2,1)} copy-done((bf16[1024,2048]{1,0:T(8,128)(2,1)}, bf16[1024,2048]{1,0:T(8,128)(2,1)S(1)}, u32[]{:S(2)}) %copy-start.5) | copy-done | bytes 4194328
  50.3 9.3 %shard_map.62 = (bf16[1024,2048]{1,0:T(8,128)(2,1)S(1)}, bf16[1024,2048]{1,0:T(8,128)(2,1)S(1)}, f32[8,128]{1,0:T(8,128)S(1)}) custom-call(s32[8,384]{1,0:T(8,128)S(1)} %get-tuple-element.42.refs_0_.refs_4_, s32[8,384]{1,0:T(8,128)S(1)} %collective-permute-done.refs_3_.refs_1_, s32[8,384]{1,0:T(8,128)S(1)} %collective-permute-done.1.refs_4_.refs_2_, ...), custom_call_target="tpu_custom_call" | custom-call | flops 13799999488 | tf_op jit(solution)/shard_map/pallas_call | solution.py:237
  59.6 1.9 %copy-done.7 = bf16[1024,2048]{1,0:T(8,128)(2,1)} copy-done((bf16[1024,2048]{1,0:T(8,128)(2,1)}, bf16[1024,2048]{1,0:T(8,128)(2,1)S(1)}, u32[]{:S(2)}) %copy-start.7) | copy-done | bytes 4194328
  61.6 2.0 %copy-done.9 = bf16[1024,2048]{1,0:T(8,128)(2,1)} copy-done((bf16[1024,2048]{1,0:T(8,128)(2,1)}, bf16[1024,2048]{1,0:T(8,128)(2,1)S(1)}, u32[]{:S(2)}) %copy-start.9) | copy-done | bytes 4194328
  64.3 1.7 collective-permute-start.18
  66.1 2.5 %collective-permute-start.16 = (bf16[256,256]{1,0:T(8,128)(2,1)S(1)}, bf16[256,256]{1,0:T(8,128)(2,1)S(1)}, u32[]{:S(2)}, u32[]{:S(2)}) collective-permute-start(bf16[256,256]{1,0:T(8,128)(2,1)S(1)} %get-tuple-element.53.refs_2_), channel_id=1, source_target_pairs={{0,4},{1,5},{2,6},{3,7},{4,0},{5,1},{6,2},{7,3},{8,12},{9,13},{10,... | collective-permute-start | bytes 393224 | tf_op jit(solution)/shard_map/ppermute | solution.py:91
  70.0 2.7 %collective-permute-done.18.refs_8_ = bf16[256,256]{1,0:T(8,128)(2,1)S(1)} collective-permute-done((bf16[256,256]{1,0:T(8,128)(2,1)S(1)}, bf16[256,256]{1,0:T(8,128)(2,1)S(1)}, u32[]{:S(2)}, u32[]{:S(2)}) %collective-permute-start.18) | collective-permute-done | bytes 131104 | tf_op jit(solution)/shard_map/ppermute | solution.py:91
  72.6 4.8 %collective-permute-done.16.refs_6_ = bf16[256,256]{1,0:T(8,128)(2,1)S(1)} collective-permute-done((bf16[256,256]{1,0:T(8,128)(2,1)S(1)}, bf16[256,256]{1,0:T(8,128)(2,1)S(1)}, u32[]{:S(2)}, u32[]{:S(2)}) %collective-permute-start.16) | collective-permute-done | bytes 131104 | tf_op jit(solution)/shard_map/ppermute | solution.py:91
  79.0 2.2 %copy-done.10 = bf16[1024,2048]{1,0:T(8,128)(2,1)S(1)} copy-done((bf16[1024,2048]{1,0:T(8,128)(2,1)S(1)}, bf16[1024,2048]{1,0:T(8,128)(2,1)}, u32[]{:S(2)}) %copy-start.10) | copy-done | bytes 4194328
  81.2 3.5 %shard_map.65 = (f32[256,256]{1,0:T(8,128)S(1)}, bf16[256,256]{1,0:T(8,128)(2,1)S(1)}, bf16[256,256]{1,0:T(8,128)(2,1)S(1)}, bf16[256,256]{1,0:T(8,128)(2,1)S(1)}, f32[8,128]{1,0:T(8,128)}) custom-call(bf16[1024,2048]{1,0:T(8,128)(2,1)S(1)} %copy-done.8, bf16[1024,2048]{1,0:T(8,128)(2,1)S(1)} %copy-done.10, bf16[256,256]{1,0:T(8,128)(2,1)S(1)} %get-tuple-element.53.refs_2_, ...), custom_call_target="tpu_custom_call" | custom-call | flops 4600000000 | tf_op jit(solution)/shard_map/pallas_call | solution.py:375
  84.7 1.6 collective-permute-start.20
  88.2 2.2 %collective-permute-done.20.refs_0_ = bf16[256,256]{1,0:T(8,128)(2,1)S(1)} collective-permute-done((bf16[256,256]{1,0:T(8,128)(2,1)S(1)}, bf16[256,256]{1,0:T(8,128)(2,1)S(1)}, u32[]{:S(2)}, u32[]{:S(2)}) %collective-permute-start.20) | collective-permute-done | bytes 131104 | tf_op jit(solution)/shard_map/ppermute | solution.py:91
  90.4 2.2 %collective-permute-done.21.refs_1_ = bf16[256,256]{1,0:T(8,128)(2,1)S(1)} collective-permute-done((bf16[256,256]{1,0:T(8,128)(2,1)S(1)}, bf16[256,256]{1,0:T(8,128)(2,1)S(1)}, u32[]{:S(2)}, u32[]{:S(2)}) %collective-permute-start.21) | collective-permute-done | bytes 131104 | tf_op jit(solution)/shard_map/ppermute | solution.py:91
  92.6 1.8 collective-permute-done.22.refs_2_
  94.5 3.0 %collective-permute-start.28 = (bf16[256,256]{1,0:T(8,128)(2,1)S(1)}, bf16[256,256]{1,0:T(8,128)(2,1)S(1)}, u32[]{:S(2)}, u32[]{:S(2)}) collective-permute-start(bf16[256,256]{1,0:T(8,128)(2,1)S(1)} %shard_map.66.refs_1_.potential_ref), channel_id=1, source_target_pairs={{0,2},{1,3},{2,4},{3,5},{4,6},{5,7},{6,0},{7,1},{8,10},{9,11},{10,... | collective-permute-start | bytes 393224 | tf_op jit(solution)/shard_map/ppermute | solution.py:91
  97.5 2.0 %collective-permute-start.26 = (bf16[256,256]{1,0:T(8,128)(2,1)S(1)}, bf16[256,256]{1,0:T(8,128)(2,1)S(1)}, u32[]{:S(2)}, u32[]{:S(2)}) collective-permute-start(bf16[256,256]{1,0:T(8,128)(2,1)S(1)} %shard_map.66.refs_1_.potential_ref), channel_id=1, source_target_pairs={{0,4},{1,5},{2,6},{3,7},{4,0},{5,1},{6,2},{7,3},{8,12},{9,13},{10,... | collective-permute-start | bytes 393224 | tf_op jit(solution)/shard_map/ppermute | solution.py:91
  99.9 3.5 %collective-permute-done.28.refs_7_ = bf16[256,256]{1,0:T(8,128)(2,1)S(1)} collective-permute-done((bf16[256,256]{1,0:T(8,128)(2,1)S(1)}, bf16[256,256]{1,0:T(8,128)(2,1)S(1)}, u32[]{:S(2)}, u32[]{:S(2)}) %collective-permute-start.28) | collective-permute-done | bytes 131104 | tf_op jit(solution)/shard_map/ppermute | solution.py:91
  103.4 4.4 %collective-permute-done.26.refs_5_ = bf16[256,256]{1,0:T(8,128)(2,1)S(1)} collective-permute-done((bf16[256,256]{1,0:T(8,128)(2,1)S(1)}, bf16[256,256]{1,0:T(8,128)(2,1)S(1)}, u32[]{:S(2)}, u32[]{:S(2)}) %collective-permute-start.26) | collective-permute-done | bytes 131104 | tf_op jit(solution)/shard_map/ppermute | solution.py:91
  109.3 2.5 %shard_map.69 = (f32[256,256]{1,0:T(8,128)S(1)}, bf16[256,256]{1,0:T(8,128)(2,1)S(1)}, bf16[256,256]{1,0:T(8,128)(2,1)S(1)}, bf16[256,256]{1,0:T(8,128)(2,1)S(1)}, f32[8,128]{1,0:T(8,128)}) custom-call(bf16[1024,2048]{1,0:T(8,128)(2,1)S(1)} %copy-done.6, bf16[256,256]{1,0:T(8,128)(2,1)S(1)} %shard_map.66.refs_1_.potential_ref, ...), custom_call_target="tpu_custom_call" | custom-call | flops 2300000000 | tf_op jit(solution)/shard_map/pallas_call | solution.py:375
  115.9 1.6 collective-permute-done.33.refs_0_
  117.5 1.9 collective-permute-done.34.refs_1_
  119.4 2.1 %collective-permute-done.35.refs_2_ = bf16[256,256]{1,0:T(8,128)(2,1)S(1)} collective-permute-done((bf16[256,256]{1,0:T(8,128)(2,1)S(1)}, bf16[256,256]{1,0:T(8,128)(2,1)S(1)}, u32[]{:S(2)}, u32[]{:S(2)}) %collective-permute-start.35) | collective-permute-done | bytes 131104 | tf_op jit(solution)/shard_map/ppermute | solution.py:91
  122.9 2.9 %collective-permute-start.41 = (bf16[256,256]{1,0:T(8,128)(2,1)S(1)}, bf16[256,256]{1,0:T(8,128)(2,1)S(1)}, u32[]{:S(2)}, u32[]{:S(2)}) collective-permute-start(bf16[256,256]{1,0:T(8,128)(2,1)S(1)} %get-tuple-element.70.refs_2_), channel_id=1, source_target_pairs={{0,2},{1,3},{2,4},{3,5},{4,6},{5,7},{6,0},{7,1},{8,10},{9,11},{10,... | collective-permute-start | bytes 393224 | tf_op jit(solution)/shard_map/ppermute | solution.py:91
  128.2 3.0 %collective-permute-done.41.refs_8_ = bf16[256,256]{1,0:T(8,128)(2,1)S(1)} collective-permute-done((bf16[256,256]{1,0:T(8,128)(2,1)S(1)}, bf16[256,256]{1,0:T(8,128)(2,1)S(1)}, u32[]{:S(2)}, u32[]{:S(2)}) %collective-permute-start.41) | collective-permute-done | bytes 131104 | tf_op jit(solution)/shard_map/ppermute | solution.py:91
  131.3 4.0 %collective-permute-done.39.refs_6_ = bf16[256,256]{1,0:T(8,128)(2,1)S(1)} collective-permute-done((bf16[256,256]{1,0:T(8,128)(2,1)S(1)}, bf16[256,256]{1,0:T(8,128)(2,1)S(1)}, u32[]{:S(2)}, u32[]{:S(2)}) %collective-permute-start.39) | collective-permute-done | bytes 131104 | tf_op jit(solution)/shard_map/ppermute | solution.py:91
  135.8 2.4 %shard_map.67 = (f32[384,256]{1,0:T(8,128)S(1)}, bf16[384,256]{1,0:T(8,128)(2,1)S(1)}, bf16[384,256]{1,0:T(8,128)(2,1)S(1)}, bf16[384,256]{1,0:T(8,128)(2,1)S(1)}, f32[8,128]{1,0:T(8,128)S(1)}) custom-call(bf16[1536,2048]{1,0:T(8,128)(2,1)S(1)} %bitcast.8, bf16[256,256]{1,0:T(8,128)(2,1)S(1)} %shard_map.66.refs_1_.potential_ref, ...), custom_call_target="tpu_custom_call" | custom-call | flops 2300000000 | tf_op jit(solution)/shard_map/pallas_call | solution.py:375
  141.8 3.5 %shard_map.71 = (f32[256,256]{1,0:T(8,128)S(1)}, bf16[256,256]{1,0:T(8,128)(2,1)S(1)}, bf16[256,256]{1,0:T(8,128)(2,1)S(1)}, bf16[256,256]{1,0:T(8,128)(2,1)S(1)}, f32[8,128]{1,0:T(8,128)}) custom-call(bf16[1024,2048]{1,0:T(8,128)(2,1)S(1)} %copy-done.8, bf16[1024,2048]{1,0:T(8,128)(2,1)S(1)} %copy-done.11, bf16[256,256]{1,0:T(8,128)(2,1)S(1)} %get-tuple-element.70.refs_2_, ...), custom_call_target="tpu_custom_call" | custom-call | flops 4600000000 | tf_op jit(solution)/shard_map/pallas_call | solution.py:375
  148.8 3.0 %collective-permute-done.32.refs_2_ = bf16[384,256]{1,0:T(8,128)(2,1)S(1)} collective-permute-done((bf16[384,256]{1,0:T(8,128)(2,1)S(1)}, bf16[384,256]{1,0:T(8,128)(2,1)S(1)}, u32[]{:S(2)}, u32[]{:S(2)}) %collective-permute-start.32) | collective-permute-done | bytes 196640 | tf_op jit(solution)/shard_map/ppermute | solution.py:91
  152.6 1.6 collective-permute-done.43.refs_0_
  154.4 1.9 %collective-permute-done.45.refs_2_ = bf16[256,256]{1,0:T(8,128)(2,1)S(1)} collective-permute-done((bf16[256,256]{1,0:T(8,128)(2,1)S(1)}, bf16[256,256]{1,0:T(8,128)(2,1)S(1)}, u32[]{:S(2)}, u32[]{:S(2)}) %collective-permute-start.45) | collective-permute-done | bytes 131104 | tf_op jit(solution)/shard_map/ppermute | solution.py:91
  157.0 3.1 %collective-permute-start.51 = (bf16[256,256]{1,0:T(8,128)(2,1)}, bf16[256,256]{1,0:T(8,128)(2,1)S(1)}, u32[]{:S(2)}, u32[]{:S(2)}) collective-permute-start(bf16[256,256]{1,0:T(8,128)(2,1)} %shard_map.72.refs_1_), channel_id=1, source_target_pairs={{0,2},{1,3},{2,4},{3,5},{4,6},{5,7},{6,0},{7,1},{8,10},{9,11},{10,... | collective-permute-start | bytes 393224 | tf_op jit(solution)/shard_map/ppermute | solution.py:91
  162.5 3.2 %collective-permute-done.51.refs_7_ = bf16[256,256]{1,0:T(8,128)(2,1)S(1)} collective-permute-done((bf16[256,256]{1,0:T(8,128)(2,1)}, bf16[256,256]{1,0:T(8,128)(2,1)S(1)}, u32[]{:S(2)}, u32[]{:S(2)}) %collective-permute-start.51) | collective-permute-done | bytes 131104 | tf_op jit(solution)/shard_map/ppermute | solution.py:91
  165.7 4.1 %collective-permute-done.49.refs_5_ = bf16[256,256]{1,0:T(8,128)(2,1)S(1)} collective-permute-done((bf16[256,256]{1,0:T(8,128)(2,1)}, bf16[256,256]{1,0:T(8,128)(2,1)S(1)}, u32[]{:S(2)}, u32[]{:S(2)}) %collective-permute-start.49) | collective-permute-done | bytes 131104 | tf_op jit(solution)/shard_map/ppermute | solution.py:91
  172.3 3.0 %shard_map.73 = (f32[384,256]{1,0:T(8,128)S(1)}, bf16[384,256]{1,0:T(8,128)(2,1)S(1)}, bf16[384,256]{1,0:T(8,128)(2,1)S(1)}, bf16[384,256]{1,0:T(8,128)(2,1)S(1)}, f32[8,128]{1,0:T(8,128)}) custom-call(bf16[1536,2048]{1,0:T(8,128)(2,1)S(1)} %bitcast.8, bf16[256,256]{1,0:T(8,128)(2,1)S(1)} %copy-done.1, bf16[256,256]{1,0:T(8,128)(2,1)S(1)} %collective-permute-done.46.refs_2_, ...), custom_call_target="tpu_custom_call" | custom-call | flops 2300000000 | tf_op jit(solution)/shard_map/pallas_call | solution.py:375
  178.7 3.6 %collective-permute-done.53.refs_0_ = bf16[384,256]{1,0:T(8,128)(2,1)S(1)} collective-permute-done((bf16[384,256]{1,0:T(8,128)(2,1)S(1)}, bf16[384,256]{1,0:T(8,128)(2,1)S(1)}, u32[]{:S(2)}, u32[]{:S(2)}) %collective-permute-start.53) | collective-permute-done | bytes 196640 | tf_op jit(solution)/shard_map/ppermute | solution.py:91
  182.4 1.9 collective-permute-done.54.refs_1_
  184.3 3.5 %collective-permute-done.55.refs_2_ = bf16[384,256]{1,0:T(8,128)(2,1)S(1)} collective-permute-done((bf16[384,256]{1,0:T(8,128)(2,1)S(1)}, bf16[384,256]{1,0:T(8,128)(2,1)S(1)}, u32[]{:S(2)}, u32[]{:S(2)}) %collective-permute-start.55) | collective-permute-done | bytes 196640 | tf_op jit(solution)/shard_map/ppermute | solution.py:91
  (119 shorter events, 42.8 us)
Async XLA Ops:
  3.1 9.9 %collective-permute-start.5 = (s32[8,384]{1,0:T(8,128)S(1)}, s32[8,384]{1,0:T(8,128)S(1)}, u32[]{:S(2)}, u32[]{:S(2)}) collective-permute-start(s32[8,384]{1,0:T(8,128)S(1)} %get-tuple-element.42.refs_0_.refs_4_), channel_id=1, source_target_pairs={{0,2},{1,3},{2,4},{3,5},{4,6},{5,7},{6,0},{7,1},{8,10},{9,11},{10,... | collective-permute-start | bytes 36872 | tf_op jit(solution)/shard_map/ppermute | solution.py:91
  6.2 10.4 %collective-permute-start.4 = (s32[8,384]{1,0:T(8,128)S(1)}, s32[8,384]{1,0:T(8,128)S(1)}, u32[]{:S(2)}, u32[]{:S(2)}) collective-permute-start(s32[8,384]{1,0:T(8,128)S(1)} %get-tuple-element.42.refs_0_.refs_4_), channel_id=1, source_target_pairs={{0,4},{1,5},{2,6},{3,7},{4,0},{5,1},{6,2},{7,3},{8,12},{9,13},{10,... | collective-permute-start | bytes 36872 | tf_op jit(solution)/shard_map/ppermute | solution.py:91
  8.8 8.1 %collective-permute-start.3 = (s32[8,384]{1,0:T(8,128)S(1)}, s32[8,384]{1,0:T(8,128)S(1)}, u32[]{:S(2)}, u32[]{:S(2)}) collective-permute-start(s32[8,384]{1,0:T(8,128)S(1)} %get-tuple-element.42.refs_0_.refs_4_), channel_id=1, source_target_pairs={{0,6},{1,7},{2,0},{3,1},{4,2},{5,3},{6,4},{7,5},{8,14},{9,15},{10,... | collective-permute-start | bytes 36872 | tf_op jit(solution)/shard_map/ppermute | solution.py:91
  10.1 7.0 %collective-permute-start.2 = (s32[8,384]{1,0:T(8,128)S(1)}, s32[8,384]{1,0:T(8,128)S(1)}, u32[]{:S(2)}, u32[]{:S(2)}) collective-permute-start(s32[8,384]{1,0:T(8,128)S(1)} %get-tuple-element.42.refs_0_.refs_4_), channel_id=1, source_target_pairs={{0,17},{1,16},{2,19},{3,18},{4,21},{5,20},{6,23},{7,22},{8,25},{9,... | collective-permute-start | bytes 36872 | tf_op jit(solution)/shard_map/ppermute | solution.py:91
  13.6 10.0 %all-to-all-start = ((s32[32,1,64]{2,1,0:T(1,128)}), s32[32,1,64]{2,1,0:T(1,128)S(1)}, u32[]{:S(2)}, u32[]{:S(2)}) async-start(s32[32,1,64]{2,1,0:T(1,128)} %bitcast.2), calls=%async_computation | async-start | bytes 32768 | tf_op jit(solution)/shard_map/all_to_all | solution.py:474
  16.6 33.8 %collective-permute-start.6 = (s32[8,384]{1,0:T(8,128)S(1)}, s32[8,384]{1,0:T(8,128)S(1)}, u32[]{:S(2)}, u32[]{:S(2)}) collective-permute-start(s32[8,384]{1,0:T(8,128)S(1)} %get-tuple-element.42.refs_0_.refs_4_), channel_id=1, source_target_pairs={{0,8},{1,9},{2,10},{3,11},{4,12},{5,13},{6,14},{7,15},{8,0},{9,1},... | collective-permute-start | bytes 36872 | tf_op jit(solution)/shard_map/ppermute | solution.py:91
  16.9 33.4 %collective-permute-start.9 = (s32[8,384]{1,0:T(8,128)S(1)}, s32[8,384]{1,0:T(8,128)S(1)}, u32[]{:S(2)}, u32[]{:S(2)}) collective-permute-start(s32[8,384]{1,0:T(8,128)S(1)} %collective-permute-done.5.refs_2_.refs_10_), channel_id=1, source_target_pairs={{0,8},{1,9},{2,10},{3,11},{4,12},{5,13},{6,14},{7,15},{8,0},{9,1},... | collective-permute-start | bytes 36872 | tf_op jit(solution)/shard_map/ppermute | solution.py:91
  23.6 40.0 %all-to-all-start.1 = ((bf16[32,64,256]{2,1,0:T(8,128)(2,1)}), bf16[32,64,256]{2,1,0:T(8,128)(2,1)S(1)}, u32[]{:S(2)}, u32[]{:S(2)}) async-start(bf16[32,64,256]{2,1,0:T(8,128)(2,1)} %bitcast.3), calls=%async_computation.1 | async-start | bytes 2097152 | tf_op jit(solution)/shard_map/all_to_all | solution.py:471
  27.5 10.5 %collective-permute-start.12 = (s32[1,2048]{1,0:T(1,128)S(1)}, s32[1,2048]{1,0:T(1,128)S(1)}, u32[]{:S(2)}, u32[]{:S(2)}) collective-permute-start(s32[1,2048]{1,0:T(1,128)S(1)} %reshape.20.refs_0_.label_ref), channel_id=1, source_target_pairs={{0,17},{1,16},{2,19},{3,18},{4,21},{5,20},{6,23},{7,22},{8,25},{9,... | collective-permute-start | bytes 24584 | tf_op jit(solution)/shard_map/ppermute | solution.py:91
  30.1 7.9 %collective-permute-start.11 = (s32[1,2048]{1,0:T(1,128)S(1)}, s32[1,2048]{1,0:T(1,128)S(1)}, u32[]{:S(2)}, u32[]{:S(2)}) collective-permute-start(s32[1,2048]{1,0:T(1,128)S(1)} %reshape.20.refs_0_.label_ref), channel_id=1, source_target_pairs={{0,16},{1,17},{2,18},{3,19},{4,20},{5,21},{6,22},{7,23},{8,24},{9,... | collective-permute-start | bytes 24584 | tf_op jit(solution)/shard_map/ppermute | solution.py:91
  30.7 7.9 %collective-permute-start.10 = (s32[1,2048]{1,0:T(1,128)S(1)}, s32[1,2048]{1,0:T(1,128)S(1)}, u32[]{:S(2)}, u32[]{:S(2)}) collective-permute-start(s32[1,2048]{1,0:T(1,128)S(1)} %reshape.20.refs_0_.label_ref), channel_id=1, source_target_pairs={{0,1},{1,0},{2,3},{3,2},{4,5},{5,4},{6,7},{7,6},{8,9},{9,8},{10,11... | collective-permute-start | bytes 24584 | tf_op jit(solution)/shard_map/ppermute | solution.py:91
  38.0 12.3 %collective-permute-start.8 = (s32[8,384]{1,0:T(8,128)S(1)}, s32[8,384]{1,0:T(8,128)S(1)}, u32[]{:S(2)}, u32[]{:S(2)}) collective-permute-start(s32[8,384]{1,0:T(8,128)S(1)} %collective-permute-done.4.refs_1_.refs_8_), channel_id=1, source_target_pairs={{0,8},{1,9},{2,10},{3,11},{4,12},{5,13},{6,14},{7,15},{8,0},{9,1},... | collective-permute-start | bytes 36872 | tf_op jit(solution)/shard_map/ppermute | solution.py:91
  38.0 12.3 %collective-permute-start.7 = (s32[8,384]{1,0:T(8,128)S(1)}, s32[8,384]{1,0:T(8,128)S(1)}, u32[]{:S(2)}, u32[]{:S(2)}) collective-permute-start(s32[8,384]{1,0:T(8,128)S(1)} %collective-permute-done.3.refs_0_.refs_6_), channel_id=1, source_target_pairs={{0,8},{1,9},{2,10},{3,11},{4,12},{5,13},{6,14},{7,15},{8,0},{9,1},... | collective-permute-start | bytes 36872 | tf_op jit(solution)/shard_map/ppermute | solution.py:91
  64.3 8.3 %collective-permute-start.18 = (bf16[256,256]{1,0:T(8,128)(2,1)S(1)}, bf16[256,256]{1,0:T(8,128)(2,1)S(1)}, u32[]{:S(2)}, u32[]{:S(2)}) collective-permute-start(bf16[256,256]{1,0:T(8,128)(2,1)S(1)} %get-tuple-element.53.refs_2_), channel_id=1, source_target_pairs={{0,2},{1,3},{2,4},{3,5},{4,6},{5,7},{6,0},{7,1},{8,10},{9,11},{10,... | collective-permute-start | bytes 393224 | tf_op jit(solution)/shard_map/ppermute | solution.py:91
  66.1 11.4 %collective-permute-start.16 = (bf16[256,256]{1,0:T(8,128)(2,1)S(1)}, bf16[256,256]{1,0:T(8,128)(2,1)S(1)}, u32[]{:S(2)}, u32[]{:S(2)}) collective-permute-start(bf16[256,256]{1,0:T(8,128)(2,1)S(1)} %get-tuple-element.53.refs_2_), channel_id=1, source_target_pairs={{0,4},{1,5},{2,6},{3,7},{4,0},{5,1},{6,2},{7,3},{8,12},{9,13},{10,... | collective-permute-start | bytes 393224 | tf_op jit(solution)/shard_map/ppermute | solution.py:91
  68.5 8.9 %collective-permute-start.14 = (bf16[256,256]{1,0:T(8,128)(2,1)S(1)}, bf16[256,256]{1,0:T(8,128)(2,1)S(1)}, u32[]{:S(2)}, u32[]{:S(2)}) collective-permute-start(bf16[256,256]{1,0:T(8,128)(2,1)S(1)} %get-tuple-element.53.refs_2_), channel_id=1, source_target_pairs={{0,6},{1,7},{2,0},{3,1},{4,2},{5,3},{6,4},{7,5},{8,14},{9,15},{10,... | collective-permute-start | bytes 393224 | tf_op jit(solution)/shard_map/ppermute | solution.py:91
  70.0 8.0 %collective-permute-start.13 = (bf16[256,256]{1,0:T(8,128)(2,1)S(1)}, bf16[256,256]{1,0:T(8,128)(2,1)S(1)}, u32[]{:S(2)}, u32[]{:S(2)}) collective-permute-start(bf16[256,256]{1,0:T(8,128)(2,1)S(1)} %get-tuple-element.53.refs_2_), channel_id=1, source_target_pairs={{0,8},{1,9},{2,10},{3,11},{4,12},{5,13},{6,14},{7,15},{8,0},{9,1},... | collective-permute-start | bytes 393224 | tf_op jit(solution)/shard_map/ppermute | solution.py:91
  72.6 5.3 %collective-permute-start.19 = (bf16[256,256]{1,0:T(8,128)(2,1)S(1)}, bf16[256,256]{1,0:T(8,128)(2,1)S(1)}, u32[]{:S(2)}, u32[]{:S(2)}) collective-permute-start(bf16[256,256]{1,0:T(8,128)(2,1)S(1)} %collective-permute-done.18.refs_8_), channel_id=1, source_target_pairs={{0,8},{1,9},{2,10},{3,11},{4,12},{5,13},{6,14},{7,15},{8,0},{9,1},... | collective-permute-start | bytes 393224 | tf_op jit(solution)/shard_map/ppermute | solution.py:91
  84.7 5.7 %collective-permute-start.20 = (bf16[256,256]{1,0:T(8,128)(2,1)S(1)}, bf16[256,256]{1,0:T(8,128)(2,1)S(1)}, u32[]{:S(2)}, u32[]{:S(2)}) collective-permute-start(bf16[256,256]{1,0:T(8,128)(2,1)S(1)} %get-tuple-element.55), channel_id=1, source_target_pairs={{0,1},{1,0},{2,3},{3,2},{4,5},{5,4},{6,7},{7,6},{8,9},{9,8},{10,11... | collective-permute-start | bytes 393224 | tf_op jit(solution)/shard_map/ppermute | solution.py:91
  86.3 6.4 %collective-permute-start.21 = (bf16[256,256]{1,0:T(8,128)(2,1)S(1)}, bf16[256,256]{1,0:T(8,128)(2,1)S(1)}, u32[]{:S(2)}, u32[]{:S(2)}) collective-permute-start(bf16[256,256]{1,0:T(8,128)(2,1)S(1)} %get-tuple-element.56), channel_id=1, source_target_pairs={{0,16},{1,17},{2,18},{3,19},{4,20},{5,21},{6,22},{7,23},{8,24},{9,... | collective-permute-start | bytes 393224 | tf_op jit(solution)/shard_map/ppermute | solution.py:91
  87.7 6.7 %collective-permute-start.22 = (bf16[256,256]{1,0:T(8,128)(2,1)S(1)}, bf16[256,256]{1,0:T(8,128)(2,1)S(1)}, u32[]{:S(2)}, u32[]{:S(2)}) collective-permute-start(bf16[256,256]{1,0:T(8,128)(2,1)S(1)} %get-tuple-element.57), channel_id=1, source_target_pairs={{0,17},{1,16},{2,19},{3,18},{4,21},{5,20},{6,23},{7,22},{8,25},{9,... | collective-permute-start | bytes 393224 | tf_op jit(solution)/shard_map/ppermute | solution.py:91
  94.5 8.9 %collective-permute-start.28 = (bf16[256,256]{1,0:T(8,128)(2,1)S(1)}, bf16[256,256]{1,0:T(8,128)(2,1)S(1)}, u32[]{:S(2)}, u32[]{:S(2)}) collective-permute-start(bf16[256,256]{1,0:T(8,128)(2,1)S(1)} %shard_map.66.refs_1_.potential_ref), channel_id=1, source_target_pairs={{0,2},{1,3},{2,4},{3,5},{4,6},{5,7},{6,0},{7,1},{8,10},{9,11},{10,... | collective-permute-start | bytes 393224 | tf_op jit(solution)/shard_map/ppermute | solution.py:91
  97.5 10.3 %collective-permute-start.26 = (bf16[256,256]{1,0:T(8,128)(2,1)S(1)}, bf16[256,256]{1,0:T(8,128)(2,1)S(1)}, u32[]{:S(2)}, u32[]{:S(2)}) collective-permute-start(bf16[256,256]{1,0:T(8,128)(2,1)S(1)} %shard_map.66.refs_1_.potential_ref), channel_id=1, source_target_pairs={{0,4},{1,5},{2,6},{3,7},{4,0},{5,1},{6,2},{7,3},{8,12},{9,13},{10,... | collective-permute-start | bytes 393224 | tf_op jit(solution)/shard_map/ppermute | solution.py:91
  99.5 8.3 %collective-permute-start.24 = (bf16[256,256]{1,0:T(8,128)(2,1)S(1)}, bf16[256,256]{1,0:T(8,128)(2,1)S(1)}, u32[]{:S(2)}, u32[]{:S(2)}) collective-permute-start(bf16[256,256]{1,0:T(8,128)(2,1)S(1)} %shard_map.66.refs_1_.potential_ref), channel_id=1, source_target_pairs={{0,6},{1,7},{2,0},{3,1},{4,2},{5,3},{6,4},{7,5},{8,14},{9,15},{10,... | collective-permute-start | bytes 393224 | tf_op jit(solution)/shard_map/ppermute | solution.py:91
  99.9 8.4 %collective-permute-start.23 = (bf16[256,256]{1,0:T(8,128)(2,1)S(1)}, bf16[256,256]{1,0:T(8,128)(2,1)S(1)}, u32[]{:S(2)}, u32[]{:S(2)}) collective-permute-start(bf16[256,256]{1,0:T(8,128)(2,1)S(1)} %shard_map.66.refs_1_.potential_ref), channel_id=1, source_target_pairs={{0,8},{1,9},{2,10},{3,11},{4,12},{5,13},{6,14},{7,15},{8,0},{9,1},... | collective-permute-start | bytes 393224 | tf_op jit(solution)/shard_map/ppermute | solution.py:91
  111.8 5.7 %collective-permute-start.33 = (bf16[256,256]{1,0:T(8,128)(2,1)S(1)}, bf16[256,256]{1,0:T(8,128)(2,1)S(1)}, u32[]{:S(2)}, u32[]{:S(2)}) collective-permute-start(bf16[256,256]{1,0:T(8,128)(2,1)S(1)} %get-tuple-element.67), channel_id=1, source_target_pairs={{0,1},{1,0},{2,3},{3,2},{4,5},{5,4},{6,7},{7,6},{8,9},{9,8},{10,11... | collective-permute-start | bytes 393224 | tf_op jit(solution)/shard_map/ppermute | solution.py:91
  113.0 6.4 %collective-permute-start.34 = (bf16[256,256]{1,0:T(8,128)(2,1)S(1)}, bf16[256,256]{1,0:T(8,128)(2,1)S(1)}, u32[]{:S(2)}, u32[]{:S(2)}) collective-permute-start(bf16[256,256]{1,0:T(8,128)(2,1)S(1)} %get-tuple-element.68), channel_id=1, source_target_pairs={{0,16},{1,17},{2,18},{3,19},{4,20},{5,21},{6,22},{7,23},{8,24},{9,... | collective-permute-start | bytes 393224 | tf_op jit(solution)/shard_map/ppermute | solution.py:91
  114.5 7.0 %collective-permute-start.35 = (bf16[256,256]{1,0:T(8,128)(2,1)S(1)}, bf16[256,256]{1,0:T(8,128)(2,1)S(1)}, u32[]{:S(2)}, u32[]{:S(2)}) collective-permute-start(bf16[256,256]{1,0:T(8,128)(2,1)S(1)} %get-tuple-element.69), channel_id=1, source_target_pairs={{0,17},{1,16},{2,19},{3,18},{4,21},{5,20},{6,23},{7,22},{8,25},{9,... | collective-permute-start | bytes 393224 | tf_op jit(solution)/shard_map/ppermute | solution.py:91
  122.9 8.3 %collective-permute-start.41 = (bf16[256,256]{1,0:T(8,128)(2,1)S(1)}, bf16[256,256]{1,0:T(8,128)(2,1)S(1)}, u32[]{:S(2)}, u32[]{:S(2)}) collective-permute-start(bf16[256,256]{1,0:T(8,128)(2,1)S(1)} %get-tuple-element.70.refs_2_), channel_id=1, source_target_pairs={{0,2},{1,3},{2,4},{3,5},{4,6},{5,7},{6,0},{7,1},{8,10},{9,11},{10,... | collective-permute-start | bytes 393224 | tf_op jit(solution)/shard_map/ppermute | solution.py:91
  125.8 9.4 %collective-permute-start.39 = (bf16[256,256]{1,0:T(8,128)(2,1)S(1)}, bf16[256,256]{1,0:T(8,128)(2,1)S(1)}, u32[]{:S(2)}, u32[]{:S(2)}) collective-permute-start(bf16[256,256]{1,0:T(8,128)(2,1)S(1)} %get-tuple-element.70.refs_2_), channel_id=1, source_target_pairs={{0,4},{1,5},{2,6},{3,7},{4,0},{5,1},{6,2},{7,3},{8,12},{9,13},{10,... | collective-permute-start | bytes 393224 | tf_op jit(solution)/shard_map/ppermute | solution.py:91
  127.0 8.5 %collective-permute-start.37 = (bf16[256,256]{1,0:T(8,128)(2,1)S(1)}, bf16[256,256]{1,0:T(8,128)(2,1)S(1)}, u32[]{:S(2)}, u32[]{:S(2)}) collective-permute-start(bf16[256,256]{1,0:T(8,128)(2,1)S(1)} %get-tuple-element.70.refs_2_), channel_id=1, source_target_pairs={{0,6},{1,7},{2,0},{3,1},{4,2},{5,3},{6,4},{7,5},{8,14},{9,15},{10,... | collective-permute-start | bytes 393224 | tf_op jit(solution)/shard_map/ppermute | solution.py:91
  128.2 11.3 %collective-permute-start.36 = (bf16[256,256]{1,0:T(8,128)(2,1)S(1)}, bf16[256,256]{1,0:T(8,128)(2,1)S(1)}, u32[]{:S(2)}, u32[]{:S(2)}) collective-permute-start(bf16[256,256]{1,0:T(8,128)(2,1)S(1)} %get-tuple-element.70.refs_2_), channel_id=1, source_target_pairs={{0,8},{1,9},{2,10},{3,11},{4,12},{5,13},{6,14},{7,15},{8,0},{9,1},... | collective-permute-start | bytes 393224 | tf_op jit(solution)/shard_map/ppermute | solution.py:91
  131.3 9.8 %collective-permute-start.42 = (bf16[256,256]{1,0:T(8,128)(2,1)S(1)}, bf16[256,256]{1,0:T(8,128)(2,1)S(1)}, u32[]{:S(2)}, u32[]{:S(2)}) collective-permute-start(bf16[256,256]{1,0:T(8,128)(2,1)S(1)} %collective-permute-done.41.refs_8_), channel_id=1, source_target_pairs={{0,8},{1,9},{2,10},{3,11},{4,12},{5,13},{6,14},{7,15},{8,0},{9,1},... | collective-permute-start | bytes 393224 | tf_op jit(solution)/shard_map/ppermute | solution.py:91
  135.3 6.5 %collective-permute-start.40 = (bf16[256,256]{1,0:T(8,128)(2,1)S(1)}, bf16[256,256]{1,0:T(8,128)(2,1)S(1)}, u32[]{:S(2)}, u32[]{:S(2)}) collective-permute-start(bf16[256,256]{1,0:T(8,128)(2,1)S(1)} %collective-permute-done.39.refs_6_), channel_id=1, source_target_pairs={{0,8},{1,9},{2,10},{3,11},{4,12},{5,13},{6,14},{7,15},{8,0},{9,1},... | collective-permute-start | bytes 393224 | tf_op jit(solution)/shard_map/ppermute | solution.py:91
  135.4 6.4 %collective-permute-start.38 = (bf16[256,256]{1,0:T(8,128)(2,1)S(1)}, bf16[256,256]{1,0:T(8,128)(2,1)S(1)}, u32[]{:S(2)}, u32[]{:S(2)}) collective-permute-start(bf16[256,256]{1,0:T(8,128)(2,1)S(1)} %collective-permute-done.37.refs_4_), channel_id=1, source_target_pairs={{0,8},{1,9},{2,10},{3,11},{4,12},{5,13},{6,14},{7,15},{8,0},{9,1},... | collective-permute-start | bytes 393224 | tf_op jit(solution)/shard_map/ppermute | solution.py:91
  138.2 9.8 %collective-permute-start.30 = (bf16[384,256]{1,0:T(8,128)(2,1)S(1)}, bf16[384,256]{1,0:T(8,128)(2,1)S(1)}, u32[]{:S(2)}, u32[]{:S(2)}) collective-permute-start(bf16[384,256]{1,0:T(8,128)(2,1)S(1)} %get-tuple-element.59), channel_id=1, source_target_pairs={{0,1},{1,0},{2,3},{3,2},{4,5},{5,4},{6,7},{7,6},{8,9},{9,8},{10,11... | collective-permute-start | bytes 589832 | tf_op jit(solution)/shard_map/ppermute | solution.py:91
  139.5 9.3 %collective-permute-start.31 = (bf16[384,256]{1,0:T(8,128)(2,1)S(1)}, bf16[384,256]{1,0:T(8,128)(2,1)S(1)}, u32[]{:S(2)}, u32[]{:S(2)}) collective-permute-start(bf16[384,256]{1,0:T(8,128)(2,1)S(1)} %get-tuple-element.60), channel_id=1, source_target_pairs={{0,16},{1,17},{2,18},{3,19},{4,20},{5,21},{6,22},{7,23},{8,24},{9,... | collective-permute-start | bytes 589832 | tf_op jit(solution)/shard_map/ppermute | solution.py:91
  141.0 10.8 %collective-permute-start.32 = (bf16[384,256]{1,0:T(8,128)(2,1)S(1)}, bf16[384,256]{1,0:T(8,128)(2,1)S(1)}, u32[]{:S(2)}, u32[]{:S(2)}) collective-permute-start(bf16[384,256]{1,0:T(8,128)(2,1)S(1)} %get-tuple-element.61), channel_id=1, source_target_pairs={{0,17},{1,16},{2,19},{3,18},{4,21},{5,20},{6,23},{7,22},{8,25},{9,... | collective-permute-start | bytes 589832 | tf_op jit(solution)/shard_map/ppermute | solution.py:91
  145.3 8.9 %collective-permute-start.43 = (bf16[256,256]{1,0:T(8,128)(2,1)S(1)}, bf16[256,256]{1,0:T(8,128)(2,1)S(1)}, u32[]{:S(2)}, u32[]{:S(2)}) collective-permute-start(bf16[256,256]{1,0:T(8,128)(2,1)S(1)} %get-tuple-element.73), channel_id=1, source_target_pairs={{0,1},{1,0},{2,3},{3,2},{4,5},{5,4},{6,7},{7,6},{8,9},{9,8},{10,11... | collective-permute-start | bytes 393224 | tf_op jit(solution)/shard_map/ppermute | solution.py:91
  146.6 7.8 %collective-permute-start.44 = (bf16[256,256]{1,0:T(8,128)(2,1)S(1)}, bf16[256,256]{1,0:T(8,128)(2,1)S(1)}, u32[]{:S(2)}, u32[]{:S(2)}) collective-permute-start(bf16[256,256]{1,0:T(8,128)(2,1)S(1)} %get-tuple-element.74), channel_id=1, source_target_pairs={{0,16},{1,17},{2,18},{3,19},{4,20},{5,21},{6,22},{7,23},{8,24},{9,... | collective-permute-start | bytes 393224 | tf_op jit(solution)/shard_map/ppermute | solution.py:91
  148.1 8.3 %collective-permute-start.45 = (bf16[256,256]{1,0:T(8,128)(2,1)S(1)}, bf16[256,256]{1,0:T(8,128)(2,1)S(1)}, u32[]{:S(2)}, u32[]{:S(2)}) collective-permute-start(bf16[256,256]{1,0:T(8,128)(2,1)S(1)} %get-tuple-element.75), channel_id=1, source_target_pairs={{0,17},{1,16},{2,19},{3,18},{4,21},{5,20},{6,23},{7,22},{8,25},{9,... | collective-permute-start | bytes 393224 | tf_op jit(solution)/shard_map/ppermute | solution.py:91
  157.0 8.7 %collective-permute-start.51 = (bf16[256,256]{1,0:T(8,128)(2,1)}, bf16[256,256]{1,0:T(8,128)(2,1)S(1)}, u32[]{:S(2)}, u32[]{:S(2)}) collective-permute-start(bf16[256,256]{1,0:T(8,128)(2,1)} %shard_map.72.refs_1_), channel_id=1, source_target_pairs={{0,2},{1,3},{2,4},{3,5},{4,6},{5,7},{6,0},{7,1},{8,10},{9,11},{10,... | collective-permute-start | bytes 393224 | tf_op jit(solution)/shard_map/ppermute | solution.py:91
  160.2 9.6 %collective-permute-start.49 = (bf16[256,256]{1,0:T(8,128)(2,1)}, bf16[256,256]{1,0:T(8,128)(2,1)S(1)}, u32[]{:S(2)}, u32[]{:S(2)}) collective-permute-start(bf16[256,256]{1,0:T(8,128)(2,1)} %shard_map.72.refs_1_), channel_id=1, source_target_pairs={{0,4},{1,5},{2,6},{3,7},{4,0},{5,1},{6,2},{7,3},{8,12},{9,13},{10,... | collective-permute-start | bytes 393224 | tf_op jit(solution)/shard_map/ppermute | solution.py:91
  161.6 8.2 %collective-permute-start.47 = (bf16[256,256]{1,0:T(8,128)(2,1)}, bf16[256,256]{1,0:T(8,128)(2,1)S(1)}, u32[]{:S(2)}, u32[]{:S(2)}) collective-permute-start(bf16[256,256]{1,0:T(8,128)(2,1)} %shard_map.72.refs_1_), channel_id=1, source_target_pairs={{0,6},{1,7},{2,0},{3,1},{4,2},{5,3},{6,4},{7,5},{8,14},{9,15},{10,... | collective-permute-start | bytes 393224 | tf_op jit(solution)/shard_map/ppermute | solution.py:91
  162.5 7.8 %collective-permute-start.46 = (bf16[256,256]{1,0:T(8,128)(2,1)}, bf16[256,256]{1,0:T(8,128)(2,1)S(1)}, u32[]{:S(2)}, u32[]{:S(2)}) collective-permute-start(bf16[256,256]{1,0:T(8,128)(2,1)} %shard_map.72.refs_1_), channel_id=1, source_target_pairs={{0,8},{1,9},{2,10},{3,11},{4,12},{5,13},{6,14},{7,15},{8,0},{9,1},... | collective-permute-start | bytes 393224 | tf_op jit(solution)/shard_map/ppermute | solution.py:91
  175.2 7.1 %collective-permute-start.53 = (bf16[384,256]{1,0:T(8,128)(2,1)S(1)}, bf16[384,256]{1,0:T(8,128)(2,1)S(1)}, u32[]{:S(2)}, u32[]{:S(2)}) collective-permute-start(bf16[384,256]{1,0:T(8,128)(2,1)S(1)} %get-tuple-element.78), channel_id=1, source_target_pairs={{0,1},{1,0},{2,3},{3,2},{4,5},{5,4},{6,7},{7,6},{8,9},{9,8},{10,11... | collective-permute-start | bytes 589832 | tf_op jit(solution)/shard_map/ppermute | solution.py:91
  176.5 7.8 %collective-permute-start.54 = (bf16[384,256]{1,0:T(8,128)(2,1)S(1)}, bf16[384,256]{1,0:T(8,128)(2,1)S(1)}, u32[]{:S(2)}, u32[]{:S(2)}) collective-permute-start(bf16[384,256]{1,0:T(8,128)(2,1)S(1)} %get-tuple-element.79), channel_id=1, source_target_pairs={{0,16},{1,17},{2,18},{3,19},{4,20},{5,21},{6,22},{7,23},{8,24},{9,... | collective-permute-start | bytes 589832 | tf_op jit(solution)/shard_map/ppermute | solution.py:91
  178.0 9.8 %collective-permute-start.55 = (bf16[384,256]{1,0:T(8,128)(2,1)S(1)}, bf16[384,256]{1,0:T(8,128)(2,1)S(1)}, u32[]{:S(2)}, u32[]{:S(2)}) collective-permute-start(bf16[384,256]{1,0:T(8,128)(2,1)S(1)} %get-tuple-element.80), channel_id=1, source_target_pairs={{0,17},{1,16},{2,19},{3,18},{4,21},{5,20},{6,23},{7,22},{8,25},{9,... | collective-permute-start | bytes 589832 | tf_op jit(solution)/shard_map/ppermute | solution.py:91
  (25 other events, 161.3 us)

commit v5 on v4

--- a/solution.py
+++ b/solution.py
@@ -84,10 +84,7 @@
     def shift(self, value, dx=0, dc=0, dz=0, dy=0):
         pairs = []
         for i in range(self.devices):
-            x, c, z, y = self.digits(i)
-            x, c = (x + dx) % self.x, (c + dc) % self.core
-            z, y = (z + dz) % self.z, (y + dy) % self.y
-            pairs.append((i, ((x * self.core + c) * self.z + z) * self.y + y))
+            pairs.append((i, self.near(i, dx, dc, dz, dy)))
         return lax.ppermute(value, AXES, pairs)
 
     def along(self, value):
@@ -100,8 +97,17 @@
             pieces += [self.shift(value, dc=-dc) for dc in range(1, self.core)]
         return pieces
 
-    def across(self, value):
-        return [value] + [self.shift(value, dx=-dx, dy=-dy) for dx, dy in self.plane[1:]]
+    def index(self, x, core, z, y):
+        x, core, z, y = x % self.x, core % self.core, z % self.z, y % self.y
+        return ((x * self.core + core) * self.z + z) * self.y + y
+
+    def near(self, me, dx=0, dc=0, dz=0, dy=0):
+        x, core, z, y = self.digits(me)
+        return self.index(x + dx, core + dc, z + dz, y + dy)
+
+    def spot(self, me, step):
+        x, _, _, y = self.digits(me)
+        return (x + step // self.y) % self.x * self.y + (y + step % self.y) % self.y
 
     def given(self, blocks):
         return [blocks[0]] + [
@@ -117,12 +123,43 @@
         return jnp.where(inside, block * tri_dev + triangle % tri_dev, -1)
 
 
-def number_kernel(slots, inc_ref, points_ref, label_ref, slot_ref, number_ref):
-    edges, tri_dev = inc_ref.shape[1], points_ref.shape[1]
-    ends, devices = 2 * edges, label_ref.shape[0]
-    number_ref[...] = jnp.zeros(number_ref.shape, I32)
-    number_ref[0:2, :edges] = inc_ref[...]
-    number_ref[2:5, :tri_dev] = points_ref[...]
+class Letter:
+    def __init__(self, edges, tri_dev, labels):
+        self.edges, self.tri_dev, self.half = edges, tri_dev, -(-tri_dev // 2)
+        sizes = [edges, tri_dev, self.half, labels]
+        starts = [0]
+        for size in sizes:
+            starts.append(starts[-1] + -(-size // 128))
+        self.starts, self.rows = starts[:4], -(-starts[4] // 8) * 8
+
+    def take(self, letter, part, size):
+        first = self.starts[part]
+        parts = [letter[first + k : first + k + 1, :] for k in range(-(-size // 128))]
+        return jnp.concatenate(parts, axis=1)[:, :size]
+
+    def ends(self, letter):
+        pair = self.take(letter, 0, self.edges)
+        return pair & 0xFFFF, lax.shift_right_logical(pair, 16)
+
+    def points(self, letter):
+        first = self.take(letter, 1, self.tri_dev)
+        third = self.take(letter, 2, self.half)
+        third = jnp.concatenate([third & 0xFFFF, lax.shift_right_logical(third, 16)], axis=1)
+        return jnp.concatenate(
+            [first & 0xFFFF, lax.shift_right_logical(first, 16), third[:, : self.tri_dev]], axis=0
+        )
+
+
+def in_rows(row):
+    size = row.shape[1]
+    if size % 128:
+        row = jnp.concatenate([row, jnp.zeros((1, -size % 128), I32)], axis=1)
+    return [row[:, k : k + 128] for k in range(0, row.shape[1], 128)]
+
+
+def letter_kernel(layout, form, slots, inc_ref, points_ref, letter_ref, slot_ref):
+    edges, tri_dev, half = form.edges, form.tri_dev, form.half
+    ends, devices = 2 * edges, layout.devices
     plus, minus = inc_ref[0:1, :], inc_ref[1:2, :]
     tri = jnp.concatenate([plus, minus], axis=1)
     other = jnp.concatenate([minus, plus], axis=1)
@@ -134,28 +171,38 @@
     slot_ref[...] = owner * slots + rank
     order = ones_where(iota((slots, ends), 0) == rank)
     label = jnp.zeros((devices, slots), I32)
-    digits = (
-        (tri % tri_dev + 1, 1),
-        (other & 255, 2 * tri_dev),
-        (other >> 8, 512 * tri_dev),
-    )
+    digits = ((tri % tri_dev + 1, 1), (other & 255, 65536), (other >> 8, 65536 * 256))
     for digit, weight in digits:
         spread = jnp.where(hits, digit.astype(F32), 0.0).astype(BF16)
         label = label + matmul_nt(spread, order).astype(I32) * weight
-    label_ref[...] = label
-
-
-def number(incidence, centroids, slots, devices):
-    edges = incidence.shape[1]
-    lanes = max(edges, centroids.shape[1])
-    return pl.pallas_call(
-        functools.partial(number_kernel, slots),
+    third = points_ref[2:3, :]
+    if tri_dev % 2:
+        third = jnp.concatenate([third, jnp.zeros((1, 1), I32)], axis=1)
+    common = (
+        in_rows(plus + (minus << 16))
+        + in_rows(points_ref[0:1, :] + (points_ref[1:2, :] << 16))
+        + in_rows(third[:, :half] + (third[:, half:] << 16))
+    )
+    places = [(x, y) for x in range(layout.x) for y in range(layout.y)]
+    for core in range(layout.core):
+        for z in range(layout.z):
+            there = [layout.index(x, core, z, y) for x, y in places]
+            mine = in_rows(jnp.concatenate([label[d : d + 1, :] for d in there], axis=1))
+            blank = form.rows - len(common) - len(mine)
+            rows = common + mine + [jnp.zeros((1, 128), I32)] * blank
+            letter = jnp.concatenate(rows, axis=0)
+            for d in there:
+                letter_ref[d] = letter
+
+
+def letters_of(layout, form, incidence, centroids, slots):
+    return pl.pallas_call(
+        functools.partial(letter_kernel, layout, form, slots),
         in_specs=[whole()] * 2,
-        out_specs=[whole()] * 3,
+        out_specs=[whole()] * 2,
         out_shape=[
-            jax.ShapeDtypeStruct((devices, slots), I32),
-            jax.ShapeDtypeStruct((1, 2 * edges), I32),
-            jax.ShapeDtypeStruct((8, lanes), I32),
+            jax.ShapeDtypeStruct((layout.devices, form.rows, 128), I32),
+            jax.ShapeDtypeStruct((1, 2 * form.edges), I32),
         ],
         compiler_params=PARAMS,
         cost_estimate=cost(1),
@@ -205,19 +252,19 @@
     return value
 
 
-def tile_kernel(count, block, tri_dev, *refs):
-    plane, line = refs[:count], refs[count:-6]
-    real_ref, imag_ref, token_ref, row_ref, col_ref = refs[-5:]
+def tile_kernel(layout, form, block, me_ref, letter_ref, after_ref, *refs):
+    real_ref, imag_ref, token_ref, col_ref = refs
     token_ref[...] = jnp.zeros_like(token_ref)
-
-    @pl.when(pl.program_id(0) == 0)
+    me, step, size = me_ref[0], pl.program_id(0), form.tri_dev
+
+    @pl.when(step == 0)
     def _():
-        for k, ref in enumerate(plane):
-            row_ref[k] = features(ref[2:5, :tri_dev], 1.0 / (TURNS * TURNS), True)
-        for k, ref in enumerate(line):
-            col_ref[:, k * tri_dev : (k + 1) * tri_dev] = features(ref[2:5, :tri_dev], 1.0, False)
-
-    row = row_ref[pl.program_id(0)]
+        for k in range(layout.z * layout.core):
+            letter = letter_ref[layout.near(me, dz=k // layout.core, dc=k % layout.core)]
+            col_ref[:, k * size : (k + 1) * size] = features(form.points(letter), 1.0, False)
+
+    letter = letter_ref[layout.near(me, dx=step // layout.y, dy=step % layout.y)]
+    row = features(form.points(letter), 1.0 / (TURNS * TURNS), True)
     for base in range(0, col_ref.shape[1], block):
         cols = slice(base, base + block)
         square = lax.dot_general(
@@ -231,19 +278,22 @@
         imag_ref[:, cols] = (poly(SIN, -SPACING / TURNS, u) * (frac * inverse)).astype(BF16)
 
 
-def build_tiles(plane, line, tri_dev, after):
-    count, cols = len(plane), len(line) * tri_dev
-    shape = plane[0].shape
-    return pl.pallas_call(
-        functools.partial(tile_kernel, count, min(512, cols), tri_dev),
+def fixed(array):
+    return pl.BlockSpec(array.shape, lambda j: (0,) * array.ndim)
+
+
+def build(kernel, outs, rows, layout, cols, me, arrays, time, scratch=()):
+    count = len(layout.plane)
+    return pl.pallas_call(
+        kernel,
         grid=(count,),
-        in_specs=[pl.BlockSpec(shape, lambda i: (0, 0))] * (count + len(line)) + [token_spec()],
-        out_specs=[pl.BlockSpec((tri_dev, cols), lambda i: (i, 0))] * 2 + [token_spec()],
-        out_shape=[jax.ShapeDtypeStruct((count * tri_dev, cols), BF16)] * 2 + [TOKEN],
-        scratch_shapes=[pltpu.VMEM((count, 16, tri_dev), BF16), pltpu.VMEM((16, cols), BF16)],
-        compiler_params=PARAMS,
-        cost_estimate=cost(12),
-    )(*plane, *line, after)
+        in_specs=[pl.BlockSpec(memory_space=pltpu.SMEM)] + [fixed(array) for array in arrays],
+        out_specs=[pl.BlockSpec((rows, cols), lambda j: (j, 0))] * outs + [token_spec()],
+        out_shape=[pltpu.HBM((count * rows, cols), BF16)] * outs + [TOKEN],
+        scratch_shapes=scratch,
+        compiler_params=PARAMS,
+        cost_estimate=cost(time),
+    )(me, *arrays)
 
 
 def pick(row, base, count):
@@ -253,85 +303,48 @@
     return jnp.where(same, jnp.ones((), BF16), jnp.zeros((), BF16))
 
 
-def adjacency_kernel(layout, tri_dev, me_ref, *refs):
-    labels, (out_ref, token_ref) = refs[:-3], refs[-2:]
+def adjacency_kernel(layout, tri_dev, me_ref, label_ref, after_ref, out_ref, token_ref):
     token_ref[...] = jnp.zeros_like(token_ref)
+    me = me_ref[0]
     rows, cols = out_ref.shape
-    for k, label_ref in enumerate(labels):
-
-        @pl.when(pl.program_id(0) == k)
-        def _(label_ref=label_ref):
-            label = label_ref[...]
-            mark = label % (2 * tri_dev) - 1
-            place = layout.place(label // (2 * tri_dev), tri_dev, me_ref[0])
-            place = jnp.where(mark >= 0, place, -1)
-            low = pick(jnp.where(place >= 0, place % rows, -1), 0, rows)
-            for base in range(0, cols, rows):
-                inside = (place >= base) & (place < base + rows)
-                here = pick(jnp.where(inside, mark, -1), 0, rows)
-                out_ref[:, base : base + rows] = matmul_nt(here, low).astype(BF16)
-
-
-def build_adjacency(layout, me, labels, rows, cols, after):
-    count, shape = len(labels), labels[0].shape
-    return pl.pallas_call(
-        functools.partial(adjacency_kernel, layout, rows),
-        grid=(count,),
-        in_specs=[pl.BlockSpec(memory_space=pltpu.SMEM)]
-        + [pl.BlockSpec(shape, lambda j: (0, 0))] * count
-        + [token_spec()],
-        out_specs=[pl.BlockSpec((rows, cols), lambda j: (j, 0)), token_spec()],
-        out_shape=[jax.ShapeDtypeStruct((count * rows, cols), BF16), TOKEN],
-        compiler_params=PARAMS,
-        cost_estimate=cost(10),
-    )(me, *labels, after)
-
-
-def incidence_kernel(layout, tri_dev, me_ref, *refs):
-    numbers, (out_ref, token_ref) = refs[:-3], refs[-2:]
+    label = label_ref[layout.spot(me, pl.program_id(0))]
+    mark = (label & 0xFFFF) - 1
+    place = layout.place(lax.shift_right_logical(label, 16), tri_dev, me)
+    place = jnp.where(mark >= 0, place, -1)
+    low = pick(jnp.where(place >= 0, place % rows, -1), 0, rows)
+    for base in range(0, cols, rows):
+        inside = (place >= base) & (place < base + rows)
+        here = pick(jnp.where(inside, mark, -1), 0, rows)
+        out_ref[:, base : base + rows] = matmul_nt(here, low).astype(BF16)
+
+
+def incidence_kernel(layout, form, me_ref, letter_ref, after_ref, out_ref, token_ref):
     token_ref[...] = jnp.zeros_like(token_ref)
+    me, step = me_ref[0], pl.program_id(0)
     edges, cols = out_ref.shape
-    for k, number_ref in enumerate(numbers):
-
-        @pl.when(pl.program_id(0) == k)
-        def _(number_ref=number_ref):
-            places = layout.place(number_ref[0:2, :edges], tri_dev, me_ref[0])
-            plus, minus = places[0:1], places[1:2]
-            eye = ones_where(iota((edges, edges), 0) == iota((edges, edges), 1))
-            for base in range(0, cols, tri_dev):
-                signed = pick(plus, base, tri_dev) - pick(minus, base, tri_dev)
-                out_ref[:, base : base + tri_dev] = matmul_nt(eye, signed).astype(BF16)
-
-
-def build_incidence(layout, me, numbers, edges, tri_dev, cols, after):
-    count, shape = len(numbers), numbers[0].shape
-    return pl.pallas_call(
-        functools.partial(incidence_kernel, layout, tri_dev),
-        grid=(count,),
-        in_specs=[pl.BlockSpec(memory_space=pltpu.SMEM)]
-        + [pl.BlockSpec(shape, lambda j: (0, 0))] * count
-        + [token_spec()],
-        out_specs=[pl.BlockSpec((edges, cols), lambda j: (j, 0)), token_spec()],
-        out_shape=[jax.ShapeDtypeStruct((count * edges, cols), BF16), TOKEN],
-        compiler_params=PARAMS,
-        cost_estimate=cost(6),
-    )(me, *numbers, after)
-
-
-def collect_kernel(tri_dev, label_ref, value_ref, *refs):
+    size = form.tri_dev
+    letter = letter_ref[layout.near(me, dx=step // layout.y, dy=step % layout.y)]
+    plus, minus = [layout.place(end, size, me) for end in form.ends(letter)]
+    eye = ones_where(iota((edges, edges), 0) == iota((edges, edges), 1))
+    for base in range(0, cols, size):
+        signed = pick(plus, base, size) - pick(minus, base, size)
+        out_ref[:, base : base + size] = matmul_nt(eye, signed).astype(BF16)
+
+
+def collect_kernel(layout, tri_dev, me_ref, label_ref, value_ref, *refs):
     charge_ref, rounded_ref, degree_ref = refs[-3:]
-    here = pick(label_ref[...] % (2 * tri_dev) - 1, 0, tri_dev)
+    here = pick((label_ref[layout.spot(me_ref[0], 0)] & 0xFFFF) - 1, 0, tri_dev)
     charge = matmul(here, value_ref[...])
     charge_ref[...] = charge
     rounded_ref[...] = charge.astype(BF16)
     degree_ref[...] = matmul(here, jnp.ones((here.shape[1], degree_ref.shape[1]), BF16))
 
 
-def collect(labels, values, tri_dev, after):
+def collect(layout, me, labels, values, tri_dev, after):
     width = values.shape[1]
     return pl.pallas_call(
-        functools.partial(collect_kernel, tri_dev),
-        in_specs=[whole()] * (2 + len(after)),
+        functools.partial(collect_kernel, layout, tri_dev),
+        in_specs=[pl.BlockSpec(memory_space=pltpu.SMEM)] + [whole()] * (2 + len(after)),
         out_specs=[whole()] * 3,
         out_shape=[
             jax.ShapeDtypeStruct((tri_dev, width), F32),
@@ -340,7 +353,7 @@
         ],
         compiler_params=PARAMS,
         cost_estimate=cost(1),
-    )(labels, values, *after)
+    )(me, labels, values, *after)
 
 
 def apply_kernel(mats, fed, count, *refs):
@@ -464,23 +477,42 @@
     count = len(layout.plane)
     cols = layout.z * layout.core * tri_dev
 
-    labels, slot, numbers = number(incidence, centroids, slots, devices)
-    along = layout.along(numbers)
-    plane = layout.across(numbers)
-    outgoing, token = route(slot, currents, cells, (*along[1:], *plane[1:]))
+    form = Letter(edge_dev, tri_dev, count * slots)
+    letters, slot = letters_of(layout, form, incidence, centroids, slots)
+    letters = lax.all_to_all(letters, AXES, split_axis=0, concat_axis=0, tiled=True)
+    outgoing, token = route(slot, currents, cells, (letters,))
     arrived = lax.all_to_all(
         outgoing.reshape(devices, slots, width), AXES, split_axis=0, concat_axis=0, tiled=True
     ).reshape(cells, width)
-    labels = lax.all_to_all(labels, AXES, split_axis=0, concat_axis=0, tiled=True)
-    labels = labels.reshape(1, cells)
+    labels = letters[:, form.starts[3] :, :].reshape(devices, -1)[:, : count * slots]
+    labels = labels.reshape(devices, count, slots).transpose(1, 0, 2).reshape(count, 1, cells)
     where = me.astype(I32).reshape(1)
-    slopes_of, token_1 = build_incidence(layout, where, plane, edge_dev, tri_dev, cols, token)
-    *tiles, token_2 = build_tiles(plane, layout.swapped(along), tri_dev, token)
-    neighbours, token_3 = build_adjacency(
-        layout, where, layout.across(labels), tri_dev, cols, token
-    )
-
-    charge, rounded, degree = collect(labels, arrived, tri_dev, (token_1, token_2, token_3))
+    make = functools.partial(build, layout=layout, cols=cols, me=where)
+    *tiles, token_1 = make(
+        functools.partial(tile_kernel, layout, form, min(512, cols)),
+        2,
+        tri_dev,
+        arrays=(letters, token),
+        time=12,
+        scratch=[pltpu.VMEM((16, cols), BF16)],
+    )
+    slopes_of, token_2 = make(
+        functools.partial(incidence_kernel, layout, form),
+        1,
+        edge_dev,
+        arrays=(letters, token),
+        time=6,
+    )
+    neighbours, token_3 = make(
+        functools.partial(adjacency_kernel, layout, tri_dev),
+        1,
+        tri_dev,
+        arrays=(labels, token),
+        time=10,
+    )
+    charge, rounded, degree = collect(
+        layout, where, labels, arrived, tri_dev, (token_1, token_2, token_3)
+    )
     current = currents
     potential = None
     slopes, after = None, ()

time: 190 us -> 176 us (0.926)
  starting transfers between devices: 61.8 us -> 50.6 us
  local copies, waits for them, and re-layouts: 14.3 us -> 5.4 us
  Pallas kernels: 46.4 us -> 50.3 us
  waiting for transfers between devices: 65.1 us -> 68.8 us
    ppermute x56 -> x43, starting transfers between devices: 56.2 us -> 40.7 us  [shift(): return lax.ppermute(value, AXES, pairs)]
    unnamed x30 -> x22, local copies, waits for them, and re-layouts: 13.1 us -> 4.52 us
    all_to_all x1, starting transfers between devices: 2.92 us -> 7.3 us  [per_device(): lax.all_to_all(letters, AXES, split_axis=0, concat_axis=0, tiled=True)]
    pallas_call x5, Pallas kernels: 25.2 us -> 29 us  [the longest x3 27.1 us: build(): pl.pallas_call(kernel, grid=(count,), in_specs=[pl.BlockSpec(memory_space...]
    all_to_all x1, waiting for transfers between devices: 4.63 us -> 7.73 us  [per_device(): lax.all_to_all(letters, AXES, split_axis=0, concat_axis=0, tiled=True)]
    ppermute x56 -> x43, waiting for transfers between devices: 60.5 us -> 60.6 us  [shift(): return lax.ppermute(value, AXES, pairs)]
  transfers between devices with their start and end apart: 58 -> 45, of which waited for: 29 -> 30; matrix products, arithmetic and copies ran while one was open for 1% -> 0% of each run, Pallas kernels for 17% -> 19%
where the time goes in v5:
time: 176 us
  waiting for transfers between devices  68.8 us (39%)
  starting transfers between devices  50.6 us (29%)
  Pallas kernels  50.3 us (29%)
  local copies, waits for them, and re-layouts  5.4 us (3%)
    ppermute x43, waiting for transfers between devices, shift(): return lax.ppermute(value, AXES, pairs)  60.6 us
    ppermute x43, starting transfers between devices, shift(): return lax.ppermute(value, AXES, pairs)  40.7 us
    pallas_call x3, Pallas kernels, build(): pl.pallas_call(kernel, grid=(count,), in_specs=[pl.BlockSpec(memory_space...  27.1 us
    pallas_call x5, Pallas kernels, apply(): pl.pallas_call(functools.partial(apply_kernel, len(matrices), len(pieces)...  14.9 us
    all_to_all x1, waiting for transfers between devices, per_device(): lax.all_to_all(letters, AXES, split_axis=0, concat_axis=0, tiled=True)  7.73 us
    all_to_all x1, starting transfers between devices, per_device(): lax.all_to_all(letters, AXES, split_axis=0, concat_axis=0, tiled=True)  7.3 us
    unnamed x22, local copies, waits for them, and re-layouts  4.52 us
  transfers between devices with their start and end apart: 45, of which 30 were waited for; matrix products, arithmetic and copies ran while one was open for 0% of the time, Pallas kernels for 19%

profile of v5, /device:TPU:0, one launch (start us, length us, event | category | flops | bytes accessed | tf_op | source)
XLA Modules:
  0.0 175.9 jit_solution(10020788250918051308)
XLA Ops:
  3.3 7.3 %all-to-all-start = ((s32[32,8,128]{2,1,0:T(8,128)}), s32[32,8,128]{2,1,0:T(8,128)S(1)}, u32[]{:S(2)}, u32[]{:S(2)}) async-start(s32[32,8,128]{2,1,0:T(8,128)} %get-tuple-element.41), calls=%async_computation | async-start | bytes 262144 | tf_op jit(solution)/shard_map/all_to_all | solution.py:482
  10.6 7.7 %all-to-all-done.refs_0_.letter_ref = s32[32,8,128]{2,1,0:T(8,128)S(1)} async-done(((s32[32,8,128]{2,1,0:T(8,128)}), s32[32,8,128]{2,1,0:T(8,128)S(1)}, u32[]{:S(2)}, u32[]{:S(2)}) %all-to-all-start) | async-done | bytes 131104 | tf_op jit(solution)/shard_map/all_to_all | solution.py:482
  18.6 1.8 %shard_map.60 = (bf16[2048,256]{1,0:T(8,128)(2,1)}, f32[8,128]{1,0:T(8,128)S(1)}) custom-call(s32[1,768]{1,0:T(1,128)S(1)} %get-tuple-element.42.slot_ref, bf16[384,256]{1,0:T(8,128)(2,1)S(1)} %copy-done, s32[32,8,128]{2,1,0:T(8,128)S(1)} %all-to-all-done.refs_0_.letter_ref), custom_call_target="tpu_custom_call" | custom-call | flops 1150000000 | tf_op jit(solution)/shard_map/pallas_call | solution.py:225
  20.4 2.6 %all-to-all-start.1 = ((bf16[32,64,256]{2,1,0:T(8,128)(2,1)}), bf16[32,64,256]{2,1,0:T(8,128)(2,1)S(1)}, u32[]{:S(2)}, u32[]{:S(2)}) async-start(bf16[32,64,256]{2,1,0:T(8,128)(2,1)} %bitcast.2), calls=%async_computation.1 | async-start | bytes 2097152 | tf_op jit(solution)/shard_map/all_to_all | solution.py:484
  23.0 10.7 %shard_map.63 = (bf16[1024,2048]{1,0:T(8,128)(2,1)}, f32[8,128]{1,0:T(8,128)S(1)}) custom-call(s32[1]{0:T(128)} %bitcast.me_ref, s32[4,1,2048]{2,1,0:T(1,128)S(1)} %reshape.17.label_ref, f32[8,128]{1,0:T(8,128)S(1)} %get-tuple-element.43.after_ref), custom_call_target="tpu_custom_call" | custom-call | flops 11500000256 | tf_op jit(solution)/shard_map/pallas_call | solution.py:287
  33.8 5.7 %shard_map.61 = (bf16[1536,2048]{1,0:T(8,128)(2,1)}, f32[8,128]{1,0:T(8,128)S(1)}) custom-call(s32[1]{0:T(128)} %bitcast.me_ref, s32[32,8,128]{2,1,0:T(8,128)S(1)} %all-to-all-done.refs_0_.letter_ref, f32[8,128]{1,0:T(8,128)S(1)} %get-tuple-element.43.after_ref), custom_call_target="tpu_custom_call" | custom-call | flops 6899999744 | tf_op jit(solution)/shard_map/pallas_call | solution.py:287
  39.5 10.6 %shard_map.62 = (bf16[1024,2048]{1,0:T(8,128)(2,1)}, bf16[1024,2048]{1,0:T(8,128)(2,1)}, f32[8,128]{1,0:T(8,128)S(1)}) custom-call(s32[1]{0:T(128)} %bitcast.me_ref, s32[32,8,128]{2,1,0:T(8,128)S(1)} %all-to-all-done.refs_0_.letter_ref, f32[8,128]{1,0:T(8,128)S(1)} %get-tuple-element.43.after_ref), custom_call_target="tpu_custom_call" | custom-call | flops 13799999488 | tf_op jit(solution)/shard_map/pallas_call | solution.py:287
  52.6 2.5 %collective-permute-start.3 = (bf16[256,256]{1,0:T(8,128)(2,1)S(1)}, bf16[256,256]{1,0:T(8,128)(2,1)S(1)}, u32[]{:S(2)}, u32[]{:S(2)}) collective-permute-start(bf16[256,256]{1,0:T(8,128)(2,1)S(1)} %get-tuple-element.51.refs_2_), channel_id=1, source_target_pairs={{0,4},{1,5},{2,6},{3,7},{4,0},{5,1},{6,2},{7,3},{8,12},{9,13},{10,... | collective-permute-start | bytes 393224 | tf_op jit(solution)/shard_map/ppermute | solution.py:88
  55.1 1.4 collective-permute-start.1
  56.5 3.2 %collective-permute-done.5.refs_8_ = bf16[256,256]{1,0:T(8,128)(2,1)S(1)} collective-permute-done((bf16[256,256]{1,0:T(8,128)(2,1)S(1)}, bf16[256,256]{1,0:T(8,128)(2,1)S(1)}, u32[]{:S(2)}, u32[]{:S(2)}) %collective-permute-start.5) | collective-permute-done | bytes 131104 | tf_op jit(solution)/shard_map/ppermute | solution.py:88
  59.7 4.4 %collective-permute-done.3.refs_6_ = bf16[256,256]{1,0:T(8,128)(2,1)S(1)} collective-permute-done((bf16[256,256]{1,0:T(8,128)(2,1)S(1)}, bf16[256,256]{1,0:T(8,128)(2,1)S(1)}, u32[]{:S(2)}, u32[]{:S(2)}) %collective-permute-start.3) | collective-permute-done | bytes 131104 | tf_op jit(solution)/shard_map/ppermute | solution.py:88
  65.6 2.2 %copy-done.6 = bf16[1024,2048]{1,0:T(8,128)(2,1)S(1)} copy-done((bf16[1024,2048]{1,0:T(8,128)(2,1)S(1)}, bf16[1024,2048]{1,0:T(8,128)(2,1)}, u32[]{:S(2)}) %copy-start.6) | copy-done | bytes 4194328
  67.8 3.5 %shard_map.65 = (f32[256,256]{1,0:T(8,128)S(1)}, bf16[256,256]{1,0:T(8,128)(2,1)S(1)}, bf16[256,256]{1,0:T(8,128)(2,1)S(1)}, bf16[256,256]{1,0:T(8,128)(2,1)S(1)}, f32[8,128]{1,0:T(8,128)}) custom-call(bf16[1024,2048]{1,0:T(8,128)(2,1)S(1)} %copy-done.5, bf16[1024,2048]{1,0:T(8,128)(2,1)S(1)} %copy-done.6, bf16[256,256]{1,0:T(8,128)(2,1)S(1)} %get-tuple-element.51.refs_2_, ...), custom_call_target="tpu_custom_call" | custom-call | flops 4600000000 | tf_op jit(solution)/shard_map/pallas_call | solution.py:388
  71.3 1.6 collective-permute-start.7
  72.9 1.5 collective-permute-start.8
  74.8 2.2 %collective-permute-done.7.refs_0_ = bf16[256,256]{1,0:T(8,128)(2,1)S(1)} collective-permute-done((bf16[256,256]{1,0:T(8,128)(2,1)S(1)}, bf16[256,256]{1,0:T(8,128)(2,1)S(1)}, u32[]{:S(2)}, u32[]{:S(2)}) %collective-permute-start.7) | collective-permute-done | bytes 131104 | tf_op jit(solution)/shard_map/ppermute | solution.py:88
  77.1 2.2 %collective-permute-done.8.refs_1_ = bf16[256,256]{1,0:T(8,128)(2,1)S(1)} collective-permute-done((bf16[256,256]{1,0:T(8,128)(2,1)S(1)}, bf16[256,256]{1,0:T(8,128)(2,1)S(1)}, u32[]{:S(2)}, u32[]{:S(2)}) %collective-permute-start.8) | collective-permute-done | bytes 131104 | tf_op jit(solution)/shard_map/ppermute | solution.py:88
  79.3 1.8 %collective-permute-done.9.refs_2_ = bf16[256,256]{1,0:T(8,128)(2,1)S(1)} collective-permute-done((bf16[256,256]{1,0:T(8,128)(2,1)S(1)}, bf16[256,256]{1,0:T(8,128)(2,1)S(1)}, u32[]{:S(2)}, u32[]{:S(2)}) %collective-permute-start.9) | collective-permute-done | bytes 131104 | tf_op jit(solution)/shard_map/ppermute | solution.py:88
  81.1 3.0 %collective-permute-start.15 = (bf16[256,256]{1,0:T(8,128)(2,1)S(1)}, bf16[256,256]{1,0:T(8,128)(2,1)S(1)}, u32[]{:S(2)}, u32[]{:S(2)}) collective-permute-start(bf16[256,256]{1,0:T(8,128)(2,1)S(1)} %shard_map.66.refs_1_.potential_ref), channel_id=1, source_target_pairs={{0,2},{1,3},{2,4},{3,5},{4,6},{5,7},{6,0},{7,1},{8,10},{9,11},{10,... | collective-permute-start | bytes 393224 | tf_op jit(solution)/shard_map/ppermute | solution.py:88
  84.1 2.1 %collective-permute-start.13 = (bf16[256,256]{1,0:T(8,128)(2,1)S(1)}, bf16[256,256]{1,0:T(8,128)(2,1)S(1)}, u32[]{:S(2)}, u32[]{:S(2)}) collective-permute-start(bf16[256,256]{1,0:T(8,128)(2,1)S(1)} %shard_map.66.refs_1_.potential_ref), channel_id=1, source_target_pairs={{0,4},{1,5},{2,6},{3,7},{4,0},{5,1},{6,2},{7,3},{8,12},{9,13},{10,... | collective-permute-start | bytes 393224 | tf_op jit(solution)/shard_map/ppermute | solution.py:88
  86.5 3.5 %collective-permute-done.15.refs_7_ = bf16[256,256]{1,0:T(8,128)(2,1)S(1)} collective-permute-done((bf16[256,256]{1,0:T(8,128)(2,1)S(1)}, bf16[256,256]{1,0:T(8,128)(2,1)S(1)}, u32[]{:S(2)}, u32[]{:S(2)}) %collective-permute-start.15) | collective-permute-done | bytes 131104 | tf_op jit(solution)/shard_map/ppermute | solution.py:88
  90.0 4.4 %collective-permute-done.13.refs_5_ = bf16[256,256]{1,0:T(8,128)(2,1)S(1)} collective-permute-done((bf16[256,256]{1,0:T(8,128)(2,1)S(1)}, bf16[256,256]{1,0:T(8,128)(2,1)S(1)}, u32[]{:S(2)}, u32[]{:S(2)}) %collective-permute-start.13) | collective-permute-done | bytes 131104 | tf_op jit(solution)/shard_map/ppermute | solution.py:88
  96.0 2.5 %shard_map.69 = (f32[256,256]{1,0:T(8,128)S(1)}, bf16[256,256]{1,0:T(8,128)(2,1)S(1)}, bf16[256,256]{1,0:T(8,128)(2,1)S(1)}, bf16[256,256]{1,0:T(8,128)(2,1)S(1)}, f32[8,128]{1,0:T(8,128)}) custom-call(bf16[1024,2048]{1,0:T(8,128)(2,1)S(1)} %copy-done.4, bf16[256,256]{1,0:T(8,128)(2,1)S(1)} %shard_map.66.refs_1_.potential_ref, ...), custom_call_target="tpu_custom_call" | custom-call | flops 2300000000 | tf_op jit(solution)/shard_map/pallas_call | solution.py:388
  99.6 1.5 collective-permute-start.21
  102.6 1.6 collective-permute-done.20.refs_0_
  104.1 1.9 %collective-permute-done.21.refs_1_ = bf16[256,256]{1,0:T(8,128)(2,1)S(1)} collective-permute-done((bf16[256,256]{1,0:T(8,128)(2,1)S(1)}, bf16[256,256]{1,0:T(8,128)(2,1)S(1)}, u32[]{:S(2)}, u32[]{:S(2)}) %collective-permute-start.21) | collective-permute-done | bytes 131104 | tf_op jit(solution)/shard_map/ppermute | solution.py:88
  106.0 2.1 %collective-permute-done.22.refs_2_ = bf16[256,256]{1,0:T(8,128)(2,1)S(1)} collective-permute-done((bf16[256,256]{1,0:T(8,128)(2,1)S(1)}, bf16[256,256]{1,0:T(8,128)(2,1)S(1)}, u32[]{:S(2)}, u32[]{:S(2)}) %collective-permute-start.22) | collective-permute-done | bytes 131104 | tf_op jit(solution)/shard_map/ppermute | solution.py:88
  108.1 1.5 shard_map.70
  109.6 2.9 %collective-permute-start.28 = (bf16[256,256]{1,0:T(8,128)(2,1)S(1)}, bf16[256,256]{1,0:T(8,128)(2,1)S(1)}, u32[]{:S(2)}, u32[]{:S(2)}) collective-permute-start(bf16[256,256]{1,0:T(8,128)(2,1)S(1)} %get-tuple-element.68.refs_2_), channel_id=1, source_target_pairs={{0,2},{1,3},{2,4},{3,5},{4,6},{5,7},{6,0},{7,1},{8,10},{9,11},{10,... | collective-permute-start | bytes 393224 | tf_op jit(solution)/shard_map/ppermute | solution.py:88
  114.9 3.0 %collective-permute-done.28.refs_8_ = bf16[256,256]{1,0:T(8,128)(2,1)S(1)} collective-permute-done((bf16[256,256]{1,0:T(8,128)(2,1)S(1)}, bf16[256,256]{1,0:T(8,128)(2,1)S(1)}, u32[]{:S(2)}, u32[]{:S(2)}) %collective-permute-start.28) | collective-permute-done | bytes 131104 | tf_op jit(solution)/shard_map/ppermute | solution.py:88
  117.9 4.0 %collective-permute-done.26.refs_6_ = bf16[256,256]{1,0:T(8,128)(2,1)S(1)} collective-permute-done((bf16[256,256]{1,0:T(8,128)(2,1)S(1)}, bf16[256,256]{1,0:T(8,128)(2,1)S(1)}, u32[]{:S(2)}, u32[]{:S(2)}) %collective-permute-start.26) | collective-permute-done | bytes 131104 | tf_op jit(solution)/shard_map/ppermute | solution.py:88
  122.4 2.4 %shard_map.67 = (f32[384,256]{1,0:T(8,128)S(1)}, bf16[384,256]{1,0:T(8,128)(2,1)S(1)}, bf16[384,256]{1,0:T(8,128)(2,1)S(1)}, bf16[384,256]{1,0:T(8,128)(2,1)S(1)}, f32[8,128]{1,0:T(8,128)S(1)}) custom-call(bf16[1536,2048]{1,0:T(8,128)(2,1)S(1)} %bitcast.8, bf16[256,256]{1,0:T(8,128)(2,1)S(1)} %shard_map.66.refs_1_.potential_ref, ...), custom_call_target="tpu_custom_call" | custom-call | flops 2300000000 | tf_op jit(solution)/shard_map/pallas_call | solution.py:388
  126.2 1.5 collective-permute-start.18
  128.4 3.5 %shard_map.71 = (f32[256,256]{1,0:T(8,128)S(1)}, bf16[256,256]{1,0:T(8,128)(2,1)S(1)}, bf16[256,256]{1,0:T(8,128)(2,1)S(1)}, bf16[256,256]{1,0:T(8,128)(2,1)S(1)}, f32[8,128]{1,0:T(8,128)}) custom-call(bf16[1024,2048]{1,0:T(8,128)(2,1)S(1)} %copy-done.5, bf16[1024,2048]{1,0:T(8,128)(2,1)S(1)} %copy-done.7, bf16[256,256]{1,0:T(8,128)(2,1)S(1)} %get-tuple-element.68.refs_2_, ...), custom_call_target="tpu_custom_call" | custom-call | flops 4600000000 | tf_op jit(solution)/shard_map/pallas_call | solution.py:388
  133.2 1.5 collective-permute-start.31
  135.5 3.0 %collective-permute-done.19.refs_2_ = bf16[384,256]{1,0:T(8,128)(2,1)S(1)} collective-permute-done((bf16[384,256]{1,0:T(8,128)(2,1)S(1)}, bf16[384,256]{1,0:T(8,128)(2,1)S(1)}, u32[]{:S(2)}, u32[]{:S(2)}) %collective-permute-start.19) | collective-permute-done | bytes 196640 | tf_op jit(solution)/shard_map/ppermute | solution.py:88
  139.2 1.7 collective-permute-done.30.refs_0_
  141.1 1.9 %collective-permute-done.32.refs_2_ = bf16[256,256]{1,0:T(8,128)(2,1)S(1)} collective-permute-done((bf16[256,256]{1,0:T(8,128)(2,1)S(1)}, bf16[256,256]{1,0:T(8,128)(2,1)S(1)}, u32[]{:S(2)}, u32[]{:S(2)}) %collective-permute-start.32) | collective-permute-done | bytes 131104 | tf_op jit(solution)/shard_map/ppermute | solution.py:88
  143.7 3.1 %collective-permute-start.38 = (bf16[256,256]{1,0:T(8,128)(2,1)}, bf16[256,256]{1,0:T(8,128)(2,1)S(1)}, u32[]{:S(2)}, u32[]{:S(2)}) collective-permute-start(bf16[256,256]{1,0:T(8,128)(2,1)} %shard_map.72.refs_1_), channel_id=1, source_target_pairs={{0,2},{1,3},{2,4},{3,5},{4,6},{5,7},{6,0},{7,1},{8,10},{9,11},{10,... | collective-permute-start | bytes 393224 | tf_op jit(solution)/shard_map/ppermute | solution.py:88
  146.8 1.5 collective-permute-start.36
  149.2 3.2 %collective-permute-done.38.refs_7_ = bf16[256,256]{1,0:T(8,128)(2,1)S(1)} collective-permute-done((bf16[256,256]{1,0:T(8,128)(2,1)}, bf16[256,256]{1,0:T(8,128)(2,1)S(1)}, u32[]{:S(2)}, u32[]{:S(2)}) %collective-permute-start.38) | collective-permute-done | bytes 131104 | tf_op jit(solution)/shard_map/ppermute | solution.py:88
  152.4 4.1 %collective-permute-done.36.refs_5_ = bf16[256,256]{1,0:T(8,128)(2,1)S(1)} collective-permute-done((bf16[256,256]{1,0:T(8,128)(2,1)}, bf16[256,256]{1,0:T(8,128)(2,1)S(1)}, u32[]{:S(2)}, u32[]{:S(2)}) %collective-permute-start.36) | collective-permute-done | bytes 131104 | tf_op jit(solution)/shard_map/ppermute | solution.py:88
  158.9 3.0 %shard_map.73 = (f32[384,256]{1,0:T(8,128)S(1)}, bf16[384,256]{1,0:T(8,128)(2,1)S(1)}, bf16[384,256]{1,0:T(8,128)(2,1)S(1)}, bf16[384,256]{1,0:T(8,128)(2,1)S(1)}, f32[8,128]{1,0:T(8,128)}) custom-call(bf16[1536,2048]{1,0:T(8,128)(2,1)S(1)} %bitcast.8, bf16[256,256]{1,0:T(8,128)(2,1)S(1)} %copy-done.1, bf16[256,256]{1,0:T(8,128)(2,1)S(1)} %collective-permute-done.33.refs_2_, ...), custom_call_target="tpu_custom_call" | custom-call | flops 2300000000 | tf_op jit(solution)/shard_map/pallas_call | solution.py:388
  163.1 1.5 collective-permute-start.41
  165.4 3.6 %collective-permute-done.40.refs_0_ = bf16[384,256]{1,0:T(8,128)(2,1)S(1)} collective-permute-done((bf16[384,256]{1,0:T(8,128)(2,1)S(1)}, bf16[384,256]{1,0:T(8,128)(2,1)S(1)}, u32[]{:S(2)}, u32[]{:S(2)}) %collective-permute-start.40) | collective-permute-done | bytes 196640 | tf_op jit(solution)/shard_map/ppermute | solution.py:88
  169.0 1.9 %collective-permute-done.41.refs_1_ = bf16[384,256]{1,0:T(8,128)(2,1)S(1)} collective-permute-done((bf16[384,256]{1,0:T(8,128)(2,1)S(1)}, bf16[384,256]{1,0:T(8,128)(2,1)S(1)}, u32[]{:S(2)}, u32[]{:S(2)}) %collective-permute-start.41) | collective-permute-done | bytes 196640 | tf_op jit(solution)/shard_map/ppermute | solution.py:88
  170.9 3.5 %collective-permute-done.42.refs_2_ = bf16[384,256]{1,0:T(8,128)(2,1)S(1)} collective-permute-done((bf16[384,256]{1,0:T(8,128)(2,1)S(1)}, bf16[384,256]{1,0:T(8,128)(2,1)S(1)}, u32[]{:S(2)}, u32[]{:S(2)}) %collective-permute-start.42) | collective-permute-done | bytes 196640 | tf_op jit(solution)/shard_map/ppermute | solution.py:88
  174.4 1.5 shard_map.74
  (86 shorter events, 25.9 us)
Async XLA Ops:
  3.3 15.0 %all-to-all-start = ((s32[32,8,128]{2,1,0:T(8,128)}), s32[32,8,128]{2,1,0:T(8,128)S(1)}, u32[]{:S(2)}, u32[]{:S(2)}) async-start(s32[32,8,128]{2,1,0:T(8,128)} %get-tuple-element.41), calls=%async_computation | async-start | bytes 262144 | tf_op jit(solution)/shard_map/all_to_all | solution.py:482
  20.4 30.2 %all-to-all-start.1 = ((bf16[32,64,256]{2,1,0:T(8,128)(2,1)}), bf16[32,64,256]{2,1,0:T(8,128)(2,1)S(1)}, u32[]{:S(2)}, u32[]{:S(2)}) async-start(bf16[32,64,256]{2,1,0:T(8,128)(2,1)} %bitcast.2), calls=%async_computation.1 | async-start | bytes 2097152 | tf_op jit(solution)/shard_map/all_to_all | solution.py:484
  51.3 8.3 %collective-permute-start.5 = (bf16[256,256]{1,0:T(8,128)(2,1)S(1)}, bf16[256,256]{1,0:T(8,128)(2,1)S(1)}, u32[]{:S(2)}, u32[]{:S(2)}) collective-permute-start(bf16[256,256]{1,0:T(8,128)(2,1)S(1)} %get-tuple-element.51.refs_2_), channel_id=1, source_target_pairs={{0,2},{1,3},{2,4},{3,5},{4,6},{5,7},{6,0},{7,1},{8,10},{9,11},{10,... | collective-permute-start | bytes 393224 | tf_op jit(solution)/shard_map/ppermute | solution.py:88
  52.6 11.5 %collective-permute-start.3 = (bf16[256,256]{1,0:T(8,128)(2,1)S(1)}, bf16[256,256]{1,0:T(8,128)(2,1)S(1)}, u32[]{:S(2)}, u32[]{:S(2)}) collective-permute-start(bf16[256,256]{1,0:T(8,128)(2,1)S(1)} %get-tuple-element.51.refs_2_), channel_id=1, source_target_pairs={{0,4},{1,5},{2,6},{3,7},{4,0},{5,1},{6,2},{7,3},{8,12},{9,13},{10,... | collective-permute-start | bytes 393224 | tf_op jit(solution)/shard_map/ppermute | solution.py:88
  55.1 9.0 %collective-permute-start.1 = (bf16[256,256]{1,0:T(8,128)(2,1)S(1)}, bf16[256,256]{1,0:T(8,128)(2,1)S(1)}, u32[]{:S(2)}, u32[]{:S(2)}) collective-permute-start(bf16[256,256]{1,0:T(8,128)(2,1)S(1)} %get-tuple-element.51.refs_2_), channel_id=1, source_target_pairs={{0,6},{1,7},{2,0},{3,1},{4,2},{5,3},{6,4},{7,5},{8,14},{9,15},{10,... | collective-permute-start | bytes 393224 | tf_op jit(solution)/shard_map/ppermute | solution.py:88
  56.5 8.1 %collective-permute-start = (bf16[256,256]{1,0:T(8,128)(2,1)S(1)}, bf16[256,256]{1,0:T(8,128)(2,1)S(1)}, u32[]{:S(2)}, u32[]{:S(2)}) collective-permute-start(bf16[256,256]{1,0:T(8,128)(2,1)S(1)} %get-tuple-element.51.refs_2_), channel_id=1, source_target_pairs={{0,8},{1,9},{2,10},{3,11},{4,12},{5,13},{6,14},{7,15},{8,0},{9,1},... | collective-permute-start | bytes 393224 | tf_op jit(solution)/shard_map/ppermute | solution.py:88
  59.7 4.9 %collective-permute-start.6 = (bf16[256,256]{1,0:T(8,128)(2,1)S(1)}, bf16[256,256]{1,0:T(8,128)(2,1)S(1)}, u32[]{:S(2)}, u32[]{:S(2)}) collective-permute-start(bf16[256,256]{1,0:T(8,128)(2,1)S(1)} %collective-permute-done.5.refs_8_), channel_id=1, source_target_pairs={{0,8},{1,9},{2,10},{3,11},{4,12},{5,13},{6,14},{7,15},{8,0},{9,1},... | collective-permute-start | bytes 393224 | tf_op jit(solution)/shard_map/ppermute | solution.py:88
  64.1 1.3 collective-permute-start.4
  64.1 1.5 collective-permute-start.2
  71.3 24.6 %copy-start.4 = (bf16[1024,2048]{1,0:T(8,128)(2,1)S(1)}, bf16[1024,2048]{1,0:T(8,128)(2,1)}, u32[]{:S(2)}) copy-start(bf16[1024,2048]{1,0:T(8,128)(2,1)} %get-tuple-element.63.refs_0_) | copy-start | bytes 12582916
  71.3 5.7 %collective-permute-start.7 = (bf16[256,256]{1,0:T(8,128)(2,1)S(1)}, bf16[256,256]{1,0:T(8,128)(2,1)S(1)}, u32[]{:S(2)}, u32[]{:S(2)}) collective-permute-start(bf16[256,256]{1,0:T(8,128)(2,1)S(1)} %get-tuple-element.53), channel_id=1, source_target_pairs={{0,1},{1,0},{2,3},{3,2},{4,5},{5,4},{6,7},{7,6},{8,9},{9,8},{10,11... | collective-permute-start | bytes 393224 | tf_op jit(solution)/shard_map/ppermute | solution.py:88
  72.9 6.4 %collective-permute-start.8 = (bf16[256,256]{1,0:T(8,128)(2,1)S(1)}, bf16[256,256]{1,0:T(8,128)(2,1)S(1)}, u32[]{:S(2)}, u32[]{:S(2)}) collective-permute-start(bf16[256,256]{1,0:T(8,128)(2,1)S(1)} %get-tuple-element.54), channel_id=1, source_target_pairs={{0,16},{1,17},{2,18},{3,19},{4,20},{5,21},{6,22},{7,23},{8,24},{9,... | collective-permute-start | bytes 393224 | tf_op jit(solution)/shard_map/ppermute | solution.py:88
  74.4 6.7 %collective-permute-start.9 = (bf16[256,256]{1,0:T(8,128)(2,1)S(1)}, bf16[256,256]{1,0:T(8,128)(2,1)S(1)}, u32[]{:S(2)}, u32[]{:S(2)}) collective-permute-start(bf16[256,256]{1,0:T(8,128)(2,1)S(1)} %get-tuple-element.55), channel_id=1, source_target_pairs={{0,17},{1,16},{2,19},{3,18},{4,21},{5,20},{6,23},{7,22},{8,25},{9,... | collective-permute-start | bytes 393224 | tf_op jit(solution)/shard_map/ppermute | solution.py:88
  81.1 8.9 %collective-permute-start.15 = (bf16[256,256]{1,0:T(8,128)(2,1)S(1)}, bf16[256,256]{1,0:T(8,128)(2,1)S(1)}, u32[]{:S(2)}, u32[]{:S(2)}) collective-permute-start(bf16[256,256]{1,0:T(8,128)(2,1)S(1)} %shard_map.66.refs_1_.potential_ref), channel_id=1, source_target_pairs={{0,2},{1,3},{2,4},{3,5},{4,6},{5,7},{6,0},{7,1},{8,10},{9,11},{10,... | collective-permute-start | bytes 393224 | tf_op jit(solution)/shard_map/ppermute | solution.py:88
  84.1 10.3 %collective-permute-start.13 = (bf16[256,256]{1,0:T(8,128)(2,1)S(1)}, bf16[256,256]{1,0:T(8,128)(2,1)S(1)}, u32[]{:S(2)}, u32[]{:S(2)}) collective-permute-start(bf16[256,256]{1,0:T(8,128)(2,1)S(1)} %shard_map.66.refs_1_.potential_ref), channel_id=1, source_target_pairs={{0,4},{1,5},{2,6},{3,7},{4,0},{5,1},{6,2},{7,3},{8,12},{9,13},{10,... | collective-permute-start | bytes 393224 | tf_op jit(solution)/shard_map/ppermute | solution.py:88
  86.1 8.3 %collective-permute-start.11 = (bf16[256,256]{1,0:T(8,128)(2,1)S(1)}, bf16[256,256]{1,0:T(8,128)(2,1)S(1)}, u32[]{:S(2)}, u32[]{:S(2)}) collective-permute-start(bf16[256,256]{1,0:T(8,128)(2,1)S(1)} %shard_map.66.refs_1_.potential_ref), channel_id=1, source_target_pairs={{0,6},{1,7},{2,0},{3,1},{4,2},{5,3},{6,4},{7,5},{8,14},{9,15},{10,... | collective-permute-start | bytes 393224 | tf_op jit(solution)/shard_map/ppermute | solution.py:88
  86.5 8.4 %collective-permute-start.10 = (bf16[256,256]{1,0:T(8,128)(2,1)S(1)}, bf16[256,256]{1,0:T(8,128)(2,1)S(1)}, u32[]{:S(2)}, u32[]{:S(2)}) collective-permute-start(bf16[256,256]{1,0:T(8,128)(2,1)S(1)} %shard_map.66.refs_1_.potential_ref), channel_id=1, source_target_pairs={{0,8},{1,9},{2,10},{3,11},{4,12},{5,13},{6,14},{7,15},{8,0},{9,1},... | collective-permute-start | bytes 393224 | tf_op jit(solution)/shard_map/ppermute | solution.py:88
  90.0 4.9 %collective-permute-start.16 = (bf16[256,256]{1,0:T(8,128)(2,1)S(1)}, bf16[256,256]{1,0:T(8,128)(2,1)S(1)}, u32[]{:S(2)}, u32[]{:S(2)}) collective-permute-start(bf16[256,256]{1,0:T(8,128)(2,1)S(1)} %collective-permute-done.15.refs_7_), channel_id=1, source_target_pairs={{0,8},{1,9},{2,10},{3,11},{4,12},{5,13},{6,14},{7,15},{8,0},{9,1},... | collective-permute-start | bytes 393224 | tf_op jit(solution)/shard_map/ppermute | solution.py:88
  94.4 1.3 collective-permute-start.14
  94.4 1.5 collective-permute-start.12
  95.9 26.5 %slice-start = ((s8[6291456]{0:T(1024)(128)(4,1)}), s8[4194304]{0:T(1024)(128)(4,1)S(1)}, s32[]{:S(2)}) async-start(s8[6291456]{0:T(1024)(128)(4,1)} %bitcast.7), calls=%async_computation.2 | async-start | bytes 8388608
  96.0 26.5 %slice-start.1 = ((s8[6291456]{0:T(1024)(128)(4,1)}), s8[2097152]{0:T(1024)(128)(4,1)S(1)}, s32[]{:S(2)}) async-start(s8[6291456]{0:T(1024)(128)(4,1)} %bitcast.7), calls=%async_computation.3 | async-start | bytes 4194304
  98.4 5.7 %collective-permute-start.20 = (bf16[256,256]{1,0:T(8,128)(2,1)S(1)}, bf16[256,256]{1,0:T(8,128)(2,1)S(1)}, u32[]{:S(2)}, u32[]{:S(2)}) collective-permute-start(bf16[256,256]{1,0:T(8,128)(2,1)S(1)} %get-tuple-element.65), channel_id=1, source_target_pairs={{0,1},{1,0},{2,3},{3,2},{4,5},{5,4},{6,7},{7,6},{8,9},{9,8},{10,11... | collective-permute-start | bytes 393224 | tf_op jit(solution)/shard_map/ppermute | solution.py:88
  99.6 6.4 %collective-permute-start.21 = (bf16[256,256]{1,0:T(8,128)(2,1)S(1)}, bf16[256,256]{1,0:T(8,128)(2,1)S(1)}, u32[]{:S(2)}, u32[]{:S(2)}) collective-permute-start(bf16[256,256]{1,0:T(8,128)(2,1)S(1)} %get-tuple-element.66), channel_id=1, source_target_pairs={{0,16},{1,17},{2,18},{3,19},{4,20},{5,21},{6,22},{7,23},{8,24},{9,... | collective-permute-start | bytes 393224 | tf_op jit(solution)/shard_map/ppermute | solution.py:88
  101.1 7.0 %collective-permute-start.22 = (bf16[256,256]{1,0:T(8,128)(2,1)S(1)}, bf16[256,256]{1,0:T(8,128)(2,1)S(1)}, u32[]{:S(2)}, u32[]{:S(2)}) collective-permute-start(bf16[256,256]{1,0:T(8,128)(2,1)S(1)} %get-tuple-element.67), channel_id=1, source_target_pairs={{0,17},{1,16},{2,19},{3,18},{4,21},{5,20},{6,23},{7,22},{8,25},{9,... | collective-permute-start | bytes 393224 | tf_op jit(solution)/shard_map/ppermute | solution.py:88
  109.6 8.3 %collective-permute-start.28 = (bf16[256,256]{1,0:T(8,128)(2,1)S(1)}, bf16[256,256]{1,0:T(8,128)(2,1)S(1)}, u32[]{:S(2)}, u32[]{:S(2)}) collective-permute-start(bf16[256,256]{1,0:T(8,128)(2,1)S(1)} %get-tuple-element.68.refs_2_), channel_id=1, source_target_pairs={{0,2},{1,3},{2,4},{3,5},{4,6},{5,7},{6,0},{7,1},{8,10},{9,11},{10,... | collective-permute-start | bytes 393224 | tf_op jit(solution)/shard_map/ppermute | solution.py:88
  112.5 9.4 %collective-permute-start.26 = (bf16[256,256]{1,0:T(8,128)(2,1)S(1)}, bf16[256,256]{1,0:T(8,128)(2,1)S(1)}, u32[]{:S(2)}, u32[]{:S(2)}) collective-permute-start(bf16[256,256]{1,0:T(8,128)(2,1)S(1)} %get-tuple-element.68.refs_2_), channel_id=1, source_target_pairs={{0,4},{1,5},{2,6},{3,7},{4,0},{5,1},{6,2},{7,3},{8,12},{9,13},{10,... | collective-permute-start | bytes 393224 | tf_op jit(solution)/shard_map/ppermute | solution.py:88
  113.6 8.5 %collective-permute-start.24 = (bf16[256,256]{1,0:T(8,128)(2,1)S(1)}, bf16[256,256]{1,0:T(8,128)(2,1)S(1)}, u32[]{:S(2)}, u32[]{:S(2)}) collective-permute-start(bf16[256,256]{1,0:T(8,128)(2,1)S(1)} %get-tuple-element.68.refs_2_), channel_id=1, source_target_pairs={{0,6},{1,7},{2,0},{3,1},{4,2},{5,3},{6,4},{7,5},{8,14},{9,15},{10,... | collective-permute-start | bytes 393224 | tf_op jit(solution)/shard_map/ppermute | solution.py:88
  114.9 11.3 %collective-permute-start.23 = (bf16[256,256]{1,0:T(8,128)(2,1)S(1)}, bf16[256,256]{1,0:T(8,128)(2,1)S(1)}, u32[]{:S(2)}, u32[]{:S(2)}) collective-permute-start(bf16[256,256]{1,0:T(8,128)(2,1)S(1)} %get-tuple-element.68.refs_2_), channel_id=1, source_target_pairs={{0,8},{1,9},{2,10},{3,11},{4,12},{5,13},{6,14},{7,15},{8,0},{9,1},... | collective-permute-start | bytes 393224 | tf_op jit(solution)/shard_map/ppermute | solution.py:88
  117.9 9.8 %collective-permute-start.29 = (bf16[256,256]{1,0:T(8,128)(2,1)S(1)}, bf16[256,256]{1,0:T(8,128)(2,1)S(1)}, u32[]{:S(2)}, u32[]{:S(2)}) collective-permute-start(bf16[256,256]{1,0:T(8,128)(2,1)S(1)} %collective-permute-done.28.refs_8_), channel_id=1, source_target_pairs={{0,8},{1,9},{2,10},{3,11},{4,12},{5,13},{6,14},{7,15},{8,0},{9,1},... | collective-permute-start | bytes 393224 | tf_op jit(solution)/shard_map/ppermute | solution.py:88
  121.9 6.5 %collective-permute-start.27 = (bf16[256,256]{1,0:T(8,128)(2,1)S(1)}, bf16[256,256]{1,0:T(8,128)(2,1)S(1)}, u32[]{:S(2)}, u32[]{:S(2)}) collective-permute-start(bf16[256,256]{1,0:T(8,128)(2,1)S(1)} %collective-permute-done.26.refs_6_), channel_id=1, source_target_pairs={{0,8},{1,9},{2,10},{3,11},{4,12},{5,13},{6,14},{7,15},{8,0},{9,1},... | collective-permute-start | bytes 393224 | tf_op jit(solution)/shard_map/ppermute | solution.py:88
  122.1 6.3 %collective-permute-start.25 = (bf16[256,256]{1,0:T(8,128)(2,1)S(1)}, bf16[256,256]{1,0:T(8,128)(2,1)S(1)}, u32[]{:S(2)}, u32[]{:S(2)}) collective-permute-start(bf16[256,256]{1,0:T(8,128)(2,1)S(1)} %collective-permute-done.24.refs_4_), channel_id=1, source_target_pairs={{0,8},{1,9},{2,10},{3,11},{4,12},{5,13},{6,14},{7,15},{8,0},{9,1},... | collective-permute-start | bytes 393224 | tf_op jit(solution)/shard_map/ppermute | solution.py:88
  124.9 9.8 %collective-permute-start.17 = (bf16[384,256]{1,0:T(8,128)(2,1)S(1)}, bf16[384,256]{1,0:T(8,128)(2,1)S(1)}, u32[]{:S(2)}, u32[]{:S(2)}) collective-permute-start(bf16[384,256]{1,0:T(8,128)(2,1)S(1)} %get-tuple-element.57), channel_id=1, source_target_pairs={{0,1},{1,0},{2,3},{3,2},{4,5},{5,4},{6,7},{7,6},{8,9},{9,8},{10,11... | collective-permute-start | bytes 589832 | tf_op jit(solution)/shard_map/ppermute | solution.py:88
  126.2 9.2 %collective-permute-start.18 = (bf16[384,256]{1,0:T(8,128)(2,1)S(1)}, bf16[384,256]{1,0:T(8,128)(2,1)S(1)}, u32[]{:S(2)}, u32[]{:S(2)}) collective-permute-start(bf16[384,256]{1,0:T(8,128)(2,1)S(1)} %get-tuple-element.58), channel_id=1, source_target_pairs={{0,16},{1,17},{2,18},{3,19},{4,20},{5,21},{6,22},{7,23},{8,24},{9,... | collective-permute-start | bytes 589832 | tf_op jit(solution)/shard_map/ppermute | solution.py:88
  127.7 10.8 %collective-permute-start.19 = (bf16[384,256]{1,0:T(8,128)(2,1)S(1)}, bf16[384,256]{1,0:T(8,128)(2,1)S(1)}, u32[]{:S(2)}, u32[]{:S(2)}) collective-permute-start(bf16[384,256]{1,0:T(8,128)(2,1)S(1)} %get-tuple-element.59), channel_id=1, source_target_pairs={{0,17},{1,16},{2,19},{3,18},{4,21},{5,20},{6,23},{7,22},{8,25},{9,... | collective-permute-start | bytes 589832 | tf_op jit(solution)/shard_map/ppermute | solution.py:88
  132.0 8.9 %collective-permute-start.30 = (bf16[256,256]{1,0:T(8,128)(2,1)S(1)}, bf16[256,256]{1,0:T(8,128)(2,1)S(1)}, u32[]{:S(2)}, u32[]{:S(2)}) collective-permute-start(bf16[256,256]{1,0:T(8,128)(2,1)S(1)} %get-tuple-element.71), channel_id=1, source_target_pairs={{0,1},{1,0},{2,3},{3,2},{4,5},{5,4},{6,7},{7,6},{8,9},{9,8},{10,11... | collective-permute-start | bytes 393224 | tf_op jit(solution)/shard_map/ppermute | solution.py:88
  133.2 7.8 %collective-permute-start.31 = (bf16[256,256]{1,0:T(8,128)(2,1)S(1)}, bf16[256,256]{1,0:T(8,128)(2,1)S(1)}, u32[]{:S(2)}, u32[]{:S(2)}) collective-permute-start(bf16[256,256]{1,0:T(8,128)(2,1)S(1)} %get-tuple-element.72), channel_id=1, source_target_pairs={{0,16},{1,17},{2,18},{3,19},{4,20},{5,21},{6,22},{7,23},{8,24},{9,... | collective-permute-start | bytes 393224 | tf_op jit(solution)/shard_map/ppermute | solution.py:88
  134.7 8.3 %collective-permute-start.32 = (bf16[256,256]{1,0:T(8,128)(2,1)S(1)}, bf16[256,256]{1,0:T(8,128)(2,1)S(1)}, u32[]{:S(2)}, u32[]{:S(2)}) collective-permute-start(bf16[256,256]{1,0:T(8,128)(2,1)S(1)} %get-tuple-element.73), channel_id=1, source_target_pairs={{0,17},{1,16},{2,19},{3,18},{4,21},{5,20},{6,23},{7,22},{8,25},{9,... | collective-permute-start | bytes 393224 | tf_op jit(solution)/shard_map/ppermute | solution.py:88
  143.7 8.7 %collective-permute-start.38 = (bf16[256,256]{1,0:T(8,128)(2,1)}, bf16[256,256]{1,0:T(8,128)(2,1)S(1)}, u32[]{:S(2)}, u32[]{:S(2)}) collective-permute-start(bf16[256,256]{1,0:T(8,128)(2,1)} %shard_map.72.refs_1_), channel_id=1, source_target_pairs={{0,2},{1,3},{2,4},{3,5},{4,6},{5,7},{6,0},{7,1},{8,10},{9,11},{10,... | collective-permute-start | bytes 393224 | tf_op jit(solution)/shard_map/ppermute | solution.py:88
  146.8 9.6 %collective-permute-start.36 = (bf16[256,256]{1,0:T(8,128)(2,1)}, bf16[256,256]{1,0:T(8,128)(2,1)S(1)}, u32[]{:S(2)}, u32[]{:S(2)}) collective-permute-start(bf16[256,256]{1,0:T(8,128)(2,1)} %shard_map.72.refs_1_), channel_id=1, source_target_pairs={{0,4},{1,5},{2,6},{3,7},{4,0},{5,1},{6,2},{7,3},{8,12},{9,13},{10,... | collective-permute-start | bytes 393224 | tf_op jit(solution)/shard_map/ppermute | solution.py:88
  148.3 8.1 %collective-permute-start.34 = (bf16[256,256]{1,0:T(8,128)(2,1)}, bf16[256,256]{1,0:T(8,128)(2,1)S(1)}, u32[]{:S(2)}, u32[]{:S(2)}) collective-permute-start(bf16[256,256]{1,0:T(8,128)(2,1)} %shard_map.72.refs_1_), channel_id=1, source_target_pairs={{0,6},{1,7},{2,0},{3,1},{4,2},{5,3},{6,4},{7,5},{8,14},{9,15},{10,... | collective-permute-start | bytes 393224 | tf_op jit(solution)/shard_map/ppermute | solution.py:88
  149.1 7.8 %collective-permute-start.33 = (bf16[256,256]{1,0:T(8,128)(2,1)}, bf16[256,256]{1,0:T(8,128)(2,1)S(1)}, u32[]{:S(2)}, u32[]{:S(2)}) collective-permute-start(bf16[256,256]{1,0:T(8,128)(2,1)} %shard_map.72.refs_1_), channel_id=1, source_target_pairs={{0,8},{1,9},{2,10},{3,11},{4,12},{5,13},{6,14},{7,15},{8,0},{9,1},... | collective-permute-start | bytes 393224 | tf_op jit(solution)/shard_map/ppermute | solution.py:88
  152.4 4.6 %collective-permute-start.39 = (bf16[256,256]{1,0:T(8,128)(2,1)S(1)}, bf16[256,256]{1,0:T(8,128)(2,1)S(1)}, u32[]{:S(2)}, u32[]{:S(2)}) collective-permute-start(bf16[256,256]{1,0:T(8,128)(2,1)S(1)} %collective-permute-done.38.refs_7_), channel_id=1, source_target_pairs={{0,8},{1,9},{2,10},{3,11},{4,12},{5,13},{6,14},{7,15},{8,0},{9,1},... | collective-permute-start | bytes 393224 | tf_op jit(solution)/shard_map/ppermute | solution.py:88
  156.4 1.3 collective-permute-start.37
  156.4 1.5 collective-permute-start.35
  161.9 7.1 %collective-permute-start.40 = (bf16[384,256]{1,0:T(8,128)(2,1)S(1)}, bf16[384,256]{1,0:T(8,128)(2,1)S(1)}, u32[]{:S(2)}, u32[]{:S(2)}) collective-permute-start(bf16[384,256]{1,0:T(8,128)(2,1)S(1)} %get-tuple-element.76), channel_id=1, source_target_pairs={{0,1},{1,0},{2,3},{3,2},{4,5},{5,4},{6,7},{7,6},{8,9},{9,8},{10,11... | collective-permute-start | bytes 589832 | tf_op jit(solution)/shard_map/ppermute | solution.py:88
  163.1 7.8 %collective-permute-start.41 = (bf16[384,256]{1,0:T(8,128)(2,1)S(1)}, bf16[384,256]{1,0:T(8,128)(2,1)S(1)}, u32[]{:S(2)}, u32[]{:S(2)}) collective-permute-start(bf16[384,256]{1,0:T(8,128)(2,1)S(1)} %get-tuple-element.77), channel_id=1, source_target_pairs={{0,16},{1,17},{2,18},{3,19},{4,20},{5,21},{6,22},{7,23},{8,24},{9,... | collective-permute-start | bytes 589832 | tf_op jit(solution)/shard_map/ppermute | solution.py:88
  164.6 9.8 %collective-permute-start.42 = (bf16[384,256]{1,0:T(8,128)(2,1)S(1)}, bf16[384,256]{1,0:T(8,128)(2,1)S(1)}, u32[]{:S(2)}, u32[]{:S(2)}) collective-permute-start(bf16[384,256]{1,0:T(8,128)(2,1)S(1)} %get-tuple-element.78), channel_id=1, source_target_pairs={{0,17},{1,16},{2,19},{3,18},{4,21},{5,20},{6,23},{7,22},{8,25},{9,... | collective-permute-start | bytes 589832 | tf_op jit(solution)/shard_map/ppermute | solution.py:88
  (8 other events, 49.4 us)

commit v6 on v5

--- a/solution.py
+++ b/solution.py
@@ -37,6 +37,10 @@
     return pl.BlockSpec(memory_space=pltpu.VMEM)
 
 
+def fixed(array):
+    return pl.BlockSpec(array.shape, lambda j: (0,) * len(array.shape))
+
+
 def cost(microseconds):
     return pl.CostEstimate(
         flops=int(microseconds * 1e-6 * PEAK), bytes_accessed=0, transcendentals=0
@@ -87,14 +91,13 @@
             pairs.append((i, self.near(i, dx, dc, dz, dy)))
         return lax.ppermute(value, AXES, pairs)
 
-    def along(self, value):
-        return [value] + [self.shift(value, dz=-dz) for dz in range(1, self.z)]
-
-    def swapped(self, values):
-        pieces = []
-        for value in values:
-            pieces.append(value)
-            pieces += [self.shift(value, dc=-dc) for dc in range(1, self.core)]
+    def gathered(self, value, after):
+        cores = range(1, self.core)
+        pieces = [value] + [self.shift(value, dc=-dc) for dc in cores]
+        along = [self.shift(value, dz=-dz) for dz in range(1, self.z)]
+        if along:
+            along = pack(along, after)
+            pieces += [along] + [self.shift(along, dc=-dc) for dc in cores]
         return pieces
 
     def index(self, x, core, z, y):
@@ -104,6 +107,15 @@
     def near(self, me, dx=0, dc=0, dz=0, dy=0):
         x, core, z, y = self.digits(me)
         return self.index(x + dx, core + dc, z + dz, y + dy)
+
+    def in_line(self, me, k):
+        if k < self.core:
+            return self.near(me, dc=k)
+        rest = k - self.core
+        return self.near(me, dc=rest // (self.z - 1), dz=1 + rest % (self.z - 1))
+
+    def in_plane(self, me, step):
+        return self.near(me, dx=step // self.y, dy=step % self.y)
 
     def spot(self, me, step):
         x, _, _, y = self.digits(me)
@@ -118,7 +130,8 @@
     def place(self, triangle, tri_dev, me):
         x, core, z, y = self.digits(triangle // tri_dev)
         mx, mcore, mz, my = self.digits(me)
-        block = (z - mz) % self.z * self.core + (core - mcore) % self.core
+        dz, dc = (z - mz) % self.z, (core - mcore) % self.core
+        block = jnp.where(dz == 0, dc, self.core + dc * (self.z - 1) + dz - 1)
         inside = (x == mx) & (y == my)
         return jnp.where(inside, block * tri_dev + triangle % tri_dev, -1)
 
@@ -157,7 +170,7 @@
     return [row[:, k : k + 128] for k in range(0, row.shape[1], 128)]
 
 
-def letter_kernel(layout, form, slots, inc_ref, points_ref, letter_ref, slot_ref):
+def letter_kernel(layout, form, slots, inc_ref, points_ref, letter_ref):
     edges, tri_dev, half = form.edges, form.tri_dev, form.half
     ends, devices = 2 * edges, layout.devices
     plus, minus = inc_ref[0:1, :], inc_ref[1:2, :]
@@ -168,7 +181,6 @@
     upper = ones_where(iota((ends, ends), 0) <= iota((ends, ends), 1))
     count = matmul(ones_where(hits), upper)
     rank = jnp.sum(jnp.where(hits, count, 0.0), axis=0, keepdims=True).astype(I32) - 1
-    slot_ref[...] = owner * slots + rank
     order = ones_where(iota((slots, ends), 0) == rank)
     label = jnp.zeros((devices, slots), I32)
     digits = ((tri % tri_dev + 1, 1), (other & 255, 65536), (other >> 8, 65536 * 256))
@@ -199,37 +211,30 @@
     return pl.pallas_call(
         functools.partial(letter_kernel, layout, form, slots),
         in_specs=[whole()] * 2,
-        out_specs=[whole()] * 2,
-        out_shape=[
-            jax.ShapeDtypeStruct((layout.devices, form.rows, 128), I32),
-            jax.ShapeDtypeStruct((1, 2 * form.edges), I32),
-        ],
+        out_specs=whole(),
+        out_shape=jax.ShapeDtypeStruct((layout.devices, form.rows, 128), I32),
         compiler_params=PARAMS,
         cost_estimate=cost(1),
     )(incidence, centroids)
 
 
-def route_kernel(slot_ref, cur_ref, *refs):
-    out_ref, token_ref = refs[-2:]
-    token_ref[...] = jnp.zeros_like(token_ref)
-    edges, cells = cur_ref.shape[0], out_ref.shape[0]
-    chunk = min(256, cells)
-    slot = slot_ref[...]
-    for base in range(0, cells, chunk):
-        mask = jnp.where(iota((chunk, 2 * edges), 0) + base == slot, 1.0, 0.0).astype(F32)
-        signed = (mask[:, :edges] - mask[:, edges:]).astype(BF16)
-        out_ref[base : base + chunk, :] = matmul(signed, cur_ref[...]).astype(BF16)
-
-
-def route(slot, currents, cells, after):
-    return pl.pallas_call(
-        route_kernel,
-        in_specs=[whole()] * (2 + len(after)),
-        out_specs=[whole()] * 2,
-        out_shape=[jax.ShapeDtypeStruct((cells, currents.shape[1]), BF16), TOKEN],
-        compiler_params=PARAMS,
-        cost_estimate=cost(1),
-    )(slot, currents, *after)
+def pack_kernel(count, *refs):
+    out_ref = refs[-1]
+    size = refs[0].shape[0]
+    for k in range(count):
+        out_ref[k * size : (k + 1) * size, :] = refs[k][...]
+
+
+def pack(pieces, after):
+    size, width = pieces[0].shape
+    return pl.pallas_call(
+        functools.partial(pack_kernel, len(pieces)),
+        in_specs=[whole()] * (len(pieces) + len(after)),
+        out_specs=whole(),
+        out_shape=jax.ShapeDtypeStruct((len(pieces) * size, width), BF16),
+        compiler_params=PARAMS,
+        cost_estimate=cost(0.5),
+    )(*pieces, *after)
 
 
 def features(points, scale, first):
@@ -252,7 +257,7 @@
     return value
 
 
-def tile_kernel(layout, form, block, me_ref, letter_ref, after_ref, *refs):
+def tile_kernel(layout, form, block, me_ref, letter_ref, *refs):
     real_ref, imag_ref, token_ref, col_ref = refs
     token_ref[...] = jnp.zeros_like(token_ref)
     me, step, size = me_ref[0], pl.program_id(0), form.tri_dev
@@ -260,10 +265,10 @@
     @pl.when(step == 0)
     def _():
         for k in range(layout.z * layout.core):
-            letter = letter_ref[layout.near(me, dz=k // layout.core, dc=k % layout.core)]
+            letter = letter_ref[layout.in_line(me, k)]
             col_ref[:, k * size : (k + 1) * size] = features(form.points(letter), 1.0, False)
 
-    letter = letter_ref[layout.near(me, dx=step // layout.y, dy=step % layout.y)]
+    letter = letter_ref[layout.in_plane(me, step)]
     row = features(form.points(letter), 1.0 / (TURNS * TURNS), True)
     for base in range(0, col_ref.shape[1], block):
         cols = slice(base, base + block)
@@ -278,18 +283,15 @@
         imag_ref[:, cols] = (poly(SIN, -SPACING / TURNS, u) * (frac * inverse)).astype(BF16)
 
 
-def fixed(array):
-    return pl.BlockSpec(array.shape, lambda j: (0,) * array.ndim)
-
-
-def build(kernel, outs, rows, layout, cols, me, arrays, time, scratch=()):
-    count = len(layout.plane)
+def build(kernel, outs, rows, span, cols, me, arrays, time, scratch=(), extra=()):
     return pl.pallas_call(
         kernel,
-        grid=(count,),
+        grid=(len(span),),
         in_specs=[pl.BlockSpec(memory_space=pltpu.SMEM)] + [fixed(array) for array in arrays],
-        out_specs=[pl.BlockSpec((rows, cols), lambda j: (j, 0))] * outs + [token_spec()],
-        out_shape=[pltpu.HBM((count * rows, cols), BF16)] * outs + [TOKEN],
+        out_specs=[pl.BlockSpec((rows, cols), lambda j: (j, 0))] * outs
+        + [fixed(array) for array in extra]
+        + [token_spec()],
+        out_shape=[pltpu.HBM((len(span) * rows, cols), BF16)] * outs + list(extra) + [TOKEN],
         scratch_shapes=scratch,
         compiler_params=PARAMS,
         cost_estimate=cost(time),
@@ -303,11 +305,11 @@
     return jnp.where(same, jnp.ones((), BF16), jnp.zeros((), BF16))
 
 
-def adjacency_kernel(layout, tri_dev, me_ref, label_ref, after_ref, out_ref, token_ref):
-    token_ref[...] = jnp.zeros_like(token_ref)
-    me = me_ref[0]
+def adjacency_kernel(layout, tri_dev, first, me_ref, label_ref, after_ref, out_ref, *refs):
+    refs[-1][...] = jnp.zeros_like(refs[-1])
+    me, step = me_ref[0], pl.program_id(0)
     rows, cols = out_ref.shape
-    label = label_ref[layout.spot(me, pl.program_id(0))]
+    label = label_ref[layout.spot(me, first + step)]
     mark = (label & 0xFFFF) - 1
     place = layout.place(lax.shift_right_logical(label, 16), tri_dev, me)
     place = jnp.where(mark >= 0, place, -1)
@@ -316,6 +318,12 @@
         inside = (place >= base) & (place < base + rows)
         here = pick(jnp.where(inside, mark, -1), 0, rows)
         out_ref[:, base : base + rows] = matmul_nt(here, low).astype(BF16)
+    if first == 0:
+
+        @pl.when(step == 0)
+        def _():
+            every = pick(mark, 0, rows)
+            refs[0][...] = matmul(every, jnp.ones((every.shape[1], 128), BF16))
 
 
 def incidence_kernel(layout, form, me_ref, letter_ref, after_ref, out_ref, token_ref):
@@ -323,7 +331,7 @@
     me, step = me_ref[0], pl.program_id(0)
     edges, cols = out_ref.shape
     size = form.tri_dev
-    letter = letter_ref[layout.near(me, dx=step // layout.y, dy=step % layout.y)]
+    letter = letter_ref[layout.in_plane(me, step)]
     plus, minus = [layout.place(end, size, me) for end in form.ends(letter)]
     eye = ones_where(iota((edges, edges), 0) == iota((edges, edges), 1))
     for base in range(0, cols, size):
@@ -331,42 +339,89 @@
         out_ref[:, base : base + size] = matmul_nt(eye, signed).astype(BF16)
 
 
-def collect_kernel(layout, tri_dev, me_ref, label_ref, value_ref, *refs):
-    charge_ref, rounded_ref, degree_ref = refs[-3:]
-    here = pick((label_ref[layout.spot(me_ref[0], 0)] & 0xFFFF) - 1, 0, tri_dev)
-    charge = matmul(here, value_ref[...])
-    charge_ref[...] = charge
-    rounded_ref[...] = charge.astype(BF16)
-    degree_ref[...] = matmul(here, jnp.ones((here.shape[1], degree_ref.shape[1]), BF16))
-
-
-def collect(layout, me, labels, values, tri_dev, after):
-    width = values.shape[1]
-    return pl.pallas_call(
-        functools.partial(collect_kernel, layout, tri_dev),
-        in_specs=[pl.BlockSpec(memory_space=pltpu.SMEM)] + [whole()] * (2 + len(after)),
-        out_specs=[whole()] * 3,
-        out_shape=[
-            jax.ShapeDtypeStruct((tri_dev, width), F32),
-            jax.ShapeDtypeStruct((tri_dev, width), BF16),
-            jax.ShapeDtypeStruct((tri_dev, 128), F32),
-        ],
-        compiler_params=PARAMS,
-        cost_estimate=cost(1),
-    )(me, labels, values, *after)
+def set_blocks(value, outs):
+    for k, out in enumerate(outs):
+
+        @pl.when(pl.program_id(0) == k)
+        def _(out=out):
+            out[...] = value.astype(out.dtype)
+
+
+def blocks_like(count, rows, width, exact):
+    return [
+        jax.ShapeDtypeStruct((rows, width), F32 if exact and k == 0 else BF16)
+        for k in range(count)
+    ]
+
+
+def first_kernel(layout, form, me_ref, letter_ref, *refs):
+    count = len(layout.plane)
+    pieces, outs, token_ref = refs[: -count - 1], refs[-count - 1 : -1], refs[-1]
+    token_ref[...] = jnp.zeros_like(token_ref)
+    me, size, edges = me_ref[0], form.tri_dev, form.edges
+    base = layout.in_plane(me, pl.program_id(0)) * size
+    total, k = None, 0
+    for piece in pieces:
+        for row in range(0, piece.shape[0], edges):
+            plus, minus = form.ends(letter_ref[layout.in_line(me, k)])
+            signed = pick(plus, base, size) - pick(minus, base, size)
+            term = matmul(signed, piece[row : row + edges, :])
+            total = term if total is None else total + term
+            k += 1
+    set_blocks(total, outs)
+
+
+def first_charges(layout, form, me, letters, pieces):
+    count, width = len(layout.plane), pieces[0].shape[1]
+    shapes = blocks_like(count, form.tri_dev, width, True) + [TOKEN]
+    return pl.pallas_call(
+        functools.partial(first_kernel, layout, form),
+        grid=(count,),
+        in_specs=[pl.BlockSpec(memory_space=pltpu.SMEM), fixed(letters)]
+        + [fixed(piece) for piece in pieces],
+        out_specs=[fixed(shape) for shape in shapes],
+        out_shape=shapes,
+        compiler_params=PARAMS,
+        cost_estimate=cost(4),
+    )(me, letters, *pieces)
 
 
 def apply_kernel(mats, fed, count, *refs):
-    matrices, pieces, outs = refs[:mats], refs[mats : mats + fed], refs[-count - 1 : -1]
-    refs[-1][...] = jnp.zeros_like(refs[-1])
-    block = pieces[0].shape[0]
+    matrices, pieces = refs[:mats], refs[mats : mats + fed]
+    outs, token_ref = refs[-count - 3 : -3], refs[-3]
+    slots, sems = refs[-2:]
+    token_ref[...] = jnp.zeros_like(token_ref)
+    step = pl.program_id(0)
+    rows = slots.shape[2]
     half = pieces[0].shape[1] // 2
+
+    def copy(m, block):
+        start = pl.multiple_of(block * rows, rows)
+        slot = block % 2
+        return pltpu.make_async_copy(
+            matrices[m].at[pl.ds(start, rows), :], slots.at[slot, m], sems.at[slot, m]
+        )
+
+    @pl.when(step == 0)
+    def _():
+        for m in range(mats):
+            copy(m, step).start()
+
+    @pl.when(step + 1 < count)
+    def _():
+        for m in range(mats):
+            copy(m, step + 1).start()
+
     sums = []
-    for matrix in matrices:
-        total = None
-        for k, piece in enumerate(pieces):
-            term = matmul(matrix[:, k * block : (k + 1) * block], piece[...])
+    for m in range(mats):
+        copy(m, step).wait()
+        matrix = slots.at[step % 2, m]
+        total, col = None, 0
+        for piece in pieces:
+            size = piece.shape[0]
+            term = matmul(matrix[:, col : col + size], piece[...])
             total = term if total is None else total + term
+            col += size
         sums.append(total)
     value = sums[0]
     if mats == 2:
@@ -374,31 +429,54 @@
         value = jnp.concatenate(
             [real[:, :half] - imag[:, half:], real[:, half:] + imag[:, :half]], axis=1
         )
-    for k, out in enumerate(outs):
-
-        @pl.when(pl.program_id(0) == k)
-        def _(out=out):
-            out[...] = value.astype(out.dtype)
-
-
-def apply(matrices, pieces, count, after=()):
+    set_blocks(value, outs)
+
+
+def apply(matrices, pieces, block, after=(), exact=True):
     rows, cols = matrices[0].shape
-    block = rows // count
-    size, width = pieces[0].shape
-    return pl.pallas_call(
-        functools.partial(apply_kernel, len(matrices), len(pieces), count),
+    count, mats = rows // block, len(matrices)
+    shapes = blocks_like(count, block, pieces[0].shape[1], exact) + [TOKEN]
+    return pl.pallas_call(
+        functools.partial(apply_kernel, mats, len(pieces), count),
         grid=(count,),
-        in_specs=[pl.BlockSpec((block, cols), lambda j: (j, 0))] * len(matrices)
-        + [pl.BlockSpec((size, width), lambda j: (0, 0))] * len(pieces)
+        in_specs=[pl.BlockSpec(memory_space=pltpu.HBM)] * mats
+        + [fixed(piece) for piece in pieces]
         + [token_spec()] * len(after),
-        out_specs=[pl.BlockSpec((block, width), lambda j: (0, 0))] * count + [token_spec()],
+        out_specs=[fixed(shape) for shape in shapes],
+        out_shape=shapes,
+        scratch_shapes=[
+            pltpu.VMEM((2, mats, block, cols), BF16),
+            pltpu.SemaphoreType.DMA((2, mats)),
+        ],
+        compiler_params=PARAMS,
+        cost_estimate=cost(2 * mats),
+    )(*matrices, *pieces, *after)
+
+
+def sum_kernel(count, own_ref, *refs):
+    total = own_ref[...]
+    for ref in refs[:count]:
+        total = total + ref[...].astype(F32)
+    out_ref, rounded_ref, token_ref = refs[-3:]
+    out_ref[...] = total
+    rounded_ref[...] = total.astype(BF16)
+    token_ref[...] = jnp.zeros_like(token_ref)
+
+
+def sum_of(blocks, after):
+    shape = blocks[0].shape
+    return pl.pallas_call(
+        functools.partial(sum_kernel, len(blocks) - 1),
+        in_specs=[whole()] * (len(blocks) + len(after)),
+        out_specs=[whole()] * 3,
         out_shape=[
-            jax.ShapeDtypeStruct((block, width), F32 if k == 0 else BF16) for k in range(count)
-        ]
-        + [TOKEN],
-        compiler_params=PARAMS,
-        cost_estimate=cost(2 * len(matrices)),
-    )(*matrices, *pieces, *after)
+            jax.ShapeDtypeStruct(shape, F32),
+            jax.ShapeDtypeStruct(shape, BF16),
+            TOKEN,
+        ],
+        compiler_params=PARAMS,
+        cost_estimate=cost(1),
+    )(*blocks, *after)
 
 
 def potential_kernel(count, own_ref, *refs):
@@ -465,81 +543,97 @@
     )(weight, current, *blocks)
 
 
-def per_device(currents, incidence, centroids, sweep_weights):
-    layout = Layout(lax.axis_size("row"), lax.axis_size("col"))
-    devices = layout.devices
-    me = lax.axis_index(AXES)
+def per_device(layout, currents, incidence, centroids, sweep_weights):
+    me = lax.axis_index(AXES).astype(I32).reshape(1)
     tri_dev = centroids.shape[1]
-    edge_dev, width = currents.shape
+    edge_dev = currents.shape[0]
+    devices, count = layout.devices, len(layout.plane)
     slots = 8 * tri_dev // devices
-    cells = devices * slots
     sweeps = sweep_weights.shape[0]
-    count = len(layout.plane)
     cols = layout.z * layout.core * tri_dev
 
     form = Letter(edge_dev, tri_dev, count * slots)
-    letters, slot = letters_of(layout, form, incidence, centroids, slots)
+    letters = letters_of(layout, form, incidence, centroids, slots)
     letters = lax.all_to_all(letters, AXES, split_axis=0, concat_axis=0, tiled=True)
-    outgoing, token = route(slot, currents, cells, (letters,))
-    arrived = lax.all_to_all(
-        outgoing.reshape(devices, slots, width), AXES, split_axis=0, concat_axis=0, tiled=True
-    ).reshape(cells, width)
     labels = letters[:, form.starts[3] :, :].reshape(devices, -1)[:, : count * slots]
-    labels = labels.reshape(devices, count, slots).transpose(1, 0, 2).reshape(count, 1, cells)
-    where = me.astype(I32).reshape(1)
-    make = functools.partial(build, layout=layout, cols=cols, me=where)
-    *tiles, token_1 = make(
+    labels = labels.reshape(devices, count, slots).transpose(1, 0, 2)
+    labels = labels.reshape(count, 1, devices * slots)
+
+    make = functools.partial(build, cols=cols, me=me)
+    plane = range(count)
+    *tiles, token = make(
         functools.partial(tile_kernel, layout, form, min(512, cols)),
         2,
         tri_dev,
-        arrays=(letters, token),
+        plane,
+        arrays=(letters,),
         time=12,
         scratch=[pltpu.VMEM((16, cols), BF16)],
     )
-    slopes_of, token_2 = make(
+    pieces = layout.gathered(currents, (token,))
+    *blocks, token = first_charges(layout, form, me, letters, pieces)
+    slopes_of, token = make(
         functools.partial(incidence_kernel, layout, form),
         1,
         edge_dev,
+        plane,
         arrays=(letters, token),
         time=6,
     )
-    neighbours, token_3 = make(
-        functools.partial(adjacency_kernel, layout, tri_dev),
-        1,
-        tri_dev,
-        arrays=(labels, token),
-        time=10,
-    )
-    charge, rounded, degree = collect(
-        layout, where, labels, arrived, tri_dev, (token_1, token_2, token_3)
-    )
+    charge, rounded, token = sum_of(layout.given(blocks), (token,))
+
+    cut = (count + 1) // 2
+
+    def adjacency(span, token):
+        *parts, token = make(
+            functools.partial(adjacency_kernel, layout, tri_dev, span[0]),
+            1,
+            tri_dev,
+            span,
+            arrays=(labels, token),
+            time=5,
+            extra=() if span[0] else (jax.ShapeDtypeStruct((tri_dev, 128), F32),),
+        )
+        return parts, token
+
+    (near, degree), token = adjacency(plane[:cut], token)
+    neighbours = [near]
     current = currents
     potential = None
-    slopes, after = None, ()
+    slopes, after = None, (token,)
     for sweep in range(sweeps):
         weight = sweep_weights[sweep].reshape(1)
-        pieces = layout.swapped(layout.along(rounded))
-        *blocks, _ = apply(tiles, pieces, count, after)
-        after = ()
+        pieces = layout.gathered(rounded, after)
+        *blocks, token = apply(tiles, pieces, tri_dev)
         if slopes is not None:
             current, token = current_of(last_weight, current, layout.given(slopes))
-            after = (token,)
-        potential = potential_of(layout.given(blocks), after)
-        pieces = layout.swapped(layout.along(potential))
+        elif cut < count:
+            (far,), token = adjacency(plane[cut:], token)
+            neighbours.append(far)
+        potential = potential_of(layout.given(blocks), (token,))
+        pieces = layout.gathered(potential, ())
         if sweep + 1 < sweeps:
-            *blocks, _ = apply([neighbours], pieces, count)
+            blocks = []
+            for part in neighbours:
+                *more, _ = apply([part], pieces, tri_dev, (), not blocks)
+                blocks += more
             charge, rounded = charge_of(
                 weight, charge, degree, potential, layout.given(blocks)
             )
-        *slopes, token = apply([slopes_of], pieces, count)
+        *slopes, token = apply([slopes_of], pieces, edge_dev)
         after, last_weight = (token,), weight
     current, _ = current_of(last_weight, current, layout.given(slopes))
     return current, potential
 
 
 def solution(mesh):
+    layout = Layout(mesh.shape["row"], mesh.shape["col"])
     in_specs = (P(AXES, None), P(None, AXES), P(None, AXES), P())
     out_specs = (P(AXES, None), P(AXES, None))
     return jax.shard_map(
-        per_device, mesh=mesh, in_specs=in_specs, out_specs=out_specs, check_vma=False
+        functools.partial(per_device, layout),
+        mesh=mesh,
+        in_specs=in_specs,
+        out_specs=out_specs,
+        check_vma=False,
     )

time: 176 us -> 176 us (level)
  Pallas kernels: 50.3 us -> 60.6 us
  waiting for transfers between devices: 68.8 us -> 60.8 us
  local copies, waits for them, and re-layouts: 5.4 us -> 3.18 us
    pallas_call x10 -> x17, Pallas kernels: 44.6 us -> 54.9 us  [the longest x4 28.5 us: build(): pl.pallas_call(kernel, grid=(len(span),), in_specs=[pl.BlockSpec(memory_s...]
    all_to_all x1, waiting for transfers between devices: 7.73 us -> 2.98 us  [per_device(): lax.all_to_all(letters, AXES, split_axis=0, concat_axis=0, tiled=True)]
    ppermute x43, waiting for transfers between devices: 60.6 us -> 57.9 us  [shift(): return lax.ppermute(value, AXES, pairs)]
    all_to_all x1 -> x0, starting transfers between devices: 2.64 us -> none  [per_device(): lax.all_to_all(outgoing.reshape(devices, slots, width), AXES, split_axis=...]
    ppermute x43, starting transfers between devices: 40.7 us -> 43 us  [shift(): return lax.ppermute(value, AXES, pairs)]
    unnamed x22, local copies, waits for them, and re-layouts: 4.52 us -> 2.34 us
  transfers between devices with their start and end apart: 45 -> 44, of which waited for: 30 -> 24; matrix products, arithmetic and copies ran while one was open for 0% -> 0% of each run, Pallas kernels for 19% -> 23%
where the time goes in v6:
time: 176 us
  waiting for transfers between devices  60.8 us (35%)
  Pallas kernels  60.6 us (34%)
  starting transfers between devices  50.3 us (29%)
  local copies, waits for them, and re-layouts  3.18 us (2%)
    ppermute x43, waiting for transfers between devices, shift(): return lax.ppermute(value, AXES, pairs)  57.9 us
    ppermute x43, starting transfers between devices, shift(): return lax.ppermute(value, AXES, pairs)  43 us
    pallas_call x4, Pallas kernels, build(): pl.pallas_call(kernel, grid=(len(span),), in_specs=[pl.BlockSpec(memory_s...  28.5 us
    pallas_call x6, Pallas kernels, apply(): pl.pallas_call(functools.partial(apply_kernel, mats, len(pieces), count),...  23.1 us
    all_to_all x1, starting transfers between devices, per_device(): lax.all_to_all(letters, AXES, split_axis=0, concat_axis=0, tiled=True)  7.3 us
  transfers between devices with their start and end apart: 44, of which 24 were waited for; matrix products, arithmetic and copies ran while one was open for 0% of the time, Pallas kernels for 23%

profile of v6, /device:TPU:0, one launch (start us, length us, event | category | flops | bytes accessed | tf_op | source)
XLA Modules:
  0.0 175.8 jit_solution(1686526140678202480)
XLA Ops:
  3.3 7.3 %all-to-all-start = ((s32[32,8,128]{2,1,0:T(8,128)}), s32[32,8,128]{2,1,0:T(8,128)S(1)}, u32[]{:S(2)}, u32[]{:S(2)}) async-start(s32[32,8,128]{2,1,0:T(8,128)} %shard_map.59), calls=%async_computation | async-start | bytes 262144 | tf_op jit(solution)/shard_map/all_to_all | solution.py:557
  10.6 3.7 %collective-permute-start.1 = (bf16[384,256]{1,0:T(8,128)(2,1)S(1)}, bf16[384,256]{1,0:T(8,128)(2,1)S(1)}, u32[]{:S(2)}, u32[]{:S(2)}) collective-permute-start(bf16[384,256]{1,0:T(8,128)(2,1)S(1)} %copy-done), channel_id=1, source_target_pairs={{0,6},{1,7},{2,0},{3,1},{4,2},{5,3},{6,4},{7,5},{8,14},{9,15},{10,... | collective-permute-start | bytes 589832 | tf_op jit(solution)/shard_map/ppermute | solution.py:92
  15.3 3.0 %all-to-all-done.letter_ref = s32[32,8,128]{2,1,0:T(8,128)S(1)} async-done(((s32[32,8,128]{2,1,0:T(8,128)}), s32[32,8,128]{2,1,0:T(8,128)S(1)}, u32[]{:S(2)}, u32[]{:S(2)}) %all-to-all-start) | async-done | bytes 131104 | tf_op jit(solution)/shard_map/all_to_all | solution.py:557
  18.3 10.6 %shard_map.60 = (bf16[1024,2048]{1,0:T(8,128)(2,1)}, bf16[1024,2048]{1,0:T(8,128)(2,1)}, f32[8,128]{1,0:T(8,128)S(1)}) custom-call(s32[1]{0:T(128)} %bitcast.me_ref, s32[32,8,128]{2,1,0:T(8,128)S(1)} %all-to-all-done.letter_ref), custom_call_target="tpu_custom_call" | custom-call | flops 13799999488 | tf_op jit(solution)/shard_map/pallas_call | solution.py:287
  28.9 5.1 %collective-permute-done.2.refs_1_ = bf16[384,256]{1,0:T(8,128)(2,1)S(1)} collective-permute-done((bf16[384,256]{1,0:T(8,128)(2,1)S(1)}, bf16[384,256]{1,0:T(8,128)(2,1)S(1)}, u32[]{:S(2)}, u32[]{:S(2)}) %collective-permute-start.2) | collective-permute-done | bytes 196640 | tf_op jit(solution)/shard_map/ppermute | solution.py:92
  34.9 1.5 collective-permute-done.refs_1_
  36.4 3.1 %shard_map.62 = (f32[256,256]{1,0:T(8,128)S(1)}, bf16[256,256]{1,0:T(8,128)(2,1)S(1)}, bf16[256,256]{1,0:T(8,128)(2,1)S(1)}, bf16[256,256]{1,0:T(8,128)(2,1)S(1)}, f32[8,128]{1,0:T(8,128)S(1)}) custom-call(s32[1]{0:T(128)} %bitcast.me_ref, s32[32,8,128]{2,1,0:T(8,128)S(1)} %all-to-all-done.letter_ref, bf16[384,256]{1,0:T(8,128)(2,1)S(1)} %copy-done, ...), custom_call_target="tpu_custom_call" | custom-call | flops 4600000000 | tf_op jit(solution)/shard_map/pallas_call | solution.py:377
  39.5 1.5 collective-permute-start.5
  41.1 1.5 collective-permute-start.6
  43.1 5.8 %shard_map.63 = (bf16[1536,2048]{1,0:T(8,128)(2,1)}, f32[8,128]{1,0:T(8,128)S(1)}) custom-call(s32[1]{0:T(128)} %bitcast.me_ref, s32[32,8,128]{2,1,0:T(8,128)S(1)} %all-to-all-done.letter_ref, f32[8,128]{1,0:T(8,128)S(1)} %get-tuple-element.47.after_ref), custom_call_target="tpu_custom_call" | custom-call | flops 6899999744 | tf_op jit(solution)/shard_map/pallas_call | solution.py:287
  49.7 3.8 %collective-permute-start.9 = (bf16[256,256]{1,0:T(8,128)(2,1)S(1)}, bf16[256,256]{1,0:T(8,128)(2,1)S(1)}, u32[]{:S(2)}, u32[]{:S(2)}) collective-permute-start(bf16[256,256]{1,0:T(8,128)(2,1)S(1)} %get-tuple-element.56.refs_2_), channel_id=1, source_target_pairs={{0,6},{1,7},{2,0},{3,1},{4,2},{5,3},{6,4},{7,5},{8,14},{9,15},{10,... | collective-permute-start | bytes 393224 | tf_op jit(solution)/shard_map/ppermute | solution.py:92
  53.5 6.2 %shard_map.65 = (bf16[512,2048]{1,0:T(8,128)(2,1)}, f32[256,128]{1,0:T(8,128)S(1)}, f32[8,128]{1,0:T(8,128)S(1)}) custom-call(s32[1]{0:T(128)} %bitcast.me_ref, s32[4,1,2048]{2,1,0:T(1,128)S(1)} %reshape.11.label_ref, f32[8,128]{1,0:T(8,128)S(1)} %get-tuple-element.57.after_ref), custom_call_target="tpu_custom_call" | custom-call | flops 5750000128 | tf_op jit(solution)/shard_map/pallas_call | solution.py:287
  61.4 1.4 collective-permute-done.8.refs_3_
  62.8 6.3 %shard_map.67 = (f32[256,256]{1,0:T(8,128)S(1)}, bf16[256,256]{1,0:T(8,128)(2,1)S(1)}, bf16[256,256]{1,0:T(8,128)(2,1)S(1)}, bf16[256,256]{1,0:T(8,128)(2,1)S(1)}, f32[8,128]{1,0:T(8,128)S(1)}) custom-call(bf16[1024,2048]{1,0:T(8,128)(2,1)S(1)} %copy-done.4, bf16[1024,2048]{1,0:T(8,128)(2,1)S(1)} %copy-done.5, ...), custom_call_target="tpu_custom_call" | custom-call | flops 4600000000 | tf_op jit(solution)/shard_map/pallas_call | solution.py:439
  70.2 1.6 collective-permute-start.14
  72.7 5.9 %shard_map.68 = (bf16[512,2048]{1,0:T(8,128)(2,1)}, f32[8,128]{1,0:T(8,128)S(1)}) custom-call(s32[1]{0:T(128)} %bitcast.me_ref, s32[4,1,2048]{2,1,0:T(1,128)S(1)} %reshape.11.label_ref, f32[8,128]{1,0:T(8,128)S(1)} %get-tuple-element.63.after_ref), custom_call_target="tpu_custom_call" | custom-call | flops 5750000128 | tf_op jit(solution)/shard_map/pallas_call | solution.py:287
  79.8 1.8 %collective-permute-start.18 = (bf16[256,256]{1,0:T(8,128)(2,1)S(1)}, bf16[256,256]{1,0:T(8,128)(2,1)S(1)}, u32[]{:S(2)}, u32[]{:S(2)}) collective-permute-start(bf16[256,256]{1,0:T(8,128)(2,1)S(1)} %shard_map.69.refs_1_.potential_ref), channel_id=1, source_target_pairs={{0,4},{1,5},{2,6},{3,7},{4,0},{5,1},{6,2},{7,3},{8,12},{9,13},{10,... | collective-permute-start | bytes 393224 | tf_op jit(solution)/shard_map/ppermute | solution.py:92
  81.6 2.5 %collective-permute-done.17.refs_0_ = bf16[256,256]{1,0:T(8,128)(2,1)S(1)} collective-permute-done((bf16[256,256]{1,0:T(8,128)(2,1)S(1)}, bf16[256,256]{1,0:T(8,128)(2,1)S(1)}, u32[]{:S(2)}, u32[]{:S(2)}) %collective-permute-start.17) | collective-permute-done | bytes 131104 | tf_op jit(solution)/shard_map/ppermute | solution.py:92
  84.1 8.6 %collective-permute-done.18.refs_1_ = bf16[256,256]{1,0:T(8,128)(2,1)S(1)} collective-permute-done((bf16[256,256]{1,0:T(8,128)(2,1)S(1)}, bf16[256,256]{1,0:T(8,128)(2,1)S(1)}, u32[]{:S(2)}, u32[]{:S(2)}) %collective-permute-start.18) | collective-permute-done | bytes 131104 | tf_op jit(solution)/shard_map/ppermute | solution.py:92
  93.3 1.4 collective-permute-done.16.refs_2_
  94.7 1.7 shard_map.74
  96.4 1.6 collective-permute-start.25
  98.0 1.5 collective-permute-start.26
  99.5 1.7 shard_map.73
  102.7 3.2 %collective-permute-done.26.refs_2_ = bf16[256,256]{1,0:T(8,128)(2,1)S(1)} collective-permute-done((bf16[256,256]{1,0:T(8,128)(2,1)S(1)}, bf16[256,256]{1,0:T(8,128)(2,1)S(1)}, u32[]{:S(2)}, u32[]{:S(2)}) %collective-permute-start.26) | collective-permute-done | bytes 131104 | tf_op jit(solution)/shard_map/ppermute | solution.py:92
  105.9 2.5 %collective-permute-done.24.refs_0_ = bf16[256,256]{1,0:T(8,128)(2,1)S(1)} collective-permute-done((bf16[256,256]{1,0:T(8,128)(2,1)S(1)}, bf16[256,256]{1,0:T(8,128)(2,1)S(1)}, u32[]{:S(2)}, u32[]{:S(2)}) %collective-permute-start.24) | collective-permute-done | bytes 131104 | tf_op jit(solution)/shard_map/ppermute | solution.py:92
  108.4 1.5 shard_map.75
  110.6 2.0 %collective-permute-start.30 = (bf16[256,256]{1,0:T(8,128)(2,1)S(1)}, bf16[256,256]{1,0:T(8,128)(2,1)S(1)}, u32[]{:S(2)}, u32[]{:S(2)}) collective-permute-start(bf16[256,256]{1,0:T(8,128)(2,1)S(1)} %get-tuple-element.78.refs_2_), channel_id=1, source_target_pairs={{0,2},{1,3},{2,4},{3,5},{4,6},{5,7},{6,0},{7,1},{8,10},{9,11},{10,... | collective-permute-start | bytes 393224 | tf_op jit(solution)/shard_map/ppermute | solution.py:92
  112.6 3.0 %shard_map.71 = (f32[384,256]{1,0:T(8,128)S(1)}, bf16[384,256]{1,0:T(8,128)(2,1)S(1)}, bf16[384,256]{1,0:T(8,128)(2,1)S(1)}, bf16[384,256]{1,0:T(8,128)(2,1)S(1)}, f32[8,128]{1,0:T(8,128)S(1)}) custom-call(bf16[1536,2048]{1,0:T(8,128)(2,1)S(1)} %bitcast.5, bf16[256,256]{1,0:T(8,128)(2,1)S(1)} %shard_map.69.refs_1_.potential_ref, ...), custom_call_target="tpu_custom_call" | custom-call | flops 2300000000 | tf_op jit(solution)/shard_map/pallas_call | solution.py:439
  116.3 6.2 %collective-permute-done.29.refs_1_ = bf16[256,256]{1,0:T(8,128)(2,1)S(1)} collective-permute-done((bf16[256,256]{1,0:T(8,128)(2,1)S(1)}, bf16[256,256]{1,0:T(8,128)(2,1)S(1)}, u32[]{:S(2)}, u32[]{:S(2)}) %collective-permute-start.29) | collective-permute-done | bytes 131104 | tf_op jit(solution)/shard_map/ppermute | solution.py:92
  123.8 1.3 collective-permute-start.22
  125.1 1.5 collective-permute-start.23
  126.6 6.9 %shard_map.77 = (f32[256,256]{1,0:T(8,128)S(1)}, bf16[256,256]{1,0:T(8,128)(2,1)S(1)}, bf16[256,256]{1,0:T(8,128)(2,1)S(1)}, bf16[256,256]{1,0:T(8,128)(2,1)S(1)}, f32[8,128]{1,0:T(8,128)}) custom-call(bf16[1024,2048]{1,0:T(8,128)(2,1)S(1)} %copy-done.4, bf16[1024,2048]{1,0:T(8,128)(2,1)S(1)} %copy-done.5, bf16[256,256]{1,0:T(8,128)(2,1)S(1)} %get-tuple-element.78.refs_2_, ...), custom_call_target="tpu_custom_call" | custom-call | flops 4600000000 | tf_op jit(solution)/shard_map/pallas_call | solution.py:439
  134.3 1.3 collective-permute-start.33
  135.6 1.5 collective-permute-start.34
  137.8 1.9 %collective-permute-done.32.refs_0_ = bf16[256,256]{1,0:T(8,128)(2,1)S(1)} collective-permute-done((bf16[256,256]{1,0:T(8,128)(2,1)S(1)}, bf16[256,256]{1,0:T(8,128)(2,1)S(1)}, u32[]{:S(2)}, u32[]{:S(2)}) %collective-permute-start.32) | collective-permute-done | bytes 131104 | tf_op jit(solution)/shard_map/ppermute | solution.py:92
  140.6 1.6 collective-permute-done.34.refs_2_
  143.3 1.8 %collective-permute-start.37 = (bf16[256,256]{1,0:T(8,128)(2,1)}, bf16[256,256]{1,0:T(8,128)(2,1)S(1)}, u32[]{:S(2)}, u32[]{:S(2)}) collective-permute-start(bf16[256,256]{1,0:T(8,128)(2,1)} %shard_map.78.refs_1_), channel_id=1, source_target_pairs={{0,4},{1,5},{2,6},{3,7},{4,0},{5,1},{6,2},{7,3},{8,12},{9,13},{10,... | collective-permute-start | bytes 393224 | tf_op jit(solution)/shard_map/ppermute | solution.py:92
  145.1 2.0 %collective-permute-start.38 = (bf16[256,256]{1,0:T(8,128)(2,1)}, bf16[256,256]{1,0:T(8,128)(2,1)S(1)}, u32[]{:S(2)}, u32[]{:S(2)}) collective-permute-start(bf16[256,256]{1,0:T(8,128)(2,1)} %shard_map.78.refs_1_), channel_id=1, source_target_pairs={{0,2},{1,3},{2,4},{3,5},{4,6},{5,7},{6,0},{7,1},{8,10},{9,11},{10,... | collective-permute-start | bytes 393224 | tf_op jit(solution)/shard_map/ppermute | solution.py:92
  148.1 7.1 %collective-permute-done.37.refs_1_ = bf16[256,256]{1,0:T(8,128)(2,1)S(1)} collective-permute-done((bf16[256,256]{1,0:T(8,128)(2,1)}, bf16[256,256]{1,0:T(8,128)(2,1)S(1)}, u32[]{:S(2)}, u32[]{:S(2)}) %collective-permute-start.37) | collective-permute-done | bytes 131104 | tf_op jit(solution)/shard_map/ppermute | solution.py:92
  155.8 1.6 collective-permute-done.35.refs_2_
  158.3 3.5 %shard_map.80 = (f32[384,256]{1,0:T(8,128)S(1)}, bf16[384,256]{1,0:T(8,128)(2,1)S(1)}, bf16[384,256]{1,0:T(8,128)(2,1)S(1)}, bf16[384,256]{1,0:T(8,128)(2,1)S(1)}, f32[8,128]{1,0:T(8,128)}) custom-call(bf16[1536,2048]{1,0:T(8,128)(2,1)S(1)} %bitcast.5, bf16[256,256]{1,0:T(8,128)(2,1)S(1)} %copy-done.1, bf16[256,256]{1,0:T(8,128)(2,1)S(1)} %collective-permute-done.35.refs_2_, ...), custom_call_target="tpu_custom_call" | custom-call | flops 2300000000 | tf_op jit(solution)/shard_map/pallas_call | solution.py:439
  161.8 1.9 %collective-permute-start.40 = (bf16[384,256]{1,0:T(8,128)(2,1)S(1)}, bf16[384,256]{1,0:T(8,128)(2,1)S(1)}, u32[]{:S(2)}, u32[]{:S(2)}) collective-permute-start(bf16[384,256]{1,0:T(8,128)(2,1)S(1)} %get-tuple-element.86), channel_id=1, source_target_pairs={{0,1},{1,0},{2,3},{3,2},{4,5},{5,4},{6,7},{7,6},{8,9},{9,8},{10,11... | collective-permute-start | bytes 589832 | tf_op jit(solution)/shard_map/ppermute | solution.py:92
  163.9 1.5 collective-permute-start.42
  165.3 3.6 %collective-permute-done.40.refs_0_ = bf16[384,256]{1,0:T(8,128)(2,1)S(1)} collective-permute-done((bf16[384,256]{1,0:T(8,128)(2,1)S(1)}, bf16[384,256]{1,0:T(8,128)(2,1)S(1)}, u32[]{:S(2)}, u32[]{:S(2)}) %collective-permute-start.40) | collective-permute-done | bytes 196640 | tf_op jit(solution)/shard_map/ppermute | solution.py:92
  168.9 2.6 %collective-permute-done.41.refs_1_ = bf16[384,256]{1,0:T(8,128)(2,1)S(1)} collective-permute-done((bf16[384,256]{1,0:T(8,128)(2,1)S(1)}, bf16[384,256]{1,0:T(8,128)(2,1)S(1)}, u32[]{:S(2)}, u32[]{:S(2)}) %collective-permute-start.41) | collective-permute-done | bytes 196640 | tf_op jit(solution)/shard_map/ppermute | solution.py:92
  171.5 2.9 %collective-permute-done.42.refs_2_ = bf16[384,256]{1,0:T(8,128)(2,1)S(1)} collective-permute-done((bf16[384,256]{1,0:T(8,128)(2,1)S(1)}, bf16[384,256]{1,0:T(8,128)(2,1)S(1)}, u32[]{:S(2)}, u32[]{:S(2)}) %collective-permute-start.42) | collective-permute-done | bytes 196640 | tf_op jit(solution)/shard_map/ppermute | solution.py:92
  174.4 1.4 shard_map.81
  (91 shorter events, 21.7 us)
Async XLA Ops:
  0.6 9.9 %copy-start = (bf16[384,256]{1,0:T(8,128)(2,1)S(1)}, bf16[384,256]{1,0:T(8,128)(2,1)}, u32[]{:S(2)}) copy-start(bf16[384,256]{1,0:T(8,128)(2,1)} %current_ref.1) | copy-start | bytes 589828
  3.3 15.0 %all-to-all-start = ((s32[32,8,128]{2,1,0:T(8,128)}), s32[32,8,128]{2,1,0:T(8,128)S(1)}, u32[]{:S(2)}, u32[]{:S(2)}) async-start(s32[32,8,128]{2,1,0:T(8,128)} %shard_map.59), calls=%async_computation | async-start | bytes 262144 | tf_op jit(solution)/shard_map/all_to_all | solution.py:557
  10.6 18.3 %collective-permute-start.1 = (bf16[384,256]{1,0:T(8,128)(2,1)S(1)}, bf16[384,256]{1,0:T(8,128)(2,1)S(1)}, u32[]{:S(2)}, u32[]{:S(2)}) collective-permute-start(bf16[384,256]{1,0:T(8,128)(2,1)S(1)} %copy-done), channel_id=1, source_target_pairs={{0,6},{1,7},{2,0},{3,1},{4,2},{5,3},{6,4},{7,5},{8,14},{9,15},{10,... | collective-permute-start | bytes 589832 | tf_op jit(solution)/shard_map/ppermute | solution.py:92
  14.3 19.7 %collective-permute-start.2 = (bf16[384,256]{1,0:T(8,128)(2,1)S(1)}, bf16[384,256]{1,0:T(8,128)(2,1)S(1)}, u32[]{:S(2)}, u32[]{:S(2)}) collective-permute-start(bf16[384,256]{1,0:T(8,128)(2,1)S(1)} %copy-done), channel_id=1, source_target_pairs={{0,4},{1,5},{2,6},{3,7},{4,0},{5,1},{6,2},{7,3},{8,12},{9,13},{10,... | collective-permute-start | bytes 589832 | tf_op jit(solution)/shard_map/ppermute | solution.py:92
  14.3 19.7 %collective-permute-start.3 = (bf16[384,256]{1,0:T(8,128)(2,1)S(1)}, bf16[384,256]{1,0:T(8,128)(2,1)S(1)}, u32[]{:S(2)}, u32[]{:S(2)}) collective-permute-start(bf16[384,256]{1,0:T(8,128)(2,1)S(1)} %copy-done), channel_id=1, source_target_pairs={{0,2},{1,3},{2,4},{3,5},{4,6},{5,7},{6,0},{7,1},{8,10},{9,11},{10,... | collective-permute-start | bytes 589832 | tf_op jit(solution)/shard_map/ppermute | solution.py:92
  34.1 2.4 %collective-permute-start.4 = (bf16[1152,256]{1,0:T(8,128)(2,1)S(1)}, bf16[1152,256]{1,0:T(8,128)(2,1)S(1)}, u32[]{:S(2)}, u32[]{:S(2)}) collective-permute-start(bf16[1152,256]{1,0:T(8,128)(2,1)S(1)} %shard_map.61.refs_2_), channel_id=1, source_target_pairs={{0,8},{1,9},{2,10},{3,11},{4,12},{5,13},{6,14},{7,15},{8,0},{9,1},... | collective-permute-start | bytes 1769480 | tf_op jit(solution)/shard_map/ppermute | solution.py:92
  34.1 2.3 %collective-permute-start = (bf16[384,256]{1,0:T(8,128)(2,1)S(1)}, bf16[384,256]{1,0:T(8,128)(2,1)S(1)}, u32[]{:S(2)}, u32[]{:S(2)}) collective-permute-start(bf16[384,256]{1,0:T(8,128)(2,1)S(1)} %copy-done), channel_id=1, source_target_pairs={{0,8},{1,9},{2,10},{3,11},{4,12},{5,13},{6,14},{7,15},{8,0},{9,1},... | collective-permute-start | bytes 589832 | tf_op jit(solution)/shard_map/ppermute | solution.py:92
  39.5 9.3 %collective-permute-start.5 = (bf16[256,256]{1,0:T(8,128)(2,1)S(1)}, bf16[256,256]{1,0:T(8,128)(2,1)S(1)}, u32[]{:S(2)}, u32[]{:S(2)}) collective-permute-start(bf16[256,256]{1,0:T(8,128)(2,1)S(1)} %get-tuple-element.52), channel_id=1, source_target_pairs={{0,1},{1,0},{2,3},{3,2},{4,5},{5,4},{6,7},{7,6},{8,9},{9,8},{10,11... | collective-permute-start | bytes 393224 | tf_op jit(solution)/shard_map/ppermute | solution.py:92
  41.1 7.8 %collective-permute-start.6 = (bf16[256,256]{1,0:T(8,128)(2,1)S(1)}, bf16[256,256]{1,0:T(8,128)(2,1)S(1)}, u32[]{:S(2)}, u32[]{:S(2)}) collective-permute-start(bf16[256,256]{1,0:T(8,128)(2,1)S(1)} %get-tuple-element.53), channel_id=1, source_target_pairs={{0,16},{1,17},{2,18},{3,19},{4,20},{5,21},{6,22},{7,23},{8,24},{9,... | collective-permute-start | bytes 393224 | tf_op jit(solution)/shard_map/ppermute | solution.py:92
  42.5 6.6 %collective-permute-start.7 = (bf16[256,256]{1,0:T(8,128)(2,1)S(1)}, bf16[256,256]{1,0:T(8,128)(2,1)S(1)}, u32[]{:S(2)}, u32[]{:S(2)}) collective-permute-start(bf16[256,256]{1,0:T(8,128)(2,1)S(1)} %get-tuple-element.54), channel_id=1, source_target_pairs={{0,17},{1,16},{2,19},{3,18},{4,21},{5,20},{6,23},{7,22},{8,25},{9,... | collective-permute-start | bytes 393224 | tf_op jit(solution)/shard_map/ppermute | solution.py:92
  49.2 10.6 %collective-permute-start.10 = (bf16[256,256]{1,0:T(8,128)(2,1)S(1)}, bf16[256,256]{1,0:T(8,128)(2,1)S(1)}, u32[]{:S(2)}, u32[]{:S(2)}) collective-permute-start(bf16[256,256]{1,0:T(8,128)(2,1)S(1)} %get-tuple-element.56.refs_2_), channel_id=1, source_target_pairs={{0,4},{1,5},{2,6},{3,7},{4,0},{5,1},{6,2},{7,3},{8,12},{9,13},{10,... | collective-permute-start | bytes 393224 | tf_op jit(solution)/shard_map/ppermute | solution.py:92
  49.7 10.1 %collective-permute-start.11 = (bf16[256,256]{1,0:T(8,128)(2,1)S(1)}, bf16[256,256]{1,0:T(8,128)(2,1)S(1)}, u32[]{:S(2)}, u32[]{:S(2)}) collective-permute-start(bf16[256,256]{1,0:T(8,128)(2,1)S(1)} %get-tuple-element.56.refs_2_), channel_id=1, source_target_pairs={{0,2},{1,3},{2,4},{3,5},{4,6},{5,7},{6,0},{7,1},{8,10},{9,11},{10,... | collective-permute-start | bytes 393224 | tf_op jit(solution)/shard_map/ppermute | solution.py:92
  49.7 11.1 %collective-permute-start.9 = (bf16[256,256]{1,0:T(8,128)(2,1)S(1)}, bf16[256,256]{1,0:T(8,128)(2,1)S(1)}, u32[]{:S(2)}, u32[]{:S(2)}) collective-permute-start(bf16[256,256]{1,0:T(8,128)(2,1)S(1)} %get-tuple-element.56.refs_2_), channel_id=1, source_target_pairs={{0,6},{1,7},{2,0},{3,1},{4,2},{5,3},{6,4},{7,5},{8,14},{9,15},{10,... | collective-permute-start | bytes 393224 | tf_op jit(solution)/shard_map/ppermute | solution.py:92
  60.8 2.0 %collective-permute-start.12 = (bf16[768,256]{1,0:T(8,128)(2,1)S(1)}, bf16[768,256]{1,0:T(8,128)(2,1)S(1)}, u32[]{:S(2)}, u32[]{:S(2)}) collective-permute-start(bf16[768,256]{1,0:T(8,128)(2,1)S(1)} %shard_map.66.refs_4_), channel_id=1, source_target_pairs={{0,8},{1,9},{2,10},{3,11},{4,12},{5,13},{6,14},{7,15},{8,0},{9,1},... | collective-permute-start | bytes 1179656 | tf_op jit(solution)/shard_map/ppermute | solution.py:92
  60.9 1.9 %collective-permute-start.8 = (bf16[256,256]{1,0:T(8,128)(2,1)S(1)}, bf16[256,256]{1,0:T(8,128)(2,1)S(1)}, u32[]{:S(2)}, u32[]{:S(2)}) collective-permute-start(bf16[256,256]{1,0:T(8,128)(2,1)S(1)} %get-tuple-element.56.refs_2_), channel_id=1, source_target_pairs={{0,8},{1,9},{2,10},{3,11},{4,12},{5,13},{6,14},{7,15},{8,0},{9,1},... | collective-permute-start | bytes 393224 | tf_op jit(solution)/shard_map/ppermute | solution.py:92
  69.1 9.5 %collective-permute-start.13 = (bf16[256,256]{1,0:T(8,128)(2,1)S(1)}, bf16[256,256]{1,0:T(8,128)(2,1)S(1)}, u32[]{:S(2)}, u32[]{:S(2)}) collective-permute-start(bf16[256,256]{1,0:T(8,128)(2,1)S(1)} %get-tuple-element.60), channel_id=1, source_target_pairs={{0,1},{1,0},{2,3},{3,2},{4,5},{5,4},{6,7},{7,6},{8,9},{9,8},{10,11... | collective-permute-start | bytes 393224 | tf_op jit(solution)/shard_map/ppermute | solution.py:92
  70.2 8.3 %collective-permute-start.14 = (bf16[256,256]{1,0:T(8,128)(2,1)S(1)}, bf16[256,256]{1,0:T(8,128)(2,1)S(1)}, u32[]{:S(2)}, u32[]{:S(2)}) collective-permute-start(bf16[256,256]{1,0:T(8,128)(2,1)S(1)} %get-tuple-element.61), channel_id=1, source_target_pairs={{0,16},{1,17},{2,18},{3,19},{4,20},{5,21},{6,22},{7,23},{8,24},{9,... | collective-permute-start | bytes 393224 | tf_op jit(solution)/shard_map/ppermute | solution.py:92
  71.8 6.9 %collective-permute-start.15 = (bf16[256,256]{1,0:T(8,128)(2,1)S(1)}, bf16[256,256]{1,0:T(8,128)(2,1)S(1)}, u32[]{:S(2)}, u32[]{:S(2)}) collective-permute-start(bf16[256,256]{1,0:T(8,128)(2,1)S(1)} %get-tuple-element.62), channel_id=1, source_target_pairs={{0,17},{1,16},{2,19},{3,18},{4,21},{5,20},{6,23},{7,22},{8,25},{9,... | collective-permute-start | bytes 393224 | tf_op jit(solution)/shard_map/ppermute | solution.py:92
  78.6 16.1 %copy-start.7 = (bf16[512,2048]{1,0:T(8,128)(2,1)S(1)}, bf16[512,2048]{1,0:T(8,128)(2,1)}, u32[]{:S(2)}) copy-start(bf16[512,2048]{1,0:T(8,128)(2,1)} %get-tuple-element.75.refs_0_) | copy-start | bytes 6291460
  78.8 5.3 %collective-permute-start.17 = (bf16[256,256]{1,0:T(8,128)(2,1)S(1)}, bf16[256,256]{1,0:T(8,128)(2,1)S(1)}, u32[]{:S(2)}, u32[]{:S(2)}) collective-permute-start(bf16[256,256]{1,0:T(8,128)(2,1)S(1)} %shard_map.69.refs_1_.potential_ref), channel_id=1, source_target_pairs={{0,6},{1,7},{2,0},{3,1},{4,2},{5,3},{6,4},{7,5},{8,14},{9,15},{10,... | collective-permute-start | bytes 393224 | tf_op jit(solution)/shard_map/ppermute | solution.py:92
  79.8 12.9 %collective-permute-start.18 = (bf16[256,256]{1,0:T(8,128)(2,1)S(1)}, bf16[256,256]{1,0:T(8,128)(2,1)S(1)}, u32[]{:S(2)}, u32[]{:S(2)}) collective-permute-start(bf16[256,256]{1,0:T(8,128)(2,1)S(1)} %shard_map.69.refs_1_.potential_ref), channel_id=1, source_target_pairs={{0,4},{1,5},{2,6},{3,7},{4,0},{5,1},{6,2},{7,3},{8,12},{9,13},{10,... | collective-permute-start | bytes 393224 | tf_op jit(solution)/shard_map/ppermute | solution.py:92
  81.6 11.1 %collective-permute-start.19 = (bf16[256,256]{1,0:T(8,128)(2,1)S(1)}, bf16[256,256]{1,0:T(8,128)(2,1)S(1)}, u32[]{:S(2)}, u32[]{:S(2)}) collective-permute-start(bf16[256,256]{1,0:T(8,128)(2,1)S(1)} %shard_map.69.refs_1_.potential_ref), channel_id=1, source_target_pairs={{0,2},{1,3},{2,4},{3,5},{4,6},{5,7},{6,0},{7,1},{8,10},{9,11},{10,... | collective-permute-start | bytes 393224 | tf_op jit(solution)/shard_map/ppermute | solution.py:92
  92.7 2.0 %collective-permute-start.20 = (bf16[768,256]{1,0:T(8,128)(2,1)S(1)}, bf16[768,256]{1,0:T(8,128)(2,1)S(1)}, u32[]{:S(2)}, u32[]{:S(2)}) collective-permute-start(bf16[768,256]{1,0:T(8,128)(2,1)S(1)} %shard_map.70.refs_3_), channel_id=1, source_target_pairs={{0,8},{1,9},{2,10},{3,11},{4,12},{5,13},{6,14},{7,15},{8,0},{9,1},... | collective-permute-start | bytes 1179656 | tf_op jit(solution)/shard_map/ppermute | solution.py:92
  92.8 1.9 %collective-permute-start.16 = (bf16[256,256]{1,0:T(8,128)(2,1)S(1)}, bf16[256,256]{1,0:T(8,128)(2,1)S(1)}, u32[]{:S(2)}, u32[]{:S(2)}) collective-permute-start(bf16[256,256]{1,0:T(8,128)(2,1)S(1)} %shard_map.69.refs_1_.potential_ref), channel_id=1, source_target_pairs={{0,8},{1,9},{2,10},{3,11},{4,12},{5,13},{6,14},{7,15},{8,0},{9,1},... | collective-permute-start | bytes 393224 | tf_op jit(solution)/shard_map/ppermute | solution.py:92
  96.4 6.2 %collective-permute-start.25 = (bf16[256,256]{1,0:T(8,128)(2,1)S(1)}, bf16[256,256]{1,0:T(8,128)(2,1)S(1)}, u32[]{:S(2)}, u32[]{:S(2)}) collective-permute-start(bf16[256,256]{1,0:T(8,128)(2,1)S(1)} %get-tuple-element.76), channel_id=1, source_target_pairs={{0,16},{1,17},{2,18},{3,19},{4,20},{5,21},{6,22},{7,23},{8,24},{9,... | collective-permute-start | bytes 393224 | tf_op jit(solution)/shard_map/ppermute | solution.py:92
  98.0 7.9 %collective-permute-start.26 = (bf16[256,256]{1,0:T(8,128)(2,1)S(1)}, bf16[256,256]{1,0:T(8,128)(2,1)S(1)}, u32[]{:S(2)}, u32[]{:S(2)}) collective-permute-start(bf16[256,256]{1,0:T(8,128)(2,1)S(1)} %get-tuple-element.77), channel_id=1, source_target_pairs={{0,17},{1,16},{2,19},{3,18},{4,21},{5,20},{6,23},{7,22},{8,25},{9,... | collective-permute-start | bytes 393224 | tf_op jit(solution)/shard_map/ppermute | solution.py:92
  99.5 13.1 %slice-start = ((s8[6291456]{0:T(1024)(128)(4,1)}), s8[4194304]{0:T(1024)(128)(4,1)S(1)}, s32[]{:S(2)}) async-start(s8[6291456]{0:T(1024)(128)(4,1)} %bitcast.4), calls=%async_computation.1 | async-start | bytes 8388608
  99.5 13.1 %slice-start.1 = ((s8[6291456]{0:T(1024)(128)(4,1)}), s8[2097152]{0:T(1024)(128)(4,1)S(1)}, s32[]{:S(2)}) async-start(s8[6291456]{0:T(1024)(128)(4,1)} %bitcast.4), calls=%async_computation.2 | async-start | bytes 4194304
  101.2 7.2 %collective-permute-start.24 = (bf16[256,256]{1,0:T(8,128)(2,1)S(1)}, bf16[256,256]{1,0:T(8,128)(2,1)S(1)}, u32[]{:S(2)}, u32[]{:S(2)}) collective-permute-start(bf16[256,256]{1,0:T(8,128)(2,1)S(1)} %get-tuple-element.74), channel_id=1, source_target_pairs={{0,1},{1,0},{2,3},{3,2},{4,5},{5,4},{6,7},{7,6},{8,9},{9,8},{10,11... | collective-permute-start | bytes 393224 | tf_op jit(solution)/shard_map/ppermute | solution.py:92
  109.9 6.4 %collective-permute-start.28 = (bf16[256,256]{1,0:T(8,128)(2,1)S(1)}, bf16[256,256]{1,0:T(8,128)(2,1)S(1)}, u32[]{:S(2)}, u32[]{:S(2)}) collective-permute-start(bf16[256,256]{1,0:T(8,128)(2,1)S(1)} %get-tuple-element.78.refs_2_), channel_id=1, source_target_pairs={{0,6},{1,7},{2,0},{3,1},{4,2},{5,3},{6,4},{7,5},{8,14},{9,15},{10,... | collective-permute-start | bytes 393224 | tf_op jit(solution)/shard_map/ppermute | solution.py:92
  109.9 12.6 %collective-permute-start.29 = (bf16[256,256]{1,0:T(8,128)(2,1)S(1)}, bf16[256,256]{1,0:T(8,128)(2,1)S(1)}, u32[]{:S(2)}, u32[]{:S(2)}) collective-permute-start(bf16[256,256]{1,0:T(8,128)(2,1)S(1)} %get-tuple-element.78.refs_2_), channel_id=1, source_target_pairs={{0,4},{1,5},{2,6},{3,7},{4,0},{5,1},{6,2},{7,3},{8,12},{9,13},{10,... | collective-permute-start | bytes 393224 | tf_op jit(solution)/shard_map/ppermute | solution.py:92
  110.6 11.9 %collective-permute-start.30 = (bf16[256,256]{1,0:T(8,128)(2,1)S(1)}, bf16[256,256]{1,0:T(8,128)(2,1)S(1)}, u32[]{:S(2)}, u32[]{:S(2)}) collective-permute-start(bf16[256,256]{1,0:T(8,128)(2,1)S(1)} %get-tuple-element.78.refs_2_), channel_id=1, source_target_pairs={{0,2},{1,3},{2,4},{3,5},{4,6},{5,7},{6,0},{7,1},{8,10},{9,11},{10,... | collective-permute-start | bytes 393224 | tf_op jit(solution)/shard_map/ppermute | solution.py:92
  122.5 4.1 %collective-permute-start.31 = (bf16[768,256]{1,0:T(8,128)(2,1)S(1)}, bf16[768,256]{1,0:T(8,128)(2,1)S(1)}, u32[]{:S(2)}, u32[]{:S(2)}) collective-permute-start(bf16[768,256]{1,0:T(8,128)(2,1)S(1)} %shard_map.76.refs_4_), channel_id=1, source_target_pairs={{0,8},{1,9},{2,10},{3,11},{4,12},{5,13},{6,14},{7,15},{8,0},{9,1},... | collective-permute-start | bytes 1179656 | tf_op jit(solution)/shard_map/ppermute | solution.py:92
  122.6 4.0 %collective-permute-start.27 = (bf16[256,256]{1,0:T(8,128)(2,1)S(1)}, bf16[256,256]{1,0:T(8,128)(2,1)S(1)}, u32[]{:S(2)}, u32[]{:S(2)}) collective-permute-start(bf16[256,256]{1,0:T(8,128)(2,1)S(1)} %get-tuple-element.78.refs_2_), channel_id=1, source_target_pairs={{0,8},{1,9},{2,10},{3,11},{4,12},{5,13},{6,14},{7,15},{8,0},{9,1},... | collective-permute-start | bytes 393224 | tf_op jit(solution)/shard_map/ppermute | solution.py:92
  123.1 12.5 %collective-permute-start.21 = (bf16[384,256]{1,0:T(8,128)(2,1)S(1)}, bf16[384,256]{1,0:T(8,128)(2,1)S(1)}, u32[]{:S(2)}, u32[]{:S(2)}) collective-permute-start(bf16[384,256]{1,0:T(8,128)(2,1)S(1)} %get-tuple-element.66), channel_id=1, source_target_pairs={{0,1},{1,0},{2,3},{3,2},{4,5},{5,4},{6,7},{7,6},{8,9},{9,8},{10,11... | collective-permute-start | bytes 589832 | tf_op jit(solution)/shard_map/ppermute | solution.py:92
  123.8 13.2 %collective-permute-start.22 = (bf16[384,256]{1,0:T(8,128)(2,1)S(1)}, bf16[384,256]{1,0:T(8,128)(2,1)S(1)}, u32[]{:S(2)}, u32[]{:S(2)}) collective-permute-start(bf16[384,256]{1,0:T(8,128)(2,1)S(1)} %get-tuple-element.67), channel_id=1, source_target_pairs={{0,16},{1,17},{2,18},{3,19},{4,20},{5,21},{6,22},{7,23},{8,24},{9,... | collective-permute-start | bytes 589832 | tf_op jit(solution)/shard_map/ppermute | solution.py:92
  125.1 11.9 %collective-permute-start.23 = (bf16[384,256]{1,0:T(8,128)(2,1)S(1)}, bf16[384,256]{1,0:T(8,128)(2,1)S(1)}, u32[]{:S(2)}, u32[]{:S(2)}) collective-permute-start(bf16[384,256]{1,0:T(8,128)(2,1)S(1)} %get-tuple-element.68), channel_id=1, source_target_pairs={{0,17},{1,16},{2,19},{3,18},{4,21},{5,20},{6,23},{7,22},{8,25},{9,... | collective-permute-start | bytes 589832 | tf_op jit(solution)/shard_map/ppermute | solution.py:92
  133.5 6.3 %collective-permute-start.32 = (bf16[256,256]{1,0:T(8,128)(2,1)S(1)}, bf16[256,256]{1,0:T(8,128)(2,1)S(1)}, u32[]{:S(2)}, u32[]{:S(2)}) collective-permute-start(bf16[256,256]{1,0:T(8,128)(2,1)S(1)} %get-tuple-element.81), channel_id=1, source_target_pairs={{0,1},{1,0},{2,3},{3,2},{4,5},{5,4},{6,7},{7,6},{8,9},{9,8},{10,11... | collective-permute-start | bytes 393224 | tf_op jit(solution)/shard_map/ppermute | solution.py:92
  134.3 6.3 %collective-permute-start.33 = (bf16[256,256]{1,0:T(8,128)(2,1)S(1)}, bf16[256,256]{1,0:T(8,128)(2,1)S(1)}, u32[]{:S(2)}, u32[]{:S(2)}) collective-permute-start(bf16[256,256]{1,0:T(8,128)(2,1)S(1)} %get-tuple-element.82), channel_id=1, source_target_pairs={{0,16},{1,17},{2,18},{3,19},{4,20},{5,21},{6,22},{7,23},{8,24},{9,... | collective-permute-start | bytes 393224 | tf_op jit(solution)/shard_map/ppermute | solution.py:92
  135.6 6.6 %collective-permute-start.34 = (bf16[256,256]{1,0:T(8,128)(2,1)S(1)}, bf16[256,256]{1,0:T(8,128)(2,1)S(1)}, u32[]{:S(2)}, u32[]{:S(2)}) collective-permute-start(bf16[256,256]{1,0:T(8,128)(2,1)S(1)} %get-tuple-element.83), channel_id=1, source_target_pairs={{0,17},{1,16},{2,19},{3,18},{4,21},{5,20},{6,23},{7,22},{8,25},{9,... | collective-permute-start | bytes 393224 | tf_op jit(solution)/shard_map/ppermute | solution.py:92
  142.9 5.2 %collective-permute-start.36 = (bf16[256,256]{1,0:T(8,128)(2,1)}, bf16[256,256]{1,0:T(8,128)(2,1)S(1)}, u32[]{:S(2)}, u32[]{:S(2)}) collective-permute-start(bf16[256,256]{1,0:T(8,128)(2,1)} %shard_map.78.refs_1_), channel_id=1, source_target_pairs={{0,6},{1,7},{2,0},{3,1},{4,2},{5,3},{6,4},{7,5},{8,14},{9,15},{10,... | collective-permute-start | bytes 393224 | tf_op jit(solution)/shard_map/ppermute | solution.py:92
  143.3 11.9 %collective-permute-start.37 = (bf16[256,256]{1,0:T(8,128)(2,1)}, bf16[256,256]{1,0:T(8,128)(2,1)S(1)}, u32[]{:S(2)}, u32[]{:S(2)}) collective-permute-start(bf16[256,256]{1,0:T(8,128)(2,1)} %shard_map.78.refs_1_), channel_id=1, source_target_pairs={{0,4},{1,5},{2,6},{3,7},{4,0},{5,1},{6,2},{7,3},{8,12},{9,13},{10,... | collective-permute-start | bytes 393224 | tf_op jit(solution)/shard_map/ppermute | solution.py:92
  145.1 10.0 %collective-permute-start.38 = (bf16[256,256]{1,0:T(8,128)(2,1)}, bf16[256,256]{1,0:T(8,128)(2,1)S(1)}, u32[]{:S(2)}, u32[]{:S(2)}) collective-permute-start(bf16[256,256]{1,0:T(8,128)(2,1)} %shard_map.78.refs_1_), channel_id=1, source_target_pairs={{0,2},{1,3},{2,4},{3,5},{4,6},{5,7},{6,0},{7,1},{8,10},{9,11},{10,... | collective-permute-start | bytes 393224 | tf_op jit(solution)/shard_map/ppermute | solution.py:92
  155.2 2.2 %collective-permute-start.39 = (bf16[768,256]{1,0:T(8,128)(2,1)S(1)}, bf16[768,256]{1,0:T(8,128)(2,1)S(1)}, u32[]{:S(2)}, u32[]{:S(2)}) collective-permute-start(bf16[768,256]{1,0:T(8,128)(2,1)S(1)} %shard_map.79.refs_3_), channel_id=1, source_target_pairs={{0,8},{1,9},{2,10},{3,11},{4,12},{5,13},{6,14},{7,15},{8,0},{9,1},... | collective-permute-start | bytes 1179656 | tf_op jit(solution)/shard_map/ppermute | solution.py:92
  155.3 2.1 %collective-permute-start.35 = (bf16[256,256]{1,0:T(8,128)(2,1)}, bf16[256,256]{1,0:T(8,128)(2,1)S(1)}, u32[]{:S(2)}, u32[]{:S(2)}) collective-permute-start(bf16[256,256]{1,0:T(8,128)(2,1)} %shard_map.78.refs_1_), channel_id=1, source_target_pairs={{0,8},{1,9},{2,10},{3,11},{4,12},{5,13},{6,14},{7,15},{8,0},{9,1},... | collective-permute-start | bytes 393224 | tf_op jit(solution)/shard_map/ppermute | solution.py:92
  161.8 7.1 %collective-permute-start.40 = (bf16[384,256]{1,0:T(8,128)(2,1)S(1)}, bf16[384,256]{1,0:T(8,128)(2,1)S(1)}, u32[]{:S(2)}, u32[]{:S(2)}) collective-permute-start(bf16[384,256]{1,0:T(8,128)(2,1)S(1)} %get-tuple-element.86), channel_id=1, source_target_pairs={{0,1},{1,0},{2,3},{3,2},{4,5},{5,4},{6,7},{7,6},{8,9},{9,8},{10,11... | collective-permute-start | bytes 589832 | tf_op jit(solution)/shard_map/ppermute | solution.py:92
  163.7 7.8 %collective-permute-start.41 = (bf16[384,256]{1,0:T(8,128)(2,1)S(1)}, bf16[384,256]{1,0:T(8,128)(2,1)S(1)}, u32[]{:S(2)}, u32[]{:S(2)}) collective-permute-start(bf16[384,256]{1,0:T(8,128)(2,1)S(1)} %get-tuple-element.87), channel_id=1, source_target_pairs={{0,16},{1,17},{2,18},{3,19},{4,20},{5,21},{6,22},{7,23},{8,24},{9,... | collective-permute-start | bytes 589832 | tf_op jit(solution)/shard_map/ppermute | solution.py:92
  163.9 10.5 %collective-permute-start.42 = (bf16[384,256]{1,0:T(8,128)(2,1)S(1)}, bf16[384,256]{1,0:T(8,128)(2,1)S(1)}, u32[]{:S(2)}, u32[]{:S(2)}) collective-permute-start(bf16[384,256]{1,0:T(8,128)(2,1)S(1)} %get-tuple-element.88), channel_id=1, source_target_pairs={{0,17},{1,16},{2,19},{3,18},{4,21},{5,20},{6,23},{7,22},{8,25},{9,... | collective-permute-start | bytes 589832 | tf_op jit(solution)/shard_map/ppermute | solution.py:92
  (7 other events, 28.0 us)

commit v7 on v6

--- a/solution.py
+++ b/solution.py
@@ -91,14 +91,13 @@
             pairs.append((i, self.near(i, dx, dc, dz, dy)))
         return lax.ppermute(value, AXES, pairs)
 
-    def gathered(self, value, after):
-        cores = range(1, self.core)
-        pieces = [value] + [self.shift(value, dc=-dc) for dc in cores]
+    def by_core(self, value):
+        return [value] + [self.shift(value, dc=-dc) for dc in range(1, self.core)]
+
+    def gathered(self, value, after, own=None):
+        pieces = own or self.by_core(value)
         along = [self.shift(value, dz=-dz) for dz in range(1, self.z)]
-        if along:
-            along = pack(along, after)
-            pieces += [along] + [self.shift(along, dc=-dc) for dc in cores]
-        return pieces
+        return pieces + (self.by_core(pack(along, after)) if along else [])
 
     def index(self, x, core, z, y):
         x, core, z, y = x % self.x, core % self.core, z % self.z, y % self.y
@@ -170,7 +169,8 @@
     return [row[:, k : k + 128] for k in range(0, row.shape[1], 128)]
 
 
-def letter_kernel(layout, form, slots, inc_ref, points_ref, letter_ref):
+def letter_kernel(layout, form, slots, inc_ref, points_ref, *refs):
+    letter_ref = refs[-1]
     edges, tri_dev, half = form.edges, form.tri_dev, form.half
     ends, devices = 2 * edges, layout.devices
     plus, minus = inc_ref[0:1, :], inc_ref[1:2, :]
@@ -207,15 +207,15 @@
                 letter_ref[d] = letter
 
 
-def letters_of(layout, form, incidence, centroids, slots):
+def letters_of(layout, form, incidence, centroids, slots, after):
     return pl.pallas_call(
         functools.partial(letter_kernel, layout, form, slots),
-        in_specs=[whole()] * 2,
+        in_specs=[whole()] * (2 + len(after)),
         out_specs=whole(),
         out_shape=jax.ShapeDtypeStruct((layout.devices, form.rows, 128), I32),
         compiler_params=PARAMS,
         cost_estimate=cost(1),
-    )(incidence, centroids)
+    )(incidence, centroids, *after)
 
 
 def pack_kernel(count, *refs):
@@ -257,7 +257,13 @@
     return value
 
 
-def tile_kernel(layout, form, block, me_ref, letter_ref, *refs):
+def rows_at(ref, step, rows):
+    if ref.shape[0] == rows:
+        return ref
+    return ref.at[pl.ds(pl.multiple_of(step * rows, rows), rows), :]
+
+
+def tile_kernel(layout, form, block, first, me_ref, letter_ref, after_ref, *refs):
     real_ref, imag_ref, token_ref, col_ref = refs
     token_ref[...] = jnp.zeros_like(token_ref)
     me, step, size = me_ref[0], pl.program_id(0), form.tri_dev
@@ -268,7 +274,8 @@
             letter = letter_ref[layout.in_line(me, k)]
             col_ref[:, k * size : (k + 1) * size] = features(form.points(letter), 1.0, False)
 
-    letter = letter_ref[layout.in_plane(me, step)]
+    real_ref, imag_ref = [rows_at(ref, step, size) for ref in (real_ref, imag_ref)]
+    letter = letter_ref[layout.in_plane(me, first + step)]
     row = features(form.points(letter), 1.0 / (TURNS * TURNS), True)
     for base in range(0, col_ref.shape[1], block):
         cols = slice(base, base + block)
@@ -283,15 +290,15 @@
         imag_ref[:, cols] = (poly(SIN, -SPACING / TURNS, u) * (frac * inverse)).astype(BF16)
 
 
-def build(kernel, outs, rows, span, cols, me, arrays, time, scratch=(), extra=()):
+def build(kernel, outs, rows, span, arrays, time, cols, me, resident, scratch=(), extra=()):
+    space = pltpu.VMEM if resident else pltpu.HBM
+    block = whole() if resident else pl.BlockSpec((rows, cols), lambda j: (j, 0))
     return pl.pallas_call(
         kernel,
         grid=(len(span),),
         in_specs=[pl.BlockSpec(memory_space=pltpu.SMEM)] + [fixed(array) for array in arrays],
-        out_specs=[pl.BlockSpec((rows, cols), lambda j: (j, 0))] * outs
-        + [fixed(array) for array in extra]
-        + [token_spec()],
-        out_shape=[pltpu.HBM((len(span) * rows, cols), BF16)] * outs + list(extra) + [TOKEN],
+        out_specs=[block] * outs + [fixed(array) for array in extra] + [token_spec()],
+        out_shape=[space((len(span) * rows, cols), BF16)] * outs + list(extra) + [TOKEN],
         scratch_shapes=scratch,
         compiler_params=PARAMS,
         cost_estimate=cost(time),
@@ -308,7 +315,8 @@
 def adjacency_kernel(layout, tri_dev, first, me_ref, label_ref, after_ref, out_ref, *refs):
     refs[-1][...] = jnp.zeros_like(refs[-1])
     me, step = me_ref[0], pl.program_id(0)
-    rows, cols = out_ref.shape
+    rows, cols = tri_dev, out_ref.shape[1]
+    out_ref = rows_at(out_ref, step, rows)
     label = label_ref[layout.spot(me, first + step)]
     mark = (label & 0xFFFF) - 1
     place = layout.place(lax.shift_right_logical(label, 16), tri_dev, me)
@@ -329,7 +337,8 @@
 def incidence_kernel(layout, form, me_ref, letter_ref, after_ref, out_ref, token_ref):
     token_ref[...] = jnp.zeros_like(token_ref)
     me, step = me_ref[0], pl.program_id(0)
-    edges, cols = out_ref.shape
+    edges, cols = form.edges, out_ref.shape[1]
+    out_ref = rows_at(out_ref, step, edges)
     size = form.tri_dev
     letter = letter_ref[layout.in_plane(me, step)]
     plus, minus = [layout.place(end, size, me) for end in form.ends(letter)]
@@ -386,36 +395,13 @@
     )(me, letters, *pieces)
 
 
-def apply_kernel(mats, fed, count, *refs):
-    matrices, pieces = refs[:mats], refs[mats : mats + fed]
-    outs, token_ref = refs[-count - 3 : -3], refs[-3]
-    slots, sems = refs[-2:]
-    token_ref[...] = jnp.zeros_like(token_ref)
-    step = pl.program_id(0)
-    rows = slots.shape[2]
+def apply_kernel(mats, fed, block, *refs):
+    matrices, pieces, outs = refs[:mats], refs[mats : mats + fed], refs[mats + fed : -1]
+    refs[-1][...] = jnp.zeros_like(refs[-1])
     half = pieces[0].shape[1] // 2
-
-    def copy(m, block):
-        start = pl.multiple_of(block * rows, rows)
-        slot = block % 2
-        return pltpu.make_async_copy(
-            matrices[m].at[pl.ds(start, rows), :], slots.at[slot, m], sems.at[slot, m]
-        )
-
-    @pl.when(step == 0)
-    def _():
-        for m in range(mats):
-            copy(m, step).start()
-
-    @pl.when(step + 1 < count)
-    def _():
-        for m in range(mats):
-            copy(m, step + 1).start()
-
     sums = []
-    for m in range(mats):
-        copy(m, step).wait()
-        matrix = slots.at[step % 2, m]
+    for matrix in matrices:
+        matrix = rows_at(matrix, pl.program_id(0), block)
         total, col = None, 0
         for piece in pieces:
             size = piece.shape[0]
@@ -432,25 +418,35 @@
     set_blocks(value, outs)
 
 
-def apply(matrices, pieces, block, after=(), exact=True):
+def apply(matrices, pieces, block, resident, exact, after):
     rows, cols = matrices[0].shape
     count, mats = rows // block, len(matrices)
     shapes = blocks_like(count, block, pieces[0].shape[1], exact) + [TOKEN]
-    return pl.pallas_call(
-        functools.partial(apply_kernel, mats, len(pieces), count),
+    spec = whole() if resident else pl.BlockSpec((block, cols), lambda j: (j, 0))
+
+    def kernel(*refs):
+        fed = len(refs) - len(shapes) - len(after)
+        apply_kernel(mats, fed - mats, block, *refs[:fed], *refs[fed + len(after) :])
+
+    return pl.pallas_call(
+        kernel,
         grid=(count,),
-        in_specs=[pl.BlockSpec(memory_space=pltpu.HBM)] * mats
+        in_specs=[spec] * mats
         + [fixed(piece) for piece in pieces]
         + [token_spec()] * len(after),
         out_specs=[fixed(shape) for shape in shapes],
         out_shape=shapes,
-        scratch_shapes=[
-            pltpu.VMEM((2, mats, block, cols), BF16),
-            pltpu.SemaphoreType.DMA((2, mats)),
-        ],
-        compiler_params=PARAMS,
-        cost_estimate=cost(2 * mats),
+        compiler_params=PARAMS,
+        cost_estimate=cost(count * mats / 2),
     )(*matrices, *pieces, *after)
+
+
+def multiply(parts, pieces, block, resident, after=()):
+    blocks, token = [], None
+    for part in parts:
+        *more, token = apply(part, pieces, block, resident, not blocks, after)
+        blocks += more
+    return blocks, token
 
 
 def sum_kernel(count, own_ref, *refs):
@@ -483,7 +479,8 @@
     total = own_ref[...]
     for ref in refs[:count]:
         total = total + ref[...].astype(F32)
-    refs[-1][...] = total.astype(BF16)
+    refs[-2][...] = total.astype(BF16)
+    refs[-1][...] = jnp.zeros_like(refs[-1])
 
 
 def potential_of(blocks, after):
@@ -491,8 +488,8 @@
     return pl.pallas_call(
         functools.partial(potential_kernel, len(got)),
         in_specs=[whole()] * (len(blocks) + len(after)),
-        out_specs=whole(),
-        out_shape=jax.ShapeDtypeStruct(blocks[0].shape, BF16),
+        out_specs=[whole()] * 2,
+        out_shape=[jax.ShapeDtypeStruct(blocks[0].shape, BF16), TOKEN],
         compiler_params=PARAMS,
         cost_estimate=cost(1),
     )(*blocks, *after)
@@ -502,25 +499,27 @@
     around = own_ref[...]
     for ref in refs[:count]:
         around = around + ref[...].astype(F32)
-    out_ref, rounded_ref = refs[-2:]
+    out_ref, rounded_ref, token_ref = refs[-3:]
+    token_ref[...] = jnp.zeros_like(token_ref)
     change = degree_ref[:, 0:1] * potential_ref[...].astype(F32) - around
     value = charge_ref[...] - weight_ref[0] * change
     out_ref[...] = value
     rounded_ref[...] = value.astype(BF16)
 
 
-def charge_of(weight, charge, degree, potential, blocks):
+def charge_of(weight, charge, degree, potential, blocks, after):
     return pl.pallas_call(
         functools.partial(charge_kernel, len(blocks) - 1),
-        in_specs=[pl.BlockSpec(memory_space=pltpu.SMEM)] + [whole()] * (3 + len(blocks)),
-        out_specs=[whole()] * 2,
+        in_specs=[pl.BlockSpec(memory_space=pltpu.SMEM)] + [whole()] * (3 + len(blocks) + len(after)),
+        out_specs=[whole()] * 3,
         out_shape=[
             jax.ShapeDtypeStruct(charge.shape, F32),
             jax.ShapeDtypeStruct(charge.shape, BF16),
+            TOKEN,
         ],
         compiler_params=PARAMS,
         cost_estimate=cost(1),
-    )(weight, charge, degree, potential, *blocks)
+    )(weight, charge, degree, potential, *blocks, *after)
 
 
 def current_kernel(count, weight_ref, current_ref, own_ref, *refs):
@@ -552,76 +551,92 @@
     sweeps = sweep_weights.shape[0]
     cols = layout.z * layout.core * tri_dev
 
+    resident = count * (3 * tri_dev + edge_dev) * cols * 2 <= 24 * 2**20
+
+    own = layout.by_core(currents)
     form = Letter(edge_dev, tri_dev, count * slots)
-    letters = letters_of(layout, form, incidence, centroids, slots)
+    letters = letters_of(
+        layout, form, incidence, centroids, slots, own[1:]
+    )
     letters = lax.all_to_all(letters, AXES, split_axis=0, concat_axis=0, tiled=True)
     labels = letters[:, form.starts[3] :, :].reshape(devices, -1)[:, : count * slots]
     labels = labels.reshape(devices, count, slots).transpose(1, 0, 2)
     labels = labels.reshape(count, 1, devices * slots)
 
-    make = functools.partial(build, cols=cols, me=me)
-    plane = range(count)
-    *tiles, token = make(
-        functools.partial(tile_kernel, layout, form, min(512, cols)),
-        2,
-        tri_dev,
-        plane,
-        arrays=(letters,),
-        time=12,
-        scratch=[pltpu.VMEM((16, cols), BF16)],
-    )
-    pieces = layout.gathered(currents, (token,))
-    *blocks, token = first_charges(layout, form, me, letters, pieces)
-    slopes_of, token = make(
-        functools.partial(incidence_kernel, layout, form),
-        1,
-        edge_dev,
-        plane,
-        arrays=(letters, token),
-        time=6,
-    )
-    charge, rounded, token = sum_of(layout.given(blocks), (token,))
-
+    make = functools.partial(build, cols=cols, me=me, resident=resident)
     cut = (count + 1) // 2
-
-    def adjacency(span, token):
-        *parts, token = make(
+    spans = [span for span in (range(cut), range(cut, count)) if span]
+
+    def tile_part(span, token):
+        *part, token = make(
+            functools.partial(tile_kernel, layout, form, min(512, cols), span[0]),
+            2,
+            tri_dev,
+            span,
+            (letters, token),
+            6,
+            scratch=[pltpu.VMEM((16, cols), BF16)],
+        )
+        return part, token
+
+    def adjacency_part(span, token):
+        extra = () if span[0] else (jax.ShapeDtypeStruct((tri_dev, 128), F32),)
+        *part, token = make(
             functools.partial(adjacency_kernel, layout, tri_dev, span[0]),
             1,
             tri_dev,
             span,
-            arrays=(labels, token),
-            time=5,
-            extra=() if span[0] else (jax.ShapeDtypeStruct((tri_dev, 128), F32),),
+            (labels, token),
+            6,
+            extra=extra,
         )
-        return parts, token
-
-    (near, degree), token = adjacency(plane[:cut], token)
-    neighbours = [near]
-    current = currents
-    potential = None
-    slopes, after = None, (token,)
+        return part, token
+
+    pieces = layout.gathered(currents, (letters,), own)
+    *blocks, token = first_charges(layout, form, me, letters, pieces)
+    part, token = tile_part(spans[0], token)
+    tiles = [part]
+    charge, rounded, token = sum_of(layout.given(blocks), (token,))
+    for span in spans[1:]:
+        part, token = tile_part(span, token)
+        tiles.append(part)
+
+    near, slopes_of = [], []
+    degree, slopes = None, None
+    current, potential = currents, None
     for sweep in range(sweeps):
         weight = sweep_weights[sweep].reshape(1)
-        pieces = layout.gathered(rounded, after)
-        *blocks, token = apply(tiles, pieces, tri_dev)
+        pieces = layout.gathered(rounded, (token,))
+        blocks, token = multiply(tiles, pieces, tri_dev, resident)
         if slopes is not None:
             current, token = current_of(last_weight, current, layout.given(slopes))
-        elif cut < count:
-            (far,), token = adjacency(plane[cut:], token)
-            neighbours.append(far)
-        potential = potential_of(layout.given(blocks), (token,))
-        pieces = layout.gathered(potential, ())
+        else:
+            (part, degree), token = adjacency_part(spans[0], token)
+            near.append([part])
+        potential, token = potential_of(layout.given(blocks), (token,))
+        if slopes is None:
+            for span in spans[1:]:
+                part, token = adjacency_part(span, token)
+                near.append(part)
+        pieces = layout.gathered(potential, (token,))
         if sweep + 1 < sweeps:
-            blocks = []
-            for part in neighbours:
-                *more, _ = apply([part], pieces, tri_dev, (), not blocks)
-                blocks += more
-            charge, rounded = charge_of(
-                weight, charge, degree, potential, layout.given(blocks)
+            blocks, token = multiply(near, pieces, tri_dev, resident)
+        if slopes is None:
+            *part, token = make(
+                functools.partial(incidence_kernel, layout, form),
+                1,
+                edge_dev,
+                range(count),
+                (letters, token),
+                6,
             )
-        *slopes, token = apply([slopes_of], pieces, edge_dev)
-        after, last_weight = (token,), weight
+            slopes_of.append(part)
+        if sweep + 1 < sweeps:
+            charge, rounded, token = charge_of(
+                weight, charge, degree, potential, layout.given(blocks), (token,)
+            )
+        slopes, token = multiply(slopes_of, pieces, edge_dev, resident, (token,))
+        last_weight = weight
     current, _ = current_of(last_weight, current, layout.given(slopes))
     return current, potential
 

time: 176 us -> 174 us (0.989)
  Pallas kernels: 60.6 us -> 48.6 us
  starting transfers between devices: 50.3 us -> 60.6 us
  waiting for transfers between devices: 60.8 us -> 54.4 us
  local copies, waits for them, and re-layouts: 3.18 us -> 9.54 us
    ppermute x43, starting transfers between devices: 43 us -> 53.4 us  [shift(): return lax.ppermute(value, AXES, pairs)]
    pallas_call x6 -> x8, Pallas kernels: 23.1 us -> 15.6 us  [apply(): pl.pallas_call(kernel, grid=(count,), in_specs=[spec] * mats + [fixed(pie...]
    unnamed x22 -> x30, local copies, waits for them, and re-layouts: 2.34 us -> 8.72 us
    pallas_call x4 -> x5, Pallas kernels: 28.5 us -> 24.1 us  [build(): pl.pallas_call(kernel, grid=(len(span),), in_specs=[pl.BlockSpec(memory_s...]
    ppermute x43, waiting for transfers between devices: 57.9 us -> 54.4 us  [shift(): return lax.ppermute(value, AXES, pairs)]
    all_to_all x1, waiting for transfers between devices: 2.98 us -> 0.01 us  [per_device(): lax.all_to_all(letters, AXES, split_axis=0, concat_axis=0, tiled=True)]
  transfers between devices with their start and end apart: 44 -> 44, of which waited for: 24 -> 23; matrix products, arithmetic and copies ran while one was open for 0% -> 0% of each run, Pallas kernels for 23% -> 20%
where the time goes in v7:
time: 174 us
  starting transfers between devices  60.6 us (35%)
  waiting for transfers between devices  54.4 us (31%)
  Pallas kernels  48.6 us (28%)
  local copies, waits for them, and re-layouts  9.54 us (5%)
    ppermute x43, waiting for transfers between devices, shift(): return lax.ppermute(value, AXES, pairs)  54.4 us
    ppermute x43, starting transfers between devices, shift(): return lax.ppermute(value, AXES, pairs)  53.4 us
    pallas_call x5, Pallas kernels, build(): pl.pallas_call(kernel, grid=(len(span),), in_specs=[pl.BlockSpec(memory_s...  24.1 us
    pallas_call x8, Pallas kernels, apply(): pl.pallas_call(kernel, grid=(count,), in_specs=[spec] * mats + [fixed(pie...  15.6 us
    unnamed x30, local copies, waits for them, and re-layouts  8.72 us
    all_to_all x1, starting transfers between devices, per_device(): lax.all_to_all(letters, AXES, split_axis=0, concat_axis=0, tiled=True)  7.22 us
  transfers between devices with their start and end apart: 44, of which 23 were waited for; matrix products, arithmetic and copies ran while one was open for 0% of the time, Pallas kernels for 20%

profile of v7, /device:TPU:0, one launch (start us, length us, event | category | flops | bytes accessed | tf_op | source)
XLA Modules:
  0.0 174.1 jit_solution(11750863046572049253)
XLA Ops:
  5.0 7.2 %all-to-all-start = ((s32[32,8,128]{2,1,0:T(8,128)}), s32[32,8,128]{2,1,0:T(8,128)S(1)}, u32[]{:S(2)}, u32[]{:S(2)}) async-start(s32[32,8,128]{2,1,0:T(8,128)} %shard_map.59), calls=%async_computation | async-start | bytes 262144 | tf_op jit(solution)/shard_map/all_to_all | solution.py:561
  12.3 1.8 %collective-permute-start.3 = (bf16[384,256]{1,0:T(8,128)(2,1)S(1)}, bf16[384,256]{1,0:T(8,128)(2,1)S(1)}, u32[]{:S(2)}, u32[]{:S(2)}) collective-permute-start(bf16[384,256]{1,0:T(8,128)(2,1)S(1)} %copy-done), channel_id=1, source_target_pairs={{0,2},{1,3},{2,4},{3,5},{4,6},{5,7},{6,0},{7,1},{8,10},{9,11},{10,... | collective-permute-start | bytes 589832 | tf_op jit(solution)/shard_map/ppermute | solution.py:92
  14.1 2.4 %collective-permute-start.2 = (bf16[384,256]{1,0:T(8,128)(2,1)S(1)}, bf16[384,256]{1,0:T(8,128)(2,1)S(1)}, u32[]{:S(2)}, u32[]{:S(2)}) collective-permute-start(bf16[384,256]{1,0:T(8,128)(2,1)S(1)} %copy-done), channel_id=1, source_target_pairs={{0,4},{1,5},{2,6},{3,7},{4,0},{5,1},{6,2},{7,3},{8,12},{9,13},{10,... | collective-permute-start | bytes 589832 | tf_op jit(solution)/shard_map/ppermute | solution.py:92
  16.5 1.4 collective-permute-start.1
  17.9 5.8 %collective-permute-done.3.refs_2_ = bf16[384,256]{1,0:T(8,128)(2,1)S(1)} collective-permute-done((bf16[384,256]{1,0:T(8,128)(2,1)S(1)}, bf16[384,256]{1,0:T(8,128)(2,1)S(1)}, u32[]{:S(2)}, u32[]{:S(2)}) %collective-permute-start.3) | collective-permute-done | bytes 196640 | tf_op jit(solution)/shard_map/ppermute | solution.py:92
  23.8 8.0 %collective-permute-done.2.refs_1_ = bf16[384,256]{1,0:T(8,128)(2,1)S(1)} collective-permute-done((bf16[384,256]{1,0:T(8,128)(2,1)S(1)}, bf16[384,256]{1,0:T(8,128)(2,1)S(1)}, u32[]{:S(2)}, u32[]{:S(2)}) %collective-permute-start.2) | collective-permute-done | bytes 196640 | tf_op jit(solution)/shard_map/ppermute | solution.py:92
  31.9 2.0 %collective-permute-done.4.refs_3_ = bf16[1152,256]{1,0:T(8,128)(2,1)S(1)} collective-permute-done((bf16[1152,256]{1,0:T(8,128)(2,1)S(1)}, bf16[1152,256]{1,0:T(8,128)(2,1)S(1)}, u32[]{:S(2)}, u32[]{:S(2)}) %collective-permute-start.4) | collective-permute-done | bytes 589856 | tf_op jit(solution)/shard_map/ppermute | solution.py:92
  33.8 3.1 %shard_map.61 = (f32[256,256]{1,0:T(8,128)S(1)}, bf16[256,256]{1,0:T(8,128)(2,1)S(1)}, bf16[256,256]{1,0:T(8,128)(2,1)S(1)}, bf16[256,256]{1,0:T(8,128)(2,1)S(1)}, f32[8,128]{1,0:T(8,128)S(1)}) custom-call(s32[1]{0:T(128)} %bitcast.me_ref, s32[32,8,128]{2,1,0:T(8,128)S(1)} %all-to-all-done.refs_3_.letter_ref, bf16[384,256]{1,0:T(8,128)(2,1)S(1)} %copy-done, ...), custom_call_target="tpu_custom_call" | custom-call | flops 4600000000 | tf_op jit(solution)/shard_map/pallas_call | solution.py:386
  36.9 1.6 collective-permute-start.5
  38.5 1.5 collective-permute-start.6
  40.5 4.7 %shard_map.62 = (bf16[512,2048]{1,0:T(8,128)(2,1)S(1)}, bf16[512,2048]{1,0:T(8,128)(2,1)S(1)}, f32[8,128]{1,0:T(8,128)S(1)}) custom-call(s32[1]{0:T(128)} %bitcast.me_ref, s32[32,8,128]{2,1,0:T(8,128)S(1)} %all-to-all-done.refs_3_.letter_ref, f32[8,128]{1,0:T(8,128)S(1)} %get-tuple-element.55.after_ref), custom_call_target="tpu_custom_call" | custom-call | flops 6899999744 | tf_op jit(solution)/shard_map/pallas_call | solution.py:296
  47.9 4.5 %collective-permute-start.11 = (bf16[256,256]{1,0:T(8,128)(2,1)S(1)}, bf16[256,256]{1,0:T(8,128)(2,1)S(1)}, u32[]{:S(2)}, u32[]{:S(2)}) collective-permute-start(bf16[256,256]{1,0:T(8,128)(2,1)S(1)} %get-tuple-element.63.refs_2_), channel_id=1, source_target_pairs={{0,2},{1,3},{2,4},{3,5},{4,6},{5,7},{6,0},{7,1},{8,10},{9,11},{10,... | collective-permute-start | bytes 393224 | tf_op jit(solution)/shard_map/ppermute | solution.py:92
  54.8 4.7 %shard_map.64 = (bf16[512,2048]{1,0:T(8,128)(2,1)S(1)}, bf16[512,2048]{1,0:T(8,128)(2,1)S(1)}, f32[8,128]{1,0:T(8,128)S(1)}) custom-call(s32[1]{0:T(128)} %bitcast.me_ref, s32[32,8,128]{2,1,0:T(8,128)S(1)} %all-to-all-done.refs_3_.letter_ref, f32[8,128]{1,0:T(8,128)S(1)} %get-tuple-element.64.after_ref), custom_call_target="tpu_custom_call" | custom-call | flops 6899999744 | tf_op jit(solution)/shard_map/pallas_call | solution.py:296
  64.1 1.6 copy-done.9
  65.7 1.6 copy-done.12
  67.3 1.5 shard_map.67
  68.7 1.6 collective-permute-start.14
  70.3 1.5 collective-permute-start.15
  71.8 2.1 %shard_map.66 = (f32[256,256]{1,0:T(8,128)S(1)}, bf16[256,256]{1,0:T(8,128)(2,1)S(1)}, f32[8,128]{1,0:T(8,128)}) custom-call(bf16[512,2048]{1,0:T(8,128)(2,1)S(1)} %copy-done.5, bf16[512,2048]{1,0:T(8,128)(2,1)S(1)} %copy-done.7, bf16[256,256]{1,0:T(8,128)(2,1)S(1)} %get-tuple-element.63.refs_2_, bf16[256,256]{1,0:T(8,128)(2,1)S(1)} %collective-permute-done.8.refs_3_, ...), custom_call_target="tpu_custom_call" | custom-call | flops 2300000000 | tf_op jit(solution)/shard_map/pallas_call | solution.py:431
  74.3 5.3 %shard_map.68 = (bf16[512,2048]{1,0:T(8,128)(2,1)S(1)}, f32[256,128]{1,0:T(8,128)S(1)}, f32[8,128]{1,0:T(8,128)S(1)}) custom-call(s32[1]{0:T(128)} %bitcast.me_ref, s32[4,1,2048]{2,1,0:T(1,128)S(1)} %reshape.11.label_ref, f32[8,128]{1,0:T(8,128)S(1)} %get-tuple-element.72.after_ref), custom_call_target="tpu_custom_call" | custom-call | flops 6899999744 | tf_op jit(solution)/shard_map/pallas_call | solution.py:296
  80.9 3.2 %collective-permute-start.19 = (bf16[256,256]{1,0:T(8,128)(2,1)S(1)}, bf16[256,256]{1,0:T(8,128)(2,1)S(1)}, u32[]{:S(2)}, u32[]{:S(2)}) collective-permute-start(bf16[256,256]{1,0:T(8,128)(2,1)S(1)} %get-tuple-element.76.refs_1_.potential_ref), channel_id=1, source_target_pairs={{0,2},{1,3},{2,4},{3,5},{4,6},{5,7},{6,0},{7,1},{8,10},{9,11},{10,... | collective-permute-start | bytes 393224 | tf_op jit(solution)/shard_map/ppermute | solution.py:92
  84.2 1.5 collective-permute-start.18
  86.6 4.9 %shard_map.70 = (bf16[512,2048]{1,0:T(8,128)(2,1)S(1)}, f32[8,128]{1,0:T(8,128)S(1)}) custom-call(s32[1]{0:T(128)} %bitcast.me_ref, s32[4,1,2048]{2,1,0:T(1,128)S(1)} %reshape.11.label_ref, f32[8,128]{1,0:T(8,128)S(1)} %get-tuple-element.74.after_ref), custom_call_target="tpu_custom_call" | custom-call | flops 6899999744 | tf_op jit(solution)/shard_map/pallas_call | solution.py:296
  91.5 2.9 %collective-permute-done.18.refs_1_ = bf16[256,256]{1,0:T(8,128)(2,1)S(1)} collective-permute-done((bf16[256,256]{1,0:T(8,128)(2,1)S(1)}, bf16[256,256]{1,0:T(8,128)(2,1)S(1)}, u32[]{:S(2)}, u32[]{:S(2)}) %collective-permute-start.18) | collective-permute-done | bytes 131104 | tf_op jit(solution)/shard_map/ppermute | solution.py:92
  97.4 1.5 collective-permute-start.22
  99.5 1.5 shard_map.74
  101.1 1.4 collective-permute-start.21
  102.5 4.6 %shard_map.73 = (bf16[1536,2048]{1,0:T(8,128)(2,1)S(1)}, f32[8,128]{1,0:T(8,128)S(1)}) custom-call(s32[1]{0:T(128)} %bitcast.me_ref, s32[32,8,128]{2,1,0:T(8,128)S(1)} %all-to-all-done.refs_3_.letter_ref, f32[8,128]{1,0:T(8,128)S(1)} %get-tuple-element.78.after_ref), custom_call_target="tpu_custom_call" | custom-call | flops 6899999744 | tf_op jit(solution)/shard_map/pallas_call | solution.py:296
  108.4 1.5 shard_map.75
  109.9 3.3 %collective-permute-start.30 = (bf16[256,256]{1,0:T(8,128)(2,1)S(1)}, bf16[256,256]{1,0:T(8,128)(2,1)S(1)}, u32[]{:S(2)}, u32[]{:S(2)}) collective-permute-start(bf16[256,256]{1,0:T(8,128)(2,1)S(1)} %get-tuple-element.94.refs_2_), channel_id=1, source_target_pairs={{0,2},{1,3},{2,4},{3,5},{4,6},{5,7},{6,0},{7,1},{8,10},{9,11},{10,... | collective-permute-start | bytes 393224 | tf_op jit(solution)/shard_map/ppermute | solution.py:92
  115.5 2.5 %shard_map.76 = (f32[384,256]{1,0:T(8,128)S(1)}, bf16[384,256]{1,0:T(8,128)(2,1)S(1)}, bf16[384,256]{1,0:T(8,128)(2,1)S(1)}, bf16[384,256]{1,0:T(8,128)(2,1)S(1)}, f32[8,128]{1,0:T(8,128)S(1)}) custom-call(bf16[1536,2048]{1,0:T(8,128)(2,1)S(1)} %get-tuple-element.79.refs_0_, bf16[256,256]{1,0:T(8,128)(2,1)S(1)} %get-tuple-element.76.refs_1_.potential_ref, ...), custom_call_target="tpu_custom_call" | custom-call | flops 2300000000 | tf_op jit(solution)/shard_map/pallas_call | solution.py:431
  118.4 4.7 %collective-permute-done.29.refs_1_ = bf16[256,256]{1,0:T(8,128)(2,1)S(1)} collective-permute-done((bf16[256,256]{1,0:T(8,128)(2,1)S(1)}, bf16[256,256]{1,0:T(8,128)(2,1)S(1)}, u32[]{:S(2)}, u32[]{:S(2)}) %collective-permute-start.29) | collective-permute-done | bytes 131104 | tf_op jit(solution)/shard_map/ppermute | solution.py:92
  125.0 1.5 collective-permute-start.25
  127.2 2.1 %shard_map.80 = (bf16[256,256]{1,0:T(8,128)(2,1)S(1)}, bf16[256,256]{1,0:T(8,128)(2,1)S(1)}, f32[8,128]{1,0:T(8,128)}) custom-call(bf16[512,2048]{1,0:T(8,128)(2,1)S(1)} %copy-done.10, bf16[512,2048]{1,0:T(8,128)(2,1)S(1)} %copy-done.13, bf16[256,256]{1,0:T(8,128)(2,1)S(1)} %get-tuple-element.94.refs_2_, ...), custom_call_target="tpu_custom_call" | custom-call | flops 2300000000 | tf_op jit(solution)/shard_map/pallas_call | solution.py:431
  130.6 1.5 collective-permute-start.34
  132.1 2.1 %shard_map.79 = (f32[256,256]{1,0:T(8,128)S(1)}, bf16[256,256]{1,0:T(8,128)(2,1)S(1)}, f32[8,128]{1,0:T(8,128)}) custom-call(bf16[512,2048]{1,0:T(8,128)(2,1)S(1)} %copy-done.5, bf16[512,2048]{1,0:T(8,128)(2,1)S(1)} %copy-done.7, bf16[256,256]{1,0:T(8,128)(2,1)S(1)} %get-tuple-element.94.refs_2_, bf16[256,256]{1,0:T(8,128)(2,1)S(1)} %collective-permute-done.27.refs_3_, ...), custom_call_target="tpu_custom_call" | custom-call | flops 2300000000 | tf_op jit(solution)/shard_map/pallas_call | solution.py:431
  134.9 2.3 %collective-permute-done.26.refs_2_ = bf16[384,256]{1,0:T(8,128)(2,1)S(1)} collective-permute-done((bf16[384,256]{1,0:T(8,128)(2,1)S(1)}, bf16[384,256]{1,0:T(8,128)(2,1)S(1)}, u32[]{:S(2)}, u32[]{:S(2)}) %collective-permute-start.26) | collective-permute-done | bytes 196640 | tf_op jit(solution)/shard_map/ppermute | solution.py:92
  138.0 1.8 %collective-permute-done.33.refs_1_ = bf16[256,256]{1,0:T(8,128)(2,1)S(1)} collective-permute-done((bf16[256,256]{1,0:T(8,128)(2,1)S(1)}, bf16[256,256]{1,0:T(8,128)(2,1)S(1)}, u32[]{:S(2)}, u32[]{:S(2)}) %collective-permute-start.33) | collective-permute-done | bytes 131104 | tf_op jit(solution)/shard_map/ppermute | solution.py:92
  139.8 1.9 %collective-permute-done.34.refs_2_ = bf16[256,256]{1,0:T(8,128)(2,1)S(1)} collective-permute-done((bf16[256,256]{1,0:T(8,128)(2,1)S(1)}, bf16[256,256]{1,0:T(8,128)(2,1)S(1)}, u32[]{:S(2)}, u32[]{:S(2)}) %collective-permute-start.34) | collective-permute-done | bytes 131104 | tf_op jit(solution)/shard_map/ppermute | solution.py:92
  142.6 3.3 %collective-permute-start.38 = (bf16[256,256]{1,0:T(8,128)(2,1)}, bf16[256,256]{1,0:T(8,128)(2,1)S(1)}, u32[]{:S(2)}, u32[]{:S(2)}) collective-permute-start(bf16[256,256]{1,0:T(8,128)(2,1)} %get-tuple-element.54.refs_1_), channel_id=1, source_target_pairs={{0,2},{1,3},{2,4},{3,5},{4,6},{5,7},{6,0},{7,1},{8,10},{9,11},{10,... | collective-permute-start | bytes 393224 | tf_op jit(solution)/shard_map/ppermute | solution.py:92
  145.9 1.5 collective-permute-start.37
  148.3 3.3 %collective-permute-done.38.refs_2_ = bf16[256,256]{1,0:T(8,128)(2,1)S(1)} collective-permute-done((bf16[256,256]{1,0:T(8,128)(2,1)}, bf16[256,256]{1,0:T(8,128)(2,1)S(1)}, u32[]{:S(2)}, u32[]{:S(2)}) %collective-permute-start.38) | collective-permute-done | bytes 131104 | tf_op jit(solution)/shard_map/ppermute | solution.py:92
  151.6 3.7 %collective-permute-done.37.refs_1_ = bf16[256,256]{1,0:T(8,128)(2,1)S(1)} collective-permute-done((bf16[256,256]{1,0:T(8,128)(2,1)}, bf16[256,256]{1,0:T(8,128)(2,1)S(1)}, u32[]{:S(2)}, u32[]{:S(2)}) %collective-permute-start.37) | collective-permute-done | bytes 131104 | tf_op jit(solution)/shard_map/ppermute | solution.py:92
  157.3 3.0 %shard_map.83 = (f32[384,256]{1,0:T(8,128)S(1)}, bf16[384,256]{1,0:T(8,128)(2,1)S(1)}, bf16[384,256]{1,0:T(8,128)(2,1)S(1)}, bf16[384,256]{1,0:T(8,128)(2,1)S(1)}, f32[8,128]{1,0:T(8,128)}) custom-call(bf16[1536,2048]{1,0:T(8,128)(2,1)S(1)} %get-tuple-element.79.refs_0_, bf16[256,256]{1,0:T(8,128)(2,1)S(1)} %copy-done.1, ...), custom_call_target="tpu_custom_call" | custom-call | flops 2300000000 | tf_op jit(solution)/shard_map/pallas_call | solution.py:431
  161.6 1.5 collective-permute-start.41
  163.9 3.5 %collective-permute-done.40.refs_0_ = bf16[384,256]{1,0:T(8,128)(2,1)S(1)} collective-permute-done((bf16[384,256]{1,0:T(8,128)(2,1)S(1)}, bf16[384,256]{1,0:T(8,128)(2,1)S(1)}, u32[]{:S(2)}, u32[]{:S(2)}) %collective-permute-start.40) | collective-permute-done | bytes 196640 | tf_op jit(solution)/shard_map/ppermute | solution.py:92
  167.3 2.1 %collective-permute-done.41.refs_1_ = bf16[384,256]{1,0:T(8,128)(2,1)S(1)} collective-permute-done((bf16[384,256]{1,0:T(8,128)(2,1)S(1)}, bf16[384,256]{1,0:T(8,128)(2,1)S(1)}, u32[]{:S(2)}, u32[]{:S(2)}) %collective-permute-start.41) | collective-permute-done | bytes 196640 | tf_op jit(solution)/shard_map/ppermute | solution.py:92
  169.4 3.3 %collective-permute-done.42.refs_2_ = bf16[384,256]{1,0:T(8,128)(2,1)S(1)} collective-permute-done((bf16[384,256]{1,0:T(8,128)(2,1)S(1)}, bf16[384,256]{1,0:T(8,128)(2,1)S(1)}, u32[]{:S(2)}, u32[]{:S(2)}) %collective-permute-start.42) | collective-permute-done | bytes 196640 | tf_op jit(solution)/shard_map/ppermute | solution.py:92
  (101 shorter events, 37.7 us)
Async XLA Ops:
  0.6 11.6 %copy-start = (bf16[384,256]{1,0:T(8,128)(2,1)S(1)}, bf16[384,256]{1,0:T(8,128)(2,1)}, u32[]{:S(2)}) copy-start(bf16[384,256]{1,0:T(8,128)(2,1)} %current_ref.1) | copy-start | bytes 589828
  0.6 1.8 %collective-permute-start = (bf16[384,256]{1,0:T(8,128)(2,1)}, bf16[384,256]{1,0:T(8,128)(2,1)S(1)}, u32[]{:S(2)}, u32[]{:S(2)}) collective-permute-start(bf16[384,256]{1,0:T(8,128)(2,1)} %current_ref.1), channel_id=1, source_target_pairs={{0,8},{1,9},{2,10},{3,11},{4,12},{5,13},{6,14},{7,15},{8,0},{9,1},... | collective-permute-start | bytes 589832 | tf_op jit(solution)/shard_map/ppermute | solution.py:92
  5.0 26.7 %all-to-all-start = ((s32[32,8,128]{2,1,0:T(8,128)}), s32[32,8,128]{2,1,0:T(8,128)S(1)}, u32[]{:S(2)}, u32[]{:S(2)}) async-start(s32[32,8,128]{2,1,0:T(8,128)} %shard_map.59), calls=%async_computation | async-start | bytes 262144 | tf_op jit(solution)/shard_map/all_to_all | solution.py:561
  12.3 11.5 %collective-permute-start.3 = (bf16[384,256]{1,0:T(8,128)(2,1)S(1)}, bf16[384,256]{1,0:T(8,128)(2,1)S(1)}, u32[]{:S(2)}, u32[]{:S(2)}) collective-permute-start(bf16[384,256]{1,0:T(8,128)(2,1)S(1)} %copy-done), channel_id=1, source_target_pairs={{0,2},{1,3},{2,4},{3,5},{4,6},{5,7},{6,0},{7,1},{8,10},{9,11},{10,... | collective-permute-start | bytes 589832 | tf_op jit(solution)/shard_map/ppermute | solution.py:92
  14.1 17.6 %collective-permute-start.2 = (bf16[384,256]{1,0:T(8,128)(2,1)S(1)}, bf16[384,256]{1,0:T(8,128)(2,1)S(1)}, u32[]{:S(2)}, u32[]{:S(2)}) collective-permute-start(bf16[384,256]{1,0:T(8,128)(2,1)S(1)} %copy-done), channel_id=1, source_target_pairs={{0,4},{1,5},{2,6},{3,7},{4,0},{5,1},{6,2},{7,3},{8,12},{9,13},{10,... | collective-permute-start | bytes 589832 | tf_op jit(solution)/shard_map/ppermute | solution.py:92
  16.5 15.2 %collective-permute-start.1 = (bf16[384,256]{1,0:T(8,128)(2,1)S(1)}, bf16[384,256]{1,0:T(8,128)(2,1)S(1)}, u32[]{:S(2)}, u32[]{:S(2)}) collective-permute-start(bf16[384,256]{1,0:T(8,128)(2,1)S(1)} %copy-done), channel_id=1, source_target_pairs={{0,6},{1,7},{2,0},{3,1},{4,2},{5,3},{6,4},{7,5},{8,14},{9,15},{10,... | collective-permute-start | bytes 589832 | tf_op jit(solution)/shard_map/ppermute | solution.py:92
  31.8 2.1 %collective-permute-start.4 = (bf16[1152,256]{1,0:T(8,128)(2,1)S(1)}, bf16[1152,256]{1,0:T(8,128)(2,1)S(1)}, u32[]{:S(2)}, u32[]{:S(2)}) collective-permute-start(bf16[1152,256]{1,0:T(8,128)(2,1)S(1)} %shard_map.60.refs_2_), channel_id=1, source_target_pairs={{0,8},{1,9},{2,10},{3,11},{4,12},{5,13},{6,14},{7,15},{8,0},{9,1},... | collective-permute-start | bytes 1769480 | tf_op jit(solution)/shard_map/ppermute | solution.py:92
  36.9 9.6 %collective-permute-start.5 = (bf16[256,256]{1,0:T(8,128)(2,1)S(1)}, bf16[256,256]{1,0:T(8,128)(2,1)S(1)}, u32[]{:S(2)}, u32[]{:S(2)}) collective-permute-start(bf16[256,256]{1,0:T(8,128)(2,1)S(1)} %get-tuple-element.59), channel_id=1, source_target_pairs={{0,1},{1,0},{2,3},{3,2},{4,5},{5,4},{6,7},{7,6},{8,9},{9,8},{10,11... | collective-permute-start | bytes 393224 | tf_op jit(solution)/shard_map/ppermute | solution.py:92
  38.5 8.0 %collective-permute-start.6 = (bf16[256,256]{1,0:T(8,128)(2,1)S(1)}, bf16[256,256]{1,0:T(8,128)(2,1)S(1)}, u32[]{:S(2)}, u32[]{:S(2)}) collective-permute-start(bf16[256,256]{1,0:T(8,128)(2,1)S(1)} %get-tuple-element.60), channel_id=1, source_target_pairs={{0,16},{1,17},{2,18},{3,19},{4,20},{5,21},{6,22},{7,23},{8,24},{9,... | collective-permute-start | bytes 393224 | tf_op jit(solution)/shard_map/ppermute | solution.py:92
  40.0 6.6 %collective-permute-start.7 = (bf16[256,256]{1,0:T(8,128)(2,1)S(1)}, bf16[256,256]{1,0:T(8,128)(2,1)S(1)}, u32[]{:S(2)}, u32[]{:S(2)}) collective-permute-start(bf16[256,256]{1,0:T(8,128)(2,1)S(1)} %get-tuple-element.61), channel_id=1, source_target_pairs={{0,17},{1,16},{2,19},{3,18},{4,21},{5,20},{6,23},{7,22},{8,25},{9,... | collective-permute-start | bytes 393224 | tf_op jit(solution)/shard_map/ppermute | solution.py:92
  47.9 12.9 %collective-permute-start.11 = (bf16[256,256]{1,0:T(8,128)(2,1)S(1)}, bf16[256,256]{1,0:T(8,128)(2,1)S(1)}, u32[]{:S(2)}, u32[]{:S(2)}) collective-permute-start(bf16[256,256]{1,0:T(8,128)(2,1)S(1)} %get-tuple-element.63.refs_2_), channel_id=1, source_target_pairs={{0,2},{1,3},{2,4},{3,5},{4,6},{5,7},{6,0},{7,1},{8,10},{9,11},{10,... | collective-permute-start | bytes 393224 | tf_op jit(solution)/shard_map/ppermute | solution.py:92
  52.4 9.4 %collective-permute-start.10 = (bf16[256,256]{1,0:T(8,128)(2,1)S(1)}, bf16[256,256]{1,0:T(8,128)(2,1)S(1)}, u32[]{:S(2)}, u32[]{:S(2)}) collective-permute-start(bf16[256,256]{1,0:T(8,128)(2,1)S(1)} %get-tuple-element.63.refs_2_), channel_id=1, source_target_pairs={{0,4},{1,5},{2,6},{3,7},{4,0},{5,1},{6,2},{7,3},{8,12},{9,13},{10,... | collective-permute-start | bytes 393224 | tf_op jit(solution)/shard_map/ppermute | solution.py:92
  53.8 8.2 %collective-permute-start.9 = (bf16[256,256]{1,0:T(8,128)(2,1)S(1)}, bf16[256,256]{1,0:T(8,128)(2,1)S(1)}, u32[]{:S(2)}, u32[]{:S(2)}) collective-permute-start(bf16[256,256]{1,0:T(8,128)(2,1)S(1)} %get-tuple-element.63.refs_2_), channel_id=1, source_target_pairs={{0,6},{1,7},{2,0},{3,1},{4,2},{5,3},{6,4},{7,5},{8,14},{9,15},{10,... | collective-permute-start | bytes 393224 | tf_op jit(solution)/shard_map/ppermute | solution.py:92
  62.2 1.9 %collective-permute-start.12 = (bf16[768,256]{1,0:T(8,128)(2,1)S(1)}, bf16[768,256]{1,0:T(8,128)(2,1)S(1)}, u32[]{:S(2)}, u32[]{:S(2)}) collective-permute-start(bf16[768,256]{1,0:T(8,128)(2,1)S(1)} %shard_map.65.refs_4_), channel_id=1, source_target_pairs={{0,8},{1,9},{2,10},{3,11},{4,12},{5,13},{6,14},{7,15},{8,0},{9,1},... | collective-permute-start | bytes 1179656 | tf_op jit(solution)/shard_map/ppermute | solution.py:92
  62.2 1.9 %collective-permute-start.8 = (bf16[256,256]{1,0:T(8,128)(2,1)S(1)}, bf16[256,256]{1,0:T(8,128)(2,1)S(1)}, u32[]{:S(2)}, u32[]{:S(2)}) collective-permute-start(bf16[256,256]{1,0:T(8,128)(2,1)S(1)} %get-tuple-element.63.refs_2_), channel_id=1, source_target_pairs={{0,8},{1,9},{2,10},{3,11},{4,12},{5,13},{6,14},{7,15},{8,0},{9,1},... | collective-permute-start | bytes 393224 | tf_op jit(solution)/shard_map/ppermute | solution.py:92
  68.7 10.9 %collective-permute-start.14 = (bf16[256,256]{1,0:T(8,128)(2,1)S(1)}, bf16[256,256]{1,0:T(8,128)(2,1)S(1)}, u32[]{:S(2)}, u32[]{:S(2)}) collective-permute-start(bf16[256,256]{1,0:T(8,128)(2,1)S(1)} %get-tuple-element.70), channel_id=1, source_target_pairs={{0,16},{1,17},{2,18},{3,19},{4,20},{5,21},{6,22},{7,23},{8,24},{9,... | collective-permute-start | bytes 393224 | tf_op jit(solution)/shard_map/ppermute | solution.py:92
  70.3 9.4 %collective-permute-start.15 = (bf16[256,256]{1,0:T(8,128)(2,1)S(1)}, bf16[256,256]{1,0:T(8,128)(2,1)S(1)}, u32[]{:S(2)}, u32[]{:S(2)}) collective-permute-start(bf16[256,256]{1,0:T(8,128)(2,1)S(1)} %get-tuple-element.71), channel_id=1, source_target_pairs={{0,17},{1,16},{2,19},{3,18},{4,21},{5,20},{6,23},{7,22},{8,25},{9,... | collective-permute-start | bytes 393224 | tf_op jit(solution)/shard_map/ppermute | solution.py:92
  73.8 7.0 %collective-permute-start.13 = (bf16[256,256]{1,0:T(8,128)(2,1)S(1)}, bf16[256,256]{1,0:T(8,128)(2,1)S(1)}, u32[]{:S(2)}, u32[]{:S(2)}) collective-permute-start(bf16[256,256]{1,0:T(8,128)(2,1)S(1)} %get-tuple-element.67), channel_id=1, source_target_pairs={{0,1},{1,0},{2,3},{3,2},{4,5},{5,4},{6,7},{7,6},{8,9},{9,8},{10,11... | collective-permute-start | bytes 393224 | tf_op jit(solution)/shard_map/ppermute | solution.py:92
  80.9 10.6 %collective-permute-start.19 = (bf16[256,256]{1,0:T(8,128)(2,1)S(1)}, bf16[256,256]{1,0:T(8,128)(2,1)S(1)}, u32[]{:S(2)}, u32[]{:S(2)}) collective-permute-start(bf16[256,256]{1,0:T(8,128)(2,1)S(1)} %get-tuple-element.76.refs_1_.potential_ref), channel_id=1, source_target_pairs={{0,2},{1,3},{2,4},{3,5},{4,6},{5,7},{6,0},{7,1},{8,10},{9,11},{10,... | collective-permute-start | bytes 393224 | tf_op jit(solution)/shard_map/ppermute | solution.py:92
  84.2 10.3 %collective-permute-start.18 = (bf16[256,256]{1,0:T(8,128)(2,1)S(1)}, bf16[256,256]{1,0:T(8,128)(2,1)S(1)}, u32[]{:S(2)}, u32[]{:S(2)}) collective-permute-start(bf16[256,256]{1,0:T(8,128)(2,1)S(1)} %get-tuple-element.76.refs_1_.potential_ref), channel_id=1, source_target_pairs={{0,4},{1,5},{2,6},{3,7},{4,0},{5,1},{6,2},{7,3},{8,12},{9,13},{10,... | collective-permute-start | bytes 393224 | tf_op jit(solution)/shard_map/ppermute | solution.py:92
  85.6 8.8 %collective-permute-start.17 = (bf16[256,256]{1,0:T(8,128)(2,1)S(1)}, bf16[256,256]{1,0:T(8,128)(2,1)S(1)}, u32[]{:S(2)}, u32[]{:S(2)}) collective-permute-start(bf16[256,256]{1,0:T(8,128)(2,1)S(1)} %get-tuple-element.76.refs_1_.potential_ref), channel_id=1, source_target_pairs={{0,6},{1,7},{2,0},{3,1},{4,2},{5,3},{6,4},{7,5},{8,14},{9,15},{10,... | collective-permute-start | bytes 393224 | tf_op jit(solution)/shard_map/ppermute | solution.py:92
  94.5 2.0 %collective-permute-start.20 = (bf16[768,256]{1,0:T(8,128)(2,1)S(1)}, bf16[768,256]{1,0:T(8,128)(2,1)S(1)}, u32[]{:S(2)}, u32[]{:S(2)}) collective-permute-start(bf16[768,256]{1,0:T(8,128)(2,1)S(1)} %shard_map.71.refs_3_), channel_id=1, source_target_pairs={{0,8},{1,9},{2,10},{3,11},{4,12},{5,13},{6,14},{7,15},{8,0},{9,1},... | collective-permute-start | bytes 1179656 | tf_op jit(solution)/shard_map/ppermute | solution.py:92
  94.5 1.9 %collective-permute-start.16 = (bf16[256,256]{1,0:T(8,128)(2,1)S(1)}, bf16[256,256]{1,0:T(8,128)(2,1)S(1)}, u32[]{:S(2)}, u32[]{:S(2)}) collective-permute-start(bf16[256,256]{1,0:T(8,128)(2,1)S(1)} %get-tuple-element.76.refs_1_.potential_ref), channel_id=1, source_target_pairs={{0,8},{1,9},{2,10},{3,11},{4,12},{5,13},{6,14},{7,15},{8,0},{9,1},... | collective-permute-start | bytes 393224 | tf_op jit(solution)/shard_map/ppermute | solution.py:92
  97.4 9.7 %collective-permute-start.22 = (bf16[256,256]{1,0:T(8,128)(2,1)S(1)}, bf16[256,256]{1,0:T(8,128)(2,1)S(1)}, u32[]{:S(2)}, u32[]{:S(2)}) collective-permute-start(bf16[256,256]{1,0:T(8,128)(2,1)S(1)} %get-tuple-element.85), channel_id=1, source_target_pairs={{0,16},{1,17},{2,18},{3,19},{4,20},{5,21},{6,22},{7,23},{8,24},{9,... | collective-permute-start | bytes 393224 | tf_op jit(solution)/shard_map/ppermute | solution.py:92
  98.9 8.1 %collective-permute-start.23 = (bf16[256,256]{1,0:T(8,128)(2,1)S(1)}, bf16[256,256]{1,0:T(8,128)(2,1)S(1)}, u32[]{:S(2)}, u32[]{:S(2)}) collective-permute-start(bf16[256,256]{1,0:T(8,128)(2,1)S(1)} %get-tuple-element.86), channel_id=1, source_target_pairs={{0,17},{1,16},{2,19},{3,18},{4,21},{5,20},{6,23},{7,22},{8,25},{9,... | collective-permute-start | bytes 393224 | tf_op jit(solution)/shard_map/ppermute | solution.py:92
  101.1 7.3 %collective-permute-start.21 = (bf16[256,256]{1,0:T(8,128)(2,1)S(1)}, bf16[256,256]{1,0:T(8,128)(2,1)S(1)}, u32[]{:S(2)}, u32[]{:S(2)}) collective-permute-start(bf16[256,256]{1,0:T(8,128)(2,1)S(1)} %get-tuple-element.84), channel_id=1, source_target_pairs={{0,1},{1,0},{2,3},{3,2},{4,5},{5,4},{6,7},{7,6},{8,9},{9,8},{10,11... | collective-permute-start | bytes 393224 | tf_op jit(solution)/shard_map/ppermute | solution.py:92
  109.9 8.5 %collective-permute-start.30 = (bf16[256,256]{1,0:T(8,128)(2,1)S(1)}, bf16[256,256]{1,0:T(8,128)(2,1)S(1)}, u32[]{:S(2)}, u32[]{:S(2)}) collective-permute-start(bf16[256,256]{1,0:T(8,128)(2,1)S(1)} %get-tuple-element.94.refs_2_), channel_id=1, source_target_pairs={{0,2},{1,3},{2,4},{3,5},{4,6},{5,7},{6,0},{7,1},{8,10},{9,11},{10,... | collective-permute-start | bytes 393224 | tf_op jit(solution)/shard_map/ppermute | solution.py:92
  113.1 10.0 %collective-permute-start.29 = (bf16[256,256]{1,0:T(8,128)(2,1)S(1)}, bf16[256,256]{1,0:T(8,128)(2,1)S(1)}, u32[]{:S(2)}, u32[]{:S(2)}) collective-permute-start(bf16[256,256]{1,0:T(8,128)(2,1)S(1)} %get-tuple-element.94.refs_2_), channel_id=1, source_target_pairs={{0,4},{1,5},{2,6},{3,7},{4,0},{5,1},{6,2},{7,3},{8,12},{9,13},{10,... | collective-permute-start | bytes 393224 | tf_op jit(solution)/shard_map/ppermute | solution.py:92
  114.5 8.6 %collective-permute-start.28 = (bf16[256,256]{1,0:T(8,128)(2,1)S(1)}, bf16[256,256]{1,0:T(8,128)(2,1)S(1)}, u32[]{:S(2)}, u32[]{:S(2)}) collective-permute-start(bf16[256,256]{1,0:T(8,128)(2,1)S(1)} %get-tuple-element.94.refs_2_), channel_id=1, source_target_pairs={{0,6},{1,7},{2,0},{3,1},{4,2},{5,3},{6,4},{7,5},{8,14},{9,15},{10,... | collective-permute-start | bytes 393224 | tf_op jit(solution)/shard_map/ppermute | solution.py:92
  115.5 11.7 %copy-start.13 = (bf16[512,2048]{1,0:T(8,128)(2,1)S(1)}, bf16[512,2048]{1,0:T(8,128)(2,1)}, u32[]{:S(2)}) copy-start(bf16[512,2048]{1,0:T(8,128)(2,1)} %copy-done.11) | copy-start | bytes 6291460
  118.0 9.3 %copy-start.10 = (bf16[512,2048]{1,0:T(8,128)(2,1)S(1)}, bf16[512,2048]{1,0:T(8,128)(2,1)}, u32[]{:S(2)}) copy-start(bf16[512,2048]{1,0:T(8,128)(2,1)} %copy-done.8) | copy-start | bytes 6291460
  123.2 4.1 %collective-permute-start.31 = (bf16[768,256]{1,0:T(8,128)(2,1)S(1)}, bf16[768,256]{1,0:T(8,128)(2,1)S(1)}, u32[]{:S(2)}, u32[]{:S(2)}) collective-permute-start(bf16[768,256]{1,0:T(8,128)(2,1)S(1)} %shard_map.78.refs_4_), channel_id=1, source_target_pairs={{0,8},{1,9},{2,10},{3,11},{4,12},{5,13},{6,14},{7,15},{8,0},{9,1},... | collective-permute-start | bytes 1179656 | tf_op jit(solution)/shard_map/ppermute | solution.py:92
  123.2 4.0 %collective-permute-start.27 = (bf16[256,256]{1,0:T(8,128)(2,1)S(1)}, bf16[256,256]{1,0:T(8,128)(2,1)S(1)}, u32[]{:S(2)}, u32[]{:S(2)}) collective-permute-start(bf16[256,256]{1,0:T(8,128)(2,1)S(1)} %get-tuple-element.94.refs_2_), channel_id=1, source_target_pairs={{0,8},{1,9},{2,10},{3,11},{4,12},{5,13},{6,14},{7,15},{8,0},{9,1},... | collective-permute-start | bytes 393224 | tf_op jit(solution)/shard_map/ppermute | solution.py:92
  123.7 10.4 %collective-permute-start.24 = (bf16[384,256]{1,0:T(8,128)(2,1)S(1)}, bf16[384,256]{1,0:T(8,128)(2,1)S(1)}, u32[]{:S(2)}, u32[]{:S(2)}) collective-permute-start(bf16[384,256]{1,0:T(8,128)(2,1)S(1)} %get-tuple-element.90), channel_id=1, source_target_pairs={{0,1},{1,0},{2,3},{3,2},{4,5},{5,4},{6,7},{7,6},{8,9},{9,8},{10,11... | collective-permute-start | bytes 589832 | tf_op jit(solution)/shard_map/ppermute | solution.py:92
  125.0 9.9 %collective-permute-start.25 = (bf16[384,256]{1,0:T(8,128)(2,1)S(1)}, bf16[384,256]{1,0:T(8,128)(2,1)S(1)}, u32[]{:S(2)}, u32[]{:S(2)}) collective-permute-start(bf16[384,256]{1,0:T(8,128)(2,1)S(1)} %get-tuple-element.91), channel_id=1, source_target_pairs={{0,16},{1,17},{2,18},{3,19},{4,20},{5,21},{6,22},{7,23},{8,24},{9,... | collective-permute-start | bytes 589832 | tf_op jit(solution)/shard_map/ppermute | solution.py:92
  126.5 10.7 %collective-permute-start.26 = (bf16[384,256]{1,0:T(8,128)(2,1)S(1)}, bf16[384,256]{1,0:T(8,128)(2,1)S(1)}, u32[]{:S(2)}, u32[]{:S(2)}) collective-permute-start(bf16[384,256]{1,0:T(8,128)(2,1)S(1)} %get-tuple-element.92), channel_id=1, source_target_pairs={{0,17},{1,16},{2,19},{3,18},{4,21},{5,20},{6,23},{7,22},{8,25},{9,... | collective-permute-start | bytes 589832 | tf_op jit(solution)/shard_map/ppermute | solution.py:92
  129.3 10.5 %collective-permute-start.33 = (bf16[256,256]{1,0:T(8,128)(2,1)S(1)}, bf16[256,256]{1,0:T(8,128)(2,1)S(1)}, u32[]{:S(2)}, u32[]{:S(2)}) collective-permute-start(bf16[256,256]{1,0:T(8,128)(2,1)S(1)} %get-tuple-element.98), channel_id=1, source_target_pairs={{0,16},{1,17},{2,18},{3,19},{4,20},{5,21},{6,22},{7,23},{8,24},{9,... | collective-permute-start | bytes 393224 | tf_op jit(solution)/shard_map/ppermute | solution.py:92
  130.6 11.1 %collective-permute-start.34 = (bf16[256,256]{1,0:T(8,128)(2,1)S(1)}, bf16[256,256]{1,0:T(8,128)(2,1)S(1)}, u32[]{:S(2)}, u32[]{:S(2)}) collective-permute-start(bf16[256,256]{1,0:T(8,128)(2,1)S(1)} %get-tuple-element.99), channel_id=1, source_target_pairs={{0,17},{1,16},{2,19},{3,18},{4,21},{5,20},{6,23},{7,22},{8,25},{9,... | collective-permute-start | bytes 393224 | tf_op jit(solution)/shard_map/ppermute | solution.py:92
  134.1 7.8 %collective-permute-start.32 = (bf16[256,256]{1,0:T(8,128)(2,1)S(1)}, bf16[256,256]{1,0:T(8,128)(2,1)S(1)}, u32[]{:S(2)}, u32[]{:S(2)}) collective-permute-start(bf16[256,256]{1,0:T(8,128)(2,1)S(1)} %get-tuple-element.97), channel_id=1, source_target_pairs={{0,1},{1,0},{2,3},{3,2},{4,5},{5,4},{6,7},{7,6},{8,9},{9,8},{10,11... | collective-permute-start | bytes 393224 | tf_op jit(solution)/shard_map/ppermute | solution.py:92
  142.6 12.8 %copy-start.1 = (bf16[256,256]{1,0:T(8,128)(2,1)S(1)}, bf16[256,256]{1,0:T(8,128)(2,1)}, u32[]{:S(2)}) copy-start(bf16[256,256]{1,0:T(8,128)(2,1)} %get-tuple-element.54.refs_1_) | copy-start | bytes 393220
  142.6 9.0 %collective-permute-start.38 = (bf16[256,256]{1,0:T(8,128)(2,1)}, bf16[256,256]{1,0:T(8,128)(2,1)S(1)}, u32[]{:S(2)}, u32[]{:S(2)}) collective-permute-start(bf16[256,256]{1,0:T(8,128)(2,1)} %get-tuple-element.54.refs_1_), channel_id=1, source_target_pairs={{0,2},{1,3},{2,4},{3,5},{4,6},{5,7},{6,0},{7,1},{8,10},{9,11},{10,... | collective-permute-start | bytes 393224 | tf_op jit(solution)/shard_map/ppermute | solution.py:92
  145.9 9.4 %collective-permute-start.37 = (bf16[256,256]{1,0:T(8,128)(2,1)}, bf16[256,256]{1,0:T(8,128)(2,1)S(1)}, u32[]{:S(2)}, u32[]{:S(2)}) collective-permute-start(bf16[256,256]{1,0:T(8,128)(2,1)} %get-tuple-element.54.refs_1_), channel_id=1, source_target_pairs={{0,4},{1,5},{2,6},{3,7},{4,0},{5,1},{6,2},{7,3},{8,12},{9,13},{10,... | collective-permute-start | bytes 393224 | tf_op jit(solution)/shard_map/ppermute | solution.py:92
  147.4 8.0 %collective-permute-start.36 = (bf16[256,256]{1,0:T(8,128)(2,1)}, bf16[256,256]{1,0:T(8,128)(2,1)S(1)}, u32[]{:S(2)}, u32[]{:S(2)}) collective-permute-start(bf16[256,256]{1,0:T(8,128)(2,1)} %get-tuple-element.54.refs_1_), channel_id=1, source_target_pairs={{0,6},{1,7},{2,0},{3,1},{4,2},{5,3},{6,4},{7,5},{8,14},{9,15},{10,... | collective-permute-start | bytes 393224 | tf_op jit(solution)/shard_map/ppermute | solution.py:92
  155.4 2.0 %collective-permute-start.39 = (bf16[768,256]{1,0:T(8,128)(2,1)S(1)}, bf16[768,256]{1,0:T(8,128)(2,1)S(1)}, u32[]{:S(2)}, u32[]{:S(2)}) collective-permute-start(bf16[768,256]{1,0:T(8,128)(2,1)S(1)} %shard_map.82.refs_3_), channel_id=1, source_target_pairs={{0,8},{1,9},{2,10},{3,11},{4,12},{5,13},{6,14},{7,15},{8,0},{9,1},... | collective-permute-start | bytes 1179656 | tf_op jit(solution)/shard_map/ppermute | solution.py:92
  155.4 1.9 %collective-permute-start.35 = (bf16[256,256]{1,0:T(8,128)(2,1)S(1)}, bf16[256,256]{1,0:T(8,128)(2,1)S(1)}, u32[]{:S(2)}, u32[]{:S(2)}) collective-permute-start(bf16[256,256]{1,0:T(8,128)(2,1)S(1)} %copy-done.1), channel_id=1, source_target_pairs={{0,8},{1,9},{2,10},{3,11},{4,12},{5,13},{6,14},{7,15},{8,0},{9,1},... | collective-permute-start | bytes 393224 | tf_op jit(solution)/shard_map/ppermute | solution.py:92
  160.4 6.9 %collective-permute-start.40 = (bf16[384,256]{1,0:T(8,128)(2,1)S(1)}, bf16[384,256]{1,0:T(8,128)(2,1)S(1)}, u32[]{:S(2)}, u32[]{:S(2)}) collective-permute-start(bf16[384,256]{1,0:T(8,128)(2,1)S(1)} %get-tuple-element.104), channel_id=1, source_target_pairs={{0,1},{1,0},{2,3},{3,2},{4,5},{5,4},{6,7},{7,6},{8,9},{9,8},{10,11... | collective-permute-start | bytes 589832 | tf_op jit(solution)/shard_map/ppermute | solution.py:92
  161.6 7.8 %collective-permute-start.41 = (bf16[384,256]{1,0:T(8,128)(2,1)S(1)}, bf16[384,256]{1,0:T(8,128)(2,1)S(1)}, u32[]{:S(2)}, u32[]{:S(2)}) collective-permute-start(bf16[384,256]{1,0:T(8,128)(2,1)S(1)} %get-tuple-element.105), channel_id=1, source_target_pairs={{0,16},{1,17},{2,18},{3,19},{4,20},{5,21},{6,22},{7,23},{8,24},{9,... | collective-permute-start | bytes 589832 | tf_op jit(solution)/shard_map/ppermute | solution.py:92
  163.1 9.6 %collective-permute-start.42 = (bf16[384,256]{1,0:T(8,128)(2,1)S(1)}, bf16[384,256]{1,0:T(8,128)(2,1)S(1)}, u32[]{:S(2)}, u32[]{:S(2)}) collective-permute-start(bf16[384,256]{1,0:T(8,128)(2,1)S(1)} %get-tuple-element.106), channel_id=1, source_target_pairs={{0,17},{1,16},{2,19},{3,18},{4,21},{5,20},{6,23},{7,22},{8,25},{9,... | collective-permute-start | bytes 589832 | tf_op jit(solution)/shard_map/ppermute | solution.py:92
  (11 other events, 22.5 us)

commit v8 on v7

--- a/solution.py
+++ b/solution.py
@@ -28,7 +28,8 @@
     41.342882354568324,
     -12.471243535026977,
 )
-PARAMS = pltpu.CompilerParams(vmem_limit_bytes=24 * 2**20)
+SMALL, LARGE = 10 * 2**20, 24 * 2**20
+PARAMS = pltpu.CompilerParams(vmem_limit_bytes=SMALL)
 PEAK = 1.15e15
 F32, BF16, I32 = jnp.float32, jnp.bfloat16, jnp.int32
 
@@ -39,6 +40,10 @@
 
 def fixed(array):
     return pl.BlockSpec(array.shape, lambda j: (0,) * len(array.shape))
+
+
+def params(resident):
+    return pltpu.CompilerParams(vmem_limit_bytes=SMALL if resident else LARGE)
 
 
 def cost(microseconds):
@@ -300,7 +305,7 @@
         out_specs=[block] * outs + [fixed(array) for array in extra] + [token_spec()],
         out_shape=[space((len(span) * rows, cols), BF16)] * outs + list(extra) + [TOKEN],
         scratch_shapes=scratch,
-        compiler_params=PARAMS,
+        compiler_params=params(resident),
         cost_estimate=cost(time),
     )(me, *arrays)
 
@@ -380,7 +385,7 @@
     set_blocks(total, outs)
 
 
-def first_charges(layout, form, me, letters, pieces):
+def first_charges(layout, form, me, letters, pieces, resident):
     count, width = len(layout.plane), pieces[0].shape[1]
     shapes = blocks_like(count, form.tri_dev, width, True) + [TOKEN]
     return pl.pallas_call(
@@ -390,7 +395,7 @@
         + [fixed(piece) for piece in pieces],
         out_specs=[fixed(shape) for shape in shapes],
         out_shape=shapes,
-        compiler_params=PARAMS,
+        compiler_params=params(resident),
         cost_estimate=cost(4),
     )(me, letters, *pieces)
 
@@ -436,7 +441,7 @@
         + [token_spec()] * len(after),
         out_specs=[fixed(shape) for shape in shapes],
         out_shape=shapes,
-        compiler_params=PARAMS,
+        compiler_params=params(resident),
         cost_estimate=cost(count * mats / 2),
     )(*matrices, *pieces, *after)
 
@@ -475,24 +480,37 @@
     )(*blocks, *after)
 
 
-def potential_kernel(count, own_ref, *refs):
+def potential_kernel(count, summed, weight_ref, own_ref, *refs):
     total = own_ref[...]
     for ref in refs[:count]:
         total = total + ref[...].astype(F32)
-    refs[-2][...] = total.astype(BF16)
-    refs[-1][...] = jnp.zeros_like(refs[-1])
-
-
-def potential_of(blocks, after):
-    got = blocks[1:]
-    return pl.pallas_call(
-        functools.partial(potential_kernel, len(got)),
-        in_specs=[whole()] * (len(blocks) + len(after)),
-        out_specs=[whole()] * 2,
-        out_shape=[jax.ShapeDtypeStruct(blocks[0].shape, BF16), TOKEN],
+    out_ref, sum_ref, rounded_ref, token_ref = refs[-4:]
+    potential = total.astype(BF16)
+    out_ref[...] = potential
+    value = weight_ref[0] * potential.astype(F32)
+    if summed:
+        value = value + refs[count][...]
+    sum_ref[...] = value
+    rounded_ref[...] = value.astype(BF16)
+    token_ref[...] = jnp.zeros_like(token_ref)
+
+
+def potential_of(weight, blocks, summed, after):
+    shape = blocks[0].shape
+    return pl.pallas_call(
+        functools.partial(potential_kernel, len(blocks) - 1, len(summed)),
+        in_specs=[pl.BlockSpec(memory_space=pltpu.SMEM)]
+        + [whole()] * (len(blocks) + len(summed) + len(after)),
+        out_specs=[whole()] * 4,
+        out_shape=[
+            jax.ShapeDtypeStruct(shape, BF16),
+            jax.ShapeDtypeStruct(shape, F32),
+            jax.ShapeDtypeStruct(shape, BF16),
+            TOKEN,
+        ],
         compiler_params=PARAMS,
         cost_estimate=cost(1),
-    )(*blocks, *after)
+    )(weight, *blocks, *summed, *after)
 
 
 def charge_kernel(count, weight_ref, charge_ref, degree_ref, potential_ref, own_ref, *refs):
@@ -522,24 +540,22 @@
     )(weight, charge, degree, potential, *blocks, *after)
 
 
-def current_kernel(count, weight_ref, current_ref, own_ref, *refs):
-    slope = own_ref[...]
+def current_kernel(count, current_ref, own_ref, *refs):
+    change = own_ref[...]
     for ref in refs[:count]:
-        slope = slope + ref[...].astype(F32)
-    out_ref, token_ref = refs[-2:]
-    out_ref[...] = (current_ref[...].astype(F32) - weight_ref[0] * slope).astype(BF16)
-    token_ref[...] = jnp.zeros_like(token_ref)
-
-
-def current_of(weight, current, blocks):
+        change = change + ref[...].astype(F32)
+    refs[-1][...] = (current_ref[...].astype(F32) - change).astype(BF16)
+
+
+def current_of(current, blocks):
     return pl.pallas_call(
         functools.partial(current_kernel, len(blocks) - 1),
-        in_specs=[pl.BlockSpec(memory_space=pltpu.SMEM)] + [whole()] * (1 + len(blocks)),
-        out_specs=[whole()] * 2,
-        out_shape=[jax.ShapeDtypeStruct(current.shape, BF16), TOKEN],
+        in_specs=[whole()] * (1 + len(blocks)),
+        out_specs=whole(),
+        out_shape=jax.ShapeDtypeStruct(current.shape, BF16),
         compiler_params=PARAMS,
         cost_estimate=cost(1),
-    )(weight, current, *blocks)
+    )(current, *blocks)
 
 
 def per_device(layout, currents, incidence, centroids, sweep_weights):
@@ -556,7 +572,7 @@
     own = layout.by_core(currents)
     form = Letter(edge_dev, tri_dev, count * slots)
     letters = letters_of(
-        layout, form, incidence, centroids, slots, own[1:]
+        layout, form, incidence, centroids, slots, ()
     )
     letters = lax.all_to_all(letters, AXES, split_axis=0, concat_axis=0, tiled=True)
     labels = letters[:, form.starts[3] :, :].reshape(devices, -1)[:, : count * slots]
@@ -592,8 +608,8 @@
         )
         return part, token
 
-    pieces = layout.gathered(currents, (letters,), own)
-    *blocks, token = first_charges(layout, form, me, letters, pieces)
+    pieces = layout.gathered(currents, (), own)
+    *blocks, token = first_charges(layout, form, me, letters, pieces, resident)
     part, token = tile_part(spans[0], token)
     tiles = [part]
     charge, rounded, token = sum_of(layout.given(blocks), (token,))
@@ -601,44 +617,47 @@
         part, token = tile_part(span, token)
         tiles.append(part)
 
-    near, slopes_of = [], []
-    degree, slopes = None, None
-    current, potential = currents, None
+    def incidence_part(token):
+        *part, token = make(
+            functools.partial(incidence_kernel, layout, form),
+            1,
+            edge_dev,
+            range(count),
+            (letters, token),
+            6,
+        )
+        return part, token
+
+    near, ends = [], None
+    summed, potential = (), None
     for sweep in range(sweeps):
         weight = sweep_weights[sweep].reshape(1)
         pieces = layout.gathered(rounded, (token,))
         blocks, token = multiply(tiles, pieces, tri_dev, resident)
-        if slopes is not None:
-            current, token = current_of(last_weight, current, layout.given(slopes))
-        else:
+        last = sweep + 1 == sweeps
+        if not near and not last:
             (part, degree), token = adjacency_part(spans[0], token)
             near.append([part])
-        potential, token = potential_of(layout.given(blocks), (token,))
-        if slopes is None:
-            for span in spans[1:]:
-                part, token = adjacency_part(span, token)
-                near.append(part)
+        potential, *summed, weighted, token = potential_of(
+            weight, layout.given(blocks), summed, (token,)
+        )
+        if last:
+            break
+        for span in spans[len(near) :]:
+            part, token = adjacency_part(span, token)
+            near.append(part)
         pieces = layout.gathered(potential, (token,))
-        if sweep + 1 < sweeps:
-            blocks, token = multiply(near, pieces, tri_dev, resident)
-        if slopes is None:
-            *part, token = make(
-                functools.partial(incidence_kernel, layout, form),
-                1,
-                edge_dev,
-                range(count),
-                (letters, token),
-                6,
-            )
-            slopes_of.append(part)
-        if sweep + 1 < sweeps:
-            charge, rounded, token = charge_of(
-                weight, charge, degree, potential, layout.given(blocks), (token,)
-            )
-        slopes, token = multiply(slopes_of, pieces, edge_dev, resident, (token,))
-        last_weight = weight
-    current, _ = current_of(last_weight, current, layout.given(slopes))
-    return current, potential
+        blocks, token = multiply(near, pieces, tri_dev, resident)
+        if ends is None:
+            ends, token = incidence_part(token)
+        charge, rounded, token = charge_of(
+            weight, charge, degree, potential, layout.given(blocks), (token,)
+        )
+    if ends is None:
+        ends, token = incidence_part(token)
+    pieces = layout.gathered(weighted, (token,))
+    blocks, _ = multiply([ends], pieces, edge_dev, resident)
+    return current_of(currents, layout.given(blocks)), potential
 
 
 def solution(mesh):

time: 174 us -> 173 us (level)
  waiting for transfers between devices: 54.4 us -> 61.7 us
  starting transfers between devices: 60.6 us -> 56.1 us
  Pallas kernels: 48.6 us -> 46.2 us
    all_to_all x1, waiting for transfers between devices: 0.01 us -> 6.22 us  [per_device(): lax.all_to_all(letters, AXES, split_axis=0, concat_axis=0, tiled=True)]
    ppermute x43 -> x40, starting transfers between devices: 53.4 us -> 48 us  [shift(): return lax.ppermute(value, AXES, pairs)]
    pallas_call x8 -> x7, Pallas kernels: 15.6 us -> 12.5 us  [apply(): pl.pallas_call(kernel, grid=(count,), in_specs=[spec] * mats + [fixed(pie...]
    pallas_call x2, Pallas kernels: 0.79 us -> 2.74 us  [potential_of(): pl.pallas_call(functools.partial(potential_kernel, len(blocks) - 1, len(s...]
    unnamed x30 -> x28, local copies, waits for them, and re-layouts: 8.72 us -> 7.19 us
    ppermute x43 -> x40, waiting for transfers between devices: 54.4 us -> 55.5 us  [shift(): return lax.ppermute(value, AXES, pairs)]
  transfers between devices with their start and end apart: 44 -> 41, of which waited for: 23 -> 22; matrix products, arithmetic and copies ran while one was open for 0% -> 0% of each run, Pallas kernels for 20% -> 18%
where the time goes in v8:
time: 173 us
  waiting for transfers between devices  61.7 us (36%)
  starting transfers between devices  56.1 us (32%)
  Pallas kernels  46.2 us (27%)
  local copies, waits for them, and re-layouts  8.02 us (5%)
    ppermute x40, waiting for transfers between devices, shift(): return lax.ppermute(value, AXES, pairs)  55.5 us
    ppermute x40, starting transfers between devices, shift(): return lax.ppermute(value, AXES, pairs)  48 us
    pallas_call x5, Pallas kernels, build(): pl.pallas_call(kernel, grid=(len(span),), in_specs=[pl.BlockSpec(memory_s...  24.1 us
    pallas_call x7, Pallas kernels, apply(): pl.pallas_call(kernel, grid=(count,), in_specs=[spec] * mats + [fixed(pie...  12.5 us
    all_to_all x1, starting transfers between devices, per_device(): lax.all_to_all(letters, AXES, split_axis=0, concat_axis=0, tiled=True)  8.05 us
    unnamed x28, local copies, waits for them, and re-layouts  7.19 us
    all_to_all x1, waiting for transfers between devices, per_device(): lax.all_to_all(letters, AXES, split_axis=0, concat_axis=0, tiled=True)  6.22 us
  transfers between devices with their start and end apart: 41, of which 22 were waited for; matrix products, arithmetic and copies ran while one was open for 0% of the time, Pallas kernels for 18%

profile of v8, /device:TPU:0, one launch (start us, length us, event | category | flops | bytes accessed | tf_op | source)
XLA Modules:
  0.0 172.9 jit_solution(2260162293634253238)
XLA Ops:
  0.6 3.1 %collective-permute-start.3 = (bf16[384,256]{1,0:T(8,128)(2,1)}, bf16[384,256]{1,0:T(8,128)(2,1)S(1)}, u32[]{:S(2)}, u32[]{:S(2)}) collective-permute-start(bf16[384,256]{1,0:T(8,128)(2,1)} %current_ref.1), channel_id=1, source_target_pairs={{0,2},{1,3},{2,4},{3,5},{4,6},{5,7},{6,0},{7,1},{8,10},{9,11},{10,... | collective-permute-start | bytes 589832 | tf_op jit(solution)/shard_map/ppermute | solution.py:97
  3.7 2.6 %collective-permute-start.2 = (bf16[384,256]{1,0:T(8,128)(2,1)}, bf16[384,256]{1,0:T(8,128)(2,1)S(1)}, u32[]{:S(2)}, u32[]{:S(2)}) collective-permute-start(bf16[384,256]{1,0:T(8,128)(2,1)} %current_ref.1), channel_id=1, source_target_pairs={{0,4},{1,5},{2,6},{3,7},{4,0},{5,1},{6,2},{7,3},{8,12},{9,13},{10,... | collective-permute-start | bytes 589832 | tf_op jit(solution)/shard_map/ppermute | solution.py:97
  7.7 4.2 %collective-permute-done.3.refs_2_ = bf16[384,256]{1,0:T(8,128)(2,1)S(1)} collective-permute-done((bf16[384,256]{1,0:T(8,128)(2,1)}, bf16[384,256]{1,0:T(8,128)(2,1)S(1)}, u32[]{:S(2)}, u32[]{:S(2)}) %collective-permute-start.3) | collective-permute-done | bytes 196640 | tf_op jit(solution)/shard_map/ppermute | solution.py:97
  11.8 7.6 %collective-permute-done.2.refs_1_ = bf16[384,256]{1,0:T(8,128)(2,1)S(1)} collective-permute-done((bf16[384,256]{1,0:T(8,128)(2,1)}, bf16[384,256]{1,0:T(8,128)(2,1)S(1)}, u32[]{:S(2)}, u32[]{:S(2)}) %collective-permute-start.2) | collective-permute-done | bytes 196640 | tf_op jit(solution)/shard_map/ppermute | solution.py:97
  20.8 8.1 %all-to-all-start = ((s32[32,8,128]{2,1,0:T(8,128)}), s32[32,8,128]{2,1,0:T(8,128)S(1)}, u32[]{:S(2)}, u32[]{:S(2)}) async-start(s32[32,8,128]{2,1,0:T(8,128)} %shard_map.59), calls=%async_computation | async-start | bytes 262144 | tf_op jit(solution)/shard_map/all_to_all | solution.py:577
  30.4 6.2 %all-to-all-done.letter_ref = s32[32,8,128]{2,1,0:T(8,128)S(1)} async-done(((s32[32,8,128]{2,1,0:T(8,128)}), s32[32,8,128]{2,1,0:T(8,128)S(1)}, u32[]{:S(2)}, u32[]{:S(2)}) %all-to-all-start) | async-done | bytes 131104 | tf_op jit(solution)/shard_map/all_to_all | solution.py:577
  36.6 3.1 %shard_map.61 = (f32[256,256]{1,0:T(8,128)S(1)}, bf16[256,256]{1,0:T(8,128)(2,1)S(1)}, bf16[256,256]{1,0:T(8,128)(2,1)S(1)}, bf16[256,256]{1,0:T(8,128)(2,1)S(1)}, f32[8,128]{1,0:T(8,128)S(1)}) custom-call(s32[1]{0:T(128)} %bitcast.me_ref, s32[32,8,128]{2,1,0:T(8,128)S(1)} %all-to-all-done.letter_ref, bf16[384,256]{1,0:T(8,128)(2,1)S(1)} %copy-done, ...), custom_call_target="tpu_custom_call" | custom-call | flops 4600000000 | tf_op jit(solution)/shard_map/pallas_call | solution.py:391
  41.7 1.5 collective-permute-start.7
  43.2 4.7 %shard_map.62 = (bf16[512,2048]{1,0:T(8,128)(2,1)S(1)}, bf16[512,2048]{1,0:T(8,128)(2,1)S(1)}, f32[8,128]{1,0:T(8,128)S(1)}) custom-call(s32[1]{0:T(128)} %bitcast.me_ref, s32[32,8,128]{2,1,0:T(8,128)S(1)} %all-to-all-done.letter_ref, f32[8,128]{1,0:T(8,128)S(1)} %get-tuple-element.50.after_ref), custom_call_target="tpu_custom_call" | custom-call | flops 6899999744 | tf_op jit(solution)/shard_map/pallas_call | solution.py:301
  52.6 2.4 %collective-permute-start.9 = (bf16[256,256]{1,0:T(8,128)(2,1)S(1)}, bf16[256,256]{1,0:T(8,128)(2,1)S(1)}, u32[]{:S(2)}, u32[]{:S(2)}) collective-permute-start(bf16[256,256]{1,0:T(8,128)(2,1)S(1)} %get-tuple-element.58.refs_2_), channel_id=1, source_target_pairs={{0,6},{1,7},{2,0},{3,1},{4,2},{5,3},{6,4},{7,5},{8,14},{9,15},{10,... | collective-permute-start | bytes 393224 | tf_op jit(solution)/shard_map/ppermute | solution.py:97
  55.0 4.7 %shard_map.64 = (bf16[512,2048]{1,0:T(8,128)(2,1)S(1)}, bf16[512,2048]{1,0:T(8,128)(2,1)S(1)}, f32[8,128]{1,0:T(8,128)S(1)}) custom-call(s32[1]{0:T(128)} %bitcast.me_ref, s32[32,8,128]{2,1,0:T(8,128)S(1)} %all-to-all-done.letter_ref, f32[8,128]{1,0:T(8,128)S(1)} %get-tuple-element.59.after_ref), custom_call_target="tpu_custom_call" | custom-call | flops 6899999744 | tf_op jit(solution)/shard_map/pallas_call | solution.py:301
  61.0 1.9 %collective-permute-done.10.refs_1_ = bf16[256,256]{1,0:T(8,128)(2,1)S(1)} collective-permute-done((bf16[256,256]{1,0:T(8,128)(2,1)S(1)}, bf16[256,256]{1,0:T(8,128)(2,1)S(1)}, u32[]{:S(2)}, u32[]{:S(2)}) %collective-permute-start.10) | collective-permute-done | bytes 131104 | tf_op jit(solution)/shard_map/ppermute | solution.py:97
  64.9 1.6 copy-done.8
  66.5 1.6 copy-done.11
  68.1 1.5 shard_map.67
  70.3 2.1 %collective-permute-start.15 = (bf16[256,256]{1,0:T(8,128)(2,1)S(1)}, bf16[256,256]{1,0:T(8,128)(2,1)S(1)}, u32[]{:S(2)}, u32[]{:S(2)}) collective-permute-start(bf16[256,256]{1,0:T(8,128)(2,1)S(1)} %get-tuple-element.66), channel_id=1, source_target_pairs={{0,17},{1,16},{2,19},{3,18},{4,21},{5,20},{6,23},{7,22},{8,25},{9,... | collective-permute-start | bytes 393224 | tf_op jit(solution)/shard_map/ppermute | solution.py:97
  72.4 2.0 %shard_map.66 = (f32[256,256]{1,0:T(8,128)S(1)}, bf16[256,256]{1,0:T(8,128)(2,1)S(1)}, f32[8,128]{1,0:T(8,128)}) custom-call(bf16[512,2048]{1,0:T(8,128)(2,1)S(1)} %copy-done.4, bf16[512,2048]{1,0:T(8,128)(2,1)S(1)} %copy-done.6, bf16[256,256]{1,0:T(8,128)(2,1)S(1)} %get-tuple-element.58.refs_2_, bf16[256,256]{1,0:T(8,128)(2,1)S(1)} %collective-permute-done.8.refs_3_, ...), custom_call_target="tpu_custom_call" | custom-call | flops 2300000000 | tf_op jit(solution)/shard_map/pallas_call | solution.py:436
  75.2 5.3 %shard_map.68 = (bf16[512,2048]{1,0:T(8,128)(2,1)S(1)}, f32[256,128]{1,0:T(8,128)S(1)}, f32[8,128]{1,0:T(8,128)S(1)}) custom-call(s32[1]{0:T(128)} %bitcast.me_ref, s32[4,1,2048]{2,1,0:T(1,128)S(1)} %reshape.11.label_ref, f32[8,128]{1,0:T(8,128)S(1)} %get-tuple-element.67.after_ref), custom_call_target="tpu_custom_call" | custom-call | flops 6899999744 | tf_op jit(solution)/shard_map/pallas_call | solution.py:301
  82.7 2.7 %collective-permute-start.19 = (bf16[256,256]{1,0:T(8,128)(2,1)S(1)}, bf16[256,256]{1,0:T(8,128)(2,1)S(1)}, u32[]{:S(2)}, u32[]{:S(2)}) collective-permute-start(bf16[256,256]{1,0:T(8,128)(2,1)S(1)} %get-tuple-element.71.refs_1_.potential_ref), channel_id=1, source_target_pairs={{0,2},{1,3},{2,4},{3,5},{4,6},{5,7},{6,0},{7,1},{8,10},{9,11},{10,... | collective-permute-start | bytes 393224 | tf_op jit(solution)/shard_map/ppermute | solution.py:97
  85.8 2.0 %collective-permute-start.17 = (bf16[256,256]{1,0:T(8,128)(2,1)S(1)}, bf16[256,256]{1,0:T(8,128)(2,1)S(1)}, u32[]{:S(2)}, u32[]{:S(2)}) collective-permute-start(bf16[256,256]{1,0:T(8,128)(2,1)S(1)} %get-tuple-element.71.refs_1_.potential_ref), channel_id=1, source_target_pairs={{0,6},{1,7},{2,0},{3,1},{4,2},{5,3},{6,4},{7,5},{8,14},{9,15},{10,... | collective-permute-start | bytes 393224 | tf_op jit(solution)/shard_map/ppermute | solution.py:97
  87.8 4.9 %shard_map.70 = (bf16[512,2048]{1,0:T(8,128)(2,1)S(1)}, f32[8,128]{1,0:T(8,128)S(1)}) custom-call(s32[1]{0:T(128)} %bitcast.me_ref, s32[4,1,2048]{2,1,0:T(1,128)S(1)} %reshape.11.label_ref, f32[8,128]{1,0:T(8,128)S(1)} %get-tuple-element.69.after_ref), custom_call_target="tpu_custom_call" | custom-call | flops 6899999744 | tf_op jit(solution)/shard_map/pallas_call | solution.py:301
  92.7 2.9 %collective-permute-done.18.refs_1_ = bf16[256,256]{1,0:T(8,128)(2,1)S(1)} collective-permute-done((bf16[256,256]{1,0:T(8,128)(2,1)S(1)}, bf16[256,256]{1,0:T(8,128)(2,1)S(1)}, u32[]{:S(2)}, u32[]{:S(2)}) %collective-permute-start.18) | collective-permute-done | bytes 131104 | tf_op jit(solution)/shard_map/ppermute | solution.py:97
  96.2 1.4 collective-permute-done.16.refs_2_
  99.2 1.7 collective-permute-start.23
  100.9 1.5 shard_map.74
  103.6 4.6 %shard_map.73 = (bf16[1536,2048]{1,0:T(8,128)(2,1)S(1)}, f32[8,128]{1,0:T(8,128)S(1)}) custom-call(s32[1]{0:T(128)} %bitcast.me_ref, s32[32,8,128]{2,1,0:T(8,128)S(1)} %all-to-all-done.letter_ref, f32[8,128]{1,0:T(8,128)S(1)} %get-tuple-element.73.after_ref), custom_call_target="tpu_custom_call" | custom-call | flops 6899999744 | tf_op jit(solution)/shard_map/pallas_call | solution.py:301
  108.2 1.5 collective-permute-done.21.refs_0_
  109.7 1.6 shard_map.75
  111.3 3.3 %collective-permute-start.27 = (bf16[256,256]{1,0:T(8,128)(2,1)S(1)}, bf16[256,256]{1,0:T(8,128)(2,1)S(1)}, u32[]{:S(2)}, u32[]{:S(2)}) collective-permute-start(bf16[256,256]{1,0:T(8,128)(2,1)S(1)} %get-tuple-element.83.refs_2_), channel_id=1, source_target_pairs={{0,2},{1,3},{2,4},{3,5},{4,6},{5,7},{6,0},{7,1},{8,10},{9,11},{10,... | collective-permute-start | bytes 393224 | tf_op jit(solution)/shard_map/ppermute | solution.py:97
  114.5 1.4 collective-permute-start.26
  116.9 2.9 %collective-permute-done.27.refs_2_ = bf16[256,256]{1,0:T(8,128)(2,1)S(1)} collective-permute-done((bf16[256,256]{1,0:T(8,128)(2,1)S(1)}, bf16[256,256]{1,0:T(8,128)(2,1)S(1)}, u32[]{:S(2)}, u32[]{:S(2)}) %collective-permute-start.27) | collective-permute-done | bytes 131104 | tf_op jit(solution)/shard_map/ppermute | solution.py:97
  119.8 4.6 %collective-permute-done.26.refs_1_ = bf16[256,256]{1,0:T(8,128)(2,1)S(1)} collective-permute-done((bf16[256,256]{1,0:T(8,128)(2,1)S(1)}, bf16[256,256]{1,0:T(8,128)(2,1)S(1)}, u32[]{:S(2)}, u32[]{:S(2)}) %collective-permute-start.26) | collective-permute-done | bytes 131104 | tf_op jit(solution)/shard_map/ppermute | solution.py:97
  125.0 1.4 collective-permute-done.24.refs_3_
  126.4 1.5 shard_map.78
  129.2 1.5 collective-permute-start.31
  130.8 2.0 %shard_map.77 = (f32[256,256]{1,0:T(8,128)S(1)}, bf16[256,256]{1,0:T(8,128)(2,1)S(1)}, f32[8,128]{1,0:T(8,128)}) custom-call(bf16[512,2048]{1,0:T(8,128)(2,1)S(1)} %copy-done.4, bf16[512,2048]{1,0:T(8,128)(2,1)S(1)} %copy-done.6, bf16[256,256]{1,0:T(8,128)(2,1)S(1)} %get-tuple-element.83.refs_2_, bf16[256,256]{1,0:T(8,128)(2,1)S(1)} %collective-permute-done.24.refs_3_, ...), custom_call_target="tpu_custom_call" | custom-call | flops 2300000000 | tf_op jit(solution)/shard_map/pallas_call | solution.py:436
  134.3 2.8 %collective-permute-done.31.refs_2_ = bf16[256,256]{1,0:T(8,128)(2,1)S(1)} collective-permute-done((bf16[256,256]{1,0:T(8,128)(2,1)S(1)}, bf16[256,256]{1,0:T(8,128)(2,1)S(1)}, u32[]{:S(2)}, u32[]{:S(2)}) %collective-permute-start.31) | collective-permute-done | bytes 131104 | tf_op jit(solution)/shard_map/ppermute | solution.py:97
  137.2 2.6 %collective-permute-done.29.refs_0_ = bf16[256,256]{1,0:T(8,128)(2,1)S(1)} collective-permute-done((bf16[256,256]{1,0:T(8,128)(2,1)S(1)}, bf16[256,256]{1,0:T(8,128)(2,1)S(1)}, u32[]{:S(2)}, u32[]{:S(2)}) %collective-permute-start.29) | collective-permute-done | bytes 131104 | tf_op jit(solution)/shard_map/ppermute | solution.py:97
  139.8 1.4 shard_map.79
  141.3 3.3 %collective-permute-start.35 = (bf16[256,256]{1,0:T(8,128)(2,1)S(1)}, bf16[256,256]{1,0:T(8,128)(2,1)S(1)}, u32[]{:S(2)}, u32[]{:S(2)}) collective-permute-start(bf16[256,256]{1,0:T(8,128)(2,1)S(1)} %get-tuple-element.91.refs_1_), channel_id=1, source_target_pairs={{0,2},{1,3},{2,4},{3,5},{4,6},{5,7},{6,0},{7,1},{8,10},{9,11},{10,... | collective-permute-start | bytes 393224 | tf_op jit(solution)/shard_map/ppermute | solution.py:97
  144.6 1.4 collective-permute-start.34
  146.9 2.9 %collective-permute-done.35.refs_2_ = bf16[256,256]{1,0:T(8,128)(2,1)S(1)} collective-permute-done((bf16[256,256]{1,0:T(8,128)(2,1)S(1)}, bf16[256,256]{1,0:T(8,128)(2,1)S(1)}, u32[]{:S(2)}, u32[]{:S(2)}) %collective-permute-start.35) | collective-permute-done | bytes 131104 | tf_op jit(solution)/shard_map/ppermute | solution.py:97
  149.8 4.9 %collective-permute-done.34.refs_1_ = bf16[256,256]{1,0:T(8,128)(2,1)S(1)} collective-permute-done((bf16[256,256]{1,0:T(8,128)(2,1)S(1)}, bf16[256,256]{1,0:T(8,128)(2,1)S(1)}, u32[]{:S(2)}, u32[]{:S(2)}) %collective-permute-start.34) | collective-permute-done | bytes 131104 | tf_op jit(solution)/shard_map/ppermute | solution.py:97
  156.8 3.0 %shard_map.81 = (f32[384,256]{1,0:T(8,128)S(1)}, bf16[384,256]{1,0:T(8,128)(2,1)S(1)}, bf16[384,256]{1,0:T(8,128)(2,1)S(1)}, bf16[384,256]{1,0:T(8,128)(2,1)S(1)}, f32[8,128]{1,0:T(8,128)}) custom-call(bf16[1536,2048]{1,0:T(8,128)(2,1)S(1)} %get-tuple-element.74.refs_0_, bf16[256,256]{1,0:T(8,128)(2,1)S(1)} %get-tuple-element.91.refs_1_, ...), custom_call_target="tpu_custom_call" | custom-call | flops 2300000000 | tf_op jit(solution)/shard_map/pallas_call | solution.py:436
  161.2 2.1 %collective-permute-start.39 = (bf16[384,256]{1,0:T(8,128)(2,1)S(1)}, bf16[384,256]{1,0:T(8,128)(2,1)S(1)}, u32[]{:S(2)}, u32[]{:S(2)}) collective-permute-start(bf16[384,256]{1,0:T(8,128)(2,1)S(1)} %get-tuple-element.96), channel_id=1, source_target_pairs={{0,17},{1,16},{2,19},{3,18},{4,21},{5,20},{6,23},{7,22},{8,25},{9,... | collective-permute-start | bytes 589832 | tf_op jit(solution)/shard_map/ppermute | solution.py:97
  163.3 3.5 %collective-permute-done.37.refs_0_ = bf16[384,256]{1,0:T(8,128)(2,1)S(1)} collective-permute-done((bf16[384,256]{1,0:T(8,128)(2,1)S(1)}, bf16[384,256]{1,0:T(8,128)(2,1)S(1)}, u32[]{:S(2)}, u32[]{:S(2)}) %collective-permute-start.37) | collective-permute-done | bytes 196640 | tf_op jit(solution)/shard_map/ppermute | solution.py:97
  166.7 1.7 collective-permute-done.38.refs_1_
  168.4 3.7 %collective-permute-done.39.refs_2_ = bf16[384,256]{1,0:T(8,128)(2,1)S(1)} collective-permute-done((bf16[384,256]{1,0:T(8,128)(2,1)S(1)}, bf16[384,256]{1,0:T(8,128)(2,1)S(1)}, u32[]{:S(2)}, u32[]{:S(2)}) %collective-permute-start.39) | collective-permute-done | bytes 196640 | tf_op jit(solution)/shard_map/ppermute | solution.py:97
  (91 shorter events, 31.2 us)
Async XLA Ops:
  0.6 18.9 %copy-start.1 = (s32[3,256]{1,0:T(4,128)S(1)}, s32[3,256]{1,0:T(4,128)}, u32[]{:S(2)}) copy-start(s32[3,256]{1,0:T(4,128)} %points_ref.1) | copy-start | bytes 9220
  0.6 18.9 %copy-start.2 = (s32[2,384]{1,0:T(2,128)S(1)}, s32[2,384]{1,0:T(2,128)}, u32[]{:S(2)}) copy-start(s32[2,384]{1,0:T(2,128)} %inc_ref.1) | copy-start | bytes 9220
  0.6 11.2 %collective-permute-start.3 = (bf16[384,256]{1,0:T(8,128)(2,1)}, bf16[384,256]{1,0:T(8,128)(2,1)S(1)}, u32[]{:S(2)}, u32[]{:S(2)}) collective-permute-start(bf16[384,256]{1,0:T(8,128)(2,1)} %current_ref.1), channel_id=1, source_target_pairs={{0,2},{1,3},{2,4},{3,5},{4,6},{5,7},{6,0},{7,1},{8,10},{9,11},{10,... | collective-permute-start | bytes 589832 | tf_op jit(solution)/shard_map/ppermute | solution.py:97
  3.7 15.7 %collective-permute-start.2 = (bf16[384,256]{1,0:T(8,128)(2,1)}, bf16[384,256]{1,0:T(8,128)(2,1)S(1)}, u32[]{:S(2)}, u32[]{:S(2)}) collective-permute-start(bf16[384,256]{1,0:T(8,128)(2,1)} %current_ref.1), channel_id=1, source_target_pairs={{0,4},{1,5},{2,6},{3,7},{4,0},{5,1},{6,2},{7,3},{8,12},{9,13},{10,... | collective-permute-start | bytes 589832 | tf_op jit(solution)/shard_map/ppermute | solution.py:97
  6.3 13.1 %collective-permute-start.1 = (bf16[384,256]{1,0:T(8,128)(2,1)}, bf16[384,256]{1,0:T(8,128)(2,1)S(1)}, u32[]{:S(2)}, u32[]{:S(2)}) collective-permute-start(bf16[384,256]{1,0:T(8,128)(2,1)} %current_ref.1), channel_id=1, source_target_pairs={{0,6},{1,7},{2,0},{3,1},{4,2},{5,3},{6,4},{7,5},{8,14},{9,15},{10,... | collective-permute-start | bytes 589832 | tf_op jit(solution)/shard_map/ppermute | solution.py:97
  19.5 9.4 %copy-start = (bf16[384,256]{1,0:T(8,128)(2,1)S(1)}, bf16[384,256]{1,0:T(8,128)(2,1)}, u32[]{:S(2)}) copy-start(bf16[384,256]{1,0:T(8,128)(2,1)} %current_ref.1) | copy-start | bytes 589828
  19.5 17.1 %collective-permute-start.4 = (bf16[1152,256]{1,0:T(8,128)(2,1)S(1)}, bf16[1152,256]{1,0:T(8,128)(2,1)S(1)}, u32[]{:S(2)}, u32[]{:S(2)}) collective-permute-start(bf16[1152,256]{1,0:T(8,128)(2,1)S(1)} %shard_map.60.refs_2_), channel_id=1, source_target_pairs={{0,8},{1,9},{2,10},{3,11},{4,12},{5,13},{6,14},{7,15},{8,0},{9,1},... | collective-permute-start | bytes 1769480 | tf_op jit(solution)/shard_map/ppermute | solution.py:97
  20.8 15.8 %all-to-all-start = ((s32[32,8,128]{2,1,0:T(8,128)}), s32[32,8,128]{2,1,0:T(8,128)S(1)}, u32[]{:S(2)}, u32[]{:S(2)}) async-start(s32[32,8,128]{2,1,0:T(8,128)} %shard_map.59), calls=%async_computation | async-start | bytes 262144 | tf_op jit(solution)/shard_map/all_to_all | solution.py:577
  28.9 1.5 collective-permute-start
  39.7 9.6 %collective-permute-start.5 = (bf16[256,256]{1,0:T(8,128)(2,1)S(1)}, bf16[256,256]{1,0:T(8,128)(2,1)S(1)}, u32[]{:S(2)}, u32[]{:S(2)}) collective-permute-start(bf16[256,256]{1,0:T(8,128)(2,1)S(1)} %get-tuple-element.54), channel_id=1, source_target_pairs={{0,1},{1,0},{2,3},{3,2},{4,5},{5,4},{6,7},{7,6},{8,9},{9,8},{10,11... | collective-permute-start | bytes 393224 | tf_op jit(solution)/shard_map/ppermute | solution.py:97
  41.0 8.3 %collective-permute-start.6 = (bf16[256,256]{1,0:T(8,128)(2,1)S(1)}, bf16[256,256]{1,0:T(8,128)(2,1)S(1)}, u32[]{:S(2)}, u32[]{:S(2)}) collective-permute-start(bf16[256,256]{1,0:T(8,128)(2,1)S(1)} %get-tuple-element.55), channel_id=1, source_target_pairs={{0,16},{1,17},{2,18},{3,19},{4,20},{5,21},{6,22},{7,23},{8,24},{9,... | collective-permute-start | bytes 393224 | tf_op jit(solution)/shard_map/ppermute | solution.py:97
  41.7 7.6 %collective-permute-start.7 = (bf16[256,256]{1,0:T(8,128)(2,1)S(1)}, bf16[256,256]{1,0:T(8,128)(2,1)S(1)}, u32[]{:S(2)}, u32[]{:S(2)}) collective-permute-start(bf16[256,256]{1,0:T(8,128)(2,1)S(1)} %get-tuple-element.56), channel_id=1, source_target_pairs={{0,17},{1,16},{2,19},{3,18},{4,21},{5,20},{6,23},{7,22},{8,25},{9,... | collective-permute-start | bytes 393224 | tf_op jit(solution)/shard_map/ppermute | solution.py:97
  50.7 10.3 %collective-permute-start.11 = (bf16[256,256]{1,0:T(8,128)(2,1)S(1)}, bf16[256,256]{1,0:T(8,128)(2,1)S(1)}, u32[]{:S(2)}, u32[]{:S(2)}) collective-permute-start(bf16[256,256]{1,0:T(8,128)(2,1)S(1)} %get-tuple-element.58.refs_2_), channel_id=1, source_target_pairs={{0,2},{1,3},{2,4},{3,5},{4,6},{5,7},{6,0},{7,1},{8,10},{9,11},{10,... | collective-permute-start | bytes 393224 | tf_op jit(solution)/shard_map/ppermute | solution.py:97
  51.7 11.2 %collective-permute-start.10 = (bf16[256,256]{1,0:T(8,128)(2,1)S(1)}, bf16[256,256]{1,0:T(8,128)(2,1)S(1)}, u32[]{:S(2)}, u32[]{:S(2)}) collective-permute-start(bf16[256,256]{1,0:T(8,128)(2,1)S(1)} %get-tuple-element.58.refs_2_), channel_id=1, source_target_pairs={{0,4},{1,5},{2,6},{3,7},{4,0},{5,1},{6,2},{7,3},{8,12},{9,13},{10,... | collective-permute-start | bytes 393224 | tf_op jit(solution)/shard_map/ppermute | solution.py:97
  52.6 10.3 %collective-permute-start.9 = (bf16[256,256]{1,0:T(8,128)(2,1)S(1)}, bf16[256,256]{1,0:T(8,128)(2,1)S(1)}, u32[]{:S(2)}, u32[]{:S(2)}) collective-permute-start(bf16[256,256]{1,0:T(8,128)(2,1)S(1)} %get-tuple-element.58.refs_2_), channel_id=1, source_target_pairs={{0,6},{1,7},{2,0},{3,1},{4,2},{5,3},{6,4},{7,5},{8,14},{9,15},{10,... | collective-permute-start | bytes 393224 | tf_op jit(solution)/shard_map/ppermute | solution.py:97
  63.0 2.0 %collective-permute-start.12 = (bf16[768,256]{1,0:T(8,128)(2,1)S(1)}, bf16[768,256]{1,0:T(8,128)(2,1)S(1)}, u32[]{:S(2)}, u32[]{:S(2)}) collective-permute-start(bf16[768,256]{1,0:T(8,128)(2,1)S(1)} %shard_map.65.refs_4_), channel_id=1, source_target_pairs={{0,8},{1,9},{2,10},{3,11},{4,12},{5,13},{6,14},{7,15},{8,0},{9,1},... | collective-permute-start | bytes 1179656 | tf_op jit(solution)/shard_map/ppermute | solution.py:97
  63.0 1.9 %collective-permute-start.8 = (bf16[256,256]{1,0:T(8,128)(2,1)S(1)}, bf16[256,256]{1,0:T(8,128)(2,1)S(1)}, u32[]{:S(2)}, u32[]{:S(2)}) collective-permute-start(bf16[256,256]{1,0:T(8,128)(2,1)S(1)} %get-tuple-element.58.refs_2_), channel_id=1, source_target_pairs={{0,8},{1,9},{2,10},{3,11},{4,12},{5,13},{6,14},{7,15},{8,0},{9,1},... | collective-permute-start | bytes 393224 | tf_op jit(solution)/shard_map/ppermute | solution.py:97
  68.1 4.2 %copy-start.4 = (bf16[512,2048]{1,0:T(8,128)(2,1)S(1)}, bf16[512,2048]{1,0:T(8,128)(2,1)}, u32[]{:S(2)}) copy-start(bf16[512,2048]{1,0:T(8,128)(2,1)} %copy-done.3) | copy-start | bytes 6291460
  68.1 4.2 %copy-start.6 = (bf16[512,2048]{1,0:T(8,128)(2,1)S(1)}, bf16[512,2048]{1,0:T(8,128)(2,1)}, u32[]{:S(2)}) copy-start(bf16[512,2048]{1,0:T(8,128)(2,1)} %copy-done.5) | copy-start | bytes 6291460
  69.6 10.9 %collective-permute-start.14 = (bf16[256,256]{1,0:T(8,128)(2,1)S(1)}, bf16[256,256]{1,0:T(8,128)(2,1)S(1)}, u32[]{:S(2)}, u32[]{:S(2)}) collective-permute-start(bf16[256,256]{1,0:T(8,128)(2,1)S(1)} %get-tuple-element.65), channel_id=1, source_target_pairs={{0,16},{1,17},{2,18},{3,19},{4,20},{5,21},{6,22},{7,23},{8,24},{9,... | collective-permute-start | bytes 393224 | tf_op jit(solution)/shard_map/ppermute | solution.py:97
  70.3 10.2 %collective-permute-start.15 = (bf16[256,256]{1,0:T(8,128)(2,1)S(1)}, bf16[256,256]{1,0:T(8,128)(2,1)S(1)}, u32[]{:S(2)}, u32[]{:S(2)}) collective-permute-start(bf16[256,256]{1,0:T(8,128)(2,1)S(1)} %get-tuple-element.66), channel_id=1, source_target_pairs={{0,17},{1,16},{2,19},{3,18},{4,21},{5,20},{6,23},{7,22},{8,25},{9,... | collective-permute-start | bytes 393224 | tf_op jit(solution)/shard_map/ppermute | solution.py:97
  74.4 7.0 %collective-permute-start.13 = (bf16[256,256]{1,0:T(8,128)(2,1)S(1)}, bf16[256,256]{1,0:T(8,128)(2,1)S(1)}, u32[]{:S(2)}, u32[]{:S(2)}) collective-permute-start(bf16[256,256]{1,0:T(8,128)(2,1)S(1)} %get-tuple-element.62), channel_id=1, source_target_pairs={{0,1},{1,0},{2,3},{3,2},{4,5},{5,4},{6,7},{7,6},{8,9},{9,8},{10,11... | collective-permute-start | bytes 393224 | tf_op jit(solution)/shard_map/ppermute | solution.py:97
  82.7 9.9 %collective-permute-start.19 = (bf16[256,256]{1,0:T(8,128)(2,1)S(1)}, bf16[256,256]{1,0:T(8,128)(2,1)S(1)}, u32[]{:S(2)}, u32[]{:S(2)}) collective-permute-start(bf16[256,256]{1,0:T(8,128)(2,1)S(1)} %get-tuple-element.71.refs_1_.potential_ref), channel_id=1, source_target_pairs={{0,2},{1,3},{2,4},{3,5},{4,6},{5,7},{6,0},{7,1},{8,10},{9,11},{10,... | collective-permute-start | bytes 393224 | tf_op jit(solution)/shard_map/ppermute | solution.py:97
  85.4 10.2 %collective-permute-start.18 = (bf16[256,256]{1,0:T(8,128)(2,1)S(1)}, bf16[256,256]{1,0:T(8,128)(2,1)S(1)}, u32[]{:S(2)}, u32[]{:S(2)}) collective-permute-start(bf16[256,256]{1,0:T(8,128)(2,1)S(1)} %get-tuple-element.71.refs_1_.potential_ref), channel_id=1, source_target_pairs={{0,4},{1,5},{2,6},{3,7},{4,0},{5,1},{6,2},{7,3},{8,12},{9,13},{10,... | collective-permute-start | bytes 393224 | tf_op jit(solution)/shard_map/ppermute | solution.py:97
  85.8 9.8 %collective-permute-start.17 = (bf16[256,256]{1,0:T(8,128)(2,1)S(1)}, bf16[256,256]{1,0:T(8,128)(2,1)S(1)}, u32[]{:S(2)}, u32[]{:S(2)}) collective-permute-start(bf16[256,256]{1,0:T(8,128)(2,1)S(1)} %get-tuple-element.71.refs_1_.potential_ref), channel_id=1, source_target_pairs={{0,6},{1,7},{2,0},{3,1},{4,2},{5,3},{6,4},{7,5},{8,14},{9,15},{10,... | collective-permute-start | bytes 393224 | tf_op jit(solution)/shard_map/ppermute | solution.py:97
  95.6 2.0 %collective-permute-start.20 = (bf16[768,256]{1,0:T(8,128)(2,1)S(1)}, bf16[768,256]{1,0:T(8,128)(2,1)S(1)}, u32[]{:S(2)}, u32[]{:S(2)}) collective-permute-start(bf16[768,256]{1,0:T(8,128)(2,1)S(1)} %shard_map.71.refs_3_), channel_id=1, source_target_pairs={{0,8},{1,9},{2,10},{3,11},{4,12},{5,13},{6,14},{7,15},{8,0},{9,1},... | collective-permute-start | bytes 1179656 | tf_op jit(solution)/shard_map/ppermute | solution.py:97
  95.7 1.9 %collective-permute-start.16 = (bf16[256,256]{1,0:T(8,128)(2,1)S(1)}, bf16[256,256]{1,0:T(8,128)(2,1)S(1)}, u32[]{:S(2)}, u32[]{:S(2)}) collective-permute-start(bf16[256,256]{1,0:T(8,128)(2,1)S(1)} %get-tuple-element.71.refs_1_.potential_ref), channel_id=1, source_target_pairs={{0,8},{1,9},{2,10},{3,11},{4,12},{5,13},{6,14},{7,15},{8,0},{9,1},... | collective-permute-start | bytes 393224 | tf_op jit(solution)/shard_map/ppermute | solution.py:97
  98.6 9.6 %collective-permute-start.22 = (bf16[256,256]{1,0:T(8,128)(2,1)S(1)}, bf16[256,256]{1,0:T(8,128)(2,1)S(1)}, u32[]{:S(2)}, u32[]{:S(2)}) collective-permute-start(bf16[256,256]{1,0:T(8,128)(2,1)S(1)} %get-tuple-element.80), channel_id=1, source_target_pairs={{0,16},{1,17},{2,18},{3,19},{4,20},{5,21},{6,22},{7,23},{8,24},{9,... | collective-permute-start | bytes 393224 | tf_op jit(solution)/shard_map/ppermute | solution.py:97
  99.2 9.0 %collective-permute-start.23 = (bf16[256,256]{1,0:T(8,128)(2,1)S(1)}, bf16[256,256]{1,0:T(8,128)(2,1)S(1)}, u32[]{:S(2)}, u32[]{:S(2)}) collective-permute-start(bf16[256,256]{1,0:T(8,128)(2,1)S(1)} %get-tuple-element.81), channel_id=1, source_target_pairs={{0,17},{1,16},{2,19},{3,18},{4,21},{5,20},{6,23},{7,22},{8,25},{9,... | collective-permute-start | bytes 393224 | tf_op jit(solution)/shard_map/ppermute | solution.py:97
  102.4 7.3 %collective-permute-start.21 = (bf16[256,256]{1,0:T(8,128)(2,1)S(1)}, bf16[256,256]{1,0:T(8,128)(2,1)S(1)}, u32[]{:S(2)}, u32[]{:S(2)}) collective-permute-start(bf16[256,256]{1,0:T(8,128)(2,1)S(1)} %get-tuple-element.79), channel_id=1, source_target_pairs={{0,1},{1,0},{2,3},{3,2},{4,5},{5,4},{6,7},{7,6},{8,9},{9,8},{10,11... | collective-permute-start | bytes 393224 | tf_op jit(solution)/shard_map/ppermute | solution.py:97
  109.7 16.7 %copy-start.12 = (bf16[512,2048]{1,0:T(8,128)(2,1)S(1)}, bf16[512,2048]{1,0:T(8,128)(2,1)}, u32[]{:S(2)}) copy-start(bf16[512,2048]{1,0:T(8,128)(2,1)} %copy-done.10) | copy-start | bytes 6291460
  111.3 15.2 %copy-start.9 = (bf16[512,2048]{1,0:T(8,128)(2,1)S(1)}, bf16[512,2048]{1,0:T(8,128)(2,1)}, u32[]{:S(2)}) copy-start(bf16[512,2048]{1,0:T(8,128)(2,1)} %copy-done.7) | copy-start | bytes 6291460
  111.3 8.6 %collective-permute-start.27 = (bf16[256,256]{1,0:T(8,128)(2,1)S(1)}, bf16[256,256]{1,0:T(8,128)(2,1)S(1)}, u32[]{:S(2)}, u32[]{:S(2)}) collective-permute-start(bf16[256,256]{1,0:T(8,128)(2,1)S(1)} %get-tuple-element.83.refs_2_), channel_id=1, source_target_pairs={{0,2},{1,3},{2,4},{3,5},{4,6},{5,7},{6,0},{7,1},{8,10},{9,11},{10,... | collective-permute-start | bytes 393224 | tf_op jit(solution)/shard_map/ppermute | solution.py:97
  114.5 9.9 %collective-permute-start.26 = (bf16[256,256]{1,0:T(8,128)(2,1)S(1)}, bf16[256,256]{1,0:T(8,128)(2,1)S(1)}, u32[]{:S(2)}, u32[]{:S(2)}) collective-permute-start(bf16[256,256]{1,0:T(8,128)(2,1)S(1)} %get-tuple-element.83.refs_2_), channel_id=1, source_target_pairs={{0,4},{1,5},{2,6},{3,7},{4,0},{5,1},{6,2},{7,3},{8,12},{9,13},{10,... | collective-permute-start | bytes 393224 | tf_op jit(solution)/shard_map/ppermute | solution.py:97
  116.0 8.4 %collective-permute-start.25 = (bf16[256,256]{1,0:T(8,128)(2,1)S(1)}, bf16[256,256]{1,0:T(8,128)(2,1)S(1)}, u32[]{:S(2)}, u32[]{:S(2)}) collective-permute-start(bf16[256,256]{1,0:T(8,128)(2,1)S(1)} %get-tuple-element.83.refs_2_), channel_id=1, source_target_pairs={{0,6},{1,7},{2,0},{3,1},{4,2},{5,3},{6,4},{7,5},{8,14},{9,15},{10,... | collective-permute-start | bytes 393224 | tf_op jit(solution)/shard_map/ppermute | solution.py:97
  124.4 2.0 %collective-permute-start.28 = (bf16[768,256]{1,0:T(8,128)(2,1)S(1)}, bf16[768,256]{1,0:T(8,128)(2,1)S(1)}, u32[]{:S(2)}, u32[]{:S(2)}) collective-permute-start(bf16[768,256]{1,0:T(8,128)(2,1)S(1)} %shard_map.76.refs_4_), channel_id=1, source_target_pairs={{0,8},{1,9},{2,10},{3,11},{4,12},{5,13},{6,14},{7,15},{8,0},{9,1},... | collective-permute-start | bytes 1179656 | tf_op jit(solution)/shard_map/ppermute | solution.py:97
  124.5 1.9 %collective-permute-start.24 = (bf16[256,256]{1,0:T(8,128)(2,1)S(1)}, bf16[256,256]{1,0:T(8,128)(2,1)S(1)}, u32[]{:S(2)}, u32[]{:S(2)}) collective-permute-start(bf16[256,256]{1,0:T(8,128)(2,1)S(1)} %get-tuple-element.83.refs_2_), channel_id=1, source_target_pairs={{0,8},{1,9},{2,10},{3,11},{4,12},{5,13},{6,14},{7,15},{8,0},{9,1},... | collective-permute-start | bytes 393224 | tf_op jit(solution)/shard_map/ppermute | solution.py:97
  127.9 6.4 %collective-permute-start.30 = (bf16[256,256]{1,0:T(8,128)(2,1)S(1)}, bf16[256,256]{1,0:T(8,128)(2,1)S(1)}, u32[]{:S(2)}, u32[]{:S(2)}) collective-permute-start(bf16[256,256]{1,0:T(8,128)(2,1)S(1)} %get-tuple-element.87), channel_id=1, source_target_pairs={{0,16},{1,17},{2,18},{3,19},{4,20},{5,21},{6,22},{7,23},{8,24},{9,... | collective-permute-start | bytes 393224 | tf_op jit(solution)/shard_map/ppermute | solution.py:97
  129.2 8.0 %collective-permute-start.31 = (bf16[256,256]{1,0:T(8,128)(2,1)S(1)}, bf16[256,256]{1,0:T(8,128)(2,1)S(1)}, u32[]{:S(2)}, u32[]{:S(2)}) collective-permute-start(bf16[256,256]{1,0:T(8,128)(2,1)S(1)} %get-tuple-element.88), channel_id=1, source_target_pairs={{0,17},{1,16},{2,19},{3,18},{4,21},{5,20},{6,23},{7,22},{8,25},{9,... | collective-permute-start | bytes 393224 | tf_op jit(solution)/shard_map/ppermute | solution.py:97
  132.8 7.0 %collective-permute-start.29 = (bf16[256,256]{1,0:T(8,128)(2,1)S(1)}, bf16[256,256]{1,0:T(8,128)(2,1)S(1)}, u32[]{:S(2)}, u32[]{:S(2)}) collective-permute-start(bf16[256,256]{1,0:T(8,128)(2,1)S(1)} %get-tuple-element.86), channel_id=1, source_target_pairs={{0,1},{1,0},{2,3},{3,2},{4,5},{5,4},{6,7},{7,6},{8,9},{9,8},{10,11... | collective-permute-start | bytes 393224 | tf_op jit(solution)/shard_map/ppermute | solution.py:97
  141.3 8.5 %collective-permute-start.35 = (bf16[256,256]{1,0:T(8,128)(2,1)S(1)}, bf16[256,256]{1,0:T(8,128)(2,1)S(1)}, u32[]{:S(2)}, u32[]{:S(2)}) collective-permute-start(bf16[256,256]{1,0:T(8,128)(2,1)S(1)} %get-tuple-element.91.refs_1_), channel_id=1, source_target_pairs={{0,2},{1,3},{2,4},{3,5},{4,6},{5,7},{6,0},{7,1},{8,10},{9,11},{10,... | collective-permute-start | bytes 393224 | tf_op jit(solution)/shard_map/ppermute | solution.py:97
  144.6 10.2 %collective-permute-start.34 = (bf16[256,256]{1,0:T(8,128)(2,1)S(1)}, bf16[256,256]{1,0:T(8,128)(2,1)S(1)}, u32[]{:S(2)}, u32[]{:S(2)}) collective-permute-start(bf16[256,256]{1,0:T(8,128)(2,1)S(1)} %get-tuple-element.91.refs_1_), channel_id=1, source_target_pairs={{0,4},{1,5},{2,6},{3,7},{4,0},{5,1},{6,2},{7,3},{8,12},{9,13},{10,... | collective-permute-start | bytes 393224 | tf_op jit(solution)/shard_map/ppermute | solution.py:97
  146.0 8.8 %collective-permute-start.33 = (bf16[256,256]{1,0:T(8,128)(2,1)S(1)}, bf16[256,256]{1,0:T(8,128)(2,1)S(1)}, u32[]{:S(2)}, u32[]{:S(2)}) collective-permute-start(bf16[256,256]{1,0:T(8,128)(2,1)S(1)} %get-tuple-element.91.refs_1_), channel_id=1, source_target_pairs={{0,6},{1,7},{2,0},{3,1},{4,2},{5,3},{6,4},{7,5},{8,14},{9,15},{10,... | collective-permute-start | bytes 393224 | tf_op jit(solution)/shard_map/ppermute | solution.py:97
  154.8 2.0 %collective-permute-start.36 = (bf16[768,256]{1,0:T(8,128)(2,1)S(1)}, bf16[768,256]{1,0:T(8,128)(2,1)S(1)}, u32[]{:S(2)}, u32[]{:S(2)}) collective-permute-start(bf16[768,256]{1,0:T(8,128)(2,1)S(1)} %shard_map.80.refs_3_), channel_id=1, source_target_pairs={{0,8},{1,9},{2,10},{3,11},{4,12},{5,13},{6,14},{7,15},{8,0},{9,1},... | collective-permute-start | bytes 1179656 | tf_op jit(solution)/shard_map/ppermute | solution.py:97
  154.9 1.9 %collective-permute-start.32 = (bf16[256,256]{1,0:T(8,128)(2,1)S(1)}, bf16[256,256]{1,0:T(8,128)(2,1)S(1)}, u32[]{:S(2)}, u32[]{:S(2)}) collective-permute-start(bf16[256,256]{1,0:T(8,128)(2,1)S(1)} %get-tuple-element.91.refs_1_), channel_id=1, source_target_pairs={{0,8},{1,9},{2,10},{3,11},{4,12},{5,13},{6,14},{7,15},{8,0},{9,1},... | collective-permute-start | bytes 393224 | tf_op jit(solution)/shard_map/ppermute | solution.py:97
  159.8 6.9 %collective-permute-start.37 = (bf16[384,256]{1,0:T(8,128)(2,1)S(1)}, bf16[384,256]{1,0:T(8,128)(2,1)S(1)}, u32[]{:S(2)}, u32[]{:S(2)}) collective-permute-start(bf16[384,256]{1,0:T(8,128)(2,1)S(1)} %get-tuple-element.94), channel_id=1, source_target_pairs={{0,1},{1,0},{2,3},{3,2},{4,5},{5,4},{6,7},{7,6},{8,9},{9,8},{10,11... | collective-permute-start | bytes 589832 | tf_op jit(solution)/shard_map/ppermute | solution.py:97
  160.6 7.8 %collective-permute-start.38 = (bf16[384,256]{1,0:T(8,128)(2,1)S(1)}, bf16[384,256]{1,0:T(8,128)(2,1)S(1)}, u32[]{:S(2)}, u32[]{:S(2)}) collective-permute-start(bf16[384,256]{1,0:T(8,128)(2,1)S(1)} %get-tuple-element.95), channel_id=1, source_target_pairs={{0,16},{1,17},{2,18},{3,19},{4,20},{5,21},{6,22},{7,23},{8,24},{9,... | collective-permute-start | bytes 589832 | tf_op jit(solution)/shard_map/ppermute | solution.py:97
  161.2 10.9 %collective-permute-start.39 = (bf16[384,256]{1,0:T(8,128)(2,1)S(1)}, bf16[384,256]{1,0:T(8,128)(2,1)S(1)}, u32[]{:S(2)}, u32[]{:S(2)}) collective-permute-start(bf16[384,256]{1,0:T(8,128)(2,1)S(1)} %get-tuple-element.96), channel_id=1, source_target_pairs={{0,17},{1,16},{2,19},{3,18},{4,21},{5,20},{6,23},{7,22},{8,25},{9,... | collective-permute-start | bytes 589832 | tf_op jit(solution)/shard_map/ppermute | solution.py:97
  (7 other events, 11.8 us)

commit v9 on v8

--- a/solution.py
+++ b/solution.py
@@ -99,10 +99,12 @@
     def by_core(self, value):
         return [value] + [self.shift(value, dc=-dc) for dc in range(1, self.core)]
 
-    def gathered(self, value, after, own=None):
-        pieces = own or self.by_core(value)
-        along = [self.shift(value, dz=-dz) for dz in range(1, self.z)]
-        return pieces + (self.by_core(pack(along, after)) if along else [])
+    def along(self, value):
+        return [self.shift(value, dz=-dz) for dz in range(1, self.z)]
+
+    def gathered(self, value, after, along=None):
+        along = self.along(value) if along is None else along
+        return self.by_core(value) + (self.by_core(pack(along, after)) if along else [])
 
     def index(self, x, core, z, y):
         x, core, z, y = x % self.x, core % self.core, z % self.z, y % self.y
@@ -295,7 +297,9 @@
         imag_ref[:, cols] = (poly(SIN, -SPACING / TURNS, u) * (frac * inverse)).astype(BF16)
 
 
-def build(kernel, outs, rows, span, arrays, time, cols, me, resident, scratch=(), extra=()):
+def build(
+    kernel, outs, rows, span, arrays, time, cols, me, resident=False, scratch=(), extra=()
+):
     space = pltpu.VMEM if resident else pltpu.HBM
     block = whole() if resident else pl.BlockSpec((rows, cols), lambda j: (j, 0))
     return pl.pallas_call(
@@ -339,13 +343,13 @@
             refs[0][...] = matmul(every, jnp.ones((every.shape[1], 128), BF16))
 
 
-def incidence_kernel(layout, form, me_ref, letter_ref, after_ref, out_ref, token_ref):
+def incidence_kernel(layout, form, first, me_ref, letter_ref, after_ref, out_ref, token_ref):
     token_ref[...] = jnp.zeros_like(token_ref)
     me, step = me_ref[0], pl.program_id(0)
     edges, cols = form.edges, out_ref.shape[1]
     out_ref = rows_at(out_ref, step, edges)
     size = form.tri_dev
-    letter = letter_ref[layout.in_plane(me, step)]
+    letter = letter_ref[layout.in_plane(me, first + step)]
     plus, minus = [layout.place(end, size, me) for end in form.ends(letter)]
     eye = ones_where(iota((edges, edges), 0) == iota((edges, edges), 1))
     for base in range(0, cols, size):
@@ -391,26 +395,24 @@
     return pl.pallas_call(
         functools.partial(first_kernel, layout, form),
         grid=(count,),
-        in_specs=[pl.BlockSpec(memory_space=pltpu.SMEM), fixed(letters)]
-        + [fixed(piece) for piece in pieces],
-        out_specs=[fixed(shape) for shape in shapes],
+        in_specs=[pl.BlockSpec(memory_space=pltpu.SMEM)] + [whole()] * (1 + len(pieces)),
+        out_specs=[whole()] * len(shapes),
         out_shape=shapes,
         compiler_params=params(resident),
         cost_estimate=cost(4),
     )(me, letters, *pieces)
 
 
-def apply_kernel(mats, fed, block, *refs):
+def apply_kernel(mats, fed, block, row, *refs):
     matrices, pieces, outs = refs[:mats], refs[mats : mats + fed], refs[mats + fed : -1]
     refs[-1][...] = jnp.zeros_like(refs[-1])
     half = pieces[0].shape[1] // 2
     sums = []
     for matrix in matrices:
-        matrix = rows_at(matrix, pl.program_id(0), block)
         total, col = None, 0
         for piece in pieces:
             size = piece.shape[0]
-            term = matmul(matrix[:, col : col + size], piece[...])
+            term = matmul(matrix[row : row + block, col : col + size], piece[...])
             total = term if total is None else total + term
             col += size
         sums.append(total)
@@ -423,34 +425,28 @@
     set_blocks(value, outs)
 
 
-def apply(matrices, pieces, block, resident, exact, after):
+def apply(matrices, pieces, block, exact, row=None):
     rows, cols = matrices[0].shape
-    count, mats = rows // block, len(matrices)
+    count, mats = rows // block if row is None else 1, len(matrices)
+    spec = pl.BlockSpec((block, cols), lambda j: (j, 0)) if row is None else whole()
     shapes = blocks_like(count, block, pieces[0].shape[1], exact) + [TOKEN]
-    spec = whole() if resident else pl.BlockSpec((block, cols), lambda j: (j, 0))
-
-    def kernel(*refs):
-        fed = len(refs) - len(shapes) - len(after)
-        apply_kernel(mats, fed - mats, block, *refs[:fed], *refs[fed + len(after) :])
-
-    return pl.pallas_call(
-        kernel,
+    return pl.pallas_call(
+        functools.partial(apply_kernel, mats, len(pieces), block, row or 0),
         grid=(count,),
-        in_specs=[spec] * mats
-        + [fixed(piece) for piece in pieces]
-        + [token_spec()] * len(after),
-        out_specs=[fixed(shape) for shape in shapes],
+        in_specs=[spec] * mats + [whole()] * len(pieces),
+        out_specs=[whole()] * len(shapes),
         out_shape=shapes,
-        compiler_params=params(resident),
+        compiler_params=params(row is not None),
         cost_estimate=cost(count * mats / 2),
-    )(*matrices, *pieces, *after)
-
-
-def multiply(parts, pieces, block, resident, after=()):
+    )(*matrices, *pieces)
+
+
+def multiply(parts, pieces, block, resident=False):
     blocks, token = [], None
     for part in parts:
-        *more, token = apply(part, pieces, block, resident, not blocks, after)
-        blocks += more
+        for row in range(0, part[0].shape[0], block) if resident else [None]:
+            *more, token = apply(part, pieces, block, not blocks, row)
+            blocks += more
     return blocks, token
 
 
@@ -567,19 +563,19 @@
     sweeps = sweep_weights.shape[0]
     cols = layout.z * layout.core * tri_dev
 
-    resident = count * (3 * tri_dev + edge_dev) * cols * 2 <= 24 * 2**20
-
-    own = layout.by_core(currents)
+    resident = count * 2 * tri_dev * cols * 2 <= 16 * 2**20
+
+    along = layout.along(currents)
     form = Letter(edge_dev, tri_dev, count * slots)
     letters = letters_of(
-        layout, form, incidence, centroids, slots, ()
+        layout, form, incidence, centroids, slots, along[-1:]
     )
     letters = lax.all_to_all(letters, AXES, split_axis=0, concat_axis=0, tiled=True)
     labels = letters[:, form.starts[3] :, :].reshape(devices, -1)[:, : count * slots]
     labels = labels.reshape(devices, count, slots).transpose(1, 0, 2)
     labels = labels.reshape(count, 1, devices * slots)
 
-    make = functools.partial(build, cols=cols, me=me, resident=resident)
+    make = functools.partial(build, cols=cols, me=me)
     cut = (count + 1) // 2
     spans = [span for span in (range(cut), range(cut, count)) if span]
 
@@ -591,6 +587,7 @@
             span,
             (letters, token),
             6,
+            resident=resident,
             scratch=[pltpu.VMEM((16, cols), BF16)],
         )
         return part, token
@@ -608,7 +605,7 @@
         )
         return part, token
 
-    pieces = layout.gathered(currents, (), own)
+    pieces = layout.gathered(currents, (letters,), along)
     *blocks, token = first_charges(layout, form, me, letters, pieces, resident)
     part, token = tile_part(spans[0], token)
     tiles = [part]
@@ -617,16 +614,19 @@
         part, token = tile_part(span, token)
         tiles.append(part)
 
-    def incidence_part(token):
-        *part, token = make(
-            functools.partial(incidence_kernel, layout, form),
-            1,
-            edge_dev,
-            range(count),
-            (letters, token),
-            6,
-        )
-        return part, token
+    def incidence_parts(token):
+        parts = []
+        for span in spans:
+            *part, token = make(
+                functools.partial(incidence_kernel, layout, form, span[0]),
+                1,
+                edge_dev,
+                span,
+                (letters, token),
+                3,
+            )
+            parts.append(part)
+        return parts, token
 
     near, ends = [], None
     summed, potential = (), None
@@ -647,16 +647,16 @@
             part, token = adjacency_part(span, token)
             near.append(part)
         pieces = layout.gathered(potential, (token,))
-        blocks, token = multiply(near, pieces, tri_dev, resident)
+        blocks, token = multiply(near, pieces, tri_dev)
         if ends is None:
-            ends, token = incidence_part(token)
+            ends, token = incidence_parts(token)
         charge, rounded, token = charge_of(
             weight, charge, degree, potential, layout.given(blocks), (token,)
         )
     if ends is None:
-        ends, token = incidence_part(token)
+        ends, token = incidence_parts(token)
     pieces = layout.gathered(weighted, (token,))
-    blocks, _ = multiply([ends], pieces, edge_dev, resident)
+    blocks, _ = multiply(ends, pieces, edge_dev)
     return current_of(currents, layout.given(blocks)), potential
 
 

time: 173 us -> 174 us (level)
  waiting for transfers between devices: 61.7 us -> 53.6 us
  Pallas kernels: 46.2 us -> 52.3 us
  local copies, waits for them, and re-layouts: 8.02 us -> 11.5 us
    all_to_all x1, waiting for transfers between devices: 6.22 us -> 0.01 us  [per_device(): lax.all_to_all(letters, AXES, split_axis=0, concat_axis=0, tiled=True)]
    pallas_call x5 -> x6, Pallas kernels: 24.1 us -> 28.3 us  [build(): pl.pallas_call(kernel, grid=(len(span),), in_specs=[pl.BlockSpec(memory_s...]
    all_to_all x1, starting transfers between devices: 8.05 us -> 3.98 us  [per_device(): lax.all_to_all(letters, AXES, split_axis=0, concat_axis=0, tiled=True)]
    ppermute x40, starting transfers between devices: 48 us -> 51.6 us  [shift(): return lax.ppermute(value, AXES, pairs)]
    ppermute x40, waiting for transfers between devices: 55.5 us -> 53.6 us  [shift(): return lax.ppermute(value, AXES, pairs)]
    pallas_call x7 -> x12, Pallas kernels: 12.5 us -> 14.2 us  [apply(): pl.pallas_call(functools.partial(apply_kernel, mats, len(pieces), block,...]
    unnamed x28 -> x34, local copies, waits for them, and re-layouts: 7.19 us -> 7.71 us
  transfers between devices with their start and end apart: 41 -> 41, of which waited for: 22 -> 18; matrix products, arithmetic and copies ran while one was open for 0% -> 2% of each run, Pallas kernels for 18% -> 22%
where the time goes in v9:
time: 174 us
  starting transfers between devices  55.6 us (32%)
  waiting for transfers between devices  53.6 us (31%)
  Pallas kernels  52.3 us (30%)
  local copies, waits for them, and re-layouts  11.5 us (7%)
    ppermute x40, waiting for transfers between devices, shift(): return lax.ppermute(value, AXES, pairs)  53.6 us
    ppermute x40, starting transfers between devices, shift(): return lax.ppermute(value, AXES, pairs)  51.6 us
    pallas_call x6, Pallas kernels, build(): pl.pallas_call(kernel, grid=(len(span),), in_specs=[pl.BlockSpec(memory_s...  28.3 us
    pallas_call x12, Pallas kernels, apply(): pl.pallas_call(functools.partial(apply_kernel, mats, len(pieces), block,...  14.2 us
    unnamed x34, local copies, waits for them, and re-layouts  7.71 us
    all_to_all x1, starting transfers between devices, per_device(): lax.all_to_all(letters, AXES, split_axis=0, concat_axis=0, tiled=True)  3.98 us
  transfers between devices with their start and end apart: 41, of which 18 were waited for; matrix products, arithmetic and copies ran while one was open for 2% of the time, Pallas kernels for 22%

profile of v9, /device:TPU:0, one launch (start us, length us, event | category | flops | bytes accessed | tf_op | source)
XLA Modules:
  0.0 173.9 jit_solution(13593616975256980639)
XLA Ops:
  0.6 3.1 %collective-permute-start = (bf16[384,256]{1,0:T(8,128)(2,1)}, bf16[384,256]{1,0:T(8,128)(2,1)S(1)}, u32[]{:S(2)}, u32[]{:S(2)}) collective-permute-start(bf16[384,256]{1,0:T(8,128)(2,1)} %current_ref.1), channel_id=1, source_target_pairs={{0,2},{1,3},{2,4},{3,5},{4,6},{5,7},{6,0},{7,1},{8,10},{9,11},{10,... | collective-permute-start | bytes 589832 | tf_op jit(solution)/shard_map/ppermute | solution.py:97
  3.7 7.1 %collective-permute-done.refs_0_.refs_2_ = bf16[384,256]{1,0:T(8,128)(2,1)S(1)} collective-permute-done((bf16[384,256]{1,0:T(8,128)(2,1)}, bf16[384,256]{1,0:T(8,128)(2,1)S(1)}, u32[]{:S(2)}, u32[]{:S(2)}) %collective-permute-start) | collective-permute-done | bytes 196640 | tf_op jit(solution)/shard_map/ppermute | solution.py:97
  13.5 4.0 %all-to-all-start = ((s32[32,8,128]{2,1,0:T(8,128)}), s32[32,8,128]{2,1,0:T(8,128)S(1)}, u32[]{:S(2)}, u32[]{:S(2)}) async-start(s32[32,8,128]{2,1,0:T(8,128)} %shard_map.59), calls=%async_computation | async-start | bytes 262144 | tf_op jit(solution)/shard_map/all_to_all | solution.py:573
  17.5 2.7 %collective-permute-start.3 = (bf16[384,256]{1,0:T(8,128)(2,1)S(1)}, bf16[384,256]{1,0:T(8,128)(2,1)S(1)}, u32[]{:S(2)}, u32[]{:S(2)}) collective-permute-start(bf16[384,256]{1,0:T(8,128)(2,1)S(1)} %copy-done.7), channel_id=1, source_target_pairs={{0,4},{1,5},{2,6},{3,7},{4,0},{5,1},{6,2},{7,3},{8,12},{9,13},{10,... | collective-permute-start | bytes 589832 | tf_op jit(solution)/shard_map/ppermute | solution.py:97
  20.2 1.5 collective-permute-start.2
  21.6 11.3 %collective-permute-done.3.refs_1_ = bf16[384,256]{1,0:T(8,128)(2,1)S(1)} collective-permute-done((bf16[384,256]{1,0:T(8,128)(2,1)S(1)}, bf16[384,256]{1,0:T(8,128)(2,1)S(1)}, u32[]{:S(2)}, u32[]{:S(2)}) %collective-permute-start.3) | collective-permute-done | bytes 196640 | tf_op jit(solution)/shard_map/ppermute | solution.py:97
  33.5 1.8 %collective-permute-done.1.refs_1_ = bf16[384,256]{1,0:T(8,128)(2,1)S(1)} collective-permute-done((bf16[384,256]{1,0:T(8,128)(2,1)S(1)}, bf16[384,256]{1,0:T(8,128)(2,1)S(1)}, u32[]{:S(2)}, u32[]{:S(2)}) %collective-permute-start.1) | collective-permute-done | bytes 196640 | tf_op jit(solution)/shard_map/ppermute | solution.py:97
  35.3 3.1 %shard_map.61 = (f32[256,256]{1,0:T(8,128)S(1)}, bf16[256,256]{1,0:T(8,128)(2,1)S(1)}, bf16[256,256]{1,0:T(8,128)(2,1)S(1)}, bf16[256,256]{1,0:T(8,128)(2,1)S(1)}, f32[8,128]{1,0:T(8,128)S(1)}) custom-call(s32[1]{0:T(128)} %bitcast.me_ref, s32[32,8,128]{2,1,0:T(8,128)S(1)} %all-to-all-done.refs_3_.letter_ref, bf16[384,256]{1,0:T(8,128)(2,1)S(1)} %copy-done.7, ...), custom_call_target="tpu_custom_call" | custom-call | flops 4600000000 | tf_op jit(solution)/shard_map/pallas_call | solution.py:395
  38.4 1.5 collective-permute-start.5
  40.0 1.5 collective-permute-start.6
  42.0 4.7 %shard_map.62 = (bf16[512,2048]{1,0:T(8,128)(2,1)S(1)}, bf16[512,2048]{1,0:T(8,128)(2,1)S(1)}, f32[8,128]{1,0:T(8,128)S(1)}) custom-call(s32[1]{0:T(128)} %bitcast.me_ref, s32[32,8,128]{2,1,0:T(8,128)S(1)} %all-to-all-done.refs_3_.letter_ref, f32[8,128]{1,0:T(8,128)S(1)} %get-tuple-element.52.after_ref), custom_call_target="tpu_custom_call" | custom-call | flops 6899999744 | tf_op jit(solution)/shard_map/pallas_call | solution.py:305
  48.8 4.3 %collective-permute-start.11 = (bf16[256,256]{1,0:T(8,128)(2,1)S(1)}, bf16[256,256]{1,0:T(8,128)(2,1)S(1)}, u32[]{:S(2)}, u32[]{:S(2)}) collective-permute-start(bf16[256,256]{1,0:T(8,128)(2,1)S(1)} %get-tuple-element.60.refs_2_), channel_id=1, source_target_pairs={{0,2},{1,3},{2,4},{3,5},{4,6},{5,7},{6,0},{7,1},{8,10},{9,11},{10,... | collective-permute-start | bytes 393224 | tf_op jit(solution)/shard_map/ppermute | solution.py:97
  55.4 4.7 %shard_map.64 = (bf16[512,2048]{1,0:T(8,128)(2,1)S(1)}, bf16[512,2048]{1,0:T(8,128)(2,1)S(1)}, f32[8,128]{1,0:T(8,128)S(1)}) custom-call(s32[1]{0:T(128)} %bitcast.me_ref, s32[32,8,128]{2,1,0:T(8,128)S(1)} %all-to-all-done.refs_3_.letter_ref, f32[8,128]{1,0:T(8,128)S(1)} %get-tuple-element.61.after_ref), custom_call_target="tpu_custom_call" | custom-call | flops 6899999744 | tf_op jit(solution)/shard_map/pallas_call | solution.py:305
  64.9 1.5 copy.6
  67.3 1.6 copy-done.1
  70.1 1.5 collective-permute-start.13
  72.7 1.5 collective-permute-start.14
  76.0 6.2 %shard_map.70 = (bf16[512,2048]{1,0:T(8,128)(2,1)}, f32[256,128]{1,0:T(8,128)S(1)}, f32[8,128]{1,0:T(8,128)S(1)}) custom-call(s32[1]{0:T(128)} %bitcast.me_ref, s32[4,1,2048]{2,1,0:T(1,128)S(1)} %reshape.11.label_ref, f32[8,128]{1,0:T(8,128)S(1)} %get-tuple-element.69.after_ref), custom_call_target="tpu_custom_call" | custom-call | flops 6899999744 | tf_op jit(solution)/shard_map/pallas_call | solution.py:305
  84.8 3.0 %collective-permute-start.19 = (bf16[256,256]{1,0:T(8,128)(2,1)S(1)}, bf16[256,256]{1,0:T(8,128)(2,1)S(1)}, u32[]{:S(2)}, u32[]{:S(2)}) collective-permute-start(bf16[256,256]{1,0:T(8,128)(2,1)S(1)} %get-tuple-element.73.refs_1_.potential_ref), channel_id=1, source_target_pairs={{0,2},{1,3},{2,4},{3,5},{4,6},{5,7},{6,0},{7,1},{8,10},{9,11},{10,... | collective-permute-start | bytes 393224 | tf_op jit(solution)/shard_map/ppermute | solution.py:97
  87.8 1.5 collective-permute-start.18
  90.1 5.8 %shard_map.72 = (bf16[512,2048]{1,0:T(8,128)(2,1)}, f32[8,128]{1,0:T(8,128)S(1)}) custom-call(s32[1]{0:T(128)} %bitcast.me_ref, s32[4,1,2048]{2,1,0:T(1,128)S(1)} %reshape.11.label_ref, f32[8,128]{1,0:T(8,128)S(1)} %get-tuple-element.71.after_ref), custom_call_target="tpu_custom_call" | custom-call | flops 6899999744 | tf_op jit(solution)/shard_map/pallas_call | solution.py:305
  96.0 1.6 collective-permute-done.18.refs_1_
  98.2 1.4 collective-permute-done.16.refs_2_
  100.5 1.5 collective-permute-start.22
  102.8 1.5 shard_map.76
  105.6 3.4 %shard_map.75 = (bf16[768,2048]{1,0:T(8,128)(2,1)}, f32[8,128]{1,0:T(8,128)S(1)}) custom-call(s32[1]{0:T(128)} %bitcast.me_ref, s32[32,8,128]{2,1,0:T(8,128)S(1)} %all-to-all-done.refs_3_.letter_ref, f32[8,128]{1,0:T(8,128)S(1)} %get-tuple-element.75.after_ref), custom_call_target="tpu_custom_call" | custom-call | flops 3449999872 | tf_op jit(solution)/shard_map/pallas_call | solution.py:305
  109.0 3.5 %shard_map.77 = (bf16[768,2048]{1,0:T(8,128)(2,1)}, f32[8,128]{1,0:T(8,128)S(1)}) custom-call(s32[1]{0:T(128)} %bitcast.me_ref, s32[32,8,128]{2,1,0:T(8,128)S(1)} %all-to-all-done.refs_3_.letter_ref, f32[8,128]{1,0:T(8,128)S(1)} %get-tuple-element.84.after_ref), custom_call_target="tpu_custom_call" | custom-call | flops 3449999872 | tf_op jit(solution)/shard_map/pallas_call | solution.py:305
  112.5 1.4 shard_map.78
  114.0 3.3 %collective-permute-start.27 = (bf16[256,256]{1,0:T(8,128)(2,1)S(1)}, bf16[256,256]{1,0:T(8,128)(2,1)S(1)}, u32[]{:S(2)}, u32[]{:S(2)}) collective-permute-start(bf16[256,256]{1,0:T(8,128)(2,1)S(1)} %get-tuple-element.86.refs_2_), channel_id=1, source_target_pairs={{0,2},{1,3},{2,4},{3,5},{4,6},{5,7},{6,0},{7,1},{8,10},{9,11},{10,... | collective-permute-start | bytes 393224 | tf_op jit(solution)/shard_map/ppermute | solution.py:97
  117.2 1.4 collective-permute-start.26
  119.6 3.0 %collective-permute-done.27.refs_2_ = bf16[256,256]{1,0:T(8,128)(2,1)S(1)} collective-permute-done((bf16[256,256]{1,0:T(8,128)(2,1)S(1)}, bf16[256,256]{1,0:T(8,128)(2,1)S(1)}, u32[]{:S(2)}, u32[]{:S(2)}) %collective-permute-start.27) | collective-permute-done | bytes 131104 | tf_op jit(solution)/shard_map/ppermute | solution.py:97
  122.6 4.2 %collective-permute-done.26.refs_1_ = bf16[256,256]{1,0:T(8,128)(2,1)S(1)} collective-permute-done((bf16[256,256]{1,0:T(8,128)(2,1)S(1)}, bf16[256,256]{1,0:T(8,128)(2,1)S(1)}, u32[]{:S(2)}, u32[]{:S(2)}) %collective-permute-start.26) | collective-permute-done | bytes 131104 | tf_op jit(solution)/shard_map/ppermute | solution.py:97
  127.5 1.4 collective-permute-done.24.refs_3_
  131.4 2.3 %collective-permute-start.31 = (bf16[256,256]{1,0:T(8,128)(2,1)S(1)}, bf16[256,256]{1,0:T(8,128)(2,1)S(1)}, u32[]{:S(2)}, u32[]{:S(2)}) collective-permute-start(bf16[256,256]{1,0:T(8,128)(2,1)S(1)} %get-tuple-element.91), channel_id=1, source_target_pairs={{0,17},{1,16},{2,19},{3,18},{4,21},{5,20},{6,23},{7,22},{8,25},{9,... | collective-permute-start | bytes 393224 | tf_op jit(solution)/shard_map/ppermute | solution.py:97
  136.5 1.8 %collective-permute-done.29.refs_0_ = bf16[256,256]{1,0:T(8,128)(2,1)S(1)} collective-permute-done((bf16[256,256]{1,0:T(8,128)(2,1)S(1)}, bf16[256,256]{1,0:T(8,128)(2,1)S(1)}, u32[]{:S(2)}, u32[]{:S(2)}) %collective-permute-start.29) | collective-permute-done | bytes 131104 | tf_op jit(solution)/shard_map/ppermute | solution.py:97
  138.4 2.0 %collective-permute-done.30.refs_1_ = bf16[256,256]{1,0:T(8,128)(2,1)S(1)} collective-permute-done((bf16[256,256]{1,0:T(8,128)(2,1)S(1)}, bf16[256,256]{1,0:T(8,128)(2,1)S(1)}, u32[]{:S(2)}, u32[]{:S(2)}) %collective-permute-start.30) | collective-permute-done | bytes 131104 | tf_op jit(solution)/shard_map/ppermute | solution.py:97
  140.3 1.6 shard_map.84
  142.0 3.2 %collective-permute-start.35 = (bf16[256,256]{1,0:T(8,128)(2,1)S(1)}, bf16[256,256]{1,0:T(8,128)(2,1)S(1)}, u32[]{:S(2)}, u32[]{:S(2)}) collective-permute-start(bf16[256,256]{1,0:T(8,128)(2,1)S(1)} %get-tuple-element.94.refs_1_), channel_id=1, source_target_pairs={{0,2},{1,3},{2,4},{3,5},{4,6},{5,7},{6,0},{7,1},{8,10},{9,11},{10,... | collective-permute-start | bytes 393224 | tf_op jit(solution)/shard_map/ppermute | solution.py:97
  145.2 1.5 collective-permute-start.34
  147.5 3.0 %collective-permute-done.35.refs_2_ = bf16[256,256]{1,0:T(8,128)(2,1)S(1)} collective-permute-done((bf16[256,256]{1,0:T(8,128)(2,1)S(1)}, bf16[256,256]{1,0:T(8,128)(2,1)S(1)}, u32[]{:S(2)}, u32[]{:S(2)}) %collective-permute-start.35) | collective-permute-done | bytes 131104 | tf_op jit(solution)/shard_map/ppermute | solution.py:97
  150.6 4.0 %collective-permute-done.34.refs_1_ = bf16[256,256]{1,0:T(8,128)(2,1)S(1)} collective-permute-done((bf16[256,256]{1,0:T(8,128)(2,1)S(1)}, bf16[256,256]{1,0:T(8,128)(2,1)S(1)}, u32[]{:S(2)}, u32[]{:S(2)}) %collective-permute-start.34) | collective-permute-done | bytes 131104 | tf_op jit(solution)/shard_map/ppermute | solution.py:97
  155.4 1.4 collective-permute-done.32.refs_2_
  156.8 1.8 %shard_map.87 = (bf16[384,256]{1,0:T(8,128)(2,1)S(1)}, bf16[384,256]{1,0:T(8,128)(2,1)S(1)}, f32[8,128]{1,0:T(8,128)}) custom-call(bf16[768,2048]{1,0:T(8,128)(2,1)S(1)} %copy-done.11, bf16[256,256]{1,0:T(8,128)(2,1)S(1)} %get-tuple-element.94.refs_1_, bf16[256,256]{1,0:T(8,128)(2,1)S(1)} %collective-permute-done.32.refs_2_, ...), custom_call_target="tpu_custom_call" | custom-call | flops 1150000000 | tf_op jit(solution)/shard_map/pallas_call | solution.py:433
  158.6 1.4 collective-permute-start.38
  160.8 1.8 %shard_map.86 = (f32[384,256]{1,0:T(8,128)S(1)}, bf16[384,256]{1,0:T(8,128)(2,1)S(1)}, f32[8,128]{1,0:T(8,128)}) custom-call(bf16[768,2048]{1,0:T(8,128)(2,1)S(1)} %copy-done.10, bf16[256,256]{1,0:T(8,128)(2,1)S(1)} %get-tuple-element.94.refs_1_, bf16[256,256]{1,0:T(8,128)(2,1)S(1)} %collective-permute-done.32.refs_2_, ...), custom_call_target="tpu_custom_call" | custom-call | flops 1150000000 | tf_op jit(solution)/shard_map/pallas_call | solution.py:433
  163.9 2.5 %collective-permute-done.38.refs_1_ = bf16[384,256]{1,0:T(8,128)(2,1)S(1)} collective-permute-done((bf16[384,256]{1,0:T(8,128)(2,1)S(1)}, bf16[384,256]{1,0:T(8,128)(2,1)S(1)}, u32[]{:S(2)}, u32[]{:S(2)}) %collective-permute-start.38) | collective-permute-done | bytes 196640 | tf_op jit(solution)/shard_map/ppermute | solution.py:97
  166.3 3.7 %collective-permute-done.39.refs_2_ = bf16[384,256]{1,0:T(8,128)(2,1)S(1)} collective-permute-done((bf16[384,256]{1,0:T(8,128)(2,1)S(1)}, bf16[384,256]{1,0:T(8,128)(2,1)S(1)}, u32[]{:S(2)}, u32[]{:S(2)}) %collective-permute-start.39) | collective-permute-done | bytes 196640 | tf_op jit(solution)/shard_map/ppermute | solution.py:97
  170.0 3.1 %collective-permute-done.37.refs_0_ = bf16[384,256]{1,0:T(8,128)(2,1)S(1)} collective-permute-done((bf16[384,256]{1,0:T(8,128)(2,1)S(1)}, bf16[384,256]{1,0:T(8,128)(2,1)S(1)}, u32[]{:S(2)}, u32[]{:S(2)}) %collective-permute-start.37) | collective-permute-done | bytes 196640 | tf_op jit(solution)/shard_map/ppermute | solution.py:97
  (103 shorter events, 36.5 us)
Async XLA Ops:
  0.6 16.8 %copy-start.7 = (bf16[384,256]{1,0:T(8,128)(2,1)S(1)}, bf16[384,256]{1,0:T(8,128)(2,1)}, u32[]{:S(2)}) copy-start(bf16[384,256]{1,0:T(8,128)(2,1)} %current_ref.1) | copy-start | bytes 589828
  0.6 10.2 %collective-permute-start = (bf16[384,256]{1,0:T(8,128)(2,1)}, bf16[384,256]{1,0:T(8,128)(2,1)S(1)}, u32[]{:S(2)}, u32[]{:S(2)}) collective-permute-start(bf16[384,256]{1,0:T(8,128)(2,1)} %current_ref.1), channel_id=1, source_target_pairs={{0,2},{1,3},{2,4},{3,5},{4,6},{5,7},{6,0},{7,1},{8,10},{9,11},{10,... | collective-permute-start | bytes 589832 | tf_op jit(solution)/shard_map/ppermute | solution.py:97
  13.5 19.5 %all-to-all-start = ((s32[32,8,128]{2,1,0:T(8,128)}), s32[32,8,128]{2,1,0:T(8,128)S(1)}, u32[]{:S(2)}, u32[]{:S(2)}) async-start(s32[32,8,128]{2,1,0:T(8,128)} %shard_map.59), calls=%async_computation | async-start | bytes 262144 | tf_op jit(solution)/shard_map/all_to_all | solution.py:573
  17.5 15.5 %collective-permute-start.3 = (bf16[384,256]{1,0:T(8,128)(2,1)S(1)}, bf16[384,256]{1,0:T(8,128)(2,1)S(1)}, u32[]{:S(2)}, u32[]{:S(2)}) collective-permute-start(bf16[384,256]{1,0:T(8,128)(2,1)S(1)} %copy-done.7), channel_id=1, source_target_pairs={{0,4},{1,5},{2,6},{3,7},{4,0},{5,1},{6,2},{7,3},{8,12},{9,13},{10,... | collective-permute-start | bytes 589832 | tf_op jit(solution)/shard_map/ppermute | solution.py:97
  20.2 12.7 %collective-permute-start.2 = (bf16[384,256]{1,0:T(8,128)(2,1)S(1)}, bf16[384,256]{1,0:T(8,128)(2,1)S(1)}, u32[]{:S(2)}, u32[]{:S(2)}) collective-permute-start(bf16[384,256]{1,0:T(8,128)(2,1)S(1)} %copy-done.7), channel_id=1, source_target_pairs={{0,6},{1,7},{2,0},{3,1},{4,2},{5,3},{6,4},{7,5},{8,14},{9,15},{10,... | collective-permute-start | bytes 589832 | tf_op jit(solution)/shard_map/ppermute | solution.py:97
  33.0 2.4 %collective-permute-start.4 = (bf16[1152,256]{1,0:T(8,128)(2,1)S(1)}, bf16[1152,256]{1,0:T(8,128)(2,1)S(1)}, u32[]{:S(2)}, u32[]{:S(2)}) collective-permute-start(bf16[1152,256]{1,0:T(8,128)(2,1)S(1)} %shard_map.60.refs_2_), channel_id=1, source_target_pairs={{0,8},{1,9},{2,10},{3,11},{4,12},{5,13},{6,14},{7,15},{8,0},{9,1},... | collective-permute-start | bytes 1769480 | tf_op jit(solution)/shard_map/ppermute | solution.py:97
  33.0 2.3 %collective-permute-start.1 = (bf16[384,256]{1,0:T(8,128)(2,1)S(1)}, bf16[384,256]{1,0:T(8,128)(2,1)S(1)}, u32[]{:S(2)}, u32[]{:S(2)}) collective-permute-start(bf16[384,256]{1,0:T(8,128)(2,1)S(1)} %copy-done.7), channel_id=1, source_target_pairs={{0,8},{1,9},{2,10},{3,11},{4,12},{5,13},{6,14},{7,15},{8,0},{9,1},... | collective-permute-start | bytes 589832 | tf_op jit(solution)/shard_map/ppermute | solution.py:97
  38.4 9.6 %collective-permute-start.5 = (bf16[256,256]{1,0:T(8,128)(2,1)S(1)}, bf16[256,256]{1,0:T(8,128)(2,1)S(1)}, u32[]{:S(2)}, u32[]{:S(2)}) collective-permute-start(bf16[256,256]{1,0:T(8,128)(2,1)S(1)} %get-tuple-element.56), channel_id=1, source_target_pairs={{0,1},{1,0},{2,3},{3,2},{4,5},{5,4},{6,7},{7,6},{8,9},{9,8},{10,11... | collective-permute-start | bytes 393224 | tf_op jit(solution)/shard_map/ppermute | solution.py:97
  40.0 8.0 %collective-permute-start.6 = (bf16[256,256]{1,0:T(8,128)(2,1)S(1)}, bf16[256,256]{1,0:T(8,128)(2,1)S(1)}, u32[]{:S(2)}, u32[]{:S(2)}) collective-permute-start(bf16[256,256]{1,0:T(8,128)(2,1)S(1)} %get-tuple-element.57), channel_id=1, source_target_pairs={{0,16},{1,17},{2,18},{3,19},{4,20},{5,21},{6,22},{7,23},{8,24},{9,... | collective-permute-start | bytes 393224 | tf_op jit(solution)/shard_map/ppermute | solution.py:97
  41.5 6.6 %collective-permute-start.7 = (bf16[256,256]{1,0:T(8,128)(2,1)S(1)}, bf16[256,256]{1,0:T(8,128)(2,1)S(1)}, u32[]{:S(2)}, u32[]{:S(2)}) collective-permute-start(bf16[256,256]{1,0:T(8,128)(2,1)S(1)} %get-tuple-element.58), channel_id=1, source_target_pairs={{0,17},{1,16},{2,19},{3,18},{4,21},{5,20},{6,23},{7,22},{8,25},{9,... | collective-permute-start | bytes 393224 | tf_op jit(solution)/shard_map/ppermute | solution.py:97
  48.8 14.1 %collective-permute-start.11 = (bf16[256,256]{1,0:T(8,128)(2,1)S(1)}, bf16[256,256]{1,0:T(8,128)(2,1)S(1)}, u32[]{:S(2)}, u32[]{:S(2)}) collective-permute-start(bf16[256,256]{1,0:T(8,128)(2,1)S(1)} %get-tuple-element.60.refs_2_), channel_id=1, source_target_pairs={{0,2},{1,3},{2,4},{3,5},{4,6},{5,7},{6,0},{7,1},{8,10},{9,11},{10,... | collective-permute-start | bytes 393224 | tf_op jit(solution)/shard_map/ppermute | solution.py:97
  53.1 9.8 %collective-permute-start.10 = (bf16[256,256]{1,0:T(8,128)(2,1)S(1)}, bf16[256,256]{1,0:T(8,128)(2,1)S(1)}, u32[]{:S(2)}, u32[]{:S(2)}) collective-permute-start(bf16[256,256]{1,0:T(8,128)(2,1)S(1)} %get-tuple-element.60.refs_2_), channel_id=1, source_target_pairs={{0,4},{1,5},{2,6},{3,7},{4,0},{5,1},{6,2},{7,3},{8,12},{9,13},{10,... | collective-permute-start | bytes 393224 | tf_op jit(solution)/shard_map/ppermute | solution.py:97
  54.4 8.4 %collective-permute-start.9 = (bf16[256,256]{1,0:T(8,128)(2,1)S(1)}, bf16[256,256]{1,0:T(8,128)(2,1)S(1)}, u32[]{:S(2)}, u32[]{:S(2)}) collective-permute-start(bf16[256,256]{1,0:T(8,128)(2,1)S(1)} %get-tuple-element.60.refs_2_), channel_id=1, source_target_pairs={{0,6},{1,7},{2,0},{3,1},{4,2},{5,3},{6,4},{7,5},{8,14},{9,15},{10,... | collective-permute-start | bytes 393224 | tf_op jit(solution)/shard_map/ppermute | solution.py:97
  62.9 4.4 %collective-permute-start.12 = (bf16[768,256]{1,0:T(8,128)(2,1)S(1)}, bf16[768,256]{1,0:T(8,128)(2,1)S(1)}, u32[]{:S(2)}, u32[]{:S(2)}) collective-permute-start(bf16[768,256]{1,0:T(8,128)(2,1)S(1)} %shard_map.65.refs_4_), channel_id=1, source_target_pairs={{0,8},{1,9},{2,10},{3,11},{4,12},{5,13},{6,14},{7,15},{8,0},{9,1},... | collective-permute-start | bytes 1179656 | tf_op jit(solution)/shard_map/ppermute | solution.py:97
  63.0 4.3 %collective-permute-start.8 = (bf16[256,256]{1,0:T(8,128)(2,1)S(1)}, bf16[256,256]{1,0:T(8,128)(2,1)S(1)}, u32[]{:S(2)}, u32[]{:S(2)}) collective-permute-start(bf16[256,256]{1,0:T(8,128)(2,1)S(1)} %get-tuple-element.60.refs_2_), channel_id=1, source_target_pairs={{0,8},{1,9},{2,10},{3,11},{4,12},{5,13},{6,14},{7,15},{8,0},{9,1},... | collective-permute-start | bytes 393224 | tf_op jit(solution)/shard_map/ppermute | solution.py:97
  70.1 13.3 %collective-permute-start.13 = (bf16[256,256]{1,0:T(8,128)(2,1)S(1)}, bf16[256,256]{1,0:T(8,128)(2,1)S(1)}, u32[]{:S(2)}, u32[]{:S(2)}) collective-permute-start(bf16[256,256]{1,0:T(8,128)(2,1)S(1)} %get-tuple-element.64), channel_id=1, source_target_pairs={{0,1},{1,0},{2,3},{3,2},{4,5},{5,4},{6,7},{7,6},{8,9},{9,8},{10,11... | collective-permute-start | bytes 393224 | tf_op jit(solution)/shard_map/ppermute | solution.py:97
  72.7 10.7 %collective-permute-start.14 = (bf16[256,256]{1,0:T(8,128)(2,1)S(1)}, bf16[256,256]{1,0:T(8,128)(2,1)S(1)}, u32[]{:S(2)}, u32[]{:S(2)}) collective-permute-start(bf16[256,256]{1,0:T(8,128)(2,1)S(1)} %get-tuple-element.67), channel_id=1, source_target_pairs={{0,16},{1,17},{2,18},{3,19},{4,20},{5,21},{6,22},{7,23},{8,24},{9,... | collective-permute-start | bytes 393224 | tf_op jit(solution)/shard_map/ppermute | solution.py:97
  74.9 8.5 %collective-permute-start.15 = (bf16[256,256]{1,0:T(8,128)(2,1)S(1)}, bf16[256,256]{1,0:T(8,128)(2,1)S(1)}, u32[]{:S(2)}, u32[]{:S(2)}) collective-permute-start(bf16[256,256]{1,0:T(8,128)(2,1)S(1)} %get-tuple-element.68), channel_id=1, source_target_pairs={{0,17},{1,16},{2,19},{3,18},{4,21},{5,20},{6,23},{7,22},{8,25},{9,... | collective-permute-start | bytes 393224 | tf_op jit(solution)/shard_map/ppermute | solution.py:97
  76.0 6.2 %copy-start.2 = (bf16[512,2048]{1,0:T(8,128)(2,1)S(1)}, bf16[512,2048]{1,0:T(8,128)(2,1)}, u32[]{:S(2)}) copy-start(bf16[512,2048]{1,0:T(8,128)(2,1)} %copy-done) | copy-start | bytes 6291460
  84.8 11.2 %collective-permute-start.19 = (bf16[256,256]{1,0:T(8,128)(2,1)S(1)}, bf16[256,256]{1,0:T(8,128)(2,1)S(1)}, u32[]{:S(2)}, u32[]{:S(2)}) collective-permute-start(bf16[256,256]{1,0:T(8,128)(2,1)S(1)} %get-tuple-element.73.refs_1_.potential_ref), channel_id=1, source_target_pairs={{0,2},{1,3},{2,4},{3,5},{4,6},{5,7},{6,0},{7,1},{8,10},{9,11},{10,... | collective-permute-start | bytes 393224 | tf_op jit(solution)/shard_map/ppermute | solution.py:97
  87.8 9.8 %collective-permute-start.18 = (bf16[256,256]{1,0:T(8,128)(2,1)S(1)}, bf16[256,256]{1,0:T(8,128)(2,1)S(1)}, u32[]{:S(2)}, u32[]{:S(2)}) collective-permute-start(bf16[256,256]{1,0:T(8,128)(2,1)S(1)} %get-tuple-element.73.refs_1_.potential_ref), channel_id=1, source_target_pairs={{0,4},{1,5},{2,6},{3,7},{4,0},{5,1},{6,2},{7,3},{8,12},{9,13},{10,... | collective-permute-start | bytes 393224 | tf_op jit(solution)/shard_map/ppermute | solution.py:97
  89.3 8.3 %collective-permute-start.17 = (bf16[256,256]{1,0:T(8,128)(2,1)S(1)}, bf16[256,256]{1,0:T(8,128)(2,1)S(1)}, u32[]{:S(2)}, u32[]{:S(2)}) collective-permute-start(bf16[256,256]{1,0:T(8,128)(2,1)S(1)} %get-tuple-element.73.refs_1_.potential_ref), channel_id=1, source_target_pairs={{0,6},{1,7},{2,0},{3,1},{4,2},{5,3},{6,4},{7,5},{8,14},{9,15},{10,... | collective-permute-start | bytes 393224 | tf_op jit(solution)/shard_map/ppermute | solution.py:97
  96.0 3.6 %copy-start.13 = (bf16[512,2048]{1,0:T(8,128)(2,1)S(1)}, bf16[512,2048]{1,0:T(8,128)(2,1)}, u32[]{:S(2)}) copy-start(bf16[512,2048]{1,0:T(8,128)(2,1)} %get-tuple-element.72.refs_0_) | copy-start | bytes 6291460
  97.6 2.0 %collective-permute-start.20 = (bf16[768,256]{1,0:T(8,128)(2,1)S(1)}, bf16[768,256]{1,0:T(8,128)(2,1)S(1)}, u32[]{:S(2)}, u32[]{:S(2)}) collective-permute-start(bf16[768,256]{1,0:T(8,128)(2,1)S(1)} %shard_map.73.refs_3_), channel_id=1, source_target_pairs={{0,8},{1,9},{2,10},{3,11},{4,12},{5,13},{6,14},{7,15},{8,0},{9,1},... | collective-permute-start | bytes 1179656 | tf_op jit(solution)/shard_map/ppermute | solution.py:97
  97.7 1.9 %collective-permute-start.16 = (bf16[256,256]{1,0:T(8,128)(2,1)S(1)}, bf16[256,256]{1,0:T(8,128)(2,1)S(1)}, u32[]{:S(2)}, u32[]{:S(2)}) collective-permute-start(bf16[256,256]{1,0:T(8,128)(2,1)S(1)} %get-tuple-element.73.refs_1_.potential_ref), channel_id=1, source_target_pairs={{0,8},{1,9},{2,10},{3,11},{4,12},{5,13},{6,14},{7,15},{8,0},{9,1},... | collective-permute-start | bytes 393224 | tf_op jit(solution)/shard_map/ppermute | solution.py:97
  99.6 3.3 %copy-start.12 = (bf16[512,2048]{1,0:T(8,128)(2,1)S(1)}, bf16[512,2048]{1,0:T(8,128)(2,1)}, u32[]{:S(2)}) copy-start(bf16[512,2048]{1,0:T(8,128)(2,1)} %get-tuple-element.79.refs_0_) | copy-start | bytes 6291460
  100.5 12.0 %collective-permute-start.22 = (bf16[256,256]{1,0:T(8,128)(2,1)S(1)}, bf16[256,256]{1,0:T(8,128)(2,1)S(1)}, u32[]{:S(2)}, u32[]{:S(2)}) collective-permute-start(bf16[256,256]{1,0:T(8,128)(2,1)S(1)} %get-tuple-element.82), channel_id=1, source_target_pairs={{0,16},{1,17},{2,18},{3,19},{4,20},{5,21},{6,22},{7,23},{8,24},{9,... | collective-permute-start | bytes 393224 | tf_op jit(solution)/shard_map/ppermute | solution.py:97
  102.1 10.4 %collective-permute-start.23 = (bf16[256,256]{1,0:T(8,128)(2,1)S(1)}, bf16[256,256]{1,0:T(8,128)(2,1)S(1)}, u32[]{:S(2)}, u32[]{:S(2)}) collective-permute-start(bf16[256,256]{1,0:T(8,128)(2,1)S(1)} %get-tuple-element.83), channel_id=1, source_target_pairs={{0,17},{1,16},{2,19},{3,18},{4,21},{5,20},{6,23},{7,22},{8,25},{9,... | collective-permute-start | bytes 393224 | tf_op jit(solution)/shard_map/ppermute | solution.py:97
  104.3 8.2 %collective-permute-start.21 = (bf16[256,256]{1,0:T(8,128)(2,1)S(1)}, bf16[256,256]{1,0:T(8,128)(2,1)S(1)}, u32[]{:S(2)}, u32[]{:S(2)}) collective-permute-start(bf16[256,256]{1,0:T(8,128)(2,1)S(1)} %get-tuple-element.81), channel_id=1, source_target_pairs={{0,1},{1,0},{2,3},{3,2},{4,5},{5,4},{6,7},{7,6},{8,9},{9,8},{10,11... | collective-permute-start | bytes 393224 | tf_op jit(solution)/shard_map/ppermute | solution.py:97
  109.0 3.5 %copy-start.15 = (f32[256,256]{1,0:T(8,128)S(1)}, f32[256,256]{1,0:T(8,128)}, u32[]{:S(2)}) copy-start(f32[256,256]{1,0:T(8,128)} %copy-done.14) | copy-start | bytes 786436
  114.0 8.6 %collective-permute-start.27 = (bf16[256,256]{1,0:T(8,128)(2,1)S(1)}, bf16[256,256]{1,0:T(8,128)(2,1)S(1)}, u32[]{:S(2)}, u32[]{:S(2)}) collective-permute-start(bf16[256,256]{1,0:T(8,128)(2,1)S(1)} %get-tuple-element.86.refs_2_), channel_id=1, source_target_pairs={{0,2},{1,3},{2,4},{3,5},{4,6},{5,7},{6,0},{7,1},{8,10},{9,11},{10,... | collective-permute-start | bytes 393224 | tf_op jit(solution)/shard_map/ppermute | solution.py:97
  117.2 9.5 %collective-permute-start.26 = (bf16[256,256]{1,0:T(8,128)(2,1)S(1)}, bf16[256,256]{1,0:T(8,128)(2,1)S(1)}, u32[]{:S(2)}, u32[]{:S(2)}) collective-permute-start(bf16[256,256]{1,0:T(8,128)(2,1)S(1)} %get-tuple-element.86.refs_2_), channel_id=1, source_target_pairs={{0,4},{1,5},{2,6},{3,7},{4,0},{5,1},{6,2},{7,3},{8,12},{9,13},{10,... | collective-permute-start | bytes 393224 | tf_op jit(solution)/shard_map/ppermute | solution.py:97
  118.7 8.2 %collective-permute-start.25 = (bf16[256,256]{1,0:T(8,128)(2,1)S(1)}, bf16[256,256]{1,0:T(8,128)(2,1)S(1)}, u32[]{:S(2)}, u32[]{:S(2)}) collective-permute-start(bf16[256,256]{1,0:T(8,128)(2,1)S(1)} %get-tuple-element.86.refs_2_), channel_id=1, source_target_pairs={{0,6},{1,7},{2,0},{3,1},{4,2},{5,3},{6,4},{7,5},{8,14},{9,15},{10,... | collective-permute-start | bytes 393224 | tf_op jit(solution)/shard_map/ppermute | solution.py:97
  126.9 2.0 %collective-permute-start.28 = (bf16[768,256]{1,0:T(8,128)(2,1)S(1)}, bf16[768,256]{1,0:T(8,128)(2,1)S(1)}, u32[]{:S(2)}, u32[]{:S(2)}) collective-permute-start(bf16[768,256]{1,0:T(8,128)(2,1)S(1)} %shard_map.79.refs_4_), channel_id=1, source_target_pairs={{0,8},{1,9},{2,10},{3,11},{4,12},{5,13},{6,14},{7,15},{8,0},{9,1},... | collective-permute-start | bytes 1179656 | tf_op jit(solution)/shard_map/ppermute | solution.py:97
  127.0 1.9 %collective-permute-start.24 = (bf16[256,256]{1,0:T(8,128)(2,1)S(1)}, bf16[256,256]{1,0:T(8,128)(2,1)S(1)}, u32[]{:S(2)}, u32[]{:S(2)}) collective-permute-start(bf16[256,256]{1,0:T(8,128)(2,1)S(1)} %get-tuple-element.86.refs_2_), channel_id=1, source_target_pairs={{0,8},{1,9},{2,10},{3,11},{4,12},{5,13},{6,14},{7,15},{8,0},{9,1},... | collective-permute-start | bytes 393224 | tf_op jit(solution)/shard_map/ppermute | solution.py:97
  130.0 8.3 %collective-permute-start.29 = (bf16[256,256]{1,0:T(8,128)(2,1)S(1)}, bf16[256,256]{1,0:T(8,128)(2,1)S(1)}, u32[]{:S(2)}, u32[]{:S(2)}) collective-permute-start(bf16[256,256]{1,0:T(8,128)(2,1)S(1)} %get-tuple-element.89), channel_id=1, source_target_pairs={{0,1},{1,0},{2,3},{3,2},{4,5},{5,4},{6,7},{7,6},{8,9},{9,8},{10,11... | collective-permute-start | bytes 393224 | tf_op jit(solution)/shard_map/ppermute | solution.py:97
  131.4 6.9 %collective-permute-start.31 = (bf16[256,256]{1,0:T(8,128)(2,1)S(1)}, bf16[256,256]{1,0:T(8,128)(2,1)S(1)}, u32[]{:S(2)}, u32[]{:S(2)}) collective-permute-start(bf16[256,256]{1,0:T(8,128)(2,1)S(1)} %get-tuple-element.91), channel_id=1, source_target_pairs={{0,17},{1,16},{2,19},{3,18},{4,21},{5,20},{6,23},{7,22},{8,25},{9,... | collective-permute-start | bytes 393224 | tf_op jit(solution)/shard_map/ppermute | solution.py:97
  134.9 5.5 %collective-permute-start.30 = (bf16[256,256]{1,0:T(8,128)(2,1)S(1)}, bf16[256,256]{1,0:T(8,128)(2,1)S(1)}, u32[]{:S(2)}, u32[]{:S(2)}) collective-permute-start(bf16[256,256]{1,0:T(8,128)(2,1)S(1)} %get-tuple-element.90), channel_id=1, source_target_pairs={{0,16},{1,17},{2,18},{3,19},{4,20},{5,21},{6,22},{7,23},{8,24},{9,... | collective-permute-start | bytes 393224 | tf_op jit(solution)/shard_map/ppermute | solution.py:97
  140.3 16.5 %copy-start.11 = (bf16[768,2048]{1,0:T(8,128)(2,1)S(1)}, bf16[768,2048]{1,0:T(8,128)(2,1)}, u32[]{:S(2)}) copy-start(bf16[768,2048]{1,0:T(8,128)(2,1)} %get-tuple-element.98.refs_0_) | copy-start | bytes 9437188
  142.0 8.6 %collective-permute-start.35 = (bf16[256,256]{1,0:T(8,128)(2,1)S(1)}, bf16[256,256]{1,0:T(8,128)(2,1)S(1)}, u32[]{:S(2)}, u32[]{:S(2)}) collective-permute-start(bf16[256,256]{1,0:T(8,128)(2,1)S(1)} %get-tuple-element.94.refs_1_), channel_id=1, source_target_pairs={{0,2},{1,3},{2,4},{3,5},{4,6},{5,7},{6,0},{7,1},{8,10},{9,11},{10,... | collective-permute-start | bytes 393224 | tf_op jit(solution)/shard_map/ppermute | solution.py:97
  145.2 9.4 %collective-permute-start.34 = (bf16[256,256]{1,0:T(8,128)(2,1)S(1)}, bf16[256,256]{1,0:T(8,128)(2,1)S(1)}, u32[]{:S(2)}, u32[]{:S(2)}) collective-permute-start(bf16[256,256]{1,0:T(8,128)(2,1)S(1)} %get-tuple-element.94.refs_1_), channel_id=1, source_target_pairs={{0,4},{1,5},{2,6},{3,7},{4,0},{5,1},{6,2},{7,3},{8,12},{9,13},{10,... | collective-permute-start | bytes 393224 | tf_op jit(solution)/shard_map/ppermute | solution.py:97
  146.7 8.1 %collective-permute-start.33 = (bf16[256,256]{1,0:T(8,128)(2,1)S(1)}, bf16[256,256]{1,0:T(8,128)(2,1)S(1)}, u32[]{:S(2)}, u32[]{:S(2)}) collective-permute-start(bf16[256,256]{1,0:T(8,128)(2,1)S(1)} %get-tuple-element.94.refs_1_), channel_id=1, source_target_pairs={{0,6},{1,7},{2,0},{3,1},{4,2},{5,3},{6,4},{7,5},{8,14},{9,15},{10,... | collective-permute-start | bytes 393224 | tf_op jit(solution)/shard_map/ppermute | solution.py:97
  154.8 2.0 %collective-permute-start.36 = (bf16[768,256]{1,0:T(8,128)(2,1)S(1)}, bf16[768,256]{1,0:T(8,128)(2,1)S(1)}, u32[]{:S(2)}, u32[]{:S(2)}) collective-permute-start(bf16[768,256]{1,0:T(8,128)(2,1)S(1)} %shard_map.85.refs_3_), channel_id=1, source_target_pairs={{0,8},{1,9},{2,10},{3,11},{4,12},{5,13},{6,14},{7,15},{8,0},{9,1},... | collective-permute-start | bytes 1179656 | tf_op jit(solution)/shard_map/ppermute | solution.py:97
  154.9 1.9 %collective-permute-start.32 = (bf16[256,256]{1,0:T(8,128)(2,1)S(1)}, bf16[256,256]{1,0:T(8,128)(2,1)S(1)}, u32[]{:S(2)}, u32[]{:S(2)}) collective-permute-start(bf16[256,256]{1,0:T(8,128)(2,1)S(1)} %get-tuple-element.94.refs_1_), channel_id=1, source_target_pairs={{0,8},{1,9},{2,10},{3,11},{4,12},{5,13},{6,14},{7,15},{8,0},{9,1},... | collective-permute-start | bytes 393224 | tf_op jit(solution)/shard_map/ppermute | solution.py:97
  156.8 4.0 %copy-start.10 = (bf16[768,2048]{1,0:T(8,128)(2,1)S(1)}, bf16[768,2048]{1,0:T(8,128)(2,1)}, u32[]{:S(2)}) copy-start(bf16[768,2048]{1,0:T(8,128)(2,1)} %get-tuple-element.76.refs_0_) | copy-start | bytes 9437188
  158.6 7.8 %collective-permute-start.38 = (bf16[384,256]{1,0:T(8,128)(2,1)S(1)}, bf16[384,256]{1,0:T(8,128)(2,1)S(1)}, u32[]{:S(2)}, u32[]{:S(2)}) collective-permute-start(bf16[384,256]{1,0:T(8,128)(2,1)S(1)} %get-tuple-element.99), channel_id=1, source_target_pairs={{0,16},{1,17},{2,18},{3,19},{4,20},{5,21},{6,22},{7,23},{8,24},{9,... | collective-permute-start | bytes 589832 | tf_op jit(solution)/shard_map/ppermute | solution.py:97
  160.0 10.0 %collective-permute-start.39 = (bf16[384,256]{1,0:T(8,128)(2,1)S(1)}, bf16[384,256]{1,0:T(8,128)(2,1)S(1)}, u32[]{:S(2)}, u32[]{:S(2)}) collective-permute-start(bf16[384,256]{1,0:T(8,128)(2,1)S(1)} %get-tuple-element.100), channel_id=1, source_target_pairs={{0,17},{1,16},{2,19},{3,18},{4,21},{5,20},{6,23},{7,22},{8,25},{9,... | collective-permute-start | bytes 589832 | tf_op jit(solution)/shard_map/ppermute | solution.py:97
  162.6 10.6 %collective-permute-start.37 = (bf16[384,256]{1,0:T(8,128)(2,1)S(1)}, bf16[384,256]{1,0:T(8,128)(2,1)S(1)}, u32[]{:S(2)}, u32[]{:S(2)}) collective-permute-start(bf16[384,256]{1,0:T(8,128)(2,1)S(1)} %get-tuple-element.97), channel_id=1, source_target_pairs={{0,1},{1,0},{2,3},{3,2},{4,5},{5,4},{6,7},{7,6},{8,9},{9,8},{10,11... | collective-permute-start | bytes 589832 | tf_op jit(solution)/shard_map/ppermute | solution.py:97
  (10 other events, 13.6 us)

commit v10 on v9

--- a/solution.py
+++ b/solution.py
@@ -102,9 +102,11 @@
     def along(self, value):
         return [self.shift(value, dz=-dz) for dz in range(1, self.z)]
 
-    def gathered(self, value, after, along=None):
-        along = self.along(value) if along is None else along
-        return self.by_core(value) + (self.by_core(pack(along, after)) if along else [])
+    def across(self, value):
+        return [self.shift(value, dx=-dx, dy=-dy) for dx, dy in self.plane[1:]]
+
+    def gathered(self, value, others, after):
+        return self.by_core(value) + (self.by_core(pack(others, after)) if others else [])
 
     def index(self, x, core, z, y):
         x, core, z, y = x % self.x, core % self.core, z % self.z, y % self.y
@@ -122,6 +124,18 @@
 
     def in_plane(self, me, step):
         return self.near(me, dx=step // self.y, dy=step % self.y)
+
+    def in_planes(self, me, k):
+        if k < self.core:
+            return self.near(me, dc=k)
+        rest, others = k - self.core, len(self.plane) - 1
+        dx, dy = self.plane[1 + rest % others]
+        return self.near(me, dx=dx, dy=dy, dc=rest // others)
+
+    def given_along(self, blocks):
+        return [blocks[0]] + [
+            self.shift(block, dz=1 + dz) for dz, block in enumerate(blocks[1:])
+        ]
 
     def spot(self, me, step):
         x, _, _, y = self.digits(me)
@@ -372,16 +386,16 @@
     ]
 
 
-def first_kernel(layout, form, me_ref, letter_ref, *refs):
-    count = len(layout.plane)
+def first_kernel(layout, form, me_ref, letter_ref, after_ref, *refs):
+    count = layout.z
     pieces, outs, token_ref = refs[: -count - 1], refs[-count - 1 : -1], refs[-1]
     token_ref[...] = jnp.zeros_like(token_ref)
     me, size, edges = me_ref[0], form.tri_dev, form.edges
-    base = layout.in_plane(me, pl.program_id(0)) * size
+    base = layout.near(me, dz=pl.program_id(0)) * size
     total, k = None, 0
     for piece in pieces:
         for row in range(0, piece.shape[0], edges):
-            plus, minus = form.ends(letter_ref[layout.in_line(me, k)])
+            plus, minus = form.ends(letter_ref[layout.in_planes(me, k)])
             signed = pick(plus, base, size) - pick(minus, base, size)
             term = matmul(signed, piece[row : row + edges, :])
             total = term if total is None else total + term
@@ -389,18 +403,18 @@
     set_blocks(total, outs)
 
 
-def first_charges(layout, form, me, letters, pieces, resident):
-    count, width = len(layout.plane), pieces[0].shape[1]
+def first_charges(layout, form, me, letters, labels, pieces, resident):
+    count, width = layout.z, pieces[0].shape[1]
     shapes = blocks_like(count, form.tri_dev, width, True) + [TOKEN]
     return pl.pallas_call(
         functools.partial(first_kernel, layout, form),
         grid=(count,),
-        in_specs=[pl.BlockSpec(memory_space=pltpu.SMEM)] + [whole()] * (1 + len(pieces)),
+        in_specs=[pl.BlockSpec(memory_space=pltpu.SMEM)] + [whole()] * (2 + len(pieces)),
         out_specs=[whole()] * len(shapes),
         out_shape=shapes,
         compiler_params=params(resident),
         cost_estimate=cost(4),
-    )(me, letters, *pieces)
+    )(me, letters, labels, *pieces)
 
 
 def apply_kernel(mats, fed, block, row, *refs):
@@ -565,10 +579,10 @@
 
     resident = count * 2 * tri_dev * cols * 2 <= 16 * 2**20
 
-    along = layout.along(currents)
+    across = layout.across(currents)
     form = Letter(edge_dev, tri_dev, count * slots)
     letters = letters_of(
-        layout, form, incidence, centroids, slots, along[-1:]
+        layout, form, incidence, centroids, slots, ()
     )
     letters = lax.all_to_all(letters, AXES, split_axis=0, concat_axis=0, tiled=True)
     labels = letters[:, form.starts[3] :, :].reshape(devices, -1)[:, : count * slots]
@@ -605,14 +619,13 @@
         )
         return part, token
 
-    pieces = layout.gathered(currents, (letters,), along)
-    *blocks, token = first_charges(layout, form, me, letters, pieces, resident)
-    part, token = tile_part(spans[0], token)
-    tiles = [part]
-    charge, rounded, token = sum_of(layout.given(blocks), (token,))
-    for span in spans[1:]:
+    pieces = layout.gathered(currents, across, (letters,))
+    *blocks, token = first_charges(layout, form, me, letters, labels, pieces, resident)
+    tiles = []
+    for span in spans:
         part, token = tile_part(span, token)
         tiles.append(part)
+    charge, rounded, token = sum_of(layout.given_along(blocks), (token,))
 
     def incidence_parts(token):
         parts = []
@@ -632,30 +645,32 @@
     summed, potential = (), None
     for sweep in range(sweeps):
         weight = sweep_weights[sweep].reshape(1)
-        pieces = layout.gathered(rounded, (token,))
-        blocks, token = multiply(tiles, pieces, tri_dev, resident)
         last = sweep + 1 == sweeps
-        if not near and not last:
+        build_now = not near and not last
+        if build_now:
             (part, degree), token = adjacency_part(spans[0], token)
             near.append([part])
+        pieces = layout.gathered(rounded, layout.along(rounded), (token,))
+        blocks, token = multiply(tiles, pieces, tri_dev, resident)
+        if build_now:
+            for span in spans[1:]:
+                part, token = adjacency_part(span, token)
+                near.append(part)
         potential, *summed, weighted, token = potential_of(
             weight, layout.given(blocks), summed, (token,)
         )
         if last:
             break
-        for span in spans[len(near) :]:
-            part, token = adjacency_part(span, token)
-            near.append(part)
-        pieces = layout.gathered(potential, (token,))
+        if build_now:
+            ends, token = incidence_parts(token)
+        pieces = layout.gathered(potential, layout.along(potential), (token,))
         blocks, token = multiply(near, pieces, tri_dev)
-        if ends is None:
-            ends, token = incidence_parts(token)
         charge, rounded, token = charge_of(
             weight, charge, degree, potential, layout.given(blocks), (token,)
         )
     if ends is None:
         ends, token = incidence_parts(token)
-    pieces = layout.gathered(weighted, (token,))
+    pieces = layout.gathered(weighted, layout.along(weighted), (token,))
     blocks, _ = multiply(ends, pieces, edge_dev)
     return current_of(currents, layout.given(blocks)), potential
 

time: 174 us -> 163 us (0.937)
  local copies, waits for them, and re-layouts: 11.5 us -> 2.23 us
    unnamed x34 -> x16, local copies, waits for them, and re-layouts: 7.71 us -> 1.43 us
    ppermute x40, starting transfers between devices: 51.6 us -> 46.8 us  [shift(): return lax.ppermute(value, AXES, pairs)]
    all_to_all x1, starting transfers between devices: 3.98 us -> 7.3 us  [per_device(): lax.all_to_all(letters, AXES, split_axis=0, concat_axis=0, tiled=True)]
  transfers between devices with their start and end apart: 41 -> 41, of which waited for: 18 -> 24; matrix products, arithmetic and copies ran while one was open for 2% -> 0% of each run, Pallas kernels for 22% -> 23%
where the time goes in v10:
time: 163 us
  starting transfers between devices  54.1 us (33%)
  waiting for transfers between devices  52.9 us (32%)
  Pallas kernels  52.4 us (32%)
  local copies, waits for them, and re-layouts  2.23 us (1%)
    ppermute x40, waiting for transfers between devices, shift(): return lax.ppermute(value, AXES, pairs)  52.9 us
    ppermute x40, starting transfers between devices, shift(): return lax.ppermute(value, AXES, pairs)  46.8 us
    pallas_call x6, Pallas kernels, build(): pl.pallas_call(kernel, grid=(len(span),), in_specs=[pl.BlockSpec(memory_s...  28.4 us
    pallas_call x12, Pallas kernels, apply(): pl.pallas_call(functools.partial(apply_kernel, mats, len(pieces), block,...  14.3 us
    all_to_all x1, starting transfers between devices, per_device(): lax.all_to_all(letters, AXES, split_axis=0, concat_axis=0, tiled=True)  7.3 us
  transfers between devices with their start and end apart: 41, of which 24 were waited for; matrix products, arithmetic and copies ran while one was open for 0% of the time, Pallas kernels for 23%

profile of v10, /device:TPU:0, one launch (start us, length us, event | category | flops | bytes accessed | tf_op | source)
XLA Modules:
  0.0 162.5 jit_solution(2804964549322104307)
XLA Ops:
  3.3 7.3 %all-to-all-start = ((s32[32,8,128]{2,1,0:T(8,128)}), s32[32,8,128]{2,1,0:T(8,128)S(1)}, u32[]{:S(2)}, u32[]{:S(2)}) async-start(s32[32,8,128]{2,1,0:T(8,128)} %shard_map.59), calls=%async_computation | async-start | bytes 262144 | tf_op jit(solution)/shard_map/all_to_all | solution.py:587
  10.6 2.7 %collective-permute-start.3 = (bf16[384,256]{1,0:T(8,128)(2,1)S(1)}, bf16[384,256]{1,0:T(8,128)(2,1)S(1)}, u32[]{:S(2)}, u32[]{:S(2)}) collective-permute-start(bf16[384,256]{1,0:T(8,128)(2,1)S(1)} %copy-done), channel_id=1, source_target_pairs={{0,17},{1,16},{2,19},{3,18},{4,21},{5,20},{6,23},{7,22},{8,25},{9,... | collective-permute-start | bytes 589832 | tf_op jit(solution)/shard_map/ppermute | solution.py:97
  14.1 6.3 %collective-permute-done.3.refs_2_ = bf16[384,256]{1,0:T(8,128)(2,1)S(1)} collective-permute-done((bf16[384,256]{1,0:T(8,128)(2,1)S(1)}, bf16[384,256]{1,0:T(8,128)(2,1)S(1)}, u32[]{:S(2)}, u32[]{:S(2)}) %collective-permute-start.3) | collective-permute-done | bytes 196640 | tf_op jit(solution)/shard_map/ppermute | solution.py:97
  20.5 3.5 %collective-permute-done.2.refs_1_ = bf16[384,256]{1,0:T(8,128)(2,1)S(1)} collective-permute-done((bf16[384,256]{1,0:T(8,128)(2,1)S(1)}, bf16[384,256]{1,0:T(8,128)(2,1)S(1)}, u32[]{:S(2)}, u32[]{:S(2)}) %collective-permute-start.2) | collective-permute-done | bytes 196640 | tf_op jit(solution)/shard_map/ppermute | solution.py:97
  25.0 1.5 collective-permute-done.refs_1_
  26.5 3.1 %shard_map.61 = (f32[256,256]{1,0:T(8,128)S(1)}, bf16[256,256]{1,0:T(8,128)(2,1)S(1)}, bf16[256,256]{1,0:T(8,128)(2,1)S(1)}, bf16[256,256]{1,0:T(8,128)(2,1)S(1)}, f32[8,128]{1,0:T(8,128)S(1)}) custom-call(s32[1]{0:T(128)} %bitcast.me_ref, s32[32,8,128]{2,1,0:T(8,128)S(1)} %all-to-all-done.refs_3_.letter_ref, s32[4,1,2048]{2,1,0:T(1,128)S(1)} %reshape.11.after_ref.label_ref, ...), custom_call_target="tpu_custom_call" | custom-call | flops 4600000000 | tf_op jit(solution)/shard_map/pallas_call | solution.py:409
  29.6 1.5 collective-permute-start.5
  31.0 2.5 %collective-permute-start.6 = (bf16[256,256]{1,0:T(8,128)(2,1)S(1)}, bf16[256,256]{1,0:T(8,128)(2,1)S(1)}, u32[]{:S(2)}, u32[]{:S(2)}) collective-permute-start(bf16[256,256]{1,0:T(8,128)(2,1)S(1)} %get-tuple-element.57), channel_id=1, source_target_pairs={{0,4},{1,5},{2,6},{3,7},{4,0},{5,1},{6,2},{7,3},{8,12},{9,13},{10,... | collective-permute-start | bytes 393224 | tf_op jit(solution)/shard_map/ppermute | solution.py:97
  34.8 4.7 %shard_map.62 = (bf16[512,2048]{1,0:T(8,128)(2,1)S(1)}, bf16[512,2048]{1,0:T(8,128)(2,1)S(1)}, f32[8,128]{1,0:T(8,128)S(1)}) custom-call(s32[1]{0:T(128)} %bitcast.me_ref, s32[32,8,128]{2,1,0:T(8,128)S(1)} %all-to-all-done.refs_3_.letter_ref, f32[8,128]{1,0:T(8,128)S(1)} %get-tuple-element.52.after_ref), custom_call_target="tpu_custom_call" | custom-call | flops 6899999744 | tf_op jit(solution)/shard_map/pallas_call | solution.py:319
  39.5 4.7 %shard_map.63 = (bf16[512,2048]{1,0:T(8,128)(2,1)S(1)}, bf16[512,2048]{1,0:T(8,128)(2,1)S(1)}, f32[8,128]{1,0:T(8,128)S(1)}) custom-call(s32[1]{0:T(128)} %bitcast.me_ref, s32[32,8,128]{2,1,0:T(8,128)S(1)} %all-to-all-done.refs_3_.letter_ref, f32[8,128]{1,0:T(8,128)S(1)} %get-tuple-element.59.after_ref), custom_call_target="tpu_custom_call" | custom-call | flops 6899999744 | tf_op jit(solution)/shard_map/pallas_call | solution.py:319
  44.3 1.8 %collective-permute-start.11 = (bf16[256,256]{1,0:T(8,128)(2,1)S(1)}, bf16[256,256]{1,0:T(8,128)(2,1)S(1)}, u32[]{:S(2)}, u32[]{:S(2)}) collective-permute-start(bf16[256,256]{1,0:T(8,128)(2,1)S(1)} %get-tuple-element.61.refs_2_), channel_id=1, source_target_pairs={{0,2},{1,3},{2,4},{3,5},{4,6},{5,7},{6,0},{7,1},{8,10},{9,11},{10,... | collective-permute-start | bytes 393224 | tf_op jit(solution)/shard_map/ppermute | solution.py:97
  46.1 1.3 collective-permute-start.10
  48.5 6.3 %shard_map.65 = (bf16[512,2048]{1,0:T(8,128)(2,1)}, f32[256,128]{1,0:T(8,128)S(1)}, f32[8,128]{1,0:T(8,128)S(1)}) custom-call(s32[1]{0:T(128)} %bitcast.me_ref, s32[4,1,2048]{2,1,0:T(1,128)S(1)} %reshape.11.after_ref.label_ref, f32[8,128]{1,0:T(8,128)S(1)} %get-tuple-element.62.after_ref), custom_call_target="tpu_custom_call" | custom-call | flops 6899999744 | tf_op jit(solution)/shard_map/pallas_call | solution.py:319
  54.9 1.7 %collective-permute-done.10.refs_1_ = bf16[256,256]{1,0:T(8,128)(2,1)S(1)} collective-permute-done((bf16[256,256]{1,0:T(8,128)(2,1)S(1)}, bf16[256,256]{1,0:T(8,128)(2,1)S(1)}, u32[]{:S(2)}, u32[]{:S(2)}) %collective-permute-start.10) | collective-permute-done | bytes 131104 | tf_op jit(solution)/shard_map/ppermute | solution.py:97
  65.1 5.8 %shard_map.71 = (bf16[512,2048]{1,0:T(8,128)(2,1)}, f32[8,128]{1,0:T(8,128)S(1)}) custom-call(s32[1]{0:T(128)} %bitcast.me_ref, s32[4,1,2048]{2,1,0:T(1,128)S(1)} %reshape.11.after_ref.label_ref, f32[8,128]{1,0:T(8,128)S(1)} %get-tuple-element.70.after_ref), custom_call_target="tpu_custom_call" | custom-call | flops 6899999744 | tf_op jit(solution)/shard_map/pallas_call | solution.py:319
  72.1 1.4 shard_map.72
  73.5 3.3 %collective-permute-start.19 = (bf16[256,256]{1,0:T(8,128)(2,1)S(1)}, bf16[256,256]{1,0:T(8,128)(2,1)S(1)}, u32[]{:S(2)}, u32[]{:S(2)}) collective-permute-start(bf16[256,256]{1,0:T(8,128)(2,1)S(1)} %get-tuple-element.76.refs_1_.potential_ref), channel_id=1, source_target_pairs={{0,2},{1,3},{2,4},{3,5},{4,6},{5,7},{6,0},{7,1},{8,10},{9,11},{10,... | collective-permute-start | bytes 393224 | tf_op jit(solution)/shard_map/ppermute | solution.py:97
  76.8 1.3 collective-permute-start.18
  79.1 3.4 %shard_map.73 = (bf16[768,2048]{1,0:T(8,128)(2,1)}, f32[8,128]{1,0:T(8,128)S(1)}) custom-call(s32[1]{0:T(128)} %bitcast.me_ref, s32[32,8,128]{2,1,0:T(8,128)S(1)} %all-to-all-done.refs_3_.letter_ref, f32[8,128]{1,0:T(8,128)S(1)} %get-tuple-element.72.after_ref), custom_call_target="tpu_custom_call" | custom-call | flops 3449999872 | tf_op jit(solution)/shard_map/pallas_call | solution.py:319
  82.6 3.5 %shard_map.74 = (bf16[768,2048]{1,0:T(8,128)(2,1)}, f32[8,128]{1,0:T(8,128)S(1)}) custom-call(s32[1]{0:T(128)} %bitcast.me_ref, s32[32,8,128]{2,1,0:T(8,128)S(1)} %all-to-all-done.refs_3_.letter_ref, f32[8,128]{1,0:T(8,128)S(1)} %get-tuple-element.78.after_ref), custom_call_target="tpu_custom_call" | custom-call | flops 3449999872 | tf_op jit(solution)/shard_map/pallas_call | solution.py:319
  86.9 1.4 collective-permute-done.16.refs_2_
  89.2 1.4 collective-permute-start.22
  90.6 1.2 collective-permute-start.23
  91.9 1.5 shard_map.76
  94.3 1.4 collective-permute-done.22.refs_1_
  95.6 2.7 %collective-permute-done.23.refs_2_ = bf16[256,256]{1,0:T(8,128)(2,1)S(1)} collective-permute-done((bf16[256,256]{1,0:T(8,128)(2,1)S(1)}, bf16[256,256]{1,0:T(8,128)(2,1)S(1)}, u32[]{:S(2)}, u32[]{:S(2)}) %collective-permute-start.23) | collective-permute-done | bytes 131104 | tf_op jit(solution)/shard_map/ppermute | solution.py:97
  98.3 2.4 %collective-permute-done.21.refs_0_ = bf16[256,256]{1,0:T(8,128)(2,1)S(1)} collective-permute-done((bf16[256,256]{1,0:T(8,128)(2,1)S(1)}, bf16[256,256]{1,0:T(8,128)(2,1)S(1)}, u32[]{:S(2)}, u32[]{:S(2)}) %collective-permute-start.21) | collective-permute-done | bytes 131104 | tf_op jit(solution)/shard_map/ppermute | solution.py:97
  100.7 1.4 shard_map.78
  102.1 3.2 %collective-permute-start.27 = (bf16[256,256]{1,0:T(8,128)(2,1)S(1)}, bf16[256,256]{1,0:T(8,128)(2,1)S(1)}, u32[]{:S(2)}, u32[]{:S(2)}) collective-permute-start(bf16[256,256]{1,0:T(8,128)(2,1)S(1)} %get-tuple-element.86.refs_2_), channel_id=1, source_target_pairs={{0,2},{1,3},{2,4},{3,5},{4,6},{5,7},{6,0},{7,1},{8,10},{9,11},{10,... | collective-permute-start | bytes 393224 | tf_op jit(solution)/shard_map/ppermute | solution.py:97
  105.3 1.6 %collective-permute-start.26 = (bf16[256,256]{1,0:T(8,128)(2,1)S(1)}, bf16[256,256]{1,0:T(8,128)(2,1)S(1)}, u32[]{:S(2)}, u32[]{:S(2)}) collective-permute-start(bf16[256,256]{1,0:T(8,128)(2,1)S(1)} %get-tuple-element.86.refs_2_), channel_id=1, source_target_pairs={{0,4},{1,5},{2,6},{3,7},{4,0},{5,1},{6,2},{7,3},{8,12},{9,13},{10,... | collective-permute-start | bytes 393224 | tf_op jit(solution)/shard_map/ppermute | solution.py:97
  107.7 3.1 %collective-permute-done.27.refs_2_ = bf16[256,256]{1,0:T(8,128)(2,1)S(1)} collective-permute-done((bf16[256,256]{1,0:T(8,128)(2,1)S(1)}, bf16[256,256]{1,0:T(8,128)(2,1)S(1)}, u32[]{:S(2)}, u32[]{:S(2)}) %collective-permute-start.27) | collective-permute-done | bytes 131104 | tf_op jit(solution)/shard_map/ppermute | solution.py:97
  110.8 4.5 %collective-permute-done.26.refs_1_ = bf16[256,256]{1,0:T(8,128)(2,1)S(1)} collective-permute-done((bf16[256,256]{1,0:T(8,128)(2,1)S(1)}, bf16[256,256]{1,0:T(8,128)(2,1)S(1)}, u32[]{:S(2)}, u32[]{:S(2)}) %collective-permute-start.26) | collective-permute-done | bytes 131104 | tf_op jit(solution)/shard_map/ppermute | solution.py:97
  116.0 1.4 collective-permute-done.24.refs_3_
  120.1 1.9 %collective-permute-start.31 = (bf16[256,256]{1,0:T(8,128)(2,1)S(1)}, bf16[256,256]{1,0:T(8,128)(2,1)S(1)}, u32[]{:S(2)}, u32[]{:S(2)}) collective-permute-start(bf16[256,256]{1,0:T(8,128)(2,1)S(1)} %get-tuple-element.91), channel_id=1, source_target_pairs={{0,17},{1,16},{2,19},{3,18},{4,21},{5,20},{6,23},{7,22},{8,25},{9,... | collective-permute-start | bytes 393224 | tf_op jit(solution)/shard_map/ppermute | solution.py:97
  125.1 1.4 collective-permute-done.29.refs_0_
  127.2 1.6 %collective-permute-done.30.refs_1_ = bf16[256,256]{1,0:T(8,128)(2,1)S(1)} collective-permute-done((bf16[256,256]{1,0:T(8,128)(2,1)S(1)}, bf16[256,256]{1,0:T(8,128)(2,1)S(1)}, u32[]{:S(2)}, u32[]{:S(2)}) %collective-permute-start.30) | collective-permute-done | bytes 131104 | tf_op jit(solution)/shard_map/ppermute | solution.py:97
  128.9 1.5 shard_map.84
  130.4 3.3 %collective-permute-start.35 = (bf16[256,256]{1,0:T(8,128)(2,1)S(1)}, bf16[256,256]{1,0:T(8,128)(2,1)S(1)}, u32[]{:S(2)}, u32[]{:S(2)}) collective-permute-start(bf16[256,256]{1,0:T(8,128)(2,1)S(1)} %get-tuple-element.94.refs_1_), channel_id=1, source_target_pairs={{0,2},{1,3},{2,4},{3,5},{4,6},{5,7},{6,0},{7,1},{8,10},{9,11},{10,... | collective-permute-start | bytes 393224 | tf_op jit(solution)/shard_map/ppermute | solution.py:97
  133.7 1.3 collective-permute-start.34
  136.0 2.8 %collective-permute-done.35.refs_2_ = bf16[256,256]{1,0:T(8,128)(2,1)S(1)} collective-permute-done((bf16[256,256]{1,0:T(8,128)(2,1)S(1)}, bf16[256,256]{1,0:T(8,128)(2,1)S(1)}, u32[]{:S(2)}, u32[]{:S(2)}) %collective-permute-start.35) | collective-permute-done | bytes 131104 | tf_op jit(solution)/shard_map/ppermute | solution.py:97
  138.8 4.2 %collective-permute-done.34.refs_1_ = bf16[256,256]{1,0:T(8,128)(2,1)S(1)} collective-permute-done((bf16[256,256]{1,0:T(8,128)(2,1)S(1)}, bf16[256,256]{1,0:T(8,128)(2,1)S(1)}, u32[]{:S(2)}, u32[]{:S(2)}) %collective-permute-start.34) | collective-permute-done | bytes 131104 | tf_op jit(solution)/shard_map/ppermute | solution.py:97
  143.7 1.4 collective-permute-done.32.refs_2_
  145.1 1.8 %shard_map.87 = (bf16[384,256]{1,0:T(8,128)(2,1)S(1)}, bf16[384,256]{1,0:T(8,128)(2,1)S(1)}, f32[8,128]{1,0:T(8,128)}) custom-call(bf16[768,2048]{1,0:T(8,128)(2,1)S(1)} %copy-done.4, bf16[256,256]{1,0:T(8,128)(2,1)S(1)} %get-tuple-element.94.refs_1_, bf16[256,256]{1,0:T(8,128)(2,1)S(1)} %collective-permute-done.32.refs_2_, ...), custom_call_target="tpu_custom_call" | custom-call | flops 1150000000 | tf_op jit(solution)/shard_map/pallas_call | solution.py:447
  146.9 1.4 collective-permute-start.38
  149.3 1.8 %shard_map.86 = (f32[384,256]{1,0:T(8,128)S(1)}, bf16[384,256]{1,0:T(8,128)(2,1)S(1)}, f32[8,128]{1,0:T(8,128)}) custom-call(bf16[768,2048]{1,0:T(8,128)(2,1)S(1)} %copy-done.3, bf16[256,256]{1,0:T(8,128)(2,1)S(1)} %get-tuple-element.94.refs_1_, bf16[256,256]{1,0:T(8,128)(2,1)S(1)} %collective-permute-done.32.refs_2_, ...), custom_call_target="tpu_custom_call" | custom-call | flops 1150000000 | tf_op jit(solution)/shard_map/pallas_call | solution.py:447
  152.2 2.5 %collective-permute-done.38.refs_1_ = bf16[384,256]{1,0:T(8,128)(2,1)S(1)} collective-permute-done((bf16[384,256]{1,0:T(8,128)(2,1)S(1)}, bf16[384,256]{1,0:T(8,128)(2,1)S(1)}, u32[]{:S(2)}, u32[]{:S(2)}) %collective-permute-start.38) | collective-permute-done | bytes 196640 | tf_op jit(solution)/shard_map/ppermute | solution.py:97
  154.7 3.9 %collective-permute-done.39.refs_2_ = bf16[384,256]{1,0:T(8,128)(2,1)S(1)} collective-permute-done((bf16[384,256]{1,0:T(8,128)(2,1)S(1)}, bf16[384,256]{1,0:T(8,128)(2,1)S(1)}, u32[]{:S(2)}, u32[]{:S(2)}) %collective-permute-start.39) | collective-permute-done | bytes 196640 | tf_op jit(solution)/shard_map/ppermute | solution.py:97
  158.6 3.1 %collective-permute-done.37.refs_0_ = bf16[384,256]{1,0:T(8,128)(2,1)S(1)} collective-permute-done((bf16[384,256]{1,0:T(8,128)(2,1)S(1)}, bf16[384,256]{1,0:T(8,128)(2,1)S(1)}, u32[]{:S(2)}, u32[]{:S(2)}) %collective-permute-start.37) | collective-permute-done | bytes 196640 | tf_op jit(solution)/shard_map/ppermute | solution.py:97
  (85 shorter events, 32.8 us)
Async XLA Ops:
  0.6 9.9 %copy-start = (bf16[384,256]{1,0:T(8,128)(2,1)S(1)}, bf16[384,256]{1,0:T(8,128)(2,1)}, u32[]{:S(2)}) copy-start(bf16[384,256]{1,0:T(8,128)(2,1)} %current_ref.1) | copy-start | bytes 589828
  0.6 0.7 copy-start.1
  3.3 20.8 %all-to-all-start = ((s32[32,8,128]{2,1,0:T(8,128)}), s32[32,8,128]{2,1,0:T(8,128)S(1)}, u32[]{:S(2)}, u32[]{:S(2)}) async-start(s32[32,8,128]{2,1,0:T(8,128)} %shard_map.59), calls=%async_computation | async-start | bytes 262144 | tf_op jit(solution)/shard_map/all_to_all | solution.py:587
  10.6 9.9 %collective-permute-start.3 = (bf16[384,256]{1,0:T(8,128)(2,1)S(1)}, bf16[384,256]{1,0:T(8,128)(2,1)S(1)}, u32[]{:S(2)}, u32[]{:S(2)}) collective-permute-start(bf16[384,256]{1,0:T(8,128)(2,1)S(1)} %copy-done), channel_id=1, source_target_pairs={{0,17},{1,16},{2,19},{3,18},{4,21},{5,20},{6,23},{7,22},{8,25},{9,... | collective-permute-start | bytes 589832 | tf_op jit(solution)/shard_map/ppermute | solution.py:97
  13.3 10.6 %collective-permute-start.2 = (bf16[384,256]{1,0:T(8,128)(2,1)S(1)}, bf16[384,256]{1,0:T(8,128)(2,1)S(1)}, u32[]{:S(2)}, u32[]{:S(2)}) collective-permute-start(bf16[384,256]{1,0:T(8,128)(2,1)S(1)} %copy-done), channel_id=1, source_target_pairs={{0,16},{1,17},{2,18},{3,19},{4,20},{5,21},{6,22},{7,23},{8,24},{9,... | collective-permute-start | bytes 589832 | tf_op jit(solution)/shard_map/ppermute | solution.py:97
  13.9 10.2 %collective-permute-start.1 = (bf16[384,256]{1,0:T(8,128)(2,1)S(1)}, bf16[384,256]{1,0:T(8,128)(2,1)S(1)}, u32[]{:S(2)}, u32[]{:S(2)}) collective-permute-start(bf16[384,256]{1,0:T(8,128)(2,1)S(1)} %copy-done), channel_id=1, source_target_pairs={{0,1},{1,0},{2,3},{3,2},{4,5},{5,4},{6,7},{7,6},{8,9},{9,8},{10,11... | collective-permute-start | bytes 589832 | tf_op jit(solution)/shard_map/ppermute | solution.py:97
  24.1 2.4 %collective-permute-start.4 = (bf16[1152,256]{1,0:T(8,128)(2,1)S(1)}, bf16[1152,256]{1,0:T(8,128)(2,1)S(1)}, u32[]{:S(2)}, u32[]{:S(2)}) collective-permute-start(bf16[1152,256]{1,0:T(8,128)(2,1)S(1)} %shard_map.60.refs_2_), channel_id=1, source_target_pairs={{0,8},{1,9},{2,10},{3,11},{4,12},{5,13},{6,14},{7,15},{8,0},{9,1},... | collective-permute-start | bytes 1769480 | tf_op jit(solution)/shard_map/ppermute | solution.py:97
  24.2 2.3 %collective-permute-start = (bf16[384,256]{1,0:T(8,128)(2,1)S(1)}, bf16[384,256]{1,0:T(8,128)(2,1)S(1)}, u32[]{:S(2)}, u32[]{:S(2)}) collective-permute-start(bf16[384,256]{1,0:T(8,128)(2,1)S(1)} %copy-done), channel_id=1, source_target_pairs={{0,8},{1,9},{2,10},{3,11},{4,12},{5,13},{6,14},{7,15},{8,0},{9,1},... | collective-permute-start | bytes 589832 | tf_op jit(solution)/shard_map/ppermute | solution.py:97
  29.6 14.6 %collective-permute-start.5 = (bf16[256,256]{1,0:T(8,128)(2,1)S(1)}, bf16[256,256]{1,0:T(8,128)(2,1)S(1)}, u32[]{:S(2)}, u32[]{:S(2)}) collective-permute-start(bf16[256,256]{1,0:T(8,128)(2,1)S(1)} %get-tuple-element.56), channel_id=1, source_target_pairs={{0,2},{1,3},{2,4},{3,5},{4,6},{5,7},{6,0},{7,1},{8,10},{9,11},{10,... | collective-permute-start | bytes 393224 | tf_op jit(solution)/shard_map/ppermute | solution.py:97
  31.0 13.2 %collective-permute-start.6 = (bf16[256,256]{1,0:T(8,128)(2,1)S(1)}, bf16[256,256]{1,0:T(8,128)(2,1)S(1)}, u32[]{:S(2)}, u32[]{:S(2)}) collective-permute-start(bf16[256,256]{1,0:T(8,128)(2,1)S(1)} %get-tuple-element.57), channel_id=1, source_target_pairs={{0,4},{1,5},{2,6},{3,7},{4,0},{5,1},{6,2},{7,3},{8,12},{9,13},{10,... | collective-permute-start | bytes 393224 | tf_op jit(solution)/shard_map/ppermute | solution.py:97
  33.6 10.6 %collective-permute-start.7 = (bf16[256,256]{1,0:T(8,128)(2,1)S(1)}, bf16[256,256]{1,0:T(8,128)(2,1)S(1)}, u32[]{:S(2)}, u32[]{:S(2)}) collective-permute-start(bf16[256,256]{1,0:T(8,128)(2,1)S(1)} %get-tuple-element.58), channel_id=1, source_target_pairs={{0,6},{1,7},{2,0},{3,1},{4,2},{5,3},{6,4},{7,5},{8,14},{9,15},{10,... | collective-permute-start | bytes 393224 | tf_op jit(solution)/shard_map/ppermute | solution.py:97
  44.3 10.6 %collective-permute-start.11 = (bf16[256,256]{1,0:T(8,128)(2,1)S(1)}, bf16[256,256]{1,0:T(8,128)(2,1)S(1)}, u32[]{:S(2)}, u32[]{:S(2)}) collective-permute-start(bf16[256,256]{1,0:T(8,128)(2,1)S(1)} %get-tuple-element.61.refs_2_), channel_id=1, source_target_pairs={{0,2},{1,3},{2,4},{3,5},{4,6},{5,7},{6,0},{7,1},{8,10},{9,11},{10,... | collective-permute-start | bytes 393224 | tf_op jit(solution)/shard_map/ppermute | solution.py:97
  46.1 10.5 %collective-permute-start.10 = (bf16[256,256]{1,0:T(8,128)(2,1)S(1)}, bf16[256,256]{1,0:T(8,128)(2,1)S(1)}, u32[]{:S(2)}, u32[]{:S(2)}) collective-permute-start(bf16[256,256]{1,0:T(8,128)(2,1)S(1)} %get-tuple-element.61.refs_2_), channel_id=1, source_target_pairs={{0,4},{1,5},{2,6},{3,7},{4,0},{5,1},{6,2},{7,3},{8,12},{9,13},{10,... | collective-permute-start | bytes 393224 | tf_op jit(solution)/shard_map/ppermute | solution.py:97
  47.4 9.1 %collective-permute-start.9 = (bf16[256,256]{1,0:T(8,128)(2,1)S(1)}, bf16[256,256]{1,0:T(8,128)(2,1)S(1)}, u32[]{:S(2)}, u32[]{:S(2)}) collective-permute-start(bf16[256,256]{1,0:T(8,128)(2,1)S(1)} %get-tuple-element.61.refs_2_), channel_id=1, source_target_pairs={{0,6},{1,7},{2,0},{3,1},{4,2},{5,3},{6,4},{7,5},{8,14},{9,15},{10,... | collective-permute-start | bytes 393224 | tf_op jit(solution)/shard_map/ppermute | solution.py:97
  54.9 2.3 %copy-start.7 = (f32[2]{0:T(128)S(1)}, f32[2]{0:T(128)}, u32[]{:S(2)}) copy-start(f32[2]{0:T(128)} %param.7) | copy-start | bytes 28
  56.6 2.0 %collective-permute-start.12 = (bf16[768,256]{1,0:T(8,128)(2,1)S(1)}, bf16[768,256]{1,0:T(8,128)(2,1)S(1)}, u32[]{:S(2)}, u32[]{:S(2)}) collective-permute-start(bf16[768,256]{1,0:T(8,128)(2,1)S(1)} %shard_map.66.refs_4_), channel_id=1, source_target_pairs={{0,8},{1,9},{2,10},{3,11},{4,12},{5,13},{6,14},{7,15},{8,0},{9,1},... | collective-permute-start | bytes 1179656 | tf_op jit(solution)/shard_map/ppermute | solution.py:97
  56.7 1.9 %collective-permute-start.8 = (bf16[256,256]{1,0:T(8,128)(2,1)S(1)}, bf16[256,256]{1,0:T(8,128)(2,1)S(1)}, u32[]{:S(2)}, u32[]{:S(2)}) collective-permute-start(bf16[256,256]{1,0:T(8,128)(2,1)S(1)} %get-tuple-element.61.refs_2_), channel_id=1, source_target_pairs={{0,8},{1,9},{2,10},{3,11},{4,12},{5,13},{6,14},{7,15},{8,0},{9,1},... | collective-permute-start | bytes 393224 | tf_op jit(solution)/shard_map/ppermute | solution.py:97
  59.7 12.4 %collective-permute-start.13 = (bf16[256,256]{1,0:T(8,128)(2,1)S(1)}, bf16[256,256]{1,0:T(8,128)(2,1)S(1)}, u32[]{:S(2)}, u32[]{:S(2)}) collective-permute-start(bf16[256,256]{1,0:T(8,128)(2,1)S(1)} %get-tuple-element.65), channel_id=1, source_target_pairs={{0,1},{1,0},{2,3},{3,2},{4,5},{5,4},{6,7},{7,6},{8,9},{9,8},{10,11... | collective-permute-start | bytes 393224 | tf_op jit(solution)/shard_map/ppermute | solution.py:97
  62.0 10.1 %collective-permute-start.14 = (bf16[256,256]{1,0:T(8,128)(2,1)S(1)}, bf16[256,256]{1,0:T(8,128)(2,1)S(1)}, u32[]{:S(2)}, u32[]{:S(2)}) collective-permute-start(bf16[256,256]{1,0:T(8,128)(2,1)S(1)} %get-tuple-element.68), channel_id=1, source_target_pairs={{0,16},{1,17},{2,18},{3,19},{4,20},{5,21},{6,22},{7,23},{8,24},{9,... | collective-permute-start | bytes 393224 | tf_op jit(solution)/shard_map/ppermute | solution.py:97
  64.0 8.2 %collective-permute-start.15 = (bf16[256,256]{1,0:T(8,128)(2,1)S(1)}, bf16[256,256]{1,0:T(8,128)(2,1)S(1)}, u32[]{:S(2)}, u32[]{:S(2)}) collective-permute-start(bf16[256,256]{1,0:T(8,128)(2,1)S(1)} %get-tuple-element.69), channel_id=1, source_target_pairs={{0,17},{1,16},{2,19},{3,18},{4,21},{5,20},{6,23},{7,22},{8,25},{9,... | collective-permute-start | bytes 393224 | tf_op jit(solution)/shard_map/ppermute | solution.py:97
  73.5 12.5 %collective-permute-start.19 = (bf16[256,256]{1,0:T(8,128)(2,1)S(1)}, bf16[256,256]{1,0:T(8,128)(2,1)S(1)}, u32[]{:S(2)}, u32[]{:S(2)}) collective-permute-start(bf16[256,256]{1,0:T(8,128)(2,1)S(1)} %get-tuple-element.76.refs_1_.potential_ref), channel_id=1, source_target_pairs={{0,2},{1,3},{2,4},{3,5},{4,6},{5,7},{6,0},{7,1},{8,10},{9,11},{10,... | collective-permute-start | bytes 393224 | tf_op jit(solution)/shard_map/ppermute | solution.py:97
  76.8 9.4 %collective-permute-start.18 = (bf16[256,256]{1,0:T(8,128)(2,1)S(1)}, bf16[256,256]{1,0:T(8,128)(2,1)S(1)}, u32[]{:S(2)}, u32[]{:S(2)}) collective-permute-start(bf16[256,256]{1,0:T(8,128)(2,1)S(1)} %get-tuple-element.76.refs_1_.potential_ref), channel_id=1, source_target_pairs={{0,4},{1,5},{2,6},{3,7},{4,0},{5,1},{6,2},{7,3},{8,12},{9,13},{10,... | collective-permute-start | bytes 393224 | tf_op jit(solution)/shard_map/ppermute | solution.py:97
  78.1 8.2 %collective-permute-start.17 = (bf16[256,256]{1,0:T(8,128)(2,1)S(1)}, bf16[256,256]{1,0:T(8,128)(2,1)S(1)}, u32[]{:S(2)}, u32[]{:S(2)}) collective-permute-start(bf16[256,256]{1,0:T(8,128)(2,1)S(1)} %get-tuple-element.76.refs_1_.potential_ref), channel_id=1, source_target_pairs={{0,6},{1,7},{2,0},{3,1},{4,2},{5,3},{6,4},{7,5},{8,14},{9,15},{10,... | collective-permute-start | bytes 393224 | tf_op jit(solution)/shard_map/ppermute | solution.py:97
  86.0 2.2 %copy-start.6 = (bf16[512,2048]{1,0:T(8,128)(2,1)S(1)}, bf16[512,2048]{1,0:T(8,128)(2,1)}, u32[]{:S(2)}) copy-start(bf16[512,2048]{1,0:T(8,128)(2,1)} %get-tuple-element.82.refs_0_) | copy-start | bytes 6291460
  86.3 2.0 %collective-permute-start.20 = (bf16[768,256]{1,0:T(8,128)(2,1)S(1)}, bf16[768,256]{1,0:T(8,128)(2,1)S(1)}, u32[]{:S(2)}, u32[]{:S(2)}) collective-permute-start(bf16[768,256]{1,0:T(8,128)(2,1)S(1)} %shard_map.75.refs_3_), channel_id=1, source_target_pairs={{0,8},{1,9},{2,10},{3,11},{4,12},{5,13},{6,14},{7,15},{8,0},{9,1},... | collective-permute-start | bytes 1179656 | tf_op jit(solution)/shard_map/ppermute | solution.py:97
  86.4 1.9 %collective-permute-start.16 = (bf16[256,256]{1,0:T(8,128)(2,1)S(1)}, bf16[256,256]{1,0:T(8,128)(2,1)S(1)}, u32[]{:S(2)}, u32[]{:S(2)}) collective-permute-start(bf16[256,256]{1,0:T(8,128)(2,1)S(1)} %get-tuple-element.76.refs_1_.potential_ref), channel_id=1, source_target_pairs={{0,8},{1,9},{2,10},{3,11},{4,12},{5,13},{6,14},{7,15},{8,0},{9,1},... | collective-permute-start | bytes 393224 | tf_op jit(solution)/shard_map/ppermute | solution.py:97
  88.3 3.6 %copy-start.5 = (bf16[512,2048]{1,0:T(8,128)(2,1)S(1)}, bf16[512,2048]{1,0:T(8,128)(2,1)}, u32[]{:S(2)}) copy-start(bf16[512,2048]{1,0:T(8,128)(2,1)} %get-tuple-element.77.refs_0_) | copy-start | bytes 6291460
  89.2 6.4 %collective-permute-start.22 = (bf16[256,256]{1,0:T(8,128)(2,1)S(1)}, bf16[256,256]{1,0:T(8,128)(2,1)S(1)}, u32[]{:S(2)}, u32[]{:S(2)}) collective-permute-start(bf16[256,256]{1,0:T(8,128)(2,1)S(1)} %get-tuple-element.83), channel_id=1, source_target_pairs={{0,16},{1,17},{2,18},{3,19},{4,20},{5,21},{6,22},{7,23},{8,24},{9,... | collective-permute-start | bytes 393224 | tf_op jit(solution)/shard_map/ppermute | solution.py:97
  90.6 7.7 %collective-permute-start.23 = (bf16[256,256]{1,0:T(8,128)(2,1)S(1)}, bf16[256,256]{1,0:T(8,128)(2,1)S(1)}, u32[]{:S(2)}, u32[]{:S(2)}) collective-permute-start(bf16[256,256]{1,0:T(8,128)(2,1)S(1)} %get-tuple-element.84), channel_id=1, source_target_pairs={{0,17},{1,16},{2,19},{3,18},{4,21},{5,20},{6,23},{7,22},{8,25},{9,... | collective-permute-start | bytes 393224 | tf_op jit(solution)/shard_map/ppermute | solution.py:97
  93.4 7.3 %collective-permute-start.21 = (bf16[256,256]{1,0:T(8,128)(2,1)S(1)}, bf16[256,256]{1,0:T(8,128)(2,1)S(1)}, u32[]{:S(2)}, u32[]{:S(2)}) collective-permute-start(bf16[256,256]{1,0:T(8,128)(2,1)S(1)} %get-tuple-element.81), channel_id=1, source_target_pairs={{0,1},{1,0},{2,3},{3,2},{4,5},{5,4},{6,7},{7,6},{8,9},{9,8},{10,11... | collective-permute-start | bytes 393224 | tf_op jit(solution)/shard_map/ppermute | solution.py:97
  102.1 8.7 %collective-permute-start.27 = (bf16[256,256]{1,0:T(8,128)(2,1)S(1)}, bf16[256,256]{1,0:T(8,128)(2,1)S(1)}, u32[]{:S(2)}, u32[]{:S(2)}) collective-permute-start(bf16[256,256]{1,0:T(8,128)(2,1)S(1)} %get-tuple-element.86.refs_2_), channel_id=1, source_target_pairs={{0,2},{1,3},{2,4},{3,5},{4,6},{5,7},{6,0},{7,1},{8,10},{9,11},{10,... | collective-permute-start | bytes 393224 | tf_op jit(solution)/shard_map/ppermute | solution.py:97
  105.3 10.1 %collective-permute-start.26 = (bf16[256,256]{1,0:T(8,128)(2,1)S(1)}, bf16[256,256]{1,0:T(8,128)(2,1)S(1)}, u32[]{:S(2)}, u32[]{:S(2)}) collective-permute-start(bf16[256,256]{1,0:T(8,128)(2,1)S(1)} %get-tuple-element.86.refs_2_), channel_id=1, source_target_pairs={{0,4},{1,5},{2,6},{3,7},{4,0},{5,1},{6,2},{7,3},{8,12},{9,13},{10,... | collective-permute-start | bytes 393224 | tf_op jit(solution)/shard_map/ppermute | solution.py:97
  106.9 8.4 %collective-permute-start.25 = (bf16[256,256]{1,0:T(8,128)(2,1)S(1)}, bf16[256,256]{1,0:T(8,128)(2,1)S(1)}, u32[]{:S(2)}, u32[]{:S(2)}) collective-permute-start(bf16[256,256]{1,0:T(8,128)(2,1)S(1)} %get-tuple-element.86.refs_2_), channel_id=1, source_target_pairs={{0,6},{1,7},{2,0},{3,1},{4,2},{5,3},{6,4},{7,5},{8,14},{9,15},{10,... | collective-permute-start | bytes 393224 | tf_op jit(solution)/shard_map/ppermute | solution.py:97
  115.4 2.0 %collective-permute-start.28 = (bf16[768,256]{1,0:T(8,128)(2,1)S(1)}, bf16[768,256]{1,0:T(8,128)(2,1)S(1)}, u32[]{:S(2)}, u32[]{:S(2)}) collective-permute-start(bf16[768,256]{1,0:T(8,128)(2,1)S(1)} %shard_map.79.refs_4_), channel_id=1, source_target_pairs={{0,8},{1,9},{2,10},{3,11},{4,12},{5,13},{6,14},{7,15},{8,0},{9,1},... | collective-permute-start | bytes 1179656 | tf_op jit(solution)/shard_map/ppermute | solution.py:97
  115.5 1.9 %collective-permute-start.24 = (bf16[256,256]{1,0:T(8,128)(2,1)S(1)}, bf16[256,256]{1,0:T(8,128)(2,1)S(1)}, u32[]{:S(2)}, u32[]{:S(2)}) collective-permute-start(bf16[256,256]{1,0:T(8,128)(2,1)S(1)} %get-tuple-element.86.refs_2_), channel_id=1, source_target_pairs={{0,8},{1,9},{2,10},{3,11},{4,12},{5,13},{6,14},{7,15},{8,0},{9,1},... | collective-permute-start | bytes 393224 | tf_op jit(solution)/shard_map/ppermute | solution.py:97
  118.5 8.0 %collective-permute-start.29 = (bf16[256,256]{1,0:T(8,128)(2,1)S(1)}, bf16[256,256]{1,0:T(8,128)(2,1)S(1)}, u32[]{:S(2)}, u32[]{:S(2)}) collective-permute-start(bf16[256,256]{1,0:T(8,128)(2,1)S(1)} %get-tuple-element.89), channel_id=1, source_target_pairs={{0,1},{1,0},{2,3},{3,2},{4,5},{5,4},{6,7},{7,6},{8,9},{9,8},{10,11... | collective-permute-start | bytes 393224 | tf_op jit(solution)/shard_map/ppermute | solution.py:97
  120.1 7.1 %collective-permute-start.31 = (bf16[256,256]{1,0:T(8,128)(2,1)S(1)}, bf16[256,256]{1,0:T(8,128)(2,1)S(1)}, u32[]{:S(2)}, u32[]{:S(2)}) collective-permute-start(bf16[256,256]{1,0:T(8,128)(2,1)S(1)} %get-tuple-element.91), channel_id=1, source_target_pairs={{0,17},{1,16},{2,19},{3,18},{4,21},{5,20},{6,23},{7,22},{8,25},{9,... | collective-permute-start | bytes 393224 | tf_op jit(solution)/shard_map/ppermute | solution.py:97
  123.2 5.7 %collective-permute-start.30 = (bf16[256,256]{1,0:T(8,128)(2,1)S(1)}, bf16[256,256]{1,0:T(8,128)(2,1)S(1)}, u32[]{:S(2)}, u32[]{:S(2)}) collective-permute-start(bf16[256,256]{1,0:T(8,128)(2,1)S(1)} %get-tuple-element.90), channel_id=1, source_target_pairs={{0,16},{1,17},{2,18},{3,19},{4,20},{5,21},{6,22},{7,23},{8,24},{9,... | collective-permute-start | bytes 393224 | tf_op jit(solution)/shard_map/ppermute | solution.py:97
  128.9 16.2 %copy-start.4 = (bf16[768,2048]{1,0:T(8,128)(2,1)S(1)}, bf16[768,2048]{1,0:T(8,128)(2,1)}, u32[]{:S(2)}) copy-start(bf16[768,2048]{1,0:T(8,128)(2,1)} %get-tuple-element.98.refs_0_) | copy-start | bytes 9437188
  130.4 8.4 %collective-permute-start.35 = (bf16[256,256]{1,0:T(8,128)(2,1)S(1)}, bf16[256,256]{1,0:T(8,128)(2,1)S(1)}, u32[]{:S(2)}, u32[]{:S(2)}) collective-permute-start(bf16[256,256]{1,0:T(8,128)(2,1)S(1)} %get-tuple-element.94.refs_1_), channel_id=1, source_target_pairs={{0,2},{1,3},{2,4},{3,5},{4,6},{5,7},{6,0},{7,1},{8,10},{9,11},{10,... | collective-permute-start | bytes 393224 | tf_op jit(solution)/shard_map/ppermute | solution.py:97
  133.7 9.4 %collective-permute-start.34 = (bf16[256,256]{1,0:T(8,128)(2,1)S(1)}, bf16[256,256]{1,0:T(8,128)(2,1)S(1)}, u32[]{:S(2)}, u32[]{:S(2)}) collective-permute-start(bf16[256,256]{1,0:T(8,128)(2,1)S(1)} %get-tuple-element.94.refs_1_), channel_id=1, source_target_pairs={{0,4},{1,5},{2,6},{3,7},{4,0},{5,1},{6,2},{7,3},{8,12},{9,13},{10,... | collective-permute-start | bytes 393224 | tf_op jit(solution)/shard_map/ppermute | solution.py:97
  135.0 8.1 %collective-permute-start.33 = (bf16[256,256]{1,0:T(8,128)(2,1)S(1)}, bf16[256,256]{1,0:T(8,128)(2,1)S(1)}, u32[]{:S(2)}, u32[]{:S(2)}) collective-permute-start(bf16[256,256]{1,0:T(8,128)(2,1)S(1)} %get-tuple-element.94.refs_1_), channel_id=1, source_target_pairs={{0,6},{1,7},{2,0},{3,1},{4,2},{5,3},{6,4},{7,5},{8,14},{9,15},{10,... | collective-permute-start | bytes 393224 | tf_op jit(solution)/shard_map/ppermute | solution.py:97
  143.1 2.0 %collective-permute-start.36 = (bf16[768,256]{1,0:T(8,128)(2,1)S(1)}, bf16[768,256]{1,0:T(8,128)(2,1)S(1)}, u32[]{:S(2)}, u32[]{:S(2)}) collective-permute-start(bf16[768,256]{1,0:T(8,128)(2,1)S(1)} %shard_map.85.refs_3_), channel_id=1, source_target_pairs={{0,8},{1,9},{2,10},{3,11},{4,12},{5,13},{6,14},{7,15},{8,0},{9,1},... | collective-permute-start | bytes 1179656 | tf_op jit(solution)/shard_map/ppermute | solution.py:97
  143.2 1.9 %collective-permute-start.32 = (bf16[256,256]{1,0:T(8,128)(2,1)S(1)}, bf16[256,256]{1,0:T(8,128)(2,1)S(1)}, u32[]{:S(2)}, u32[]{:S(2)}) collective-permute-start(bf16[256,256]{1,0:T(8,128)(2,1)S(1)} %get-tuple-element.94.refs_1_), channel_id=1, source_target_pairs={{0,8},{1,9},{2,10},{3,11},{4,12},{5,13},{6,14},{7,15},{8,0},{9,1},... | collective-permute-start | bytes 393224 | tf_op jit(solution)/shard_map/ppermute | solution.py:97
  145.1 4.2 %copy-start.3 = (bf16[768,2048]{1,0:T(8,128)(2,1)S(1)}, bf16[768,2048]{1,0:T(8,128)(2,1)}, u32[]{:S(2)}) copy-start(bf16[768,2048]{1,0:T(8,128)(2,1)} %get-tuple-element.73.refs_0_) | copy-start | bytes 9437188
  146.9 7.8 %collective-permute-start.38 = (bf16[384,256]{1,0:T(8,128)(2,1)S(1)}, bf16[384,256]{1,0:T(8,128)(2,1)S(1)}, u32[]{:S(2)}, u32[]{:S(2)}) collective-permute-start(bf16[384,256]{1,0:T(8,128)(2,1)S(1)} %get-tuple-element.99), channel_id=1, source_target_pairs={{0,16},{1,17},{2,18},{3,19},{4,20},{5,21},{6,22},{7,23},{8,24},{9,... | collective-permute-start | bytes 589832 | tf_op jit(solution)/shard_map/ppermute | solution.py:97
  148.3 10.3 %collective-permute-start.39 = (bf16[384,256]{1,0:T(8,128)(2,1)S(1)}, bf16[384,256]{1,0:T(8,128)(2,1)S(1)}, u32[]{:S(2)}, u32[]{:S(2)}) collective-permute-start(bf16[384,256]{1,0:T(8,128)(2,1)S(1)} %get-tuple-element.100), channel_id=1, source_target_pairs={{0,17},{1,16},{2,19},{3,18},{4,21},{5,20},{6,23},{7,22},{8,25},{9,... | collective-permute-start | bytes 589832 | tf_op jit(solution)/shard_map/ppermute | solution.py:97
  151.1 10.6 %collective-permute-start.37 = (bf16[384,256]{1,0:T(8,128)(2,1)S(1)}, bf16[384,256]{1,0:T(8,128)(2,1)S(1)}, u32[]{:S(2)}, u32[]{:S(2)}) collective-permute-start(bf16[384,256]{1,0:T(8,128)(2,1)S(1)} %get-tuple-element.97), channel_id=1, source_target_pairs={{0,1},{1,0},{2,3},{3,2},{4,5},{5,4},{6,7},{7,6},{8,9},{9,8},{10,11... | collective-permute-start | bytes 589832 | tf_op jit(solution)/shard_map/ppermute | solution.py:97
  (1 other events, 0.7 us)

commit v11 on v10

--- a/solution.py
+++ b/solution.py
@@ -386,35 +386,16 @@
     ]
 
 
-def first_kernel(layout, form, me_ref, letter_ref, after_ref, *refs):
-    count = layout.z
-    pieces, outs, token_ref = refs[: -count - 1], refs[-count - 1 : -1], refs[-1]
+def first_kernel(layout, form, me_ref, letter_ref, after_ref, out_ref, token_ref):
     token_ref[...] = jnp.zeros_like(token_ref)
-    me, size, edges = me_ref[0], form.tri_dev, form.edges
-    base = layout.near(me, dz=pl.program_id(0)) * size
-    total, k = None, 0
-    for piece in pieces:
-        for row in range(0, piece.shape[0], edges):
-            plus, minus = form.ends(letter_ref[layout.in_planes(me, k)])
-            signed = pick(plus, base, size) - pick(minus, base, size)
-            term = matmul(signed, piece[row : row + edges, :])
-            total = term if total is None else total + term
-            k += 1
-    set_blocks(total, outs)
-
-
-def first_charges(layout, form, me, letters, labels, pieces, resident):
-    count, width = layout.z, pieces[0].shape[1]
-    shapes = blocks_like(count, form.tri_dev, width, True) + [TOKEN]
-    return pl.pallas_call(
-        functools.partial(first_kernel, layout, form),
-        grid=(count,),
-        in_specs=[pl.BlockSpec(memory_space=pltpu.SMEM)] + [whole()] * (2 + len(pieces)),
-        out_specs=[whole()] * len(shapes),
-        out_shape=shapes,
-        compiler_params=params(resident),
-        cost_estimate=cost(4),
-    )(me, letters, labels, *pieces)
+    me, step = me_ref[0], pl.program_id(0)
+    size, edges = form.tri_dev, form.edges
+    out_ref = rows_at(out_ref, step, size)
+    base = layout.near(me, dz=step) * size
+    for k in range(out_ref.shape[1] // edges):
+        plus, minus = form.ends(letter_ref[layout.in_planes(me, k)])
+        signed = pick(plus, base, size) - pick(minus, base, size)
+        out_ref[:, k * edges : (k + 1) * edges] = signed
 
 
 def apply_kernel(mats, fed, block, row, *refs):
@@ -619,8 +600,18 @@
         )
         return part, token
 
-    pieces = layout.gathered(currents, across, (letters,))
-    *blocks, token = first_charges(layout, form, me, letters, labels, pieces, resident)
+    first, token = make(
+        functools.partial(first_kernel, layout, form),
+        1,
+        tri_dev,
+        range(layout.z),
+        (letters, labels),
+        3,
+        cols=count * layout.core * edge_dev,
+        resident=resident,
+    )
+    pieces = layout.gathered(currents, across, (token,))
+    blocks, token = multiply([[first]], pieces, tri_dev, resident)
     tiles = []
     for span in spans:
         part, token = tile_part(span, token)
@@ -664,14 +655,14 @@
         if build_now:
             ends, token = incidence_parts(token)
         pieces = layout.gathered(potential, layout.along(potential), (token,))
-        blocks, token = multiply(near, pieces, tri_dev)
+        blocks, token = multiply(near, pieces, tri_dev, resident)
         charge, rounded, token = charge_of(
             weight, charge, degree, potential, layout.given(blocks), (token,)
         )
     if ends is None:
         ends, token = incidence_parts(token)
     pieces = layout.gathered(weighted, layout.along(weighted), (token,))
-    blocks, _ = multiply(ends, pieces, edge_dev)
+    blocks, _ = multiply(ends, pieces, edge_dev, resident)
     return current_of(currents, layout.given(blocks)), potential
 
 

time: 163 us -> 160 us (0.982)
  waiting for transfers between devices: 52.9 us -> 46.4 us
  Pallas kernels: 52.4 us -> 56.6 us
    ppermute x40, waiting for transfers between devices: 52.9 us -> 42.1 us  [shift(): return lax.ppermute(value, AXES, pairs)]
    pallas_call x12 -> x20, Pallas kernels: 14.3 us -> 19.8 us  [apply(): pl.pallas_call(functools.partial(apply_kernel, mats, len(pieces), block,...]
    all_to_all x1, waiting for transfers between devices: 0.01 us -> 4.27 us  [per_device(): lax.all_to_all(letters, AXES, split_axis=0, concat_axis=0, tiled=True)]
    pallas_call x1 -> x0, Pallas kernels: 3.08 us -> none  [first_charges(): pl.pallas_call(functools.partial(first_kernel, layout, form), grid=(count...]
    pallas_call x6 -> x7, Pallas kernels: 28.4 us -> 30.3 us  [build(): pl.pallas_call(kernel, grid=(len(span),), in_specs=[pl.BlockSpec(memory_s...]
  transfers between devices with their start and end apart: 41 -> 41, of which waited for: 24 -> 24; matrix products, arithmetic and copies ran while one was open for 0% -> 1% of each run, Pallas kernels for 23% -> 28%
where the time goes in v11:
time: 160 us; the launch traced here: 159 us
  Pallas kernels  56.6 us (35%)
  starting transfers between devices  53.2 us (33%)
  waiting for transfers between devices  46.4 us (29%)
  local copies, waits for them, and re-layouts  2.27 us (1%)
    ppermute x40, starting transfers between devices, shift(): return lax.ppermute(value, AXES, pairs)  45.9 us
    ppermute x40, waiting for transfers between devices, shift(): return lax.ppermute(value, AXES, pairs)  42.1 us
    pallas_call x7, Pallas kernels, build(): pl.pallas_call(kernel, grid=(len(span),), in_specs=[pl.BlockSpec(memory_s...  30.3 us
    pallas_call x20, Pallas kernels, apply(): pl.pallas_call(functools.partial(apply_kernel, mats, len(pieces), block,...  19.8 us
    all_to_all x1, starting transfers between devices, per_device(): lax.all_to_all(letters, AXES, split_axis=0, concat_axis=0, tiled=True)  7.3 us
    all_to_all x1, waiting for transfers between devices, per_device(): lax.all_to_all(letters, AXES, split_axis=0, concat_axis=0, tiled=True)  4.27 us
  transfers between devices with their start and end apart: 41, of which 24 were waited for; matrix products, arithmetic and copies ran while one was open for 1% of the time, Pallas kernels for 28%

profile of v11, /device:TPU:0, one launch (start us, length us, event | category | flops | bytes accessed | tf_op | source)
XLA Modules:
  0.0 159.3 jit_solution(11449787919206735132)
XLA Ops:
  2.1 1.2 shard_map.59
  3.3 7.3 %all-to-all-start = ((s32[32,8,128]{2,1,0:T(8,128)}), s32[32,8,128]{2,1,0:T(8,128)S(1)}, u32[]{:S(2)}, u32[]{:S(2)}) async-start(s32[32,8,128]{2,1,0:T(8,128)} %shard_map.59), calls=%async_computation | async-start | bytes 262144 | tf_op jit(solution)/shard_map/all_to_all | solution.py:568
  10.6 2.7 %collective-permute-start.3 = (bf16[384,256]{1,0:T(8,128)(2,1)S(1)}, bf16[384,256]{1,0:T(8,128)(2,1)S(1)}, u32[]{:S(2)}, u32[]{:S(2)}) collective-permute-start(bf16[384,256]{1,0:T(8,128)(2,1)S(1)} %copy-done.4), channel_id=1, source_target_pairs={{0,17},{1,16},{2,19},{3,18},{4,21},{5,20},{6,23},{7,22},{8,25},{9,... | collective-permute-start | bytes 589832 | tf_op jit(solution)/shard_map/ppermute | solution.py:97
  14.1 4.3 %all-to-all-done.letter_ref = s32[32,8,128]{2,1,0:T(8,128)S(1)} async-done(((s32[32,8,128]{2,1,0:T(8,128)}), s32[32,8,128]{2,1,0:T(8,128)S(1)}, u32[]{:S(2)}, u32[]{:S(2)}) %all-to-all-start) | async-done | bytes 131104 | tf_op jit(solution)/shard_map/all_to_all | solution.py:568
  18.7 1.8 %shard_map.60 = (bf16[1024,3072]{1,0:T(8,128)(2,1)S(1)}, f32[8,128]{1,0:T(8,128)S(1)}) custom-call(s32[1]{0:T(128)} %bitcast.me_ref, s32[32,8,128]{2,1,0:T(8,128)S(1)} %all-to-all-done.letter_ref, s32[4,1,2048]{2,1,0:T(1,128)S(1)} %reshape.11.after_ref.label_ref), custom_call_target="tpu_custom_call" | custom-call | flops 3449999872 | tf_op jit(solution)/shard_map/pallas_call | solution.py:319
  20.5 3.5 %collective-permute-done.2.refs_1_ = bf16[384,256]{1,0:T(8,128)(2,1)S(1)} collective-permute-done((bf16[384,256]{1,0:T(8,128)(2,1)S(1)}, bf16[384,256]{1,0:T(8,128)(2,1)S(1)}, u32[]{:S(2)}, u32[]{:S(2)}) %collective-permute-start.2) | collective-permute-done | bytes 196640 | tf_op jit(solution)/shard_map/ppermute | solution.py:97
  24.7 1.8 %collective-permute-done.refs_2_ = bf16[384,256]{1,0:T(8,128)(2,1)S(1)} collective-permute-done((bf16[384,256]{1,0:T(8,128)(2,1)S(1)}, bf16[384,256]{1,0:T(8,128)(2,1)S(1)}, u32[]{:S(2)}, u32[]{:S(2)}) %collective-permute-start) | collective-permute-done | bytes 196640 | tf_op jit(solution)/shard_map/ppermute | solution.py:97
  26.5 1.2 shard_map.65
  27.7 1.4 collective-permute-start.5
  29.1 1.2 shard_map.66
  30.3 2.5 %collective-permute-start.6 = (bf16[256,256]{1,0:T(8,128)(2,1)S(1)}, bf16[256,256]{1,0:T(8,128)(2,1)S(1)}, u32[]{:S(2)}, u32[]{:S(2)}) collective-permute-start(bf16[256,256]{1,0:T(8,128)(2,1)S(1)} %get-tuple-element.61), channel_id=1, source_target_pairs={{0,4},{1,5},{2,6},{3,7},{4,0},{5,1},{6,2},{7,3},{8,12},{9,13},{10,... | collective-permute-start | bytes 393224 | tf_op jit(solution)/shard_map/ppermute | solution.py:97
  33.4 1.3 collective-permute-start.7
  34.7 4.7 %shard_map.63 = (bf16[512,2048]{1,0:T(8,128)(2,1)S(1)}, bf16[512,2048]{1,0:T(8,128)(2,1)S(1)}, f32[8,128]{1,0:T(8,128)S(1)}) custom-call(s32[1]{0:T(128)} %bitcast.me_ref, s32[32,8,128]{2,1,0:T(8,128)S(1)} %all-to-all-done.letter_ref, f32[8,128]{1,0:T(8,128)S(1)} %get-tuple-element.56.after_ref), custom_call_target="tpu_custom_call" | custom-call | flops 6899999744 | tf_op jit(solution)/shard_map/pallas_call | solution.py:319
  39.4 4.7 %shard_map.67 = (bf16[512,2048]{1,0:T(8,128)(2,1)S(1)}, bf16[512,2048]{1,0:T(8,128)(2,1)S(1)}, f32[8,128]{1,0:T(8,128)S(1)}) custom-call(s32[1]{0:T(128)} %bitcast.me_ref, s32[32,8,128]{2,1,0:T(8,128)S(1)} %all-to-all-done.letter_ref, f32[8,128]{1,0:T(8,128)S(1)} %get-tuple-element.63.after_ref), custom_call_target="tpu_custom_call" | custom-call | flops 6899999744 | tf_op jit(solution)/shard_map/pallas_call | solution.py:319
  44.1 1.2 shard_map.64
  46.7 2.6 %collective-permute-start.9 = (bf16[256,256]{1,0:T(8,128)(2,1)S(1)}, bf16[256,256]{1,0:T(8,128)(2,1)S(1)}, u32[]{:S(2)}, u32[]{:S(2)}) collective-permute-start(bf16[256,256]{1,0:T(8,128)(2,1)S(1)} %get-tuple-element.65.refs_2_), channel_id=1, source_target_pairs={{0,6},{1,7},{2,0},{3,1},{4,2},{5,3},{6,4},{7,5},{8,14},{9,15},{10,... | collective-permute-start | bytes 393224 | tf_op jit(solution)/shard_map/ppermute | solution.py:97
  49.3 6.3 %shard_map.69 = (bf16[512,2048]{1,0:T(8,128)(2,1)}, f32[256,128]{1,0:T(8,128)S(1)}, f32[8,128]{1,0:T(8,128)S(1)}) custom-call(s32[1]{0:T(128)} %bitcast.me_ref, s32[4,1,2048]{2,1,0:T(1,128)S(1)} %reshape.11.after_ref.label_ref, f32[8,128]{1,0:T(8,128)S(1)} %get-tuple-element.66.after_ref), custom_call_target="tpu_custom_call" | custom-call | flops 6899999744 | tf_op jit(solution)/shard_map/pallas_call | solution.py:319
  55.6 2.1 %collective-permute-done.10.refs_1_ = bf16[256,256]{1,0:T(8,128)(2,1)S(1)} collective-permute-done((bf16[256,256]{1,0:T(8,128)(2,1)S(1)}, bf16[256,256]{1,0:T(8,128)(2,1)S(1)}, u32[]{:S(2)}, u32[]{:S(2)}) %collective-permute-start.10) | collective-permute-done | bytes 131104 | tf_op jit(solution)/shard_map/ppermute | solution.py:97
  63.1 1.2 collective-permute-start.14
  65.1 1.2 collective-permute-start.15
  66.3 5.9 %shard_map.75 = (bf16[512,2048]{1,0:T(8,128)(2,1)}, f32[8,128]{1,0:T(8,128)S(1)}) custom-call(s32[1]{0:T(128)} %bitcast.me_ref, s32[4,1,2048]{2,1,0:T(1,128)S(1)} %reshape.11.after_ref.label_ref, f32[8,128]{1,0:T(8,128)S(1)} %get-tuple-element.74.after_ref), custom_call_target="tpu_custom_call" | custom-call | flops 6899999744 | tf_op jit(solution)/shard_map/pallas_call | solution.py:319
  73.3 1.3 shard_map.76
  74.6 2.8 %collective-permute-start.19 = (bf16[256,256]{1,0:T(8,128)(2,1)S(1)}, bf16[256,256]{1,0:T(8,128)(2,1)S(1)}, u32[]{:S(2)}, u32[]{:S(2)}) collective-permute-start(bf16[256,256]{1,0:T(8,128)(2,1)S(1)} %get-tuple-element.80.refs_1_.potential_ref), channel_id=1, source_target_pairs={{0,2},{1,3},{2,4},{3,5},{4,6},{5,7},{6,0},{7,1},{8,10},{9,11},{10,... | collective-permute-start | bytes 393224 | tf_op jit(solution)/shard_map/ppermute | solution.py:97
  77.8 1.9 %collective-permute-start.17 = (bf16[256,256]{1,0:T(8,128)(2,1)S(1)}, bf16[256,256]{1,0:T(8,128)(2,1)S(1)}, u32[]{:S(2)}, u32[]{:S(2)}) collective-permute-start(bf16[256,256]{1,0:T(8,128)(2,1)S(1)} %get-tuple-element.80.refs_1_.potential_ref), channel_id=1, source_target_pairs={{0,6},{1,7},{2,0},{3,1},{4,2},{5,3},{6,4},{7,5},{8,14},{9,15},{10,... | collective-permute-start | bytes 393224 | tf_op jit(solution)/shard_map/ppermute | solution.py:97
  79.8 3.4 %shard_map.77 = (bf16[768,2048]{1,0:T(8,128)(2,1)}, f32[8,128]{1,0:T(8,128)S(1)}) custom-call(s32[1]{0:T(128)} %bitcast.me_ref, s32[32,8,128]{2,1,0:T(8,128)S(1)} %all-to-all-done.letter_ref, f32[8,128]{1,0:T(8,128)S(1)} %get-tuple-element.76.after_ref), custom_call_target="tpu_custom_call" | custom-call | flops 3449999872 | tf_op jit(solution)/shard_map/pallas_call | solution.py:319
  83.2 3.5 %shard_map.78 = (bf16[768,2048]{1,0:T(8,128)(2,1)}, f32[8,128]{1,0:T(8,128)S(1)}) custom-call(s32[1]{0:T(128)} %bitcast.me_ref, s32[32,8,128]{2,1,0:T(8,128)S(1)} %all-to-all-done.letter_ref, f32[8,128]{1,0:T(8,128)S(1)} %get-tuple-element.82.after_ref), custom_call_target="tpu_custom_call" | custom-call | flops 3449999872 | tf_op jit(solution)/shard_map/pallas_call | solution.py:319
  87.4 1.4 collective-permute-done.16.refs_2_
  91.2 1.6 %collective-permute-start.23 = (bf16[256,256]{1,0:T(8,128)(2,1)S(1)}, bf16[256,256]{1,0:T(8,128)(2,1)S(1)}, u32[]{:S(2)}, u32[]{:S(2)}) collective-permute-start(bf16[256,256]{1,0:T(8,128)(2,1)S(1)} %get-tuple-element.88), channel_id=1, source_target_pairs={{0,17},{1,16},{2,19},{3,18},{4,21},{5,20},{6,23},{7,22},{8,25},{9,... | collective-permute-start | bytes 393224 | tf_op jit(solution)/shard_map/ppermute | solution.py:97
  95.4 2.0 %collective-permute-done.21.refs_0_ = bf16[256,256]{1,0:T(8,128)(2,1)S(1)} collective-permute-done((bf16[256,256]{1,0:T(8,128)(2,1)S(1)}, bf16[256,256]{1,0:T(8,128)(2,1)S(1)}, u32[]{:S(2)}, u32[]{:S(2)}) %collective-permute-start.21) | collective-permute-done | bytes 131104 | tf_op jit(solution)/shard_map/ppermute | solution.py:97
  97.4 1.2 collective-permute-done.23.refs_2_
  99.8 1.4 shard_map.84
  101.2 3.3 %collective-permute-start.27 = (bf16[256,256]{1,0:T(8,128)(2,1)S(1)}, bf16[256,256]{1,0:T(8,128)(2,1)S(1)}, u32[]{:S(2)}, u32[]{:S(2)}) collective-permute-start(bf16[256,256]{1,0:T(8,128)(2,1)S(1)} %get-tuple-element.90.refs_2_), channel_id=1, source_target_pairs={{0,2},{1,3},{2,4},{3,5},{4,6},{5,7},{6,0},{7,1},{8,10},{9,11},{10,... | collective-permute-start | bytes 393224 | tf_op jit(solution)/shard_map/ppermute | solution.py:97
  104.4 1.6 %collective-permute-start.26 = (bf16[256,256]{1,0:T(8,128)(2,1)S(1)}, bf16[256,256]{1,0:T(8,128)(2,1)S(1)}, u32[]{:S(2)}, u32[]{:S(2)}) collective-permute-start(bf16[256,256]{1,0:T(8,128)(2,1)S(1)} %get-tuple-element.90.refs_2_), channel_id=1, source_target_pairs={{0,4},{1,5},{2,6},{3,7},{4,0},{5,1},{6,2},{7,3},{8,12},{9,13},{10,... | collective-permute-start | bytes 393224 | tf_op jit(solution)/shard_map/ppermute | solution.py:97
  106.8 3.2 %collective-permute-done.27.refs_2_ = bf16[256,256]{1,0:T(8,128)(2,1)S(1)} collective-permute-done((bf16[256,256]{1,0:T(8,128)(2,1)S(1)}, bf16[256,256]{1,0:T(8,128)(2,1)S(1)}, u32[]{:S(2)}, u32[]{:S(2)}) %collective-permute-start.27) | collective-permute-done | bytes 131104 | tf_op jit(solution)/shard_map/ppermute | solution.py:97
  110.0 3.9 %collective-permute-done.26.refs_1_ = bf16[256,256]{1,0:T(8,128)(2,1)S(1)} collective-permute-done((bf16[256,256]{1,0:T(8,128)(2,1)S(1)}, bf16[256,256]{1,0:T(8,128)(2,1)S(1)}, u32[]{:S(2)}, u32[]{:S(2)}) %collective-permute-start.26) | collective-permute-done | bytes 131104 | tf_op jit(solution)/shard_map/ppermute | solution.py:97
  114.7 1.4 collective-permute-done.24.refs_3_
  118.8 1.6 %collective-permute-start.31 = (bf16[256,256]{1,0:T(8,128)(2,1)S(1)}, bf16[256,256]{1,0:T(8,128)(2,1)S(1)}, u32[]{:S(2)}, u32[]{:S(2)}) collective-permute-start(bf16[256,256]{1,0:T(8,128)(2,1)S(1)} %get-tuple-element.95), channel_id=1, source_target_pairs={{0,17},{1,16},{2,19},{3,18},{4,21},{5,20},{6,23},{7,22},{8,25},{9,... | collective-permute-start | bytes 393224 | tf_op jit(solution)/shard_map/ppermute | solution.py:97
  123.8 1.6 collective-permute-done.29.refs_0_
  125.8 1.8 %collective-permute-done.30.refs_1_ = bf16[256,256]{1,0:T(8,128)(2,1)S(1)} collective-permute-done((bf16[256,256]{1,0:T(8,128)(2,1)S(1)}, bf16[256,256]{1,0:T(8,128)(2,1)S(1)}, u32[]{:S(2)}, u32[]{:S(2)}) %collective-permute-start.30) | collective-permute-done | bytes 131104 | tf_op jit(solution)/shard_map/ppermute | solution.py:97
  127.6 1.6 shard_map.90
  129.2 3.1 %collective-permute-start.35 = (bf16[256,256]{1,0:T(8,128)(2,1)S(1)}, bf16[256,256]{1,0:T(8,128)(2,1)S(1)}, u32[]{:S(2)}, u32[]{:S(2)}) collective-permute-start(bf16[256,256]{1,0:T(8,128)(2,1)S(1)} %get-tuple-element.98.refs_1_), channel_id=1, source_target_pairs={{0,2},{1,3},{2,4},{3,5},{4,6},{5,7},{6,0},{7,1},{8,10},{9,11},{10,... | collective-permute-start | bytes 393224 | tf_op jit(solution)/shard_map/ppermute | solution.py:97
  132.3 1.3 collective-permute-start.34
  134.7 2.8 %collective-permute-done.35.refs_2_ = bf16[256,256]{1,0:T(8,128)(2,1)S(1)} collective-permute-done((bf16[256,256]{1,0:T(8,128)(2,1)S(1)}, bf16[256,256]{1,0:T(8,128)(2,1)S(1)}, u32[]{:S(2)}, u32[]{:S(2)}) %collective-permute-start.35) | collective-permute-done | bytes 131104 | tf_op jit(solution)/shard_map/ppermute | solution.py:97
  137.5 4.2 %collective-permute-done.34.refs_1_ = bf16[256,256]{1,0:T(8,128)(2,1)S(1)} collective-permute-done((bf16[256,256]{1,0:T(8,128)(2,1)S(1)}, bf16[256,256]{1,0:T(8,128)(2,1)S(1)}, u32[]{:S(2)}, u32[]{:S(2)}) %collective-permute-start.34) | collective-permute-done | bytes 131104 | tf_op jit(solution)/shard_map/ppermute | solution.py:97
  142.4 1.4 collective-permute-done.32.refs_2_
  147.1 1.4 collective-permute-start.39
  151.7 4.4 %collective-permute-done.37.refs_0_ = bf16[384,256]{1,0:T(8,128)(2,1)S(1)} collective-permute-done((bf16[384,256]{1,0:T(8,128)(2,1)S(1)}, bf16[384,256]{1,0:T(8,128)(2,1)S(1)}, u32[]{:S(2)}, u32[]{:S(2)}) %collective-permute-start.37) | collective-permute-done | bytes 196640 | tf_op jit(solution)/shard_map/ppermute | solution.py:97
  156.1 2.5 %collective-permute-done.38.refs_1_ = bf16[384,256]{1,0:T(8,128)(2,1)S(1)} collective-permute-done((bf16[384,256]{1,0:T(8,128)(2,1)S(1)}, bf16[384,256]{1,0:T(8,128)(2,1)S(1)}, u32[]{:S(2)}, u32[]{:S(2)}) %collective-permute-start.38) | collective-permute-done | bytes 196640 | tf_op jit(solution)/shard_map/ppermute | solution.py:97
  (93 shorter events, 36.8 us)
Async XLA Ops:
  0.6 9.9 %copy-start.4 = (bf16[384,256]{1,0:T(8,128)(2,1)S(1)}, bf16[384,256]{1,0:T(8,128)(2,1)}, u32[]{:S(2)}) copy-start(bf16[384,256]{1,0:T(8,128)(2,1)} %current_ref.1) | copy-start | bytes 589828
  0.6 0.7 copy-start.5
  3.3 15.1 %all-to-all-start = ((s32[32,8,128]{2,1,0:T(8,128)}), s32[32,8,128]{2,1,0:T(8,128)S(1)}, u32[]{:S(2)}, u32[]{:S(2)}) async-start(s32[32,8,128]{2,1,0:T(8,128)} %shard_map.59), calls=%async_computation | async-start | bytes 262144 | tf_op jit(solution)/shard_map/all_to_all | solution.py:568
  10.6 9.9 %collective-permute-start.3 = (bf16[384,256]{1,0:T(8,128)(2,1)S(1)}, bf16[384,256]{1,0:T(8,128)(2,1)S(1)}, u32[]{:S(2)}, u32[]{:S(2)}) collective-permute-start(bf16[384,256]{1,0:T(8,128)(2,1)S(1)} %copy-done.4), channel_id=1, source_target_pairs={{0,17},{1,16},{2,19},{3,18},{4,21},{5,20},{6,23},{7,22},{8,25},{9,... | collective-permute-start | bytes 589832 | tf_op jit(solution)/shard_map/ppermute | solution.py:97
  13.3 10.6 %collective-permute-start.2 = (bf16[384,256]{1,0:T(8,128)(2,1)S(1)}, bf16[384,256]{1,0:T(8,128)(2,1)S(1)}, u32[]{:S(2)}, u32[]{:S(2)}) collective-permute-start(bf16[384,256]{1,0:T(8,128)(2,1)S(1)} %copy-done.4), channel_id=1, source_target_pairs={{0,16},{1,17},{2,18},{3,19},{4,20},{5,21},{6,22},{7,23},{8,24},{9,... | collective-permute-start | bytes 589832 | tf_op jit(solution)/shard_map/ppermute | solution.py:97
  13.9 10.2 %collective-permute-start.1 = (bf16[384,256]{1,0:T(8,128)(2,1)S(1)}, bf16[384,256]{1,0:T(8,128)(2,1)S(1)}, u32[]{:S(2)}, u32[]{:S(2)}) collective-permute-start(bf16[384,256]{1,0:T(8,128)(2,1)S(1)} %copy-done.4), channel_id=1, source_target_pairs={{0,1},{1,0},{2,3},{3,2},{4,5},{5,4},{6,7},{7,6},{8,9},{9,8},{10,11... | collective-permute-start | bytes 589832 | tf_op jit(solution)/shard_map/ppermute | solution.py:97
  24.1 2.4 %collective-permute-start.4 = (bf16[1152,256]{1,0:T(8,128)(2,1)S(1)}, bf16[1152,256]{1,0:T(8,128)(2,1)S(1)}, u32[]{:S(2)}, u32[]{:S(2)}) collective-permute-start(bf16[1152,256]{1,0:T(8,128)(2,1)S(1)} %shard_map.61.refs_3_), channel_id=1, source_target_pairs={{0,8},{1,9},{2,10},{3,11},{4,12},{5,13},{6,14},{7,15},{8,0},{9,1},... | collective-permute-start | bytes 1769480 | tf_op jit(solution)/shard_map/ppermute | solution.py:97
  24.2 2.3 %collective-permute-start = (bf16[384,256]{1,0:T(8,128)(2,1)S(1)}, bf16[384,256]{1,0:T(8,128)(2,1)S(1)}, u32[]{:S(2)}, u32[]{:S(2)}) collective-permute-start(bf16[384,256]{1,0:T(8,128)(2,1)S(1)} %copy-done.4), channel_id=1, source_target_pairs={{0,8},{1,9},{2,10},{3,11},{4,12},{5,13},{6,14},{7,15},{8,0},{9,1},... | collective-permute-start | bytes 589832 | tf_op jit(solution)/shard_map/ppermute | solution.py:97
  27.7 17.6 %collective-permute-start.5 = (bf16[256,256]{1,0:T(8,128)(2,1)S(1)}, bf16[256,256]{1,0:T(8,128)(2,1)S(1)}, u32[]{:S(2)}, u32[]{:S(2)}) collective-permute-start(bf16[256,256]{1,0:T(8,128)(2,1)S(1)} %get-tuple-element.60), channel_id=1, source_target_pairs={{0,2},{1,3},{2,4},{3,5},{4,6},{5,7},{6,0},{7,1},{8,10},{9,11},{10,... | collective-permute-start | bytes 393224 | tf_op jit(solution)/shard_map/ppermute | solution.py:97
  30.3 15.0 %collective-permute-start.6 = (bf16[256,256]{1,0:T(8,128)(2,1)S(1)}, bf16[256,256]{1,0:T(8,128)(2,1)S(1)}, u32[]{:S(2)}, u32[]{:S(2)}) collective-permute-start(bf16[256,256]{1,0:T(8,128)(2,1)S(1)} %get-tuple-element.61), channel_id=1, source_target_pairs={{0,4},{1,5},{2,6},{3,7},{4,0},{5,1},{6,2},{7,3},{8,12},{9,13},{10,... | collective-permute-start | bytes 393224 | tf_op jit(solution)/shard_map/ppermute | solution.py:97
  33.4 11.9 %collective-permute-start.7 = (bf16[256,256]{1,0:T(8,128)(2,1)S(1)}, bf16[256,256]{1,0:T(8,128)(2,1)S(1)}, u32[]{:S(2)}, u32[]{:S(2)}) collective-permute-start(bf16[256,256]{1,0:T(8,128)(2,1)S(1)} %get-tuple-element.62), channel_id=1, source_target_pairs={{0,6},{1,7},{2,0},{3,1},{4,2},{5,3},{6,4},{7,5},{8,14},{9,15},{10,... | collective-permute-start | bytes 393224 | tf_op jit(solution)/shard_map/ppermute | solution.py:97
  45.4 10.2 %collective-permute-start.11 = (bf16[256,256]{1,0:T(8,128)(2,1)S(1)}, bf16[256,256]{1,0:T(8,128)(2,1)S(1)}, u32[]{:S(2)}, u32[]{:S(2)}) collective-permute-start(bf16[256,256]{1,0:T(8,128)(2,1)S(1)} %get-tuple-element.65.refs_2_), channel_id=1, source_target_pairs={{0,2},{1,3},{2,4},{3,5},{4,6},{5,7},{6,0},{7,1},{8,10},{9,11},{10,... | collective-permute-start | bytes 393224 | tf_op jit(solution)/shard_map/ppermute | solution.py:97
  46.2 11.5 %collective-permute-start.10 = (bf16[256,256]{1,0:T(8,128)(2,1)S(1)}, bf16[256,256]{1,0:T(8,128)(2,1)S(1)}, u32[]{:S(2)}, u32[]{:S(2)}) collective-permute-start(bf16[256,256]{1,0:T(8,128)(2,1)S(1)} %get-tuple-element.65.refs_2_), channel_id=1, source_target_pairs={{0,4},{1,5},{2,6},{3,7},{4,0},{5,1},{6,2},{7,3},{8,12},{9,13},{10,... | collective-permute-start | bytes 393224 | tf_op jit(solution)/shard_map/ppermute | solution.py:97
  46.7 11.1 %collective-permute-start.9 = (bf16[256,256]{1,0:T(8,128)(2,1)S(1)}, bf16[256,256]{1,0:T(8,128)(2,1)S(1)}, u32[]{:S(2)}, u32[]{:S(2)}) collective-permute-start(bf16[256,256]{1,0:T(8,128)(2,1)S(1)} %get-tuple-element.65.refs_2_), channel_id=1, source_target_pairs={{0,6},{1,7},{2,0},{3,1},{4,2},{5,3},{6,4},{7,5},{8,14},{9,15},{10,... | collective-permute-start | bytes 393224 | tf_op jit(solution)/shard_map/ppermute | solution.py:97
  55.6 2.7 %copy-start.7 = (f32[2]{0:T(128)S(1)}, f32[2]{0:T(128)}, u32[]{:S(2)}) copy-start(f32[2]{0:T(128)} %param.7) | copy-start | bytes 28
  57.8 2.0 %collective-permute-start.12 = (bf16[768,256]{1,0:T(8,128)(2,1)S(1)}, bf16[768,256]{1,0:T(8,128)(2,1)S(1)}, u32[]{:S(2)}, u32[]{:S(2)}) collective-permute-start(bf16[768,256]{1,0:T(8,128)(2,1)S(1)} %shard_map.70.refs_4_), channel_id=1, source_target_pairs={{0,8},{1,9},{2,10},{3,11},{4,12},{5,13},{6,14},{7,15},{8,0},{9,1},... | collective-permute-start | bytes 1179656 | tf_op jit(solution)/shard_map/ppermute | solution.py:97
  57.8 1.9 %collective-permute-start.8 = (bf16[256,256]{1,0:T(8,128)(2,1)S(1)}, bf16[256,256]{1,0:T(8,128)(2,1)S(1)}, u32[]{:S(2)}, u32[]{:S(2)}) collective-permute-start(bf16[256,256]{1,0:T(8,128)(2,1)S(1)} %get-tuple-element.65.refs_2_), channel_id=1, source_target_pairs={{0,8},{1,9},{2,10},{3,11},{4,12},{5,13},{6,14},{7,15},{8,0},{9,1},... | collective-permute-start | bytes 393224 | tf_op jit(solution)/shard_map/ppermute | solution.py:97
  60.9 12.4 %collective-permute-start.13 = (bf16[256,256]{1,0:T(8,128)(2,1)S(1)}, bf16[256,256]{1,0:T(8,128)(2,1)S(1)}, u32[]{:S(2)}, u32[]{:S(2)}) collective-permute-start(bf16[256,256]{1,0:T(8,128)(2,1)S(1)} %get-tuple-element.69), channel_id=1, source_target_pairs={{0,1},{1,0},{2,3},{3,2},{4,5},{5,4},{6,7},{7,6},{8,9},{9,8},{10,11... | collective-permute-start | bytes 393224 | tf_op jit(solution)/shard_map/ppermute | solution.py:97
  63.1 10.1 %collective-permute-start.14 = (bf16[256,256]{1,0:T(8,128)(2,1)S(1)}, bf16[256,256]{1,0:T(8,128)(2,1)S(1)}, u32[]{:S(2)}, u32[]{:S(2)}) collective-permute-start(bf16[256,256]{1,0:T(8,128)(2,1)S(1)} %get-tuple-element.72), channel_id=1, source_target_pairs={{0,16},{1,17},{2,18},{3,19},{4,20},{5,21},{6,22},{7,23},{8,24},{9,... | collective-permute-start | bytes 393224 | tf_op jit(solution)/shard_map/ppermute | solution.py:97
  65.1 8.2 %collective-permute-start.15 = (bf16[256,256]{1,0:T(8,128)(2,1)S(1)}, bf16[256,256]{1,0:T(8,128)(2,1)S(1)}, u32[]{:S(2)}, u32[]{:S(2)}) collective-permute-start(bf16[256,256]{1,0:T(8,128)(2,1)S(1)} %get-tuple-element.73), channel_id=1, source_target_pairs={{0,17},{1,16},{2,19},{3,18},{4,21},{5,20},{6,23},{7,22},{8,25},{9,... | collective-permute-start | bytes 393224 | tf_op jit(solution)/shard_map/ppermute | solution.py:97
  74.6 12.1 %collective-permute-start.19 = (bf16[256,256]{1,0:T(8,128)(2,1)S(1)}, bf16[256,256]{1,0:T(8,128)(2,1)S(1)}, u32[]{:S(2)}, u32[]{:S(2)}) collective-permute-start(bf16[256,256]{1,0:T(8,128)(2,1)S(1)} %get-tuple-element.80.refs_1_.potential_ref), channel_id=1, source_target_pairs={{0,2},{1,3},{2,4},{3,5},{4,6},{5,7},{6,0},{7,1},{8,10},{9,11},{10,... | collective-permute-start | bytes 393224 | tf_op jit(solution)/shard_map/ppermute | solution.py:97
  77.4 9.4 %collective-permute-start.18 = (bf16[256,256]{1,0:T(8,128)(2,1)S(1)}, bf16[256,256]{1,0:T(8,128)(2,1)S(1)}, u32[]{:S(2)}, u32[]{:S(2)}) collective-permute-start(bf16[256,256]{1,0:T(8,128)(2,1)S(1)} %get-tuple-element.80.refs_1_.potential_ref), channel_id=1, source_target_pairs={{0,4},{1,5},{2,6},{3,7},{4,0},{5,1},{6,2},{7,3},{8,12},{9,13},{10,... | collective-permute-start | bytes 393224 | tf_op jit(solution)/shard_map/ppermute | solution.py:97
  77.8 9.0 %collective-permute-start.17 = (bf16[256,256]{1,0:T(8,128)(2,1)S(1)}, bf16[256,256]{1,0:T(8,128)(2,1)S(1)}, u32[]{:S(2)}, u32[]{:S(2)}) collective-permute-start(bf16[256,256]{1,0:T(8,128)(2,1)S(1)} %get-tuple-element.80.refs_1_.potential_ref), channel_id=1, source_target_pairs={{0,6},{1,7},{2,0},{3,1},{4,2},{5,3},{6,4},{7,5},{8,14},{9,15},{10,... | collective-permute-start | bytes 393224 | tf_op jit(solution)/shard_map/ppermute | solution.py:97
  86.7 2.1 %copy-start.2 = (bf16[512,2048]{1,0:T(8,128)(2,1)S(1)}, bf16[512,2048]{1,0:T(8,128)(2,1)}, u32[]{:S(2)}) copy-start(bf16[512,2048]{1,0:T(8,128)(2,1)} %get-tuple-element.81.refs_0_) | copy-start | bytes 6291460
  86.8 4.0 %copy-start.3 = (bf16[512,2048]{1,0:T(8,128)(2,1)S(1)}, bf16[512,2048]{1,0:T(8,128)(2,1)}, u32[]{:S(2)}) copy-start(bf16[512,2048]{1,0:T(8,128)(2,1)} %get-tuple-element.86.refs_0_) | copy-start | bytes 6291460
  86.8 2.0 %collective-permute-start.20 = (bf16[768,256]{1,0:T(8,128)(2,1)S(1)}, bf16[768,256]{1,0:T(8,128)(2,1)S(1)}, u32[]{:S(2)}, u32[]{:S(2)}) collective-permute-start(bf16[768,256]{1,0:T(8,128)(2,1)S(1)} %shard_map.79.refs_3_), channel_id=1, source_target_pairs={{0,8},{1,9},{2,10},{3,11},{4,12},{5,13},{6,14},{7,15},{8,0},{9,1},... | collective-permute-start | bytes 1179656 | tf_op jit(solution)/shard_map/ppermute | solution.py:97
  86.9 1.9 %collective-permute-start.16 = (bf16[256,256]{1,0:T(8,128)(2,1)S(1)}, bf16[256,256]{1,0:T(8,128)(2,1)S(1)}, u32[]{:S(2)}, u32[]{:S(2)}) collective-permute-start(bf16[256,256]{1,0:T(8,128)(2,1)S(1)} %get-tuple-element.80.refs_1_.potential_ref), channel_id=1, source_target_pairs={{0,8},{1,9},{2,10},{3,11},{4,12},{5,13},{6,14},{7,15},{8,0},{9,1},... | collective-permute-start | bytes 393224 | tf_op jit(solution)/shard_map/ppermute | solution.py:97
  89.7 7.7 %collective-permute-start.21 = (bf16[256,256]{1,0:T(8,128)(2,1)S(1)}, bf16[256,256]{1,0:T(8,128)(2,1)S(1)}, u32[]{:S(2)}, u32[]{:S(2)}) collective-permute-start(bf16[256,256]{1,0:T(8,128)(2,1)S(1)} %get-tuple-element.85), channel_id=1, source_target_pairs={{0,1},{1,0},{2,3},{3,2},{4,5},{5,4},{6,7},{7,6},{8,9},{9,8},{10,11... | collective-permute-start | bytes 393224 | tf_op jit(solution)/shard_map/ppermute | solution.py:97
  91.2 7.4 %collective-permute-start.23 = (bf16[256,256]{1,0:T(8,128)(2,1)S(1)}, bf16[256,256]{1,0:T(8,128)(2,1)S(1)}, u32[]{:S(2)}, u32[]{:S(2)}) collective-permute-start(bf16[256,256]{1,0:T(8,128)(2,1)S(1)} %get-tuple-element.88), channel_id=1, source_target_pairs={{0,17},{1,16},{2,19},{3,18},{4,21},{5,20},{6,23},{7,22},{8,25},{9,... | collective-permute-start | bytes 393224 | tf_op jit(solution)/shard_map/ppermute | solution.py:97
  93.7 6.0 %collective-permute-start.22 = (bf16[256,256]{1,0:T(8,128)(2,1)S(1)}, bf16[256,256]{1,0:T(8,128)(2,1)S(1)}, u32[]{:S(2)}, u32[]{:S(2)}) collective-permute-start(bf16[256,256]{1,0:T(8,128)(2,1)S(1)} %get-tuple-element.87), channel_id=1, source_target_pairs={{0,16},{1,17},{2,18},{3,19},{4,20},{5,21},{6,22},{7,23},{8,24},{9,... | collective-permute-start | bytes 393224 | tf_op jit(solution)/shard_map/ppermute | solution.py:97
  101.2 8.9 %collective-permute-start.27 = (bf16[256,256]{1,0:T(8,128)(2,1)S(1)}, bf16[256,256]{1,0:T(8,128)(2,1)S(1)}, u32[]{:S(2)}, u32[]{:S(2)}) collective-permute-start(bf16[256,256]{1,0:T(8,128)(2,1)S(1)} %get-tuple-element.90.refs_2_), channel_id=1, source_target_pairs={{0,2},{1,3},{2,4},{3,5},{4,6},{5,7},{6,0},{7,1},{8,10},{9,11},{10,... | collective-permute-start | bytes 393224 | tf_op jit(solution)/shard_map/ppermute | solution.py:97
  104.4 9.5 %collective-permute-start.26 = (bf16[256,256]{1,0:T(8,128)(2,1)S(1)}, bf16[256,256]{1,0:T(8,128)(2,1)S(1)}, u32[]{:S(2)}, u32[]{:S(2)}) collective-permute-start(bf16[256,256]{1,0:T(8,128)(2,1)S(1)} %get-tuple-element.90.refs_2_), channel_id=1, source_target_pairs={{0,4},{1,5},{2,6},{3,7},{4,0},{5,1},{6,2},{7,3},{8,12},{9,13},{10,... | collective-permute-start | bytes 393224 | tf_op jit(solution)/shard_map/ppermute | solution.py:97
  106.1 8.0 %collective-permute-start.25 = (bf16[256,256]{1,0:T(8,128)(2,1)S(1)}, bf16[256,256]{1,0:T(8,128)(2,1)S(1)}, u32[]{:S(2)}, u32[]{:S(2)}) collective-permute-start(bf16[256,256]{1,0:T(8,128)(2,1)S(1)} %get-tuple-element.90.refs_2_), channel_id=1, source_target_pairs={{0,6},{1,7},{2,0},{3,1},{4,2},{5,3},{6,4},{7,5},{8,14},{9,15},{10,... | collective-permute-start | bytes 393224 | tf_op jit(solution)/shard_map/ppermute | solution.py:97
  114.2 2.0 %collective-permute-start.28 = (bf16[768,256]{1,0:T(8,128)(2,1)S(1)}, bf16[768,256]{1,0:T(8,128)(2,1)S(1)}, u32[]{:S(2)}, u32[]{:S(2)}) collective-permute-start(bf16[768,256]{1,0:T(8,128)(2,1)S(1)} %shard_map.85.refs_4_), channel_id=1, source_target_pairs={{0,8},{1,9},{2,10},{3,11},{4,12},{5,13},{6,14},{7,15},{8,0},{9,1},... | collective-permute-start | bytes 1179656 | tf_op jit(solution)/shard_map/ppermute | solution.py:97
  114.2 1.9 %collective-permute-start.24 = (bf16[256,256]{1,0:T(8,128)(2,1)S(1)}, bf16[256,256]{1,0:T(8,128)(2,1)S(1)}, u32[]{:S(2)}, u32[]{:S(2)}) collective-permute-start(bf16[256,256]{1,0:T(8,128)(2,1)S(1)} %get-tuple-element.90.refs_2_), channel_id=1, source_target_pairs={{0,8},{1,9},{2,10},{3,11},{4,12},{5,13},{6,14},{7,15},{8,0},{9,1},... | collective-permute-start | bytes 393224 | tf_op jit(solution)/shard_map/ppermute | solution.py:97
  117.3 8.1 %collective-permute-start.29 = (bf16[256,256]{1,0:T(8,128)(2,1)S(1)}, bf16[256,256]{1,0:T(8,128)(2,1)S(1)}, u32[]{:S(2)}, u32[]{:S(2)}) collective-permute-start(bf16[256,256]{1,0:T(8,128)(2,1)S(1)} %get-tuple-element.93), channel_id=1, source_target_pairs={{0,1},{1,0},{2,3},{3,2},{4,5},{5,4},{6,7},{7,6},{8,9},{9,8},{10,11... | collective-permute-start | bytes 393224 | tf_op jit(solution)/shard_map/ppermute | solution.py:97
  118.8 7.0 %collective-permute-start.31 = (bf16[256,256]{1,0:T(8,128)(2,1)S(1)}, bf16[256,256]{1,0:T(8,128)(2,1)S(1)}, u32[]{:S(2)}, u32[]{:S(2)}) collective-permute-start(bf16[256,256]{1,0:T(8,128)(2,1)S(1)} %get-tuple-element.95), channel_id=1, source_target_pairs={{0,17},{1,16},{2,19},{3,18},{4,21},{5,20},{6,23},{7,22},{8,25},{9,... | collective-permute-start | bytes 393224 | tf_op jit(solution)/shard_map/ppermute | solution.py:97
  121.6 6.0 %collective-permute-start.30 = (bf16[256,256]{1,0:T(8,128)(2,1)S(1)}, bf16[256,256]{1,0:T(8,128)(2,1)S(1)}, u32[]{:S(2)}, u32[]{:S(2)}) collective-permute-start(bf16[256,256]{1,0:T(8,128)(2,1)S(1)} %get-tuple-element.94), channel_id=1, source_target_pairs={{0,16},{1,17},{2,18},{3,19},{4,20},{5,21},{6,22},{7,23},{8,24},{9,... | collective-permute-start | bytes 393224 | tf_op jit(solution)/shard_map/ppermute | solution.py:97
  127.6 16.2 %copy-start = (bf16[768,2048]{1,0:T(8,128)(2,1)S(1)}, bf16[768,2048]{1,0:T(8,128)(2,1)}, u32[]{:S(2)}) copy-start(bf16[768,2048]{1,0:T(8,128)(2,1)} %get-tuple-element.77.refs_0_) | copy-start | bytes 9437188
  129.2 8.3 %collective-permute-start.35 = (bf16[256,256]{1,0:T(8,128)(2,1)S(1)}, bf16[256,256]{1,0:T(8,128)(2,1)S(1)}, u32[]{:S(2)}, u32[]{:S(2)}) collective-permute-start(bf16[256,256]{1,0:T(8,128)(2,1)S(1)} %get-tuple-element.98.refs_1_), channel_id=1, source_target_pairs={{0,2},{1,3},{2,4},{3,5},{4,6},{5,7},{6,0},{7,1},{8,10},{9,11},{10,... | collective-permute-start | bytes 393224 | tf_op jit(solution)/shard_map/ppermute | solution.py:97
  132.3 9.4 %collective-permute-start.34 = (bf16[256,256]{1,0:T(8,128)(2,1)S(1)}, bf16[256,256]{1,0:T(8,128)(2,1)S(1)}, u32[]{:S(2)}, u32[]{:S(2)}) collective-permute-start(bf16[256,256]{1,0:T(8,128)(2,1)S(1)} %get-tuple-element.98.refs_1_), channel_id=1, source_target_pairs={{0,4},{1,5},{2,6},{3,7},{4,0},{5,1},{6,2},{7,3},{8,12},{9,13},{10,... | collective-permute-start | bytes 393224 | tf_op jit(solution)/shard_map/ppermute | solution.py:97
  133.6 8.2 %collective-permute-start.33 = (bf16[256,256]{1,0:T(8,128)(2,1)S(1)}, bf16[256,256]{1,0:T(8,128)(2,1)S(1)}, u32[]{:S(2)}, u32[]{:S(2)}) collective-permute-start(bf16[256,256]{1,0:T(8,128)(2,1)S(1)} %get-tuple-element.98.refs_1_), channel_id=1, source_target_pairs={{0,6},{1,7},{2,0},{3,1},{4,2},{5,3},{6,4},{7,5},{8,14},{9,15},{10,... | collective-permute-start | bytes 393224 | tf_op jit(solution)/shard_map/ppermute | solution.py:97
  141.8 2.0 %collective-permute-start.36 = (bf16[768,256]{1,0:T(8,128)(2,1)S(1)}, bf16[768,256]{1,0:T(8,128)(2,1)S(1)}, u32[]{:S(2)}, u32[]{:S(2)}) collective-permute-start(bf16[768,256]{1,0:T(8,128)(2,1)S(1)} %shard_map.91.refs_3_), channel_id=1, source_target_pairs={{0,8},{1,9},{2,10},{3,11},{4,12},{5,13},{6,14},{7,15},{8,0},{9,1},... | collective-permute-start | bytes 1179656 | tf_op jit(solution)/shard_map/ppermute | solution.py:97
  141.9 1.9 %collective-permute-start.32 = (bf16[256,256]{1,0:T(8,128)(2,1)S(1)}, bf16[256,256]{1,0:T(8,128)(2,1)S(1)}, u32[]{:S(2)}, u32[]{:S(2)}) collective-permute-start(bf16[256,256]{1,0:T(8,128)(2,1)S(1)} %get-tuple-element.98.refs_1_), channel_id=1, source_target_pairs={{0,8},{1,9},{2,10},{3,11},{4,12},{5,13},{6,14},{7,15},{8,0},{9,1},... | collective-permute-start | bytes 393224 | tf_op jit(solution)/shard_map/ppermute | solution.py:97
  143.8 2.2 %copy-start.1 = (bf16[768,2048]{1,0:T(8,128)(2,1)S(1)}, bf16[768,2048]{1,0:T(8,128)(2,1)}, u32[]{:S(2)}) copy-start(bf16[768,2048]{1,0:T(8,128)(2,1)} %get-tuple-element.102.refs_0_) | copy-start | bytes 9437188
  144.9 11.2 %collective-permute-start.37 = (bf16[384,256]{1,0:T(8,128)(2,1)S(1)}, bf16[384,256]{1,0:T(8,128)(2,1)S(1)}, u32[]{:S(2)}, u32[]{:S(2)}) collective-permute-start(bf16[384,256]{1,0:T(8,128)(2,1)S(1)} %get-tuple-element.101), channel_id=1, source_target_pairs={{0,1},{1,0},{2,3},{3,2},{4,5},{5,4},{6,7},{7,6},{8,9},{9,8},{10,11... | collective-permute-start | bytes 589832 | tf_op jit(solution)/shard_map/ppermute | solution.py:97
  147.1 9.0 %collective-permute-start.39 = (bf16[384,256]{1,0:T(8,128)(2,1)S(1)}, bf16[384,256]{1,0:T(8,128)(2,1)S(1)}, u32[]{:S(2)}, u32[]{:S(2)}) collective-permute-start(bf16[384,256]{1,0:T(8,128)(2,1)S(1)} %get-tuple-element.104), channel_id=1, source_target_pairs={{0,17},{1,16},{2,19},{3,18},{4,21},{5,20},{6,23},{7,22},{8,25},{9,... | collective-permute-start | bytes 589832 | tf_op jit(solution)/shard_map/ppermute | solution.py:97
  149.6 8.9 %collective-permute-start.38 = (bf16[384,256]{1,0:T(8,128)(2,1)S(1)}, bf16[384,256]{1,0:T(8,128)(2,1)S(1)}, u32[]{:S(2)}, u32[]{:S(2)}) collective-permute-start(bf16[384,256]{1,0:T(8,128)(2,1)S(1)} %get-tuple-element.103), channel_id=1, source_target_pairs={{0,16},{1,17},{2,18},{3,19},{4,20},{5,21},{6,22},{7,23},{8,24},{9,... | collective-permute-start | bytes 589832 | tf_op jit(solution)/shard_map/ppermute | solution.py:97
  (1 other events, 0.7 us)

commit v12 on v11

--- a/solution.py
+++ b/solution.py
@@ -612,10 +612,8 @@
     )
     pieces = layout.gathered(currents, across, (token,))
     blocks, token = multiply([[first]], pieces, tri_dev, resident)
-    tiles = []
-    for span in spans:
-        part, token = tile_part(span, token)
-        tiles.append(part)
+    part, token = tile_part(spans[0], token)
+    tiles = [part]
     charge, rounded, token = sum_of(layout.given_along(blocks), (token,))
 
     def incidence_parts(token):
@@ -632,32 +630,40 @@
             parts.append(part)
         return parts, token
 
-    near, ends = [], None
+    near, degree, ends = [], [], None
+
+    def more_adjacency(goal, token):
+        for row in range(len(near), goal):
+            (part, *extra), token = adjacency_part(range(row, row + 1), token)
+            near.append([part])
+            degree.extend(extra)
+        return token
+
     summed, potential = (), None
     for sweep in range(sweeps):
         weight = sweep_weights[sweep].reshape(1)
         last = sweep + 1 == sweeps
-        build_now = not near and not last
-        if build_now:
-            (part, degree), token = adjacency_part(spans[0], token)
-            near.append([part])
+        for span in spans[len(tiles) :]:
+            part, token = tile_part(span, token)
+            tiles.append(part)
+        if sweep > 0 and ends is None:
+            ends, token = incidence_parts(token)
+        if not last:
+            token = more_adjacency(count // 4, token)
         pieces = layout.gathered(rounded, layout.along(rounded), (token,))
         blocks, token = multiply(tiles, pieces, tri_dev, resident)
-        if build_now:
-            for span in spans[1:]:
-                part, token = adjacency_part(span, token)
-                near.append(part)
+        if not last:
+            token = more_adjacency(count // 2, token)
         potential, *summed, weighted, token = potential_of(
             weight, layout.given(blocks), summed, (token,)
         )
         if last:
             break
-        if build_now:
-            ends, token = incidence_parts(token)
+        token = more_adjacency(count, token)
         pieces = layout.gathered(potential, layout.along(potential), (token,))
         blocks, token = multiply(near, pieces, tri_dev, resident)
         charge, rounded, token = charge_of(
-            weight, charge, degree, potential, layout.given(blocks), (token,)
+            weight, charge, degree[0], potential, layout.given(blocks), (token,)
         )
     if ends is None:
         ends, token = incidence_parts(token)

time: 160 us -> 155 us (0.969)
  waiting for transfers between devices: 46.4 us -> 38.8 us
    ppermute x40, waiting for transfers between devices: 42.1 us -> 34.6 us  [shift(): return lax.ppermute(value, AXES, pairs)]
    pallas_call x7 -> x9, Pallas kernels: 30.3 us -> 31.6 us  [build(): pl.pallas_call(kernel, grid=(len(span),), in_specs=[pl.BlockSpec(memory_s...]
  transfers between devices with their start and end apart: 41 -> 41, of which waited for: 24 -> 25; matrix products, arithmetic and copies ran while one was open for 1% -> 1% of each run, Pallas kernels for 28% -> 30%
where the time goes in v12:
time: 155 us; the launch traced here: 154 us
  Pallas kernels  58.1 us (37%)
  starting transfers between devices  54.2 us (35%)
  waiting for transfers between devices  38.8 us (25%)
  local copies, waits for them, and re-layouts  2.35 us (2%)
    ppermute x40, starting transfers between devices, shift(): return lax.ppermute(value, AXES, pairs)  46.9 us
    ppermute x40, waiting for transfers between devices, shift(): return lax.ppermute(value, AXES, pairs)  34.6 us
    pallas_call x9, Pallas kernels, build(): pl.pallas_call(kernel, grid=(len(span),), in_specs=[pl.BlockSpec(memory_s...  31.6 us
    pallas_call x20, Pallas kernels, apply(): pl.pallas_call(functools.partial(apply_kernel, mats, len(pieces), block,...  19.8 us
    all_to_all x1, starting transfers between devices, per_device(): lax.all_to_all(letters, AXES, split_axis=0, concat_axis=0, tiled=True)  7.3 us
    all_to_all x1, waiting for transfers between devices, per_device(): lax.all_to_all(letters, AXES, split_axis=0, concat_axis=0, tiled=True)  4.27 us
  transfers between devices with their start and end apart: 41, of which 25 were waited for; matrix products, arithmetic and copies ran while one was open for 1% of the time, Pallas kernels for 30%

profile of v12, /device:TPU:0, one launch (start us, length us, event | category | flops | bytes accessed | tf_op | source)
XLA Modules:
  0.0 154.3 jit_solution(17673256325436284050)
XLA Ops:
  2.1 1.2 shard_map.59
  3.3 7.3 %all-to-all-start = ((s32[32,8,128]{2,1,0:T(8,128)}), s32[32,8,128]{2,1,0:T(8,128)S(1)}, u32[]{:S(2)}, u32[]{:S(2)}) async-start(s32[32,8,128]{2,1,0:T(8,128)} %shard_map.59), calls=%async_computation | async-start | bytes 262144 | tf_op jit(solution)/shard_map/all_to_all | solution.py:568
  10.6 2.7 %collective-permute-start.3 = (bf16[384,256]{1,0:T(8,128)(2,1)S(1)}, bf16[384,256]{1,0:T(8,128)(2,1)S(1)}, u32[]{:S(2)}, u32[]{:S(2)}) collective-permute-start(bf16[384,256]{1,0:T(8,128)(2,1)S(1)} %copy-done.2), channel_id=1, source_target_pairs={{0,17},{1,16},{2,19},{3,18},{4,21},{5,20},{6,23},{7,22},{8,25},{9,... | collective-permute-start | bytes 589832 | tf_op jit(solution)/shard_map/ppermute | solution.py:97
  14.1 4.3 %all-to-all-done.letter_ref = s32[32,8,128]{2,1,0:T(8,128)S(1)} async-done(((s32[32,8,128]{2,1,0:T(8,128)}), s32[32,8,128]{2,1,0:T(8,128)S(1)}, u32[]{:S(2)}, u32[]{:S(2)}) %all-to-all-start) | async-done | bytes 131104 | tf_op jit(solution)/shard_map/all_to_all | solution.py:568
  18.7 1.8 %shard_map.60 = (bf16[1024,3072]{1,0:T(8,128)(2,1)S(1)}, f32[8,128]{1,0:T(8,128)S(1)}) custom-call(s32[1]{0:T(128)} %bitcast.me_ref, s32[32,8,128]{2,1,0:T(8,128)S(1)} %all-to-all-done.letter_ref, s32[4,1,2048]{2,1,0:T(1,128)S(1)} %reshape.11.after_ref.label_ref), custom_call_target="tpu_custom_call" | custom-call | flops 3449999872 | tf_op jit(solution)/shard_map/pallas_call | solution.py:319
  20.5 3.5 %collective-permute-done.2.refs_1_ = bf16[384,256]{1,0:T(8,128)(2,1)S(1)} collective-permute-done((bf16[384,256]{1,0:T(8,128)(2,1)S(1)}, bf16[384,256]{1,0:T(8,128)(2,1)S(1)}, u32[]{:S(2)}, u32[]{:S(2)}) %collective-permute-start.2) | collective-permute-done | bytes 196640 | tf_op jit(solution)/shard_map/ppermute | solution.py:97
  24.7 1.8 %collective-permute-done.refs_2_ = bf16[384,256]{1,0:T(8,128)(2,1)S(1)} collective-permute-done((bf16[384,256]{1,0:T(8,128)(2,1)S(1)}, bf16[384,256]{1,0:T(8,128)(2,1)S(1)}, u32[]{:S(2)}, u32[]{:S(2)}) %collective-permute-start) | collective-permute-done | bytes 196640 | tf_op jit(solution)/shard_map/ppermute | solution.py:97
  26.5 1.2 shard_map.63
  27.7 1.4 collective-permute-start.5
  29.1 1.2 shard_map.64
  30.3 2.5 %collective-permute-start.6 = (bf16[256,256]{1,0:T(8,128)(2,1)S(1)}, bf16[256,256]{1,0:T(8,128)(2,1)S(1)}, u32[]{:S(2)}, u32[]{:S(2)}) collective-permute-start(bf16[256,256]{1,0:T(8,128)(2,1)S(1)} %get-tuple-element.62), channel_id=1, source_target_pairs={{0,4},{1,5},{2,6},{3,7},{4,0},{5,1},{6,2},{7,3},{8,12},{9,13},{10,... | collective-permute-start | bytes 393224 | tf_op jit(solution)/shard_map/ppermute | solution.py:97
  33.4 1.3 collective-permute-start.7
  34.7 4.7 %shard_map.66 = (bf16[512,2048]{1,0:T(8,128)(2,1)S(1)}, bf16[512,2048]{1,0:T(8,128)(2,1)S(1)}, f32[8,128]{1,0:T(8,128)S(1)}) custom-call(s32[1]{0:T(128)} %bitcast.me_ref, s32[32,8,128]{2,1,0:T(8,128)S(1)} %all-to-all-done.letter_ref, f32[8,128]{1,0:T(8,128)S(1)} %get-tuple-element.64.after_ref), custom_call_target="tpu_custom_call" | custom-call | flops 6899999744 | tf_op jit(solution)/shard_map/pallas_call | solution.py:319
  39.4 1.2 shard_map.62
  41.3 2.9 %collective-permute-start.11 = (bf16[256,256]{1,0:T(8,128)(2,1)S(1)}, bf16[256,256]{1,0:T(8,128)(2,1)S(1)}, u32[]{:S(2)}, u32[]{:S(2)}) collective-permute-start(bf16[256,256]{1,0:T(8,128)(2,1)S(1)} %get-tuple-element.72.refs_2_), channel_id=1, source_target_pairs={{0,2},{1,3},{2,4},{3,5},{4,6},{5,7},{6,0},{7,1},{8,10},{9,11},{10,... | collective-permute-start | bytes 393224 | tf_op jit(solution)/shard_map/ppermute | solution.py:97
  44.2 1.3 collective-permute-start.10
  46.6 4.7 %shard_map.68 = (bf16[512,2048]{1,0:T(8,128)(2,1)S(1)}, bf16[512,2048]{1,0:T(8,128)(2,1)S(1)}, f32[8,128]{1,0:T(8,128)S(1)}) custom-call(s32[1]{0:T(128)} %bitcast.me_ref, s32[32,8,128]{2,1,0:T(8,128)S(1)} %all-to-all-done.letter_ref, f32[8,128]{1,0:T(8,128)S(1)} %get-tuple-element.67.after_ref), custom_call_target="tpu_custom_call" | custom-call | flops 6899999744 | tf_op jit(solution)/shard_map/pallas_call | solution.py:319
  51.3 3.4 %shard_map.69 = (bf16[256,2048]{1,0:T(8,128)(2,1)}, f32[256,128]{1,0:T(8,128)S(1)}, f32[8,128]{1,0:T(8,128)S(1)}) custom-call(s32[1]{0:T(128)} %bitcast.me_ref, s32[4,1,2048]{2,1,0:T(1,128)S(1)} %reshape.11.after_ref.label_ref, f32[8,128]{1,0:T(8,128)S(1)} %get-tuple-element.68.after_ref), custom_call_target="tpu_custom_call" | custom-call | flops 6899999744 | tf_op jit(solution)/shard_map/pallas_call | solution.py:319
  57.9 1.1 collective-permute-start.13
  60.1 1.4 collective-permute-start.14
  63.3 3.4 %shard_map.75 = (bf16[256,2048]{1,0:T(8,128)(2,1)}, f32[8,128]{1,0:T(8,128)S(1)}) custom-call(s32[1]{0:T(128)} %bitcast.me_ref, s32[4,1,2048]{2,1,0:T(1,128)S(1)} %reshape.11.after_ref.label_ref, f32[8,128]{1,0:T(8,128)S(1)} %get-tuple-element.80.after_ref), custom_call_target="tpu_custom_call" | custom-call | flops 6899999744 | tf_op jit(solution)/shard_map/pallas_call | solution.py:319
  68.5 1.4 shard_map.76
  69.9 2.3 %collective-permute-start.19 = (bf16[256,256]{1,0:T(8,128)(2,1)S(1)}, bf16[256,256]{1,0:T(8,128)(2,1)S(1)}, u32[]{:S(2)}, u32[]{:S(2)}) collective-permute-start(bf16[256,256]{1,0:T(8,128)(2,1)S(1)} %get-tuple-element.82.refs_1_.potential_ref), channel_id=1, source_target_pairs={{0,2},{1,3},{2,4},{3,5},{4,6},{5,7},{6,0},{7,1},{8,10},{9,11},{10,... | collective-permute-start | bytes 393224 | tf_op jit(solution)/shard_map/ppermute | solution.py:97
  72.2 2.1 %collective-permute-start.18 = (bf16[256,256]{1,0:T(8,128)(2,1)S(1)}, bf16[256,256]{1,0:T(8,128)(2,1)S(1)}, u32[]{:S(2)}, u32[]{:S(2)}) collective-permute-start(bf16[256,256]{1,0:T(8,128)(2,1)S(1)} %get-tuple-element.82.refs_1_.potential_ref), channel_id=1, source_target_pairs={{0,4},{1,5},{2,6},{3,7},{4,0},{5,1},{6,2},{7,3},{8,12},{9,13},{10,... | collective-permute-start | bytes 393224 | tf_op jit(solution)/shard_map/ppermute | solution.py:97
  74.6 3.4 %shard_map.77 = (bf16[256,2048]{1,0:T(8,128)(2,1)}, f32[8,128]{1,0:T(8,128)S(1)}) custom-call(s32[1]{0:T(128)} %bitcast.me_ref, s32[4,1,2048]{2,1,0:T(1,128)S(1)} %reshape.11.after_ref.label_ref, f32[8,128]{1,0:T(8,128)S(1)} %get-tuple-element.84.after_ref), custom_call_target="tpu_custom_call" | custom-call | flops 6899999744 | tf_op jit(solution)/shard_map/pallas_call | solution.py:319
  78.0 3.4 %shard_map.78 = (bf16[256,2048]{1,0:T(8,128)(2,1)}, f32[8,128]{1,0:T(8,128)S(1)}) custom-call(s32[1]{0:T(128)} %bitcast.me_ref, s32[4,1,2048]{2,1,0:T(1,128)S(1)} %reshape.11.after_ref.label_ref, f32[8,128]{1,0:T(8,128)S(1)} %get-tuple-element.85.after_ref), custom_call_target="tpu_custom_call" | custom-call | flops 6899999744 | tf_op jit(solution)/shard_map/pallas_call | solution.py:319
  82.9 1.4 collective-permute-done.16.refs_2_
  84.8 2.1 %collective-permute-start.23 = (bf16[256,256]{1,0:T(8,128)(2,1)S(1)}, bf16[256,256]{1,0:T(8,128)(2,1)S(1)}, u32[]{:S(2)}, u32[]{:S(2)}) collective-permute-start(bf16[256,256]{1,0:T(8,128)(2,1)S(1)} %get-tuple-element.93), channel_id=1, source_target_pairs={{0,17},{1,16},{2,19},{3,18},{4,21},{5,20},{6,23},{7,22},{8,25},{9,... | collective-permute-start | bytes 393224 | tf_op jit(solution)/shard_map/ppermute | solution.py:97
  92.0 2.0 %collective-permute-done.22.refs_1_ = bf16[256,256]{1,0:T(8,128)(2,1)S(1)} collective-permute-done((bf16[256,256]{1,0:T(8,128)(2,1)S(1)}, bf16[256,256]{1,0:T(8,128)(2,1)S(1)}, u32[]{:S(2)}, u32[]{:S(2)}) %collective-permute-start.22) | collective-permute-done | bytes 131104 | tf_op jit(solution)/shard_map/ppermute | solution.py:97
  94.6 1.4 shard_map.84
  96.1 3.2 %collective-permute-start.27 = (bf16[256,256]{1,0:T(8,128)(2,1)S(1)}, bf16[256,256]{1,0:T(8,128)(2,1)S(1)}, u32[]{:S(2)}, u32[]{:S(2)}) collective-permute-start(bf16[256,256]{1,0:T(8,128)(2,1)S(1)} %get-tuple-element.97.refs_2_), channel_id=1, source_target_pairs={{0,2},{1,3},{2,4},{3,5},{4,6},{5,7},{6,0},{7,1},{8,10},{9,11},{10,... | collective-permute-start | bytes 393224 | tf_op jit(solution)/shard_map/ppermute | solution.py:97
  100.3 1.3 collective-permute-start.25
  101.6 3.4 %shard_map.85 = (bf16[768,2048]{1,0:T(8,128)(2,1)}, f32[8,128]{1,0:T(8,128)S(1)}) custom-call(s32[1]{0:T(128)} %bitcast.me_ref, s32[32,8,128]{2,1,0:T(8,128)S(1)} %all-to-all-done.letter_ref, f32[8,128]{1,0:T(8,128)S(1)} %get-tuple-element.95.after_ref), custom_call_target="tpu_custom_call" | custom-call | flops 3449999872 | tf_op jit(solution)/shard_map/pallas_call | solution.py:319
  105.0 3.5 %shard_map.86 = (bf16[768,2048]{1,0:T(8,128)(2,1)}, f32[8,128]{1,0:T(8,128)S(1)}) custom-call(s32[1]{0:T(128)} %bitcast.me_ref, s32[32,8,128]{2,1,0:T(8,128)S(1)} %all-to-all-done.letter_ref, f32[8,128]{1,0:T(8,128)S(1)} %get-tuple-element.98.after_ref), custom_call_target="tpu_custom_call" | custom-call | flops 3449999872 | tf_op jit(solution)/shard_map/pallas_call | solution.py:319
  109.1 1.4 collective-permute-done.24.refs_3_
  113.5 1.7 %collective-permute-start.31 = (bf16[256,256]{1,0:T(8,128)(2,1)S(1)}, bf16[256,256]{1,0:T(8,128)(2,1)S(1)}, u32[]{:S(2)}, u32[]{:S(2)}) collective-permute-start(bf16[256,256]{1,0:T(8,128)(2,1)S(1)} %get-tuple-element.103), channel_id=1, source_target_pairs={{0,17},{1,16},{2,19},{3,18},{4,21},{5,20},{6,23},{7,22},{8,25},{9,... | collective-permute-start | bytes 393224 | tf_op jit(solution)/shard_map/ppermute | solution.py:97
  118.2 1.3 collective-permute-done.29.refs_0_
  120.5 1.5 collective-permute-done.30.refs_1_
  122.0 1.6 %shard_map.92 = (bf16[256,256]{1,0:T(8,128)(2,1)}, f32[256,256]{1,0:T(8,128)}, bf16[256,256]{1,0:T(8,128)(2,1)S(1)}, f32[8,128]{1,0:T(8,128)S(1)}) custom-call(f32[1]{0:T(128)} %get-tuple-element.114.weight_ref, f32[256,256]{1,0:T(8,128)S(1)} %get-tuple-element.100.own_ref, bf16[256,256]{1,0:T(8,128)(2,1)S(1)} %collective-permute-done.29.refs_0_, ...), custom_call_target="tpu_custom_call" | custom-call | flops 1150000000 | tf_op jit(solution)/shard_map/pallas_call | solution.py:491
  123.7 2.9 %collective-permute-start.35 = (bf16[256,256]{1,0:T(8,128)(2,1)S(1)}, bf16[256,256]{1,0:T(8,128)(2,1)S(1)}, u32[]{:S(2)}, u32[]{:S(2)}) collective-permute-start(bf16[256,256]{1,0:T(8,128)(2,1)S(1)} %get-tuple-element.106.refs_1_), channel_id=1, source_target_pairs={{0,2},{1,3},{2,4},{3,5},{4,6},{5,7},{6,0},{7,1},{8,10},{9,11},{10,... | collective-permute-start | bytes 393224 | tf_op jit(solution)/shard_map/ppermute | solution.py:97
  126.6 1.7 %collective-permute-start.34 = (bf16[256,256]{1,0:T(8,128)(2,1)S(1)}, bf16[256,256]{1,0:T(8,128)(2,1)S(1)}, u32[]{:S(2)}, u32[]{:S(2)}) collective-permute-start(bf16[256,256]{1,0:T(8,128)(2,1)S(1)} %get-tuple-element.106.refs_1_), channel_id=1, source_target_pairs={{0,4},{1,5},{2,6},{3,7},{4,0},{5,1},{6,2},{7,3},{8,12},{9,13},{10,... | collective-permute-start | bytes 393224 | tf_op jit(solution)/shard_map/ppermute | solution.py:97
  128.9 3.2 %collective-permute-done.35.refs_2_ = bf16[256,256]{1,0:T(8,128)(2,1)S(1)} collective-permute-done((bf16[256,256]{1,0:T(8,128)(2,1)S(1)}, bf16[256,256]{1,0:T(8,128)(2,1)S(1)}, u32[]{:S(2)}, u32[]{:S(2)}) %collective-permute-start.35) | collective-permute-done | bytes 131104 | tf_op jit(solution)/shard_map/ppermute | solution.py:97
  132.2 4.1 %collective-permute-done.34.refs_1_ = bf16[256,256]{1,0:T(8,128)(2,1)S(1)} collective-permute-done((bf16[256,256]{1,0:T(8,128)(2,1)S(1)}, bf16[256,256]{1,0:T(8,128)(2,1)S(1)}, u32[]{:S(2)}, u32[]{:S(2)}) %collective-permute-start.34) | collective-permute-done | bytes 131104 | tf_op jit(solution)/shard_map/ppermute | solution.py:97
  137.0 1.4 collective-permute-done.32.refs_2_
  139.5 1.5 collective-permute-start.37
  142.1 1.4 collective-permute-start.39
  146.5 4.0 %collective-permute-done.37.refs_0_ = bf16[384,256]{1,0:T(8,128)(2,1)S(1)} collective-permute-done((bf16[384,256]{1,0:T(8,128)(2,1)S(1)}, bf16[384,256]{1,0:T(8,128)(2,1)S(1)}, u32[]{:S(2)}, u32[]{:S(2)}) %collective-permute-start.37) | collective-permute-done | bytes 196640 | tf_op jit(solution)/shard_map/ppermute | solution.py:97
  150.8 2.7 %collective-permute-done.38.refs_1_ = bf16[384,256]{1,0:T(8,128)(2,1)S(1)} collective-permute-done((bf16[384,256]{1,0:T(8,128)(2,1)S(1)}, bf16[384,256]{1,0:T(8,128)(2,1)S(1)}, u32[]{:S(2)}, u32[]{:S(2)}) %collective-permute-start.38) | collective-permute-done | bytes 196640 | tf_op jit(solution)/shard_map/ppermute | solution.py:97
  (99 shorter events, 37.9 us)
Async XLA Ops:
  0.6 9.9 %copy-start.2 = (bf16[384,256]{1,0:T(8,128)(2,1)S(1)}, bf16[384,256]{1,0:T(8,128)(2,1)}, u32[]{:S(2)}) copy-start(bf16[384,256]{1,0:T(8,128)(2,1)} %current_ref.1) | copy-start | bytes 589828
  3.3 15.1 %all-to-all-start = ((s32[32,8,128]{2,1,0:T(8,128)}), s32[32,8,128]{2,1,0:T(8,128)S(1)}, u32[]{:S(2)}, u32[]{:S(2)}) async-start(s32[32,8,128]{2,1,0:T(8,128)} %shard_map.59), calls=%async_computation | async-start | bytes 262144 | tf_op jit(solution)/shard_map/all_to_all | solution.py:568
  10.6 9.9 %collective-permute-start.3 = (bf16[384,256]{1,0:T(8,128)(2,1)S(1)}, bf16[384,256]{1,0:T(8,128)(2,1)S(1)}, u32[]{:S(2)}, u32[]{:S(2)}) collective-permute-start(bf16[384,256]{1,0:T(8,128)(2,1)S(1)} %copy-done.2), channel_id=1, source_target_pairs={{0,17},{1,16},{2,19},{3,18},{4,21},{5,20},{6,23},{7,22},{8,25},{9,... | collective-permute-start | bytes 589832 | tf_op jit(solution)/shard_map/ppermute | solution.py:97
  13.3 10.6 %collective-permute-start.2 = (bf16[384,256]{1,0:T(8,128)(2,1)S(1)}, bf16[384,256]{1,0:T(8,128)(2,1)S(1)}, u32[]{:S(2)}, u32[]{:S(2)}) collective-permute-start(bf16[384,256]{1,0:T(8,128)(2,1)S(1)} %copy-done.2), channel_id=1, source_target_pairs={{0,16},{1,17},{2,18},{3,19},{4,20},{5,21},{6,22},{7,23},{8,24},{9,... | collective-permute-start | bytes 589832 | tf_op jit(solution)/shard_map/ppermute | solution.py:97
  13.9 10.2 %collective-permute-start.1 = (bf16[384,256]{1,0:T(8,128)(2,1)S(1)}, bf16[384,256]{1,0:T(8,128)(2,1)S(1)}, u32[]{:S(2)}, u32[]{:S(2)}) collective-permute-start(bf16[384,256]{1,0:T(8,128)(2,1)S(1)} %copy-done.2), channel_id=1, source_target_pairs={{0,1},{1,0},{2,3},{3,2},{4,5},{5,4},{6,7},{7,6},{8,9},{9,8},{10,11... | collective-permute-start | bytes 589832 | tf_op jit(solution)/shard_map/ppermute | solution.py:97
  24.1 2.4 %collective-permute-start.4 = (bf16[1152,256]{1,0:T(8,128)(2,1)S(1)}, bf16[1152,256]{1,0:T(8,128)(2,1)S(1)}, u32[]{:S(2)}, u32[]{:S(2)}) collective-permute-start(bf16[1152,256]{1,0:T(8,128)(2,1)S(1)} %shard_map.61.refs_3_), channel_id=1, source_target_pairs={{0,8},{1,9},{2,10},{3,11},{4,12},{5,13},{6,14},{7,15},{8,0},{9,1},... | collective-permute-start | bytes 1769480 | tf_op jit(solution)/shard_map/ppermute | solution.py:97
  24.2 2.3 %collective-permute-start = (bf16[384,256]{1,0:T(8,128)(2,1)S(1)}, bf16[384,256]{1,0:T(8,128)(2,1)S(1)}, u32[]{:S(2)}, u32[]{:S(2)}) collective-permute-start(bf16[384,256]{1,0:T(8,128)(2,1)S(1)} %copy-done.2), channel_id=1, source_target_pairs={{0,8},{1,9},{2,10},{3,11},{4,12},{5,13},{6,14},{7,15},{8,0},{9,1},... | collective-permute-start | bytes 589832 | tf_op jit(solution)/shard_map/ppermute | solution.py:97
  27.7 12.9 %collective-permute-start.5 = (bf16[256,256]{1,0:T(8,128)(2,1)S(1)}, bf16[256,256]{1,0:T(8,128)(2,1)S(1)}, u32[]{:S(2)}, u32[]{:S(2)}) collective-permute-start(bf16[256,256]{1,0:T(8,128)(2,1)S(1)} %get-tuple-element.61), channel_id=1, source_target_pairs={{0,2},{1,3},{2,4},{3,5},{4,6},{5,7},{6,0},{7,1},{8,10},{9,11},{10,... | collective-permute-start | bytes 393224 | tf_op jit(solution)/shard_map/ppermute | solution.py:97
  30.3 10.5 %collective-permute-start.6 = (bf16[256,256]{1,0:T(8,128)(2,1)S(1)}, bf16[256,256]{1,0:T(8,128)(2,1)S(1)}, u32[]{:S(2)}, u32[]{:S(2)}) collective-permute-start(bf16[256,256]{1,0:T(8,128)(2,1)S(1)} %get-tuple-element.62), channel_id=1, source_target_pairs={{0,4},{1,5},{2,6},{3,7},{4,0},{5,1},{6,2},{7,3},{8,12},{9,13},{10,... | collective-permute-start | bytes 393224 | tf_op jit(solution)/shard_map/ppermute | solution.py:97
  33.4 7.7 %collective-permute-start.7 = (bf16[256,256]{1,0:T(8,128)(2,1)S(1)}, bf16[256,256]{1,0:T(8,128)(2,1)S(1)}, u32[]{:S(2)}, u32[]{:S(2)}) collective-permute-start(bf16[256,256]{1,0:T(8,128)(2,1)S(1)} %get-tuple-element.63), channel_id=1, source_target_pairs={{0,6},{1,7},{2,0},{3,1},{4,2},{5,3},{6,4},{7,5},{8,14},{9,15},{10,... | collective-permute-start | bytes 393224 | tf_op jit(solution)/shard_map/ppermute | solution.py:97
  41.3 13.4 %collective-permute-start.11 = (bf16[256,256]{1,0:T(8,128)(2,1)S(1)}, bf16[256,256]{1,0:T(8,128)(2,1)S(1)}, u32[]{:S(2)}, u32[]{:S(2)}) collective-permute-start(bf16[256,256]{1,0:T(8,128)(2,1)S(1)} %get-tuple-element.72.refs_2_), channel_id=1, source_target_pairs={{0,2},{1,3},{2,4},{3,5},{4,6},{5,7},{6,0},{7,1},{8,10},{9,11},{10,... | collective-permute-start | bytes 393224 | tf_op jit(solution)/shard_map/ppermute | solution.py:97
  44.2 10.5 %collective-permute-start.10 = (bf16[256,256]{1,0:T(8,128)(2,1)S(1)}, bf16[256,256]{1,0:T(8,128)(2,1)S(1)}, u32[]{:S(2)}, u32[]{:S(2)}) collective-permute-start(bf16[256,256]{1,0:T(8,128)(2,1)S(1)} %get-tuple-element.72.refs_2_), channel_id=1, source_target_pairs={{0,4},{1,5},{2,6},{3,7},{4,0},{5,1},{6,2},{7,3},{8,12},{9,13},{10,... | collective-permute-start | bytes 393224 | tf_op jit(solution)/shard_map/ppermute | solution.py:97
  45.5 9.2 %collective-permute-start.9 = (bf16[256,256]{1,0:T(8,128)(2,1)S(1)}, bf16[256,256]{1,0:T(8,128)(2,1)S(1)}, u32[]{:S(2)}, u32[]{:S(2)}) collective-permute-start(bf16[256,256]{1,0:T(8,128)(2,1)S(1)} %get-tuple-element.72.refs_2_), channel_id=1, source_target_pairs={{0,6},{1,7},{2,0},{3,1},{4,2},{5,3},{6,4},{7,5},{8,14},{9,15},{10,... | collective-permute-start | bytes 393224 | tf_op jit(solution)/shard_map/ppermute | solution.py:97
  54.8 2.0 %collective-permute-start.12 = (bf16[768,256]{1,0:T(8,128)(2,1)S(1)}, bf16[768,256]{1,0:T(8,128)(2,1)S(1)}, u32[]{:S(2)}, u32[]{:S(2)}) collective-permute-start(bf16[768,256]{1,0:T(8,128)(2,1)S(1)} %shard_map.70.refs_4_), channel_id=1, source_target_pairs={{0,8},{1,9},{2,10},{3,11},{4,12},{5,13},{6,14},{7,15},{8,0},{9,1},... | collective-permute-start | bytes 1179656 | tf_op jit(solution)/shard_map/ppermute | solution.py:97
  54.8 1.9 %collective-permute-start.8 = (bf16[256,256]{1,0:T(8,128)(2,1)S(1)}, bf16[256,256]{1,0:T(8,128)(2,1)S(1)}, u32[]{:S(2)}, u32[]{:S(2)}) collective-permute-start(bf16[256,256]{1,0:T(8,128)(2,1)S(1)} %get-tuple-element.72.refs_2_), channel_id=1, source_target_pairs={{0,8},{1,9},{2,10},{3,11},{4,12},{5,13},{6,14},{7,15},{8,0},{9,1},... | collective-permute-start | bytes 393224 | tf_op jit(solution)/shard_map/ppermute | solution.py:97
  57.9 9.9 %collective-permute-start.13 = (bf16[256,256]{1,0:T(8,128)(2,1)S(1)}, bf16[256,256]{1,0:T(8,128)(2,1)S(1)}, u32[]{:S(2)}, u32[]{:S(2)}) collective-permute-start(bf16[256,256]{1,0:T(8,128)(2,1)S(1)} %get-tuple-element.75), channel_id=1, source_target_pairs={{0,1},{1,0},{2,3},{3,2},{4,5},{5,4},{6,7},{7,6},{8,9},{9,8},{10,11... | collective-permute-start | bytes 393224 | tf_op jit(solution)/shard_map/ppermute | solution.py:97
  60.1 7.6 %collective-permute-start.14 = (bf16[256,256]{1,0:T(8,128)(2,1)S(1)}, bf16[256,256]{1,0:T(8,128)(2,1)S(1)}, u32[]{:S(2)}, u32[]{:S(2)}) collective-permute-start(bf16[256,256]{1,0:T(8,128)(2,1)S(1)} %get-tuple-element.78), channel_id=1, source_target_pairs={{0,16},{1,17},{2,18},{3,19},{4,20},{5,21},{6,22},{7,23},{8,24},{9,... | collective-permute-start | bytes 393224 | tf_op jit(solution)/shard_map/ppermute | solution.py:97
  62.3 6.3 %collective-permute-start.15 = (bf16[256,256]{1,0:T(8,128)(2,1)S(1)}, bf16[256,256]{1,0:T(8,128)(2,1)S(1)}, u32[]{:S(2)}, u32[]{:S(2)}) collective-permute-start(bf16[256,256]{1,0:T(8,128)(2,1)S(1)} %get-tuple-element.79), channel_id=1, source_target_pairs={{0,17},{1,16},{2,19},{3,18},{4,21},{5,20},{6,23},{7,22},{8,25},{9,... | collective-permute-start | bytes 393224 | tf_op jit(solution)/shard_map/ppermute | solution.py:97
  69.9 11.5 %collective-permute-start.19 = (bf16[256,256]{1,0:T(8,128)(2,1)S(1)}, bf16[256,256]{1,0:T(8,128)(2,1)S(1)}, u32[]{:S(2)}, u32[]{:S(2)}) collective-permute-start(bf16[256,256]{1,0:T(8,128)(2,1)S(1)} %get-tuple-element.82.refs_1_.potential_ref), channel_id=1, source_target_pairs={{0,2},{1,3},{2,4},{3,5},{4,6},{5,7},{6,0},{7,1},{8,10},{9,11},{10,... | collective-permute-start | bytes 393224 | tf_op jit(solution)/shard_map/ppermute | solution.py:97
  72.2 9.9 %collective-permute-start.18 = (bf16[256,256]{1,0:T(8,128)(2,1)S(1)}, bf16[256,256]{1,0:T(8,128)(2,1)S(1)}, u32[]{:S(2)}, u32[]{:S(2)}) collective-permute-start(bf16[256,256]{1,0:T(8,128)(2,1)S(1)} %get-tuple-element.82.refs_1_.potential_ref), channel_id=1, source_target_pairs={{0,4},{1,5},{2,6},{3,7},{4,0},{5,1},{6,2},{7,3},{8,12},{9,13},{10,... | collective-permute-start | bytes 393224 | tf_op jit(solution)/shard_map/ppermute | solution.py:97
  74.4 7.9 %collective-permute-start.17 = (bf16[256,256]{1,0:T(8,128)(2,1)S(1)}, bf16[256,256]{1,0:T(8,128)(2,1)S(1)}, u32[]{:S(2)}, u32[]{:S(2)}) collective-permute-start(bf16[256,256]{1,0:T(8,128)(2,1)S(1)} %get-tuple-element.82.refs_1_.potential_ref), channel_id=1, source_target_pairs={{0,6},{1,7},{2,0},{3,1},{4,2},{5,3},{6,4},{7,5},{8,14},{9,15},{10,... | collective-permute-start | bytes 393224 | tf_op jit(solution)/shard_map/ppermute | solution.py:97
  81.4 3.0 %copy-start.8 = (bf16[256,2048]{1,0:T(8,128)(2,1)S(1)}, bf16[256,2048]{1,0:T(8,128)(2,1)}, u32[]{:S(2)}) copy-start(bf16[256,2048]{1,0:T(8,128)(2,1)} %get-tuple-element.92.refs_0_) | copy-start | bytes 3145732
  82.3 4.5 %copy-start.7 = (bf16[256,2048]{1,0:T(8,128)(2,1)S(1)}, bf16[256,2048]{1,0:T(8,128)(2,1)}, u32[]{:S(2)}) copy-start(bf16[256,2048]{1,0:T(8,128)(2,1)} %get-tuple-element.90.refs_0_) | copy-start | bytes 3145732
  82.4 2.0 %collective-permute-start.20 = (bf16[768,256]{1,0:T(8,128)(2,1)S(1)}, bf16[768,256]{1,0:T(8,128)(2,1)S(1)}, u32[]{:S(2)}, u32[]{:S(2)}) collective-permute-start(bf16[768,256]{1,0:T(8,128)(2,1)S(1)} %shard_map.79.refs_3_), channel_id=1, source_target_pairs={{0,8},{1,9},{2,10},{3,11},{4,12},{5,13},{6,14},{7,15},{8,0},{9,1},... | collective-permute-start | bytes 1179656 | tf_op jit(solution)/shard_map/ppermute | solution.py:97
  82.4 1.9 %collective-permute-start.16 = (bf16[256,256]{1,0:T(8,128)(2,1)S(1)}, bf16[256,256]{1,0:T(8,128)(2,1)S(1)}, u32[]{:S(2)}, u32[]{:S(2)}) collective-permute-start(bf16[256,256]{1,0:T(8,128)(2,1)S(1)} %get-tuple-element.82.refs_1_.potential_ref), channel_id=1, source_target_pairs={{0,8},{1,9},{2,10},{3,11},{4,12},{5,13},{6,14},{7,15},{8,0},{9,1},... | collective-permute-start | bytes 393224 | tf_op jit(solution)/shard_map/ppermute | solution.py:97
  84.3 4.2 %copy-start.6 = (bf16[256,2048]{1,0:T(8,128)(2,1)S(1)}, bf16[256,2048]{1,0:T(8,128)(2,1)}, u32[]{:S(2)}) copy-start(bf16[256,2048]{1,0:T(8,128)(2,1)} %get-tuple-element.88.refs_0_) | copy-start | bytes 3145732
  84.8 7.3 %collective-permute-start.23 = (bf16[256,256]{1,0:T(8,128)(2,1)S(1)}, bf16[256,256]{1,0:T(8,128)(2,1)S(1)}, u32[]{:S(2)}, u32[]{:S(2)}) collective-permute-start(bf16[256,256]{1,0:T(8,128)(2,1)S(1)} %get-tuple-element.93), channel_id=1, source_target_pairs={{0,17},{1,16},{2,19},{3,18},{4,21},{5,20},{6,23},{7,22},{8,25},{9,... | collective-permute-start | bytes 393224 | tf_op jit(solution)/shard_map/ppermute | solution.py:97
  86.9 3.2 %copy-start.5 = (bf16[256,2048]{1,0:T(8,128)(2,1)S(1)}, bf16[256,2048]{1,0:T(8,128)(2,1)}, u32[]{:S(2)}) copy-start(bf16[256,2048]{1,0:T(8,128)(2,1)} %get-tuple-element.83.refs_0_) | copy-start | bytes 3145732
  87.7 6.3 %collective-permute-start.22 = (bf16[256,256]{1,0:T(8,128)(2,1)S(1)}, bf16[256,256]{1,0:T(8,128)(2,1)S(1)}, u32[]{:S(2)}, u32[]{:S(2)}) collective-permute-start(bf16[256,256]{1,0:T(8,128)(2,1)S(1)} %get-tuple-element.91), channel_id=1, source_target_pairs={{0,16},{1,17},{2,18},{3,19},{4,20},{5,21},{6,22},{7,23},{8,24},{9,... | collective-permute-start | bytes 393224 | tf_op jit(solution)/shard_map/ppermute | solution.py:97
  89.4 5.2 %collective-permute-start.21 = (bf16[256,256]{1,0:T(8,128)(2,1)S(1)}, bf16[256,256]{1,0:T(8,128)(2,1)S(1)}, u32[]{:S(2)}, u32[]{:S(2)}) collective-permute-start(bf16[256,256]{1,0:T(8,128)(2,1)S(1)} %get-tuple-element.89), channel_id=1, source_target_pairs={{0,1},{1,0},{2,3},{3,2},{4,5},{5,4},{6,7},{7,6},{8,9},{9,8},{10,11... | collective-permute-start | bytes 393224 | tf_op jit(solution)/shard_map/ppermute | solution.py:97
  96.1 12.4 %collective-permute-start.27 = (bf16[256,256]{1,0:T(8,128)(2,1)S(1)}, bf16[256,256]{1,0:T(8,128)(2,1)S(1)}, u32[]{:S(2)}, u32[]{:S(2)}) collective-permute-start(bf16[256,256]{1,0:T(8,128)(2,1)S(1)} %get-tuple-element.97.refs_2_), channel_id=1, source_target_pairs={{0,2},{1,3},{2,4},{3,5},{4,6},{5,7},{6,0},{7,1},{8,10},{9,11},{10,... | collective-permute-start | bytes 393224 | tf_op jit(solution)/shard_map/ppermute | solution.py:97
  99.2 9.3 %collective-permute-start.26 = (bf16[256,256]{1,0:T(8,128)(2,1)S(1)}, bf16[256,256]{1,0:T(8,128)(2,1)S(1)}, u32[]{:S(2)}, u32[]{:S(2)}) collective-permute-start(bf16[256,256]{1,0:T(8,128)(2,1)S(1)} %get-tuple-element.97.refs_2_), channel_id=1, source_target_pairs={{0,4},{1,5},{2,6},{3,7},{4,0},{5,1},{6,2},{7,3},{8,12},{9,13},{10,... | collective-permute-start | bytes 393224 | tf_op jit(solution)/shard_map/ppermute | solution.py:97
  100.3 8.2 %collective-permute-start.25 = (bf16[256,256]{1,0:T(8,128)(2,1)S(1)}, bf16[256,256]{1,0:T(8,128)(2,1)S(1)}, u32[]{:S(2)}, u32[]{:S(2)}) collective-permute-start(bf16[256,256]{1,0:T(8,128)(2,1)S(1)} %get-tuple-element.97.refs_2_), channel_id=1, source_target_pairs={{0,6},{1,7},{2,0},{3,1},{4,2},{5,3},{6,4},{7,5},{8,14},{9,15},{10,... | collective-permute-start | bytes 393224 | tf_op jit(solution)/shard_map/ppermute | solution.py:97
  108.5 2.0 %collective-permute-start.28 = (bf16[768,256]{1,0:T(8,128)(2,1)S(1)}, bf16[768,256]{1,0:T(8,128)(2,1)S(1)}, u32[]{:S(2)}, u32[]{:S(2)}) collective-permute-start(bf16[768,256]{1,0:T(8,128)(2,1)S(1)} %shard_map.87.refs_4_), channel_id=1, source_target_pairs={{0,8},{1,9},{2,10},{3,11},{4,12},{5,13},{6,14},{7,15},{8,0},{9,1},... | collective-permute-start | bytes 1179656 | tf_op jit(solution)/shard_map/ppermute | solution.py:97
  108.6 1.9 %collective-permute-start.24 = (bf16[256,256]{1,0:T(8,128)(2,1)S(1)}, bf16[256,256]{1,0:T(8,128)(2,1)S(1)}, u32[]{:S(2)}, u32[]{:S(2)}) collective-permute-start(bf16[256,256]{1,0:T(8,128)(2,1)S(1)} %get-tuple-element.97.refs_2_), channel_id=1, source_target_pairs={{0,8},{1,9},{2,10},{3,11},{4,12},{5,13},{6,14},{7,15},{8,0},{9,1},... | collective-permute-start | bytes 393224 | tf_op jit(solution)/shard_map/ppermute | solution.py:97
  111.7 7.9 %collective-permute-start.29 = (bf16[256,256]{1,0:T(8,128)(2,1)S(1)}, bf16[256,256]{1,0:T(8,128)(2,1)S(1)}, u32[]{:S(2)}, u32[]{:S(2)}) collective-permute-start(bf16[256,256]{1,0:T(8,128)(2,1)S(1)} %get-tuple-element.101), channel_id=1, source_target_pairs={{0,1},{1,0},{2,3},{3,2},{4,5},{5,4},{6,7},{7,6},{8,9},{9,8},{10,11... | collective-permute-start | bytes 393224 | tf_op jit(solution)/shard_map/ppermute | solution.py:97
  113.5 7.0 %collective-permute-start.31 = (bf16[256,256]{1,0:T(8,128)(2,1)S(1)}, bf16[256,256]{1,0:T(8,128)(2,1)S(1)}, u32[]{:S(2)}, u32[]{:S(2)}) collective-permute-start(bf16[256,256]{1,0:T(8,128)(2,1)S(1)} %get-tuple-element.103), channel_id=1, source_target_pairs={{0,17},{1,16},{2,19},{3,18},{4,21},{5,20},{6,23},{7,22},{8,25},{9,... | collective-permute-start | bytes 393224 | tf_op jit(solution)/shard_map/ppermute | solution.py:97
  116.3 5.7 %collective-permute-start.30 = (bf16[256,256]{1,0:T(8,128)(2,1)S(1)}, bf16[256,256]{1,0:T(8,128)(2,1)S(1)}, u32[]{:S(2)}, u32[]{:S(2)}) collective-permute-start(bf16[256,256]{1,0:T(8,128)(2,1)S(1)} %get-tuple-element.102), channel_id=1, source_target_pairs={{0,16},{1,17},{2,18},{3,19},{4,20},{5,21},{6,22},{7,23},{8,24},{9,... | collective-permute-start | bytes 393224 | tf_op jit(solution)/shard_map/ppermute | solution.py:97
  122.0 16.4 %copy-start = (bf16[768,2048]{1,0:T(8,128)(2,1)S(1)}, bf16[768,2048]{1,0:T(8,128)(2,1)}, u32[]{:S(2)}) copy-start(bf16[768,2048]{1,0:T(8,128)(2,1)} %get-tuple-element.96.refs_0_) | copy-start | bytes 9437188
  123.7 8.5 %collective-permute-start.35 = (bf16[256,256]{1,0:T(8,128)(2,1)S(1)}, bf16[256,256]{1,0:T(8,128)(2,1)S(1)}, u32[]{:S(2)}, u32[]{:S(2)}) collective-permute-start(bf16[256,256]{1,0:T(8,128)(2,1)S(1)} %get-tuple-element.106.refs_1_), channel_id=1, source_target_pairs={{0,2},{1,3},{2,4},{3,5},{4,6},{5,7},{6,0},{7,1},{8,10},{9,11},{10,... | collective-permute-start | bytes 393224 | tf_op jit(solution)/shard_map/ppermute | solution.py:97
  126.6 9.7 %collective-permute-start.34 = (bf16[256,256]{1,0:T(8,128)(2,1)S(1)}, bf16[256,256]{1,0:T(8,128)(2,1)S(1)}, u32[]{:S(2)}, u32[]{:S(2)}) collective-permute-start(bf16[256,256]{1,0:T(8,128)(2,1)S(1)} %get-tuple-element.106.refs_1_), channel_id=1, source_target_pairs={{0,4},{1,5},{2,6},{3,7},{4,0},{5,1},{6,2},{7,3},{8,12},{9,13},{10,... | collective-permute-start | bytes 393224 | tf_op jit(solution)/shard_map/ppermute | solution.py:97
  128.3 8.1 %collective-permute-start.33 = (bf16[256,256]{1,0:T(8,128)(2,1)S(1)}, bf16[256,256]{1,0:T(8,128)(2,1)S(1)}, u32[]{:S(2)}, u32[]{:S(2)}) collective-permute-start(bf16[256,256]{1,0:T(8,128)(2,1)S(1)} %get-tuple-element.106.refs_1_), channel_id=1, source_target_pairs={{0,6},{1,7},{2,0},{3,1},{4,2},{5,3},{6,4},{7,5},{8,14},{9,15},{10,... | collective-permute-start | bytes 393224 | tf_op jit(solution)/shard_map/ppermute | solution.py:97
  136.4 2.0 %collective-permute-start.36 = (bf16[768,256]{1,0:T(8,128)(2,1)S(1)}, bf16[768,256]{1,0:T(8,128)(2,1)S(1)}, u32[]{:S(2)}, u32[]{:S(2)}) collective-permute-start(bf16[768,256]{1,0:T(8,128)(2,1)S(1)} %shard_map.93.refs_3_), channel_id=1, source_target_pairs={{0,8},{1,9},{2,10},{3,11},{4,12},{5,13},{6,14},{7,15},{8,0},{9,1},... | collective-permute-start | bytes 1179656 | tf_op jit(solution)/shard_map/ppermute | solution.py:97
  136.5 1.9 %collective-permute-start.32 = (bf16[256,256]{1,0:T(8,128)(2,1)S(1)}, bf16[256,256]{1,0:T(8,128)(2,1)S(1)}, u32[]{:S(2)}, u32[]{:S(2)}) collective-permute-start(bf16[256,256]{1,0:T(8,128)(2,1)S(1)} %get-tuple-element.106.refs_1_), channel_id=1, source_target_pairs={{0,8},{1,9},{2,10},{3,11},{4,12},{5,13},{6,14},{7,15},{8,0},{9,1},... | collective-permute-start | bytes 393224 | tf_op jit(solution)/shard_map/ppermute | solution.py:97
  138.4 2.6 %copy-start.1 = (bf16[768,2048]{1,0:T(8,128)(2,1)S(1)}, bf16[768,2048]{1,0:T(8,128)(2,1)}, u32[]{:S(2)}) copy-start(bf16[768,2048]{1,0:T(8,128)(2,1)} %get-tuple-element.110.refs_0_) | copy-start | bytes 9437188
  139.5 11.0 %collective-permute-start.37 = (bf16[384,256]{1,0:T(8,128)(2,1)S(1)}, bf16[384,256]{1,0:T(8,128)(2,1)S(1)}, u32[]{:S(2)}, u32[]{:S(2)}) collective-permute-start(bf16[384,256]{1,0:T(8,128)(2,1)S(1)} %get-tuple-element.109), channel_id=1, source_target_pairs={{0,1},{1,0},{2,3},{3,2},{4,5},{5,4},{6,7},{7,6},{8,9},{9,8},{10,11... | collective-permute-start | bytes 589832 | tf_op jit(solution)/shard_map/ppermute | solution.py:97
  142.1 8.7 %collective-permute-start.39 = (bf16[384,256]{1,0:T(8,128)(2,1)S(1)}, bf16[384,256]{1,0:T(8,128)(2,1)S(1)}, u32[]{:S(2)}, u32[]{:S(2)}) collective-permute-start(bf16[384,256]{1,0:T(8,128)(2,1)S(1)} %get-tuple-element.112), channel_id=1, source_target_pairs={{0,17},{1,16},{2,19},{3,18},{4,21},{5,20},{6,23},{7,22},{8,25},{9,... | collective-permute-start | bytes 589832 | tf_op jit(solution)/shard_map/ppermute | solution.py:97
  144.5 9.0 %collective-permute-start.38 = (bf16[384,256]{1,0:T(8,128)(2,1)S(1)}, bf16[384,256]{1,0:T(8,128)(2,1)S(1)}, u32[]{:S(2)}, u32[]{:S(2)}) collective-permute-start(bf16[384,256]{1,0:T(8,128)(2,1)S(1)} %get-tuple-element.111), channel_id=1, source_target_pairs={{0,16},{1,17},{2,18},{3,19},{4,20},{5,21},{6,22},{7,23},{8,24},{9,... | collective-permute-start | bytes 589832 | tf_op jit(solution)/shard_map/ppermute | solution.py:97
  (3 other events, 2.1 us)

commit v13 on v12

--- a/solution.py
+++ b/solution.py
@@ -475,28 +475,26 @@
     total = own_ref[...]
     for ref in refs[:count]:
         total = total + ref[...].astype(F32)
-    out_ref, sum_ref, rounded_ref, token_ref = refs[-4:]
+    out_ref, sum_ref, token_ref = refs[-3:]
     potential = total.astype(BF16)
     out_ref[...] = potential
     value = weight_ref[0] * potential.astype(F32)
     if summed:
         value = value + refs[count][...]
-    sum_ref[...] = value
-    rounded_ref[...] = value.astype(BF16)
+    sum_ref[...] = value.astype(sum_ref.dtype)
     token_ref[...] = jnp.zeros_like(token_ref)
 
 
-def potential_of(weight, blocks, summed, after):
+def potential_of(weight, blocks, summed, after, last):
     shape = blocks[0].shape
     return pl.pallas_call(
         functools.partial(potential_kernel, len(blocks) - 1, len(summed)),
         in_specs=[pl.BlockSpec(memory_space=pltpu.SMEM)]
         + [whole()] * (len(blocks) + len(summed) + len(after)),
-        out_specs=[whole()] * 4,
+        out_specs=[whole()] * 3,
         out_shape=[
             jax.ShapeDtypeStruct(shape, BF16),
-            jax.ShapeDtypeStruct(shape, F32),
-            jax.ShapeDtypeStruct(shape, BF16),
+            jax.ShapeDtypeStruct(shape, BF16 if last else F32),
             TOKEN,
         ],
         compiler_params=PARAMS,
@@ -654,9 +652,10 @@
         blocks, token = multiply(tiles, pieces, tri_dev, resident)
         if not last:
             token = more_adjacency(count // 2, token)
-        potential, *summed, weighted, token = potential_of(
-            weight, layout.given(blocks), summed, (token,)
+        potential, weighted, token = potential_of(
+            weight, layout.given(blocks), summed, (token,), last
         )
+        summed = (weighted,)
         if last:
             break
         token = more_adjacency(count, token)

time: 155 us -> 154 us (level)
  no operation moved by 1% of the time
where the time goes in v13:
time: 154 us
  Pallas kernels  57.2 us (37%)
  starting transfers between devices  54.3 us (35%)
  waiting for transfers between devices  38.8 us (25%)
  local copies, waits for them, and re-layouts  2.26 us (1%)
    ppermute x40, starting transfers between devices, shift(): return lax.ppermute(value, AXES, pairs)  47 us
    ppermute x40, waiting for transfers between devices, shift(): return lax.ppermute(value, AXES, pairs)  34.6 us
    pallas_call x9, Pallas kernels, build(): pl.pallas_call(kernel, grid=(len(span),), in_specs=[pl.BlockSpec(memory_s...  31.6 us
    pallas_call x20, Pallas kernels, apply(): pl.pallas_call(functools.partial(apply_kernel, mats, len(pieces), block,...  19.8 us
    all_to_all x1, starting transfers between devices, per_device(): lax.all_to_all(letters, AXES, split_axis=0, concat_axis=0, tiled=True)  7.3 us
    all_to_all x1, waiting for transfers between devices, per_device(): lax.all_to_all(letters, AXES, split_axis=0, concat_axis=0, tiled=True)  4.27 us
  transfers between devices with their start and end apart: 41, of which 25 were waited for; matrix products, arithmetic and copies ran while one was open for 1% of the time, Pallas kernels for 30%

profile of v13, /device:TPU:0, one launch (start us, length us, event | category | flops | bytes accessed | tf_op | source)
XLA Modules:
  0.0 153.5 jit_solution(5889469730533958983)
XLA Ops:
  2.1 1.2 shard_map.59
  3.3 7.3 %all-to-all-start = ((s32[32,8,128]{2,1,0:T(8,128)}), s32[32,8,128]{2,1,0:T(8,128)S(1)}, u32[]{:S(2)}, u32[]{:S(2)}) async-start(s32[32,8,128]{2,1,0:T(8,128)} %shard_map.59), calls=%async_computation | async-start | bytes 262144 | tf_op jit(solution)/shard_map/all_to_all | solution.py:566
  10.6 2.7 %collective-permute-start.3 = (bf16[384,256]{1,0:T(8,128)(2,1)S(1)}, bf16[384,256]{1,0:T(8,128)(2,1)S(1)}, u32[]{:S(2)}, u32[]{:S(2)}) collective-permute-start(bf16[384,256]{1,0:T(8,128)(2,1)S(1)} %copy-done.2), channel_id=1, source_target_pairs={{0,17},{1,16},{2,19},{3,18},{4,21},{5,20},{6,23},{7,22},{8,25},{9,... | collective-permute-start | bytes 589832 | tf_op jit(solution)/shard_map/ppermute | solution.py:97
  14.1 4.3 %all-to-all-done.letter_ref = s32[32,8,128]{2,1,0:T(8,128)S(1)} async-done(((s32[32,8,128]{2,1,0:T(8,128)}), s32[32,8,128]{2,1,0:T(8,128)S(1)}, u32[]{:S(2)}, u32[]{:S(2)}) %all-to-all-start) | async-done | bytes 131104 | tf_op jit(solution)/shard_map/all_to_all | solution.py:566
  18.7 1.8 %shard_map.60 = (bf16[1024,3072]{1,0:T(8,128)(2,1)S(1)}, f32[8,128]{1,0:T(8,128)S(1)}) custom-call(s32[1]{0:T(128)} %bitcast.me_ref, s32[32,8,128]{2,1,0:T(8,128)S(1)} %all-to-all-done.letter_ref, s32[4,1,2048]{2,1,0:T(1,128)S(1)} %reshape.11.after_ref.label_ref), custom_call_target="tpu_custom_call" | custom-call | flops 3449999872 | tf_op jit(solution)/shard_map/pallas_call | solution.py:319
  20.5 3.5 %collective-permute-done.2.refs_1_ = bf16[384,256]{1,0:T(8,128)(2,1)S(1)} collective-permute-done((bf16[384,256]{1,0:T(8,128)(2,1)S(1)}, bf16[384,256]{1,0:T(8,128)(2,1)S(1)}, u32[]{:S(2)}, u32[]{:S(2)}) %collective-permute-start.2) | collective-permute-done | bytes 196640 | tf_op jit(solution)/shard_map/ppermute | solution.py:97
  24.7 1.8 %collective-permute-done.refs_2_ = bf16[384,256]{1,0:T(8,128)(2,1)S(1)} collective-permute-done((bf16[384,256]{1,0:T(8,128)(2,1)S(1)}, bf16[384,256]{1,0:T(8,128)(2,1)S(1)}, u32[]{:S(2)}, u32[]{:S(2)}) %collective-permute-start) | collective-permute-done | bytes 196640 | tf_op jit(solution)/shard_map/ppermute | solution.py:97
  26.5 1.2 shard_map.63
  27.7 1.4 collective-permute-start.5
  29.1 1.2 shard_map.64
  30.3 2.5 %collective-permute-start.6 = (bf16[256,256]{1,0:T(8,128)(2,1)S(1)}, bf16[256,256]{1,0:T(8,128)(2,1)S(1)}, u32[]{:S(2)}, u32[]{:S(2)}) collective-permute-start(bf16[256,256]{1,0:T(8,128)(2,1)S(1)} %get-tuple-element.62), channel_id=1, source_target_pairs={{0,4},{1,5},{2,6},{3,7},{4,0},{5,1},{6,2},{7,3},{8,12},{9,13},{10,... | collective-permute-start | bytes 393224 | tf_op jit(solution)/shard_map/ppermute | solution.py:97
  33.4 1.3 collective-permute-start.7
  34.7 4.7 %shard_map.66 = (bf16[512,2048]{1,0:T(8,128)(2,1)S(1)}, bf16[512,2048]{1,0:T(8,128)(2,1)S(1)}, f32[8,128]{1,0:T(8,128)S(1)}) custom-call(s32[1]{0:T(128)} %bitcast.me_ref, s32[32,8,128]{2,1,0:T(8,128)S(1)} %all-to-all-done.letter_ref, f32[8,128]{1,0:T(8,128)S(1)} %get-tuple-element.64.after_ref), custom_call_target="tpu_custom_call" | custom-call | flops 6899999744 | tf_op jit(solution)/shard_map/pallas_call | solution.py:319
  39.4 1.2 shard_map.62
  41.3 2.9 %collective-permute-start.11 = (bf16[256,256]{1,0:T(8,128)(2,1)S(1)}, bf16[256,256]{1,0:T(8,128)(2,1)S(1)}, u32[]{:S(2)}, u32[]{:S(2)}) collective-permute-start(bf16[256,256]{1,0:T(8,128)(2,1)S(1)} %get-tuple-element.72.refs_2_), channel_id=1, source_target_pairs={{0,2},{1,3},{2,4},{3,5},{4,6},{5,7},{6,0},{7,1},{8,10},{9,11},{10,... | collective-permute-start | bytes 393224 | tf_op jit(solution)/shard_map/ppermute | solution.py:97
  44.2 1.3 collective-permute-start.10
  46.6 4.7 %shard_map.68 = (bf16[512,2048]{1,0:T(8,128)(2,1)S(1)}, bf16[512,2048]{1,0:T(8,128)(2,1)S(1)}, f32[8,128]{1,0:T(8,128)S(1)}) custom-call(s32[1]{0:T(128)} %bitcast.me_ref, s32[32,8,128]{2,1,0:T(8,128)S(1)} %all-to-all-done.letter_ref, f32[8,128]{1,0:T(8,128)S(1)} %get-tuple-element.67.after_ref), custom_call_target="tpu_custom_call" | custom-call | flops 6899999744 | tf_op jit(solution)/shard_map/pallas_call | solution.py:319
  51.3 3.4 %shard_map.69 = (bf16[256,2048]{1,0:T(8,128)(2,1)}, f32[256,128]{1,0:T(8,128)S(1)}, f32[8,128]{1,0:T(8,128)S(1)}) custom-call(s32[1]{0:T(128)} %bitcast.me_ref, s32[4,1,2048]{2,1,0:T(1,128)S(1)} %reshape.11.after_ref.label_ref, f32[8,128]{1,0:T(8,128)S(1)} %get-tuple-element.68.after_ref), custom_call_target="tpu_custom_call" | custom-call | flops 6899999744 | tf_op jit(solution)/shard_map/pallas_call | solution.py:319
  57.9 1.1 collective-permute-start.13
  60.1 1.4 collective-permute-start.14
  63.3 3.4 %shard_map.75 = (bf16[256,2048]{1,0:T(8,128)(2,1)}, f32[8,128]{1,0:T(8,128)S(1)}) custom-call(s32[1]{0:T(128)} %bitcast.me_ref, s32[4,1,2048]{2,1,0:T(1,128)S(1)} %reshape.11.after_ref.label_ref, f32[8,128]{1,0:T(8,128)S(1)} %get-tuple-element.80.after_ref), custom_call_target="tpu_custom_call" | custom-call | flops 6899999744 | tf_op jit(solution)/shard_map/pallas_call | solution.py:319
  69.2 2.4 %collective-permute-start.19 = (bf16[256,256]{1,0:T(8,128)(2,1)S(1)}, bf16[256,256]{1,0:T(8,128)(2,1)S(1)}, u32[]{:S(2)}, u32[]{:S(2)}) collective-permute-start(bf16[256,256]{1,0:T(8,128)(2,1)S(1)} %get-tuple-element.82.refs_1_.potential_ref), channel_id=1, source_target_pairs={{0,2},{1,3},{2,4},{3,5},{4,6},{5,7},{6,0},{7,1},{8,10},{9,11},{10,... | collective-permute-start | bytes 393224 | tf_op jit(solution)/shard_map/ppermute | solution.py:97
  71.6 2.1 %collective-permute-start.18 = (bf16[256,256]{1,0:T(8,128)(2,1)S(1)}, bf16[256,256]{1,0:T(8,128)(2,1)S(1)}, u32[]{:S(2)}, u32[]{:S(2)}) collective-permute-start(bf16[256,256]{1,0:T(8,128)(2,1)S(1)} %get-tuple-element.82.refs_1_.potential_ref), channel_id=1, source_target_pairs={{0,4},{1,5},{2,6},{3,7},{4,0},{5,1},{6,2},{7,3},{8,12},{9,13},{10,... | collective-permute-start | bytes 393224 | tf_op jit(solution)/shard_map/ppermute | solution.py:97
  74.1 3.4 %shard_map.77 = (bf16[256,2048]{1,0:T(8,128)(2,1)}, f32[8,128]{1,0:T(8,128)S(1)}) custom-call(s32[1]{0:T(128)} %bitcast.me_ref, s32[4,1,2048]{2,1,0:T(1,128)S(1)} %reshape.11.after_ref.label_ref, f32[8,128]{1,0:T(8,128)S(1)} %get-tuple-element.84.after_ref), custom_call_target="tpu_custom_call" | custom-call | flops 6899999744 | tf_op jit(solution)/shard_map/pallas_call | solution.py:319
  77.5 3.4 %shard_map.78 = (bf16[256,2048]{1,0:T(8,128)(2,1)}, f32[8,128]{1,0:T(8,128)S(1)}) custom-call(s32[1]{0:T(128)} %bitcast.me_ref, s32[4,1,2048]{2,1,0:T(1,128)S(1)} %reshape.11.after_ref.label_ref, f32[8,128]{1,0:T(8,128)S(1)} %get-tuple-element.85.after_ref), custom_call_target="tpu_custom_call" | custom-call | flops 6899999744 | tf_op jit(solution)/shard_map/pallas_call | solution.py:319
  82.3 1.4 collective-permute-done.16.refs_2_
  84.2 2.1 %collective-permute-start.23 = (bf16[256,256]{1,0:T(8,128)(2,1)S(1)}, bf16[256,256]{1,0:T(8,128)(2,1)S(1)}, u32[]{:S(2)}, u32[]{:S(2)}) collective-permute-start(bf16[256,256]{1,0:T(8,128)(2,1)S(1)} %get-tuple-element.93), channel_id=1, source_target_pairs={{0,17},{1,16},{2,19},{3,18},{4,21},{5,20},{6,23},{7,22},{8,25},{9,... | collective-permute-start | bytes 393224 | tf_op jit(solution)/shard_map/ppermute | solution.py:97
  91.4 2.0 %collective-permute-done.22.refs_1_ = bf16[256,256]{1,0:T(8,128)(2,1)S(1)} collective-permute-done((bf16[256,256]{1,0:T(8,128)(2,1)S(1)}, bf16[256,256]{1,0:T(8,128)(2,1)S(1)}, u32[]{:S(2)}, u32[]{:S(2)}) %collective-permute-start.22) | collective-permute-done | bytes 131104 | tf_op jit(solution)/shard_map/ppermute | solution.py:97
  94.0 1.4 shard_map.84
  95.5 3.2 %collective-permute-start.27 = (bf16[256,256]{1,0:T(8,128)(2,1)S(1)}, bf16[256,256]{1,0:T(8,128)(2,1)S(1)}, u32[]{:S(2)}, u32[]{:S(2)}) collective-permute-start(bf16[256,256]{1,0:T(8,128)(2,1)S(1)} %get-tuple-element.97.refs_2_), channel_id=1, source_target_pairs={{0,2},{1,3},{2,4},{3,5},{4,6},{5,7},{6,0},{7,1},{8,10},{9,11},{10,... | collective-permute-start | bytes 393224 | tf_op jit(solution)/shard_map/ppermute | solution.py:97
  99.7 1.3 collective-permute-start.25
  101.0 3.4 %shard_map.85 = (bf16[768,2048]{1,0:T(8,128)(2,1)}, f32[8,128]{1,0:T(8,128)S(1)}) custom-call(s32[1]{0:T(128)} %bitcast.me_ref, s32[32,8,128]{2,1,0:T(8,128)S(1)} %all-to-all-done.letter_ref, f32[8,128]{1,0:T(8,128)S(1)} %get-tuple-element.95.after_ref), custom_call_target="tpu_custom_call" | custom-call | flops 3449999872 | tf_op jit(solution)/shard_map/pallas_call | solution.py:319
  104.4 3.5 %shard_map.86 = (bf16[768,2048]{1,0:T(8,128)(2,1)}, f32[8,128]{1,0:T(8,128)S(1)}) custom-call(s32[1]{0:T(128)} %bitcast.me_ref, s32[32,8,128]{2,1,0:T(8,128)S(1)} %all-to-all-done.letter_ref, f32[8,128]{1,0:T(8,128)S(1)} %get-tuple-element.98.after_ref), custom_call_target="tpu_custom_call" | custom-call | flops 3449999872 | tf_op jit(solution)/shard_map/pallas_call | solution.py:319
  108.5 1.4 collective-permute-done.24.refs_3_
  109.9 1.1 shard_map.89
  112.9 1.7 %collective-permute-start.31 = (bf16[256,256]{1,0:T(8,128)(2,1)S(1)}, bf16[256,256]{1,0:T(8,128)(2,1)S(1)}, u32[]{:S(2)}, u32[]{:S(2)}) collective-permute-start(bf16[256,256]{1,0:T(8,128)(2,1)S(1)} %get-tuple-element.103), channel_id=1, source_target_pairs={{0,17},{1,16},{2,19},{3,18},{4,21},{5,20},{6,23},{7,22},{8,25},{9,... | collective-permute-start | bytes 393224 | tf_op jit(solution)/shard_map/ppermute | solution.py:97
  117.6 1.3 collective-permute-done.29.refs_0_
  119.9 1.5 %collective-permute-done.30.refs_1_ = bf16[256,256]{1,0:T(8,128)(2,1)S(1)} collective-permute-done((bf16[256,256]{1,0:T(8,128)(2,1)S(1)}, bf16[256,256]{1,0:T(8,128)(2,1)S(1)}, u32[]{:S(2)}, u32[]{:S(2)}) %collective-permute-start.30) | collective-permute-done | bytes 131104 | tf_op jit(solution)/shard_map/ppermute | solution.py:97
  121.4 1.4 shard_map.92
  122.9 2.9 %collective-permute-start.35 = (bf16[256,256]{1,0:T(8,128)(2,1)S(1)}, bf16[256,256]{1,0:T(8,128)(2,1)S(1)}, u32[]{:S(2)}, u32[]{:S(2)}) collective-permute-start(bf16[256,256]{1,0:T(8,128)(2,1)S(1)} %get-tuple-element.106.refs_1_), channel_id=1, source_target_pairs={{0,2},{1,3},{2,4},{3,5},{4,6},{5,7},{6,0},{7,1},{8,10},{9,11},{10,... | collective-permute-start | bytes 393224 | tf_op jit(solution)/shard_map/ppermute | solution.py:97
  125.8 1.7 %collective-permute-start.34 = (bf16[256,256]{1,0:T(8,128)(2,1)S(1)}, bf16[256,256]{1,0:T(8,128)(2,1)S(1)}, u32[]{:S(2)}, u32[]{:S(2)}) collective-permute-start(bf16[256,256]{1,0:T(8,128)(2,1)S(1)} %get-tuple-element.106.refs_1_), channel_id=1, source_target_pairs={{0,4},{1,5},{2,6},{3,7},{4,0},{5,1},{6,2},{7,3},{8,12},{9,13},{10,... | collective-permute-start | bytes 393224 | tf_op jit(solution)/shard_map/ppermute | solution.py:97
  128.1 3.2 %collective-permute-done.35.refs_2_ = bf16[256,256]{1,0:T(8,128)(2,1)S(1)} collective-permute-done((bf16[256,256]{1,0:T(8,128)(2,1)S(1)}, bf16[256,256]{1,0:T(8,128)(2,1)S(1)}, u32[]{:S(2)}, u32[]{:S(2)}) %collective-permute-start.35) | collective-permute-done | bytes 131104 | tf_op jit(solution)/shard_map/ppermute | solution.py:97
  131.4 4.1 %collective-permute-done.34.refs_1_ = bf16[256,256]{1,0:T(8,128)(2,1)S(1)} collective-permute-done((bf16[256,256]{1,0:T(8,128)(2,1)S(1)}, bf16[256,256]{1,0:T(8,128)(2,1)S(1)}, u32[]{:S(2)}, u32[]{:S(2)}) %collective-permute-start.34) | collective-permute-done | bytes 131104 | tf_op jit(solution)/shard_map/ppermute | solution.py:97
  136.2 1.4 collective-permute-done.32.refs_2_
  138.7 1.5 collective-permute-start.37
  141.3 1.4 collective-permute-start.39
  145.7 4.0 %collective-permute-done.37.refs_0_ = bf16[384,256]{1,0:T(8,128)(2,1)S(1)} collective-permute-done((bf16[384,256]{1,0:T(8,128)(2,1)S(1)}, bf16[384,256]{1,0:T(8,128)(2,1)S(1)}, u32[]{:S(2)}, u32[]{:S(2)}) %collective-permute-start.37) | collective-permute-done | bytes 196640 | tf_op jit(solution)/shard_map/ppermute | solution.py:97
  150.0 2.7 %collective-permute-done.38.refs_1_ = bf16[384,256]{1,0:T(8,128)(2,1)S(1)} collective-permute-done((bf16[384,256]{1,0:T(8,128)(2,1)S(1)}, bf16[384,256]{1,0:T(8,128)(2,1)S(1)}, u32[]{:S(2)}, u32[]{:S(2)}) %collective-permute-start.38) | collective-permute-done | bytes 196640 | tf_op jit(solution)/shard_map/ppermute | solution.py:97
  (99 shorter events, 37.4 us)
Async XLA Ops:
  0.6 9.9 %copy-start.2 = (bf16[384,256]{1,0:T(8,128)(2,1)S(1)}, bf16[384,256]{1,0:T(8,128)(2,1)}, u32[]{:S(2)}) copy-start(bf16[384,256]{1,0:T(8,128)(2,1)} %current_ref.1) | copy-start | bytes 589828
  3.3 15.1 %all-to-all-start = ((s32[32,8,128]{2,1,0:T(8,128)}), s32[32,8,128]{2,1,0:T(8,128)S(1)}, u32[]{:S(2)}, u32[]{:S(2)}) async-start(s32[32,8,128]{2,1,0:T(8,128)} %shard_map.59), calls=%async_computation | async-start | bytes 262144 | tf_op jit(solution)/shard_map/all_to_all | solution.py:566
  10.6 9.9 %collective-permute-start.3 = (bf16[384,256]{1,0:T(8,128)(2,1)S(1)}, bf16[384,256]{1,0:T(8,128)(2,1)S(1)}, u32[]{:S(2)}, u32[]{:S(2)}) collective-permute-start(bf16[384,256]{1,0:T(8,128)(2,1)S(1)} %copy-done.2), channel_id=1, source_target_pairs={{0,17},{1,16},{2,19},{3,18},{4,21},{5,20},{6,23},{7,22},{8,25},{9,... | collective-permute-start | bytes 589832 | tf_op jit(solution)/shard_map/ppermute | solution.py:97
  13.3 10.6 %collective-permute-start.2 = (bf16[384,256]{1,0:T(8,128)(2,1)S(1)}, bf16[384,256]{1,0:T(8,128)(2,1)S(1)}, u32[]{:S(2)}, u32[]{:S(2)}) collective-permute-start(bf16[384,256]{1,0:T(8,128)(2,1)S(1)} %copy-done.2), channel_id=1, source_target_pairs={{0,16},{1,17},{2,18},{3,19},{4,20},{5,21},{6,22},{7,23},{8,24},{9,... | collective-permute-start | bytes 589832 | tf_op jit(solution)/shard_map/ppermute | solution.py:97
  13.9 10.2 %collective-permute-start.1 = (bf16[384,256]{1,0:T(8,128)(2,1)S(1)}, bf16[384,256]{1,0:T(8,128)(2,1)S(1)}, u32[]{:S(2)}, u32[]{:S(2)}) collective-permute-start(bf16[384,256]{1,0:T(8,128)(2,1)S(1)} %copy-done.2), channel_id=1, source_target_pairs={{0,1},{1,0},{2,3},{3,2},{4,5},{5,4},{6,7},{7,6},{8,9},{9,8},{10,11... | collective-permute-start | bytes 589832 | tf_op jit(solution)/shard_map/ppermute | solution.py:97
  24.1 2.4 %collective-permute-start.4 = (bf16[1152,256]{1,0:T(8,128)(2,1)S(1)}, bf16[1152,256]{1,0:T(8,128)(2,1)S(1)}, u32[]{:S(2)}, u32[]{:S(2)}) collective-permute-start(bf16[1152,256]{1,0:T(8,128)(2,1)S(1)} %shard_map.61.refs_3_), channel_id=1, source_target_pairs={{0,8},{1,9},{2,10},{3,11},{4,12},{5,13},{6,14},{7,15},{8,0},{9,1},... | collective-permute-start | bytes 1769480 | tf_op jit(solution)/shard_map/ppermute | solution.py:97
  24.2 2.3 %collective-permute-start = (bf16[384,256]{1,0:T(8,128)(2,1)S(1)}, bf16[384,256]{1,0:T(8,128)(2,1)S(1)}, u32[]{:S(2)}, u32[]{:S(2)}) collective-permute-start(bf16[384,256]{1,0:T(8,128)(2,1)S(1)} %copy-done.2), channel_id=1, source_target_pairs={{0,8},{1,9},{2,10},{3,11},{4,12},{5,13},{6,14},{7,15},{8,0},{9,1},... | collective-permute-start | bytes 589832 | tf_op jit(solution)/shard_map/ppermute | solution.py:97
  27.7 12.9 %collective-permute-start.5 = (bf16[256,256]{1,0:T(8,128)(2,1)S(1)}, bf16[256,256]{1,0:T(8,128)(2,1)S(1)}, u32[]{:S(2)}, u32[]{:S(2)}) collective-permute-start(bf16[256,256]{1,0:T(8,128)(2,1)S(1)} %get-tuple-element.61), channel_id=1, source_target_pairs={{0,2},{1,3},{2,4},{3,5},{4,6},{5,7},{6,0},{7,1},{8,10},{9,11},{10,... | collective-permute-start | bytes 393224 | tf_op jit(solution)/shard_map/ppermute | solution.py:97
  30.3 10.5 %collective-permute-start.6 = (bf16[256,256]{1,0:T(8,128)(2,1)S(1)}, bf16[256,256]{1,0:T(8,128)(2,1)S(1)}, u32[]{:S(2)}, u32[]{:S(2)}) collective-permute-start(bf16[256,256]{1,0:T(8,128)(2,1)S(1)} %get-tuple-element.62), channel_id=1, source_target_pairs={{0,4},{1,5},{2,6},{3,7},{4,0},{5,1},{6,2},{7,3},{8,12},{9,13},{10,... | collective-permute-start | bytes 393224 | tf_op jit(solution)/shard_map/ppermute | solution.py:97
  33.4 7.7 %collective-permute-start.7 = (bf16[256,256]{1,0:T(8,128)(2,1)S(1)}, bf16[256,256]{1,0:T(8,128)(2,1)S(1)}, u32[]{:S(2)}, u32[]{:S(2)}) collective-permute-start(bf16[256,256]{1,0:T(8,128)(2,1)S(1)} %get-tuple-element.63), channel_id=1, source_target_pairs={{0,6},{1,7},{2,0},{3,1},{4,2},{5,3},{6,4},{7,5},{8,14},{9,15},{10,... | collective-permute-start | bytes 393224 | tf_op jit(solution)/shard_map/ppermute | solution.py:97
  41.3 13.4 %collective-permute-start.11 = (bf16[256,256]{1,0:T(8,128)(2,1)S(1)}, bf16[256,256]{1,0:T(8,128)(2,1)S(1)}, u32[]{:S(2)}, u32[]{:S(2)}) collective-permute-start(bf16[256,256]{1,0:T(8,128)(2,1)S(1)} %get-tuple-element.72.refs_2_), channel_id=1, source_target_pairs={{0,2},{1,3},{2,4},{3,5},{4,6},{5,7},{6,0},{7,1},{8,10},{9,11},{10,... | collective-permute-start | bytes 393224 | tf_op jit(solution)/shard_map/ppermute | solution.py:97
  44.2 10.5 %collective-permute-start.10 = (bf16[256,256]{1,0:T(8,128)(2,1)S(1)}, bf16[256,256]{1,0:T(8,128)(2,1)S(1)}, u32[]{:S(2)}, u32[]{:S(2)}) collective-permute-start(bf16[256,256]{1,0:T(8,128)(2,1)S(1)} %get-tuple-element.72.refs_2_), channel_id=1, source_target_pairs={{0,4},{1,5},{2,6},{3,7},{4,0},{5,1},{6,2},{7,3},{8,12},{9,13},{10,... | collective-permute-start | bytes 393224 | tf_op jit(solution)/shard_map/ppermute | solution.py:97
  45.5 9.2 %collective-permute-start.9 = (bf16[256,256]{1,0:T(8,128)(2,1)S(1)}, bf16[256,256]{1,0:T(8,128)(2,1)S(1)}, u32[]{:S(2)}, u32[]{:S(2)}) collective-permute-start(bf16[256,256]{1,0:T(8,128)(2,1)S(1)} %get-tuple-element.72.refs_2_), channel_id=1, source_target_pairs={{0,6},{1,7},{2,0},{3,1},{4,2},{5,3},{6,4},{7,5},{8,14},{9,15},{10,... | collective-permute-start | bytes 393224 | tf_op jit(solution)/shard_map/ppermute | solution.py:97
  54.8 2.0 %collective-permute-start.12 = (bf16[768,256]{1,0:T(8,128)(2,1)S(1)}, bf16[768,256]{1,0:T(8,128)(2,1)S(1)}, u32[]{:S(2)}, u32[]{:S(2)}) collective-permute-start(bf16[768,256]{1,0:T(8,128)(2,1)S(1)} %shard_map.70.refs_4_), channel_id=1, source_target_pairs={{0,8},{1,9},{2,10},{3,11},{4,12},{5,13},{6,14},{7,15},{8,0},{9,1},... | collective-permute-start | bytes 1179656 | tf_op jit(solution)/shard_map/ppermute | solution.py:97
  54.8 1.9 %collective-permute-start.8 = (bf16[256,256]{1,0:T(8,128)(2,1)S(1)}, bf16[256,256]{1,0:T(8,128)(2,1)S(1)}, u32[]{:S(2)}, u32[]{:S(2)}) collective-permute-start(bf16[256,256]{1,0:T(8,128)(2,1)S(1)} %get-tuple-element.72.refs_2_), channel_id=1, source_target_pairs={{0,8},{1,9},{2,10},{3,11},{4,12},{5,13},{6,14},{7,15},{8,0},{9,1},... | collective-permute-start | bytes 393224 | tf_op jit(solution)/shard_map/ppermute | solution.py:97
  57.9 9.9 %collective-permute-start.13 = (bf16[256,256]{1,0:T(8,128)(2,1)S(1)}, bf16[256,256]{1,0:T(8,128)(2,1)S(1)}, u32[]{:S(2)}, u32[]{:S(2)}) collective-permute-start(bf16[256,256]{1,0:T(8,128)(2,1)S(1)} %get-tuple-element.75), channel_id=1, source_target_pairs={{0,1},{1,0},{2,3},{3,2},{4,5},{5,4},{6,7},{7,6},{8,9},{9,8},{10,11... | collective-permute-start | bytes 393224 | tf_op jit(solution)/shard_map/ppermute | solution.py:97
  60.1 7.6 %collective-permute-start.14 = (bf16[256,256]{1,0:T(8,128)(2,1)S(1)}, bf16[256,256]{1,0:T(8,128)(2,1)S(1)}, u32[]{:S(2)}, u32[]{:S(2)}) collective-permute-start(bf16[256,256]{1,0:T(8,128)(2,1)S(1)} %get-tuple-element.78), channel_id=1, source_target_pairs={{0,16},{1,17},{2,18},{3,19},{4,20},{5,21},{6,22},{7,23},{8,24},{9,... | collective-permute-start | bytes 393224 | tf_op jit(solution)/shard_map/ppermute | solution.py:97
  62.3 6.3 %collective-permute-start.15 = (bf16[256,256]{1,0:T(8,128)(2,1)S(1)}, bf16[256,256]{1,0:T(8,128)(2,1)S(1)}, u32[]{:S(2)}, u32[]{:S(2)}) collective-permute-start(bf16[256,256]{1,0:T(8,128)(2,1)S(1)} %get-tuple-element.79), channel_id=1, source_target_pairs={{0,17},{1,16},{2,19},{3,18},{4,21},{5,20},{6,23},{7,22},{8,25},{9,... | collective-permute-start | bytes 393224 | tf_op jit(solution)/shard_map/ppermute | solution.py:97
  69.2 11.6 %collective-permute-start.19 = (bf16[256,256]{1,0:T(8,128)(2,1)S(1)}, bf16[256,256]{1,0:T(8,128)(2,1)S(1)}, u32[]{:S(2)}, u32[]{:S(2)}) collective-permute-start(bf16[256,256]{1,0:T(8,128)(2,1)S(1)} %get-tuple-element.82.refs_1_.potential_ref), channel_id=1, source_target_pairs={{0,2},{1,3},{2,4},{3,5},{4,6},{5,7},{6,0},{7,1},{8,10},{9,11},{10,... | collective-permute-start | bytes 393224 | tf_op jit(solution)/shard_map/ppermute | solution.py:97
  71.6 9.9 %collective-permute-start.18 = (bf16[256,256]{1,0:T(8,128)(2,1)S(1)}, bf16[256,256]{1,0:T(8,128)(2,1)S(1)}, u32[]{:S(2)}, u32[]{:S(2)}) collective-permute-start(bf16[256,256]{1,0:T(8,128)(2,1)S(1)} %get-tuple-element.82.refs_1_.potential_ref), channel_id=1, source_target_pairs={{0,4},{1,5},{2,6},{3,7},{4,0},{5,1},{6,2},{7,3},{8,12},{9,13},{10,... | collective-permute-start | bytes 393224 | tf_op jit(solution)/shard_map/ppermute | solution.py:97
  73.8 7.9 %collective-permute-start.17 = (bf16[256,256]{1,0:T(8,128)(2,1)S(1)}, bf16[256,256]{1,0:T(8,128)(2,1)S(1)}, u32[]{:S(2)}, u32[]{:S(2)}) collective-permute-start(bf16[256,256]{1,0:T(8,128)(2,1)S(1)} %get-tuple-element.82.refs_1_.potential_ref), channel_id=1, source_target_pairs={{0,6},{1,7},{2,0},{3,1},{4,2},{5,3},{6,4},{7,5},{8,14},{9,15},{10,... | collective-permute-start | bytes 393224 | tf_op jit(solution)/shard_map/ppermute | solution.py:97
  80.9 2.9 %copy-start.8 = (bf16[256,2048]{1,0:T(8,128)(2,1)S(1)}, bf16[256,2048]{1,0:T(8,128)(2,1)}, u32[]{:S(2)}) copy-start(bf16[256,2048]{1,0:T(8,128)(2,1)} %get-tuple-element.92.refs_0_) | copy-start | bytes 3145732
  81.7 4.5 %copy-start.7 = (bf16[256,2048]{1,0:T(8,128)(2,1)S(1)}, bf16[256,2048]{1,0:T(8,128)(2,1)}, u32[]{:S(2)}) copy-start(bf16[256,2048]{1,0:T(8,128)(2,1)} %get-tuple-element.90.refs_0_) | copy-start | bytes 3145732
  81.8 2.0 %collective-permute-start.20 = (bf16[768,256]{1,0:T(8,128)(2,1)S(1)}, bf16[768,256]{1,0:T(8,128)(2,1)S(1)}, u32[]{:S(2)}, u32[]{:S(2)}) collective-permute-start(bf16[768,256]{1,0:T(8,128)(2,1)S(1)} %shard_map.79.refs_3_), channel_id=1, source_target_pairs={{0,8},{1,9},{2,10},{3,11},{4,12},{5,13},{6,14},{7,15},{8,0},{9,1},... | collective-permute-start | bytes 1179656 | tf_op jit(solution)/shard_map/ppermute | solution.py:97
  81.8 1.9 %collective-permute-start.16 = (bf16[256,256]{1,0:T(8,128)(2,1)S(1)}, bf16[256,256]{1,0:T(8,128)(2,1)S(1)}, u32[]{:S(2)}, u32[]{:S(2)}) collective-permute-start(bf16[256,256]{1,0:T(8,128)(2,1)S(1)} %get-tuple-element.82.refs_1_.potential_ref), channel_id=1, source_target_pairs={{0,8},{1,9},{2,10},{3,11},{4,12},{5,13},{6,14},{7,15},{8,0},{9,1},... | collective-permute-start | bytes 393224 | tf_op jit(solution)/shard_map/ppermute | solution.py:97
  83.7 4.2 %copy-start.6 = (bf16[256,2048]{1,0:T(8,128)(2,1)S(1)}, bf16[256,2048]{1,0:T(8,128)(2,1)}, u32[]{:S(2)}) copy-start(bf16[256,2048]{1,0:T(8,128)(2,1)} %get-tuple-element.88.refs_0_) | copy-start | bytes 3145732
  84.2 7.3 %collective-permute-start.23 = (bf16[256,256]{1,0:T(8,128)(2,1)S(1)}, bf16[256,256]{1,0:T(8,128)(2,1)S(1)}, u32[]{:S(2)}, u32[]{:S(2)}) collective-permute-start(bf16[256,256]{1,0:T(8,128)(2,1)S(1)} %get-tuple-element.93), channel_id=1, source_target_pairs={{0,17},{1,16},{2,19},{3,18},{4,21},{5,20},{6,23},{7,22},{8,25},{9,... | collective-permute-start | bytes 393224 | tf_op jit(solution)/shard_map/ppermute | solution.py:97
  86.3 3.2 %copy-start.5 = (bf16[256,2048]{1,0:T(8,128)(2,1)S(1)}, bf16[256,2048]{1,0:T(8,128)(2,1)}, u32[]{:S(2)}) copy-start(bf16[256,2048]{1,0:T(8,128)(2,1)} %get-tuple-element.83.refs_0_) | copy-start | bytes 3145732
  87.1 6.3 %collective-permute-start.22 = (bf16[256,256]{1,0:T(8,128)(2,1)S(1)}, bf16[256,256]{1,0:T(8,128)(2,1)S(1)}, u32[]{:S(2)}, u32[]{:S(2)}) collective-permute-start(bf16[256,256]{1,0:T(8,128)(2,1)S(1)} %get-tuple-element.91), channel_id=1, source_target_pairs={{0,16},{1,17},{2,18},{3,19},{4,20},{5,21},{6,22},{7,23},{8,24},{9,... | collective-permute-start | bytes 393224 | tf_op jit(solution)/shard_map/ppermute | solution.py:97
  88.8 5.2 %collective-permute-start.21 = (bf16[256,256]{1,0:T(8,128)(2,1)S(1)}, bf16[256,256]{1,0:T(8,128)(2,1)S(1)}, u32[]{:S(2)}, u32[]{:S(2)}) collective-permute-start(bf16[256,256]{1,0:T(8,128)(2,1)S(1)} %get-tuple-element.89), channel_id=1, source_target_pairs={{0,1},{1,0},{2,3},{3,2},{4,5},{5,4},{6,7},{7,6},{8,9},{9,8},{10,11... | collective-permute-start | bytes 393224 | tf_op jit(solution)/shard_map/ppermute | solution.py:97
  95.5 12.4 %collective-permute-start.27 = (bf16[256,256]{1,0:T(8,128)(2,1)S(1)}, bf16[256,256]{1,0:T(8,128)(2,1)S(1)}, u32[]{:S(2)}, u32[]{:S(2)}) collective-permute-start(bf16[256,256]{1,0:T(8,128)(2,1)S(1)} %get-tuple-element.97.refs_2_), channel_id=1, source_target_pairs={{0,2},{1,3},{2,4},{3,5},{4,6},{5,7},{6,0},{7,1},{8,10},{9,11},{10,... | collective-permute-start | bytes 393224 | tf_op jit(solution)/shard_map/ppermute | solution.py:97
  98.6 9.3 %collective-permute-start.26 = (bf16[256,256]{1,0:T(8,128)(2,1)S(1)}, bf16[256,256]{1,0:T(8,128)(2,1)S(1)}, u32[]{:S(2)}, u32[]{:S(2)}) collective-permute-start(bf16[256,256]{1,0:T(8,128)(2,1)S(1)} %get-tuple-element.97.refs_2_), channel_id=1, source_target_pairs={{0,4},{1,5},{2,6},{3,7},{4,0},{5,1},{6,2},{7,3},{8,12},{9,13},{10,... | collective-permute-start | bytes 393224 | tf_op jit(solution)/shard_map/ppermute | solution.py:97
  99.7 8.2 %collective-permute-start.25 = (bf16[256,256]{1,0:T(8,128)(2,1)S(1)}, bf16[256,256]{1,0:T(8,128)(2,1)S(1)}, u32[]{:S(2)}, u32[]{:S(2)}) collective-permute-start(bf16[256,256]{1,0:T(8,128)(2,1)S(1)} %get-tuple-element.97.refs_2_), channel_id=1, source_target_pairs={{0,6},{1,7},{2,0},{3,1},{4,2},{5,3},{6,4},{7,5},{8,14},{9,15},{10,... | collective-permute-start | bytes 393224 | tf_op jit(solution)/shard_map/ppermute | solution.py:97
  107.9 2.0 %collective-permute-start.28 = (bf16[768,256]{1,0:T(8,128)(2,1)S(1)}, bf16[768,256]{1,0:T(8,128)(2,1)S(1)}, u32[]{:S(2)}, u32[]{:S(2)}) collective-permute-start(bf16[768,256]{1,0:T(8,128)(2,1)S(1)} %shard_map.87.refs_4_), channel_id=1, source_target_pairs={{0,8},{1,9},{2,10},{3,11},{4,12},{5,13},{6,14},{7,15},{8,0},{9,1},... | collective-permute-start | bytes 1179656 | tf_op jit(solution)/shard_map/ppermute | solution.py:97
  108.0 1.9 %collective-permute-start.24 = (bf16[256,256]{1,0:T(8,128)(2,1)S(1)}, bf16[256,256]{1,0:T(8,128)(2,1)S(1)}, u32[]{:S(2)}, u32[]{:S(2)}) collective-permute-start(bf16[256,256]{1,0:T(8,128)(2,1)S(1)} %get-tuple-element.97.refs_2_), channel_id=1, source_target_pairs={{0,8},{1,9},{2,10},{3,11},{4,12},{5,13},{6,14},{7,15},{8,0},{9,1},... | collective-permute-start | bytes 393224 | tf_op jit(solution)/shard_map/ppermute | solution.py:97
  111.1 7.9 %collective-permute-start.29 = (bf16[256,256]{1,0:T(8,128)(2,1)S(1)}, bf16[256,256]{1,0:T(8,128)(2,1)S(1)}, u32[]{:S(2)}, u32[]{:S(2)}) collective-permute-start(bf16[256,256]{1,0:T(8,128)(2,1)S(1)} %get-tuple-element.101), channel_id=1, source_target_pairs={{0,1},{1,0},{2,3},{3,2},{4,5},{5,4},{6,7},{7,6},{8,9},{9,8},{10,11... | collective-permute-start | bytes 393224 | tf_op jit(solution)/shard_map/ppermute | solution.py:97
  112.9 7.0 %collective-permute-start.31 = (bf16[256,256]{1,0:T(8,128)(2,1)S(1)}, bf16[256,256]{1,0:T(8,128)(2,1)S(1)}, u32[]{:S(2)}, u32[]{:S(2)}) collective-permute-start(bf16[256,256]{1,0:T(8,128)(2,1)S(1)} %get-tuple-element.103), channel_id=1, source_target_pairs={{0,17},{1,16},{2,19},{3,18},{4,21},{5,20},{6,23},{7,22},{8,25},{9,... | collective-permute-start | bytes 393224 | tf_op jit(solution)/shard_map/ppermute | solution.py:97
  115.7 5.7 %collective-permute-start.30 = (bf16[256,256]{1,0:T(8,128)(2,1)S(1)}, bf16[256,256]{1,0:T(8,128)(2,1)S(1)}, u32[]{:S(2)}, u32[]{:S(2)}) collective-permute-start(bf16[256,256]{1,0:T(8,128)(2,1)S(1)} %get-tuple-element.102), channel_id=1, source_target_pairs={{0,16},{1,17},{2,18},{3,19},{4,20},{5,21},{6,22},{7,23},{8,24},{9,... | collective-permute-start | bytes 393224 | tf_op jit(solution)/shard_map/ppermute | solution.py:97
  121.4 16.2 %copy-start = (bf16[768,2048]{1,0:T(8,128)(2,1)S(1)}, bf16[768,2048]{1,0:T(8,128)(2,1)}, u32[]{:S(2)}) copy-start(bf16[768,2048]{1,0:T(8,128)(2,1)} %get-tuple-element.96.refs_0_) | copy-start | bytes 9437188
  122.9 8.5 %collective-permute-start.35 = (bf16[256,256]{1,0:T(8,128)(2,1)S(1)}, bf16[256,256]{1,0:T(8,128)(2,1)S(1)}, u32[]{:S(2)}, u32[]{:S(2)}) collective-permute-start(bf16[256,256]{1,0:T(8,128)(2,1)S(1)} %get-tuple-element.106.refs_1_), channel_id=1, source_target_pairs={{0,2},{1,3},{2,4},{3,5},{4,6},{5,7},{6,0},{7,1},{8,10},{9,11},{10,... | collective-permute-start | bytes 393224 | tf_op jit(solution)/shard_map/ppermute | solution.py:97
  125.8 9.7 %collective-permute-start.34 = (bf16[256,256]{1,0:T(8,128)(2,1)S(1)}, bf16[256,256]{1,0:T(8,128)(2,1)S(1)}, u32[]{:S(2)}, u32[]{:S(2)}) collective-permute-start(bf16[256,256]{1,0:T(8,128)(2,1)S(1)} %get-tuple-element.106.refs_1_), channel_id=1, source_target_pairs={{0,4},{1,5},{2,6},{3,7},{4,0},{5,1},{6,2},{7,3},{8,12},{9,13},{10,... | collective-permute-start | bytes 393224 | tf_op jit(solution)/shard_map/ppermute | solution.py:97
  127.5 8.1 %collective-permute-start.33 = (bf16[256,256]{1,0:T(8,128)(2,1)S(1)}, bf16[256,256]{1,0:T(8,128)(2,1)S(1)}, u32[]{:S(2)}, u32[]{:S(2)}) collective-permute-start(bf16[256,256]{1,0:T(8,128)(2,1)S(1)} %get-tuple-element.106.refs_1_), channel_id=1, source_target_pairs={{0,6},{1,7},{2,0},{3,1},{4,2},{5,3},{6,4},{7,5},{8,14},{9,15},{10,... | collective-permute-start | bytes 393224 | tf_op jit(solution)/shard_map/ppermute | solution.py:97
  135.6 2.0 %collective-permute-start.36 = (bf16[768,256]{1,0:T(8,128)(2,1)S(1)}, bf16[768,256]{1,0:T(8,128)(2,1)S(1)}, u32[]{:S(2)}, u32[]{:S(2)}) collective-permute-start(bf16[768,256]{1,0:T(8,128)(2,1)S(1)} %shard_map.93.refs_3_), channel_id=1, source_target_pairs={{0,8},{1,9},{2,10},{3,11},{4,12},{5,13},{6,14},{7,15},{8,0},{9,1},... | collective-permute-start | bytes 1179656 | tf_op jit(solution)/shard_map/ppermute | solution.py:97
  135.7 1.9 %collective-permute-start.32 = (bf16[256,256]{1,0:T(8,128)(2,1)S(1)}, bf16[256,256]{1,0:T(8,128)(2,1)S(1)}, u32[]{:S(2)}, u32[]{:S(2)}) collective-permute-start(bf16[256,256]{1,0:T(8,128)(2,1)S(1)} %get-tuple-element.106.refs_1_), channel_id=1, source_target_pairs={{0,8},{1,9},{2,10},{3,11},{4,12},{5,13},{6,14},{7,15},{8,0},{9,1},... | collective-permute-start | bytes 393224 | tf_op jit(solution)/shard_map/ppermute | solution.py:97
  137.6 2.6 %copy-start.1 = (bf16[768,2048]{1,0:T(8,128)(2,1)S(1)}, bf16[768,2048]{1,0:T(8,128)(2,1)}, u32[]{:S(2)}) copy-start(bf16[768,2048]{1,0:T(8,128)(2,1)} %get-tuple-element.110.refs_0_) | copy-start | bytes 9437188
  138.7 11.0 %collective-permute-start.37 = (bf16[384,256]{1,0:T(8,128)(2,1)S(1)}, bf16[384,256]{1,0:T(8,128)(2,1)S(1)}, u32[]{:S(2)}, u32[]{:S(2)}) collective-permute-start(bf16[384,256]{1,0:T(8,128)(2,1)S(1)} %get-tuple-element.109), channel_id=1, source_target_pairs={{0,1},{1,0},{2,3},{3,2},{4,5},{5,4},{6,7},{7,6},{8,9},{9,8},{10,11... | collective-permute-start | bytes 589832 | tf_op jit(solution)/shard_map/ppermute | solution.py:97
  141.3 8.7 %collective-permute-start.39 = (bf16[384,256]{1,0:T(8,128)(2,1)S(1)}, bf16[384,256]{1,0:T(8,128)(2,1)S(1)}, u32[]{:S(2)}, u32[]{:S(2)}) collective-permute-start(bf16[384,256]{1,0:T(8,128)(2,1)S(1)} %get-tuple-element.112), channel_id=1, source_target_pairs={{0,17},{1,16},{2,19},{3,18},{4,21},{5,20},{6,23},{7,22},{8,25},{9,... | collective-permute-start | bytes 589832 | tf_op jit(solution)/shard_map/ppermute | solution.py:97
  143.7 9.0 %collective-permute-start.38 = (bf16[384,256]{1,0:T(8,128)(2,1)S(1)}, bf16[384,256]{1,0:T(8,128)(2,1)S(1)}, u32[]{:S(2)}, u32[]{:S(2)}) collective-permute-start(bf16[384,256]{1,0:T(8,128)(2,1)S(1)} %get-tuple-element.111), channel_id=1, source_target_pairs={{0,16},{1,17},{2,18},{3,19},{4,20},{5,21},{6,22},{7,23},{8,24},{9,... | collective-permute-start | bytes 589832 | tf_op jit(solution)/shard_map/ppermute | solution.py:97
  (3 other events, 2.1 us)
